TPU v7x, 32 devices: a whole 2x2x4 slice. The times are simulated.
32 devices in a mesh: gx: 8 (over z, core), gy: 4 (over y, x).
Axes of the slice: x: 2, y: 2, z: 4, core: 2. Of those that a mesh axis runs over, the one named last changes fastest.
Arguments:
- velocity: float32 [4, 2, 512, 512], P(None, None, 'gx', 'gy'), may hold values from -6 to 6
- marker_cell: int32 [3, 8, 4, 2048], P(None, 'gx', 'gy'), may hold values from 0 to 511, as said below
- marker_frac: float32 [2, 8, 4, 2048], P(None, 'gx', 'gy'), may hold values from 0 to 1
- marker_force: float32 [2, 8, 4, 2048], P(None, 'gx', 'gy'), may hold values from -6 to 6
- fish_owner: int32 [48], replicated, may hold values from 0 to 31, as said below
Outputs:
- velocity_next: float32 [4, 2, 512, 512], P(None, None, 'gx', 'gy')
- marker_velocity: float32 [2, 8, 4, 2048], P(None, 'gx', 'gy')
Inputs may be any that keep to these rules, and one draw needn't show every extreme that they name: `fish_owner`: device number i * 4 + j is the one at index i of gx and j of gy. No device holds more than 2 fish, and some device holds exactly 2. `marker_cell`: components are x cell, y cell and level. For the device at index i of gx and j of gy, every slot's x cell lies cyclically modulo 512 from i * 64 - 15 to (i + 1) * 64 + 13 and its y cell from j * 128 - 15 to (j + 1) * 128 + 13; on every device both ends are reached. A device holding k fish has their markers in slots 0 to k * 1024 - 1; its other slots are unused.
All inputs are finite; a program needn't handle non-finite values.
Results may differ from a plain program's by a relative error of at most 0.0025.
Values may be sent and summed in bfloat16 or wider, within the bound.
No kernel may reach another device: no remote copies, remote signals or barrier semaphores. Data moves between devices by JAX's collectives and lax.ppermute only.
A program may use at most 64 MiB of HBM per device.

v0:
```python
import jax
import jax.numpy as jnp
from jax import lax
from jax.sharding import PartitionSpec as P

MARGIN = 16
FISH_MARK = 1024


COURANT = 0.25
VISCOUS = 1.5


def extended(shard, sides, width):
    for axis, dim in sides:
        size, length = (lax.axis_size(axis), shard.shape[dim])
        up = [(i, (i + 1) % size) for i in range(size)]
        down = [(j, i) for i, j in up]
        last = lax.slice_in_dim(shard, length - width, length, axis=dim)
        initial = lax.slice_in_dim(shard, 0, width, axis=dim)
        before = lax.ppermute(last, axis, up)
        after = lax.ppermute(initial, axis, down)
        shard = jnp.concatenate([before, shard, after], axis=dim)
    return shard


def kernel_weight(offset):
    return jnp.where(jnp.abs(offset) < 2.0, 0.25 * (1.0 + jnp.cos(0.5 * jnp.pi * offset)), 0.0)


def advect(padded):
    center = padded[:, :, 1:-1, 1:-1]
    speed_x = COURANT * center[:, 0:1]
    speed_y = COURANT * center[:, 1:2]
    back_x = center - padded[:, :, :-2, 1:-1]
    fore_x = padded[:, :, 2:, 1:-1] - center
    back_y = center - padded[:, :, 1:-1, :-2]
    fore_y = padded[:, :, 1:-1, 2:] - center
    change = jnp.maximum(speed_x, 0.0) * back_x + jnp.minimum(speed_x, 0.0) * fore_x
    change = change + jnp.maximum(speed_y, 0.0) * back_y + jnp.minimum(speed_y, 0.0) * fore_y
    return center - change


def smooth(source, padded):
    center = padded[:, :, 1:-1, 1:-1]
    above = jnp.concatenate([center[1:], center[-1:]], axis=0)
    below = jnp.concatenate([center[:1], center[:-1]], axis=0)
    summed = padded[:, :, 2:, 1:-1] + padded[:, :, :-2, 1:-1]
    summed = summed + padded[:, :, 1:-1, 2:] + padded[:, :, 1:-1, :-2]
    summed = summed + above + below
    return (source + VISCOUS * summed) / (1.0 + 6.0 * VISCOUS)


def wrapped(offset, extent, width):
    middle = float(width // 2)
    half_extent = float(extent // 2)
    return jnp.mod(offset - middle + half_extent, float(extent)) - half_extent + middle


def marker_weights(markers, low_x, low_y, width_x, width_y, extent_x, extent_y, levels):
    offset_x = wrapped(markers[0] - low_x, extent_x, width_x)
    offset_y = wrapped(markers[1] - low_y, extent_y, width_y)
    cells_x = jnp.arange(width_x, dtype=jnp.float32)
    cells_y = jnp.arange(width_y, dtype=jnp.float32)
    weight_x = kernel_weight(cells_x[None, :] - offset_x[:, None] - markers[3][:, None])
    weight_y = kernel_weight(cells_y[None, :] - offset_y[:, None] - markers[4][:, None]).astype(
        jnp.bfloat16
    )
    level_hot = (markers[2][:, None] == jnp.arange(levels, dtype=jnp.float32)[None, :]).astype(
        jnp.float32
    )
    return (weight_x, weight_y, level_hot)


def spread_block(markers, alive_mask, low_x, low_y, width_x, width_y, extent_x, extent_y, levels):
    weight_x, weight_y, level_hot = marker_weights(
        markers, low_x, low_y, width_x, width_y, extent_x, extent_y, levels
    )
    force = jnp.transpose(markers[5:7] * alive_mask[None, :])
    left = level_hot[:, :, None, None] * (force[:, None, :, None] * weight_x[:, None, None, :])
    left = left.astype(jnp.bfloat16).reshape(markers.shape[1], levels * 2 * width_x)
    return lax.dot_general(
        left, weight_y, (((0,), (0,)), ((), ())), preferred_element_type=jnp.float32
    )


def spread_all(markers, alive_count, low_x, low_y, width_x, width_y, extent_x, extent_y, levels):
    slots = markers.shape[1]
    block_size = min(256, slots)
    block_count = (alive_count + block_size - 1) // block_size

    def spread_advance(block_index, summed):
        first_slot = block_index * block_size
        marker_piece = lax.dynamic_slice_in_dim(markers, first_slot, block_size, 1)
        alive_mask = (first_slot + jnp.arange(block_size, dtype=jnp.int32) < alive_count).astype(
            jnp.float32
        )
        return summed + spread_block(
            marker_piece, alive_mask, low_x, low_y, width_x, width_y, extent_x, extent_y, levels
        )

    initial = jnp.zeros((levels * 2 * width_x, width_y), jnp.float32)
    return lax.fori_loop(0, block_count, spread_advance, initial)


def sample_block(velocity_tile, markers, low_x, low_y, extent_x, extent_y):
    levels, comps, width_x, width_y = velocity_tile.shape
    weight_x, weight_y, level_hot = marker_weights(
        markers, low_x, low_y, width_x, width_y, extent_x, extent_y, levels
    )
    flat_tile = velocity_tile.reshape(levels * comps * width_x, width_y)
    partial_sums = lax.dot_general(
        flat_tile, weight_y, (((1,), (1,)), ((), ())), preferred_element_type=jnp.float32
    )
    partial_sums = partial_sums.reshape(levels, comps, width_x, markers.shape[1])
    picked = jnp.sum(partial_sums * jnp.transpose(level_hot)[:, None, None, :], axis=0)
    return jnp.sum(picked * jnp.transpose(weight_x)[None, :, :], axis=1)


def sample_all(velocity_tile, markers, alive_count, low_x, low_y, extent_x, extent_y):
    slots = markers.shape[1]
    block_size = min(256, slots)
    block_count = (alive_count + block_size - 1) // block_size

    def sample_advance(block_index, result):
        first_slot = block_index * block_size
        marker_piece = lax.dynamic_slice_in_dim(markers, first_slot, block_size, 1)
        alive_mask = (first_slot + jnp.arange(block_size, dtype=jnp.int32) < alive_count).astype(
            jnp.float32
        )
        values = (
            sample_block(velocity_tile, marker_piece, low_x, low_y, extent_x, extent_y)
            * alive_mask[None, :]
        )
        return lax.dynamic_update_slice_in_dim(result, values, first_slot, 1)

    return lax.fori_loop(0, block_count, sample_advance, jnp.zeros((2, slots), jnp.float32))


def body(velocity, marker_cell, marker_frac, marker_force, fish_owner):
    levels, comps, cells_x, cells_y = velocity.shape
    count_x = lax.axis_size("gx")
    count_y = lax.axis_size("gy")
    extent_x = cells_x * count_x
    extent_y = cells_y * count_y
    grid_row = lax.axis_index("gx")
    grid_col = lax.axis_index("gy")
    anchor_x = (grid_row * cells_x).astype(jnp.float32)
    anchor_y = (grid_col * cells_y).astype(jnp.float32)
    slots = marker_cell.shape[3]
    packed = jnp.concatenate([marker_cell.astype(jnp.float32), marker_frac, marker_force], axis=0)
    own_markers = packed.reshape(7, slots)
    own_count = FISH_MARK * jnp.sum((fish_owner == grid_row * count_y + grid_col).astype(jnp.int32))
    wide_x = cells_x + 2 * MARGIN
    wide_y = cells_y + 2 * MARGIN
    spread = spread_all(
        own_markers,
        own_count,
        anchor_x - MARGIN,
        anchor_y - MARGIN,
        wide_x,
        wide_y,
        extent_x,
        extent_y,
        levels,
    )
    spread = spread.reshape(levels, comps, wide_x, wide_y)
    edges_x = jnp.concatenate([spread[:, :, :MARGIN], spread[:, :, cells_x + MARGIN :]], axis=2)
    received_x = extended(edges_x, (("gx", 2),), MARGIN)
    inner_x = spread[:, :, MARGIN : MARGIN + cells_x]
    inner_x = inner_x + jnp.pad(
        received_x[:, :, :MARGIN], ((0, 0), (0, 0), (0, cells_x - MARGIN), (0, 0))
    )
    inner_x = inner_x + jnp.pad(
        received_x[:, :, 3 * MARGIN :], ((0, 0), (0, 0), (cells_x - MARGIN, 0), (0, 0))
    )
    edges_y = jnp.concatenate(
        [inner_x[:, :, :, :MARGIN], inner_x[:, :, :, cells_y + MARGIN :]], axis=3
    )
    received_y = extended(edges_y, (("gy", 3),), MARGIN)
    forcing = inner_x[:, :, :, MARGIN : MARGIN + cells_y]
    forcing = forcing + jnp.pad(
        received_y[:, :, :, :MARGIN], ((0, 0), (0, 0), (0, 0), (0, cells_y - MARGIN))
    )
    forcing = forcing + jnp.pad(
        received_y[:, :, :, 3 * MARGIN :], ((0, 0), (0, 0), (0, 0), (cells_y - MARGIN, 0))
    )
    moved = velocity + forcing
    deep_field = extended(moved, (("gx", 2), ("gy", 3)), 3)
    carried = advect(deep_field)
    first_sweep = smooth(carried[:, :, 1:-1, 1:-1], carried)
    smoothed = smooth(carried[:, :, 2:-2, 2:-2], first_sweep)
    rounded = smoothed.astype(jnp.bfloat16)
    velocity_tile = extended(rounded, (("gx", 2), ("gy", 3)), MARGIN)
    sampled = sample_all(
        velocity_tile,
        own_markers,
        own_count,
        anchor_x - MARGIN,
        anchor_y - MARGIN,
        extent_x,
        extent_y,
    )
    return (smoothed, sampled.reshape(comps, 1, 1, slots))


def solution(mesh):
    placed = (
        P(None, None, "gx", "gy"),
        P(None, "gx", "gy", None),
        P(None, "gx", "gy", None),
        P(None, "gx", "gy", None),
        P(),
    )
    return jax.shard_map(
        body,
        mesh=mesh,
        in_specs=placed,
        out_specs=(P(None, None, "gx", "gy"), P(None, "gx", "gy", None)),
        check_vma=False,
    )
```

profile of v0, /device:TPU:0, one launch (start us, length us, event | category | flops | bytes accessed | tf_op | source)
XLA Modules:
  0.0 103.5 jit_solution(17833358378774042790)
XLA Ops:
  4.2 16.4 %while.30 = (s32[]{:T(128)}, f32[768,160]{0,1:T(8,128)S(1)}, s32[]{:T(128)}, f32[7,2048]{1,0:T(8,128)S(1)}, s32[]{:T(128)}, /*index=5*/f32[]{:T(128)}, f32[]{:T(...) while((s32[]{:T(128)}, f32[768,160]{0,1:T(8,128)S(1)}, ...), condition=%wide.region_2.3_spmd, body=%wide.region_1.2_spmd.sunk | while | flops 64053000 | bytes 2395435 | solution.py:103
  21.0 3.5 %collective-permute-start.1 = (f32[4,2,16,160]{3,2,1,0:T(8,128)S(1)}, f32[4,2,16,160]{3,2,1,0:T(8,128)S(1)}, u32[]{:S(2)}, u32[]{:S(2)}) collective-permute-start(f32[4,2,16,160]{3,2,1,0:T(8,128)S(1)} %get-tuple-element.420), channel_id=1, source_target_pairs={{4,0},{8,4},{12,8},{16,12},{20,16},{24,20},{28,24},{0,28},{5,1},{9... | collective-permute-start | bytes 245768 | tf_op jit(solution)/shard_map/ppermute | solution.py:22
  24.5 2.7 %collective-permute-done = f32[4,2,16,160]{3,2,1,0:T(8,128)S(1)} collective-permute-done((f32[4,2,16,160]{3,2,1,0:T(8,128)S(1)}, f32[4,2,16,160]{3,2,1,0:T(8,128)S(1)}, u32[]{:S(2)}, u32[]{:S(2)}) %collective-permute-start) | collective-permute-done | bytes 81952 | tf_op jit(solution)/shard_map/ppermute | solution.py:21
  27.5 4.1 %collective-permute-start.2 = (f32[4,2,64,16]{3,2,1,0:T(8,128)S(1)}, f32[4,2,64,16]{3,2,1,0:T(8,128)S(1)}, u32[]{:S(2)}, u32[]{:S(2)}) collective-permute-start(f32[4,2,64,16]{3,2,1,0:T(8,128)S(1)} %get-tuple-element.433), channel_id=1, source_target_pairs={{0,1},{1,2},{2,3},{3,0},{4,5},{5,6},{6,7},{7,4},{8,9},{9,10},{10,1... | collective-permute-start | bytes 98312 | tf_op jit(solution)/shard_map/ppermute | solution.py:21
  31.6 6.7 %collective-permute-done.2 = f32[4,2,64,16]{3,2,1,0:T(8,128)S(1)} collective-permute-done((f32[4,2,64,16]{3,2,1,0:T(8,128)S(1)}, f32[4,2,64,16]{3,2,1,0:T(8,128)S(1)}, u32[]{:S(2)}, u32[]{:S(2)}) %collective-permute-start.2) | collective-permute-done | bytes 32800 | tf_op jit(solution)/shard_map/ppermute | solution.py:21
  38.2 5.5 %collective-permute-done.3 = f32[4,2,64,16]{3,2,1,0:T(8,128)S(1)} collective-permute-done((f32[4,2,64,16]{3,2,1,0:T(8,128)S(1)}, f32[4,2,64,16]{3,2,1,0:T(8,128)S(1)}, u32[]{:S(2)}, u32[]{:S(2)}) %collective-permute-start.3) | collective-permute-done | bytes 32800 | tf_op jit(solution)/shard_map/ppermute | solution.py:22
  44.1 3.5 %collective-permute-start.5 = (f32[4,2,3,128]{3,2,1,0:T(4,128)S(1)}, f32[4,2,3,128]{3,2,1,0:T(4,128)S(1)}, u32[]{:S(2)}, u32[]{:S(2)}) collective-permute-start(f32[4,2,3,128]{3,2,1,0:T(4,128)S(1)} %get-tuple-element.438), channel_id=1, source_target_pairs={{4,0},{8,4},{12,8},{16,12},{20,16},{24,20},{28,24},{0,28},{5,1},{9... | collective-permute-start | bytes 36872 | tf_op jit(solution)/shard_map/ppermute | solution.py:22
  49.3 2.9 %collective-permute-start.7 = (f32[4,2,70,3]{3,2,1,0:T(8,128)S(1)}, f32[4,2,70,3]{3,2,1,0:T(8,128)S(1)}, u32[]{:S(2)}, u32[]{:S(2)}) collective-permute-start(f32[4,2,70,3]{3,2,1,0:T(8,128)S(1)} %get-tuple-element.436), channel_id=1, source_target_pairs={{1,0},{2,1},{3,2},{0,3},{5,4},{6,5},{7,6},{4,7},{9,8},{10,9},{11,1... | collective-permute-start | bytes 20168 | tf_op jit(solution)/shard_map/ppermute | solution.py:22
  52.2 7.9 %collective-permute-done.6 = f32[4,2,70,3]{3,2,1,0:T(8,128)S(1)} collective-permute-done((f32[4,2,70,3]{3,2,1,0:T(8,128)S(1)}, f32[4,2,70,3]{3,2,1,0:T(8,128)S(1)}, u32[]{:S(2)}, u32[]{:S(2)}) %collective-permute-start.6) | collective-permute-done | bytes 6752 | tf_op jit(solution)/shard_map/ppermute | solution.py:21
  60.1 3.1 %collective-permute-done.7 = f32[4,2,70,3]{3,2,1,0:T(8,128)S(1)} collective-permute-done((f32[4,2,70,3]{3,2,1,0:T(8,128)S(1)}, f32[4,2,70,3]{3,2,1,0:T(8,128)S(1)}, u32[]{:S(2)}, u32[]{:S(2)}) %collective-permute-start.7) | collective-permute-done | bytes 6752 | tf_op jit(solution)/shard_map/ppermute | solution.py:22
  67.0 3.5 %collective-permute-start.9 = (bf16[4,2,16,128]{3,2,1,0:T(8,128)(2,1)S(1)}, bf16[4,2,16,128]{3,2,1,0:T(8,128)(2,1)S(1)}, u32[]{:S(2)}, u32[]{:S(2)}) collective-permute-start(bf16[4,2,16,128]{3,2,1,0:T(8,128)(2,1)S(1)} %get-tuple-element.442), channel_id=1, source_target_pairs={{4,0},{8,4},{12,8},{16,12},{20,16},{24,20},{28,24},{0,28},{5,1},{9... | collective-permute-start | bytes 98312 | tf_op jit(solution)/shard_map/ppermute | solution.py:22
  70.6 1.6 %collective-permute-done.8 = bf16[4,2,16,128]{3,2,1,0:T(8,128)(2,1)S(1)} collective-permute-done((bf16[4,2,16,128]{3,2,1,0:T(8,128)(2,1)S(1)}, bf16[4,2,16,128]{3,2,1,0:T(8,128)(2,1)S(1)}, u32[]{:S(2)}, u32[]{:S(2)}) %collective-permute-start.8) | collective-permute-done | bytes 32800 | tf_op jit(solution)/shard_map/ppermute | solution.py:21
  72.3 2.6 %collective-permute-start.10 = (bf16[4,2,96,16]{3,2,1,0:T(8,128)(2,1)S(1)}, bf16[4,2,96,16]{3,2,1,0:T(8,128)(2,1)S(1)}, u32[]{:S(2)}, u32[]{:S(2)}) collective-permute-start(bf16[4,2,96,16]{3,2,1,0:T(8,128)(2,1)S(1)} %get-tuple-element.439), channel_id=1, source_target_pairs={{0,1},{1,2},{2,3},{3,0},{4,5},{5,6},{6,7},{7,4},{8,9},{9,10},{10,1... | collective-permute-start | bytes 73736 | tf_op jit(solution)/shard_map/ppermute | solution.py:21
  75.3 5.1 %collective-permute-done.10 = bf16[4,2,96,16]{3,2,1,0:T(8,128)(2,1)S(1)} collective-permute-done((bf16[4,2,96,16]{3,2,1,0:T(8,128)(2,1)S(1)}, bf16[4,2,96,16]{3,2,1,0:T(8,128)(2,1)S(1)}, u32[]{:S(2)}, u32[]{:S(2)}) %collective-permute-start.10) | collective-permute-done | bytes 24608 | tf_op jit(solution)/shard_map/ppermute | solution.py:21
  80.3 3.1 %collective-permute-done.11 = bf16[4,2,96,16]{3,2,1,0:T(8,128)(2,1)S(1)} collective-permute-done((bf16[4,2,96,16]{3,2,1,0:T(8,128)(2,1)S(1)}, bf16[4,2,96,16]{3,2,1,0:T(8,128)(2,1)S(1)}, u32[]{:S(2)}, u32[]{:S(2)}) %collective-permute-start.11) | collective-permute-done | bytes 24608 | tf_op jit(solution)/shard_map/ppermute | solution.py:22
  83.7 19.2 %while.31 = (s32[]{:T(128)}, f32[2,2048]{1,0:T(2,128)S(1)}, s32[]{:T(128)}, f32[7,2048]{1,0:T(8,128)S(1)}, f32[]{:T(128)}, /*index=5*/bf16[4,2,96,160]{3,2,1,0:T...) while((s32[]{:T(128)}, f32[2,2048]{1,0:T(2,128)S(1)}, ...), condition=%wide.region_6.7_spmd, body=%wide.region_3.6_spmd.sunk | while | flops 63929608 | bytes 4017435 | solution.py:137
  83.9 1.4 %convolution_bitcast_fusion.2 = f32[768,256]{0,1:T(8,128)S(1)} fusion(bf16[768,160]{1,0:T(8,128)(2,1)S(1)} %bitcast.66, f32[256]{0:T(256)S(1)} %bitcast.71, f32[256]{0:T(256)S(1)} %fusion.94), kind=kOutput, calls=%fused_computation.34.clone.1 | convolution fusion | flops 63283200 | bytes 1034240 | tf_op jit(solution)/shard_map/while/body/dot_general | solution.py:112
  86.3 1.4 %convolution_bitcast_fusion.2 = f32[768,256]{0,1:T(8,128)S(1)} fusion(bf16[768,160]{1,0:T(8,128)(2,1)S(1)} %bitcast.66, f32[256]{0:T(256)S(1)} %bitcast.71, f32[256]{0:T(256)S(1)} %fusion.94), kind=kOutput, calls=%fused_computation.34.clone.1 | convolution fusion | flops 63283200 | bytes 1034240 | tf_op jit(solution)/shard_map/while/body/dot_general | solution.py:112
  88.6 1.4 %convolution_bitcast_fusion.2 = f32[768,256]{0,1:T(8,128)S(1)} fusion(bf16[768,160]{1,0:T(8,128)(2,1)S(1)} %bitcast.66, f32[256]{0:T(256)S(1)} %bitcast.71, f32[256]{0:T(256)S(1)} %fusion.94), kind=kOutput, calls=%fused_computation.34.clone.1 | convolution fusion | flops 63283200 | bytes 1034240 | tf_op jit(solution)/shard_map/while/body/dot_general | solution.py:112
  91.0 1.4 %convolution_bitcast_fusion.2 = f32[768,256]{0,1:T(8,128)S(1)} fusion(bf16[768,160]{1,0:T(8,128)(2,1)S(1)} %bitcast.66, f32[256]{0:T(256)S(1)} %bitcast.71, f32[256]{0:T(256)S(1)} %fusion.94), kind=kOutput, calls=%fused_computation.34.clone.1 | convolution fusion | flops 63283200 | bytes 1034240 | tf_op jit(solution)/shard_map/while/body/dot_general | solution.py:112
  93.4 1.4 %convolution_bitcast_fusion.2 = f32[768,256]{0,1:T(8,128)S(1)} fusion(bf16[768,160]{1,0:T(8,128)(2,1)S(1)} %bitcast.66, f32[256]{0:T(256)S(1)} %bitcast.71, f32[256]{0:T(256)S(1)} %fusion.94), kind=kOutput, calls=%fused_computation.34.clone.1 | convolution fusion | flops 63283200 | bytes 1034240 | tf_op jit(solution)/shard_map/while/body/dot_general | solution.py:112
  95.8 1.4 %convolution_bitcast_fusion.2 = f32[768,256]{0,1:T(8,128)S(1)} fusion(bf16[768,160]{1,0:T(8,128)(2,1)S(1)} %bitcast.66, f32[256]{0:T(256)S(1)} %bitcast.71, f32[256]{0:T(256)S(1)} %fusion.94), kind=kOutput, calls=%fused_computation.34.clone.1 | convolution fusion | flops 63283200 | bytes 1034240 | tf_op jit(solution)/shard_map/while/body/dot_general | solution.py:112
  98.2 1.4 %convolution_bitcast_fusion.2 = f32[768,256]{0,1:T(8,128)S(1)} fusion(bf16[768,160]{1,0:T(8,128)(2,1)S(1)} %bitcast.66, f32[256]{0:T(256)S(1)} %bitcast.71, f32[256]{0:T(256)S(1)} %fusion.94), kind=kOutput, calls=%fused_computation.34.clone.1 | convolution fusion | flops 63283200 | bytes 1034240 | tf_op jit(solution)/shard_map/while/body/dot_general | solution.py:112
  100.6 1.4 %convolution_bitcast_fusion.2 = f32[768,256]{0,1:T(8,128)S(1)} fusion(bf16[768,160]{1,0:T(8,128)(2,1)S(1)} %bitcast.66, f32[256]{0:T(256)S(1)} %bitcast.71, f32[256]{0:T(256)S(1)} %fusion.94), kind=kOutput, calls=%fused_computation.34.clone.1 | convolution fusion | flops 63283200 | bytes 1034240 | tf_op jit(solution)/shard_map/while/body/dot_general | solution.py:112
  (209 shorter events, 33.2 us)
Async XLA Ops:
  0.6 0.7 copy-start.4
  0.6 2.0 %copy-start.1 = (s32[3,1,1,2048]{3,2,1,0:T(1,128)S(1)}, s32[3,1,1,2048]{3,2,1,0:T(1,128)}, u32[]{:S(2)}) copy-start(s32[3,1,1,2048]{3,2,1,0:T(1,128)} %param.10) | copy-start | bytes 73732
  2.6 0.7 copy-start.2
  3.3 0.7 copy-start.3
  20.9 6.3 %collective-permute-start = (f32[4,2,16,160]{3,2,1,0:T(8,128)S(1)}, f32[4,2,16,160]{3,2,1,0:T(8,128)S(1)}, u32[]{:S(2)}, u32[]{:S(2)}) collective-permute-start(f32[4,2,16,160]{3,2,1,0:T(8,128)S(1)} %get-tuple-element.419), channel_id=1, source_target_pairs={{0,4},{4,8},{8,12},{12,16},{16,20},{20,24},{24,28},{28,0},{1,5},{5... | collective-permute-start | bytes 245768 | tf_op jit(solution)/shard_map/ppermute | solution.py:21
  21.0 6.3 %collective-permute-start.1 = (f32[4,2,16,160]{3,2,1,0:T(8,128)S(1)}, f32[4,2,16,160]{3,2,1,0:T(8,128)S(1)}, u32[]{:S(2)}, u32[]{:S(2)}) collective-permute-start(f32[4,2,16,160]{3,2,1,0:T(8,128)S(1)} %get-tuple-element.420), channel_id=1, source_target_pairs={{4,0},{8,4},{12,8},{16,12},{20,16},{24,20},{28,24},{0,28},{5,1},{9... | collective-permute-start | bytes 245768 | tf_op jit(solution)/shard_map/ppermute | solution.py:22
  27.4 16.4 %copy-start = (f32[4,2,64,128]{3,2,1,0:T(8,128)S(1)}, f32[4,2,64,128]{3,2,1,0:T(8,128)}, u32[]{:S(2)}) copy-start(f32[4,2,64,128]{3,2,1,0:T(8,128)} %param.9) | copy-start | bytes 786436
  27.5 10.7 %collective-permute-start.2 = (f32[4,2,64,16]{3,2,1,0:T(8,128)S(1)}, f32[4,2,64,16]{3,2,1,0:T(8,128)S(1)}, u32[]{:S(2)}, u32[]{:S(2)}) collective-permute-start(f32[4,2,64,16]{3,2,1,0:T(8,128)S(1)} %get-tuple-element.433), channel_id=1, source_target_pairs={{0,1},{1,2},{2,3},{3,0},{4,5},{5,6},{6,7},{7,4},{8,9},{9,10},{10,1... | collective-permute-start | bytes 98312 | tf_op jit(solution)/shard_map/ppermute | solution.py:21
  31.6 12.2 %collective-permute-start.3 = (f32[4,2,64,16]{3,2,1,0:T(8,128)S(1)}, f32[4,2,64,16]{3,2,1,0:T(8,128)S(1)}, u32[]{:S(2)}, u32[]{:S(2)}) collective-permute-start(f32[4,2,64,16]{3,2,1,0:T(8,128)S(1)} %get-tuple-element.434), channel_id=1, source_target_pairs={{1,0},{2,1},{3,2},{0,3},{5,4},{6,5},{7,6},{4,7},{9,8},{10,9},{11,1... | collective-permute-start | bytes 98312 | tf_op jit(solution)/shard_map/ppermute | solution.py:22
  44.0 5.0 %collective-permute-start.4 = (f32[4,2,3,128]{3,2,1,0:T(4,128)S(1)}, f32[4,2,3,128]{3,2,1,0:T(4,128)S(1)}, u32[]{:S(2)}, u32[]{:S(2)}) collective-permute-start(f32[4,2,3,128]{3,2,1,0:T(4,128)S(1)} %get-tuple-element.437), channel_id=1, source_target_pairs={{0,4},{4,8},{8,12},{12,16},{16,20},{20,24},{24,28},{28,0},{1,5},{5... | collective-permute-start | bytes 36872 | tf_op jit(solution)/shard_map/ppermute | solution.py:21
  44.1 5.0 %collective-permute-start.5 = (f32[4,2,3,128]{3,2,1,0:T(4,128)S(1)}, f32[4,2,3,128]{3,2,1,0:T(4,128)S(1)}, u32[]{:S(2)}, u32[]{:S(2)}) collective-permute-start(f32[4,2,3,128]{3,2,1,0:T(4,128)S(1)} %get-tuple-element.438), channel_id=1, source_target_pairs={{4,0},{8,4},{12,8},{16,12},{20,16},{24,20},{28,24},{0,28},{5,1},{9... | collective-permute-start | bytes 36872 | tf_op jit(solution)/shard_map/ppermute | solution.py:22
  49.2 10.9 %collective-permute-start.6 = (f32[4,2,70,3]{3,2,1,0:T(8,128)S(1)}, f32[4,2,70,3]{3,2,1,0:T(8,128)S(1)}, u32[]{:S(2)}, u32[]{:S(2)}) collective-permute-start(f32[4,2,70,3]{3,2,1,0:T(8,128)S(1)} %get-tuple-element.435), channel_id=1, source_target_pairs={{0,1},{1,2},{2,3},{3,0},{4,5},{5,6},{6,7},{7,4},{8,9},{9,10},{10,1... | collective-permute-start | bytes 20168 | tf_op jit(solution)/shard_map/ppermute | solution.py:21
  49.3 14.0 %collective-permute-start.7 = (f32[4,2,70,3]{3,2,1,0:T(8,128)S(1)}, f32[4,2,70,3]{3,2,1,0:T(8,128)S(1)}, u32[]{:S(2)}, u32[]{:S(2)}) collective-permute-start(f32[4,2,70,3]{3,2,1,0:T(8,128)S(1)} %get-tuple-element.436), channel_id=1, source_target_pairs={{1,0},{2,1},{3,2},{0,3},{5,4},{6,5},{7,6},{4,7},{9,8},{10,9},{11,1... | collective-permute-start | bytes 20168 | tf_op jit(solution)/shard_map/ppermute | solution.py:22
  67.0 5.2 %collective-permute-start.8 = (bf16[4,2,16,128]{3,2,1,0:T(8,128)(2,1)S(1)}, bf16[4,2,16,128]{3,2,1,0:T(8,128)(2,1)S(1)}, u32[]{:S(2)}, u32[]{:S(2)}) collective-permute-start(bf16[4,2,16,128]{3,2,1,0:T(8,128)(2,1)S(1)} %get-tuple-element.441), channel_id=1, source_target_pairs={{0,4},{4,8},{8,12},{12,16},{16,20},{20,24},{24,28},{28,0},{1,5},{5... | collective-permute-start | bytes 98312 | tf_op jit(solution)/shard_map/ppermute | solution.py:21
  67.0 5.2 %collective-permute-start.9 = (bf16[4,2,16,128]{3,2,1,0:T(8,128)(2,1)S(1)}, bf16[4,2,16,128]{3,2,1,0:T(8,128)(2,1)S(1)}, u32[]{:S(2)}, u32[]{:S(2)}) collective-permute-start(bf16[4,2,16,128]{3,2,1,0:T(8,128)(2,1)S(1)} %get-tuple-element.442), channel_id=1, source_target_pairs={{4,0},{8,4},{12,8},{16,12},{20,16},{24,20},{28,24},{0,28},{5,1},{9... | collective-permute-start | bytes 98312 | tf_op jit(solution)/shard_map/ppermute | solution.py:22
  72.3 8.0 %collective-permute-start.10 = (bf16[4,2,96,16]{3,2,1,0:T(8,128)(2,1)S(1)}, bf16[4,2,96,16]{3,2,1,0:T(8,128)(2,1)S(1)}, u32[]{:S(2)}, u32[]{:S(2)}) collective-permute-start(bf16[4,2,96,16]{3,2,1,0:T(8,128)(2,1)S(1)} %get-tuple-element.439), channel_id=1, source_target_pairs={{0,1},{1,2},{2,3},{3,0},{4,5},{5,6},{6,7},{7,4},{8,9},{9,10},{10,1... | collective-permute-start | bytes 73736 | tf_op jit(solution)/shard_map/ppermute | solution.py:21
  74.9 8.6 %collective-permute-start.11 = (bf16[4,2,96,16]{3,2,1,0:T(8,128)(2,1)S(1)}, bf16[4,2,96,16]{3,2,1,0:T(8,128)(2,1)S(1)}, u32[]{:S(2)}, u32[]{:S(2)}) collective-permute-start(bf16[4,2,96,16]{3,2,1,0:T(8,128)(2,1)S(1)} %get-tuple-element.440), channel_id=1, source_target_pairs={{1,0},{2,1},{3,2},{0,3},{5,4},{6,5},{7,6},{4,7},{9,8},{10,9},{11,1... | collective-permute-start | bytes 73736 | tf_op jit(solution)/shard_map/ppermute | solution.py:22
where the time goes:
time: 103 us; the launch traced here: 104 us
  waiting for transfers between devices  37.2 us (36%)
  matrix products  22.2 us (22%)
  starting transfers between devices  20.7 us (20%)
  other arithmetic  14.2 us (14%)
  local copies, waits for them, and re-layouts  6.22 us (6%)
  between operations  1.58 us (2%)
  loops' own time  1.27 us (1%)
    ppermute x6, waiting for transfers between devices, extended(): before = lax.ppermute(last, axis, up)  25.4 us
    ppermute x6, starting transfers between devices, extended(): after = lax.ppermute(initial, axis, down)  13.9 us
    ppermute x6, waiting for transfers between devices, extended(): after = lax.ppermute(initial, axis, down)  11.9 us
    dot_general x8, matrix products, sample_block(): lax.dot_general(flat_tile, weight_y, (((1,), (1,)), ((), ())), preferred_...  11.6 us
    dot_general x8, matrix products, spread_block(): lax.dot_general(left, weight_y, (((0,), (0,)), ((), ())), preferred_eleme...  10.6 us
    ppermute x6, starting transfers between devices, extended(): before = lax.ppermute(last, axis, up)  6.8 us
    select_n x16, other arithmetic, kernel_weight(): jnp.where(jnp.abs(offset) < 2.0, 0.25 * (1.0 + jnp.cos(0.5 * jnp.pi * off...  5.84 us
    dot_general x8, local copies, waits for them, and re-layouts, sample_block(): lax.dot_general(flat_tile, weight_y, (((1,), (1,)), ((), ())), preferred_...  2.11 us
  transfers between devices with their start and end apart: 12, of which 10 were waited for; matrix products, arithmetic and copies ran while one was open for 0% of the time, Pallas kernels for 0%

commit v1 on v0

v1 whole, which is shorter than its diff:
```python
import functools

import jax
import jax.numpy as jnp
import numpy as np
from jax import lax
from jax.experimental import pallas as pl
from jax.experimental.pallas import tpu as pltpu
from jax.sharding import PartitionSpec as P

MARGIN = 16
FISH_MARK = 1024
HALO = 3
LANES = 128
COURANT = 0.25
VISCOUS = 1.5
ROWS = 8

REACH = MARGIN + HALO
PAD = -(-REACH // ROWS) * ROWS
STRIP = PAD + MARGIN
WIDE = REACH + MARGIN
EDGE_PER = LANES // (2 * MARGIN)
WIDE_PER = LANES // WIDE
WIDE_STEP = LANES // WIDE_PER


def half_turn(terms):
    nodes = 0.5 - 0.5 * np.cos(np.pi * (np.arange(64) + 0.5) / 64)
    square = nodes * nodes
    cosine = np.polynomial.polynomial.polyfit(square, np.cos(0.5 * np.pi * nodes), terms)
    sine = np.polynomial.polynomial.polyfit(square, np.sin(0.5 * np.pi * nodes) / nodes, terms)
    return [float(v) for v in cosine], [float(v) for v in sine]


COS_FIT, SIN_FIT = half_turn(6)


def horner(coefficients, value):
    total = jnp.full_like(value, coefficients[-1])
    for coefficient in coefficients[-2::-1]:
        total = total * value + coefficient
    return total


def four_weights(frac):
    square = frac * frac
    cosine = horner(COS_FIT, square)
    sine = frac * horner(SIN_FIT, square)
    return (0.25 - 0.25 * sine, 0.25 + 0.25 * cosine, 0.25 + 0.25 * sine, 0.25 - 0.25 * cosine)


def local_cell(cell, low, extent):
    offset = cell - low
    offset = jnp.where(offset < -MARGIN, offset + extent, offset)
    return jnp.where(offset >= extent - MARGIN, offset - extent, offset)


def placed_weights(first, rows, offset, weights):
    width = offset.shape[1]
    shift = lax.broadcasted_iota(jnp.int32, (rows, width), 0) + first - offset
    dense = jnp.where(shift == 2, weights[3], 0.0)
    dense = jnp.where(shift == 1, weights[2], dense)
    dense = jnp.where(shift == 0, weights[1], dense)
    return jnp.where(shift == -1, weights[0], dense)


def marker_weights(cell_ref, frac_ref, lanes, shape):
    cells_x, cells_y, extent_x, extent_y = shape
    low_x = lax.axis_index("gx") * cells_x
    low_y = lax.axis_index("gy") * cells_y
    offset_x = local_cell(cell_ref[0, 0, :, lanes], low_x, extent_x)
    offset_y = local_cell(cell_ref[1, 0, :, lanes], low_y, extent_y)
    weights_x = four_weights(frac_ref[0, 0, :, lanes])
    weights_y = four_weights(frac_ref[1, 0, :, lanes])
    dense_x = placed_weights(-MARGIN, cells_x + 2 * MARGIN, offset_x, weights_x)
    inner_y = placed_weights(0, cells_y + MARGIN, offset_y, weights_y)
    outer_y = placed_weights(-MARGIN, MARGIN, offset_y, weights_y)
    gap = jnp.zeros((LANES - 2 * MARGIN, offset_y.shape[1]), jnp.float32)
    dense_y = jnp.concatenate([inner_y, gap, outer_y], axis=0).astype(jnp.bfloat16)
    return dense_x, dense_y


def alive_count(fish_ref):
    me = lax.axis_index("gx") * lax.axis_size("gy") + lax.axis_index("gy")
    mine = jnp.where(fish_ref[...] == me, 1.0, 0.0)
    return FISH_MARK * jnp.sum(mine)


def alive_lanes(count, first, width):
    slot = lax.broadcasted_iota(jnp.int32, (1, width), 1) + first
    return jnp.where(slot.astype(jnp.float32) < count, 1.0, 0.0)


def spread_kernel(
    shape, chunk, fish_ref, velocity_ref, cell_ref, frac_ref, force_ref,
    grid_ref, up_ref, down_ref, left_ref, weight_ref,
):
    cells_x, cells_y, _, _ = shape
    levels, comps = velocity_ref.shape[:2]
    slots = cell_ref.shape[3]
    wide_x = cells_x + 2 * MARGIN
    count = alive_count(fish_ref)
    for first in range(0, slots, chunk):
        lanes = slice(first, first + chunk)
        dense_x, dense_y = marker_weights(cell_ref, frac_ref, lanes, shape)
        weight_ref[:, lanes] = dense_y
        alive = alive_lanes(count, first, chunk)
        level = cell_ref[2, 0, :, lanes]
        lefts = [
            ((force_ref[c, 0, :, lanes] * alive) * dense_x).astype(jnp.bfloat16)
            for c in range(comps)
        ]
        for l in range(levels):
            hot = jnp.broadcast_to(jnp.where(level == l, 1.0, 0.0), (16, chunk))
            hot = hot.astype(jnp.bfloat16)
            for c in range(comps):
                k = l * comps + c
                product = lefts[c].reshape(wide_x // 16, 16, chunk) * hot[None]
                left_ref[k * wide_x : (k + 1) * wide_x, lanes] = product.reshape(wide_x, chunk)
    total = lax.dot_general(
        left_ref[...], weight_ref[...], (((1,), (1,)), ((), ())),
        preferred_element_type=jnp.float32,
    )
    items = levels * comps
    grid_ref[...] = total.reshape(items, wide_x, cells_y + LANES)
    for k in range(items):
        grid_ref[k, MARGIN : MARGIN + cells_x, :cells_y] += velocity_ref[k // comps, k % comps]
    for out_ref, row in ((down_ref, 0), (up_ref, wide_x - STRIP)):
        parts = [grid_ref[k, row : row + STRIP, :cells_y] for k in range(items)]
        for group in range(0, items, EDGE_PER):
            edge = None
            for k in range(group, min(group + EDGE_PER, items)):
                piece = grid_ref[k, row : row + STRIP, cells_y:]
                if k > group:
                    piece = pltpu.roll(piece, 2 * MARGIN * (k - group), 1)
                    piece = piece + edge
                edge = piece
            parts.append(edge)
        out_ref[...] = jnp.concatenate(parts, axis=0).astype(jnp.bfloat16)


def lane_index(rows):
    return lax.broadcasted_iota(jnp.int32, (rows, LANES), 1)


def strip_parts(ref, k, items):
    lane = lane_index(STRIP)
    inner = ref[k * STRIP : (k + 1) * STRIP].astype(jnp.float32)
    row = (items + k // EDGE_PER) * STRIP
    edge = ref[row : row + STRIP].astype(jnp.float32)
    if k % EDGE_PER:
        edge = pltpu.roll(edge, LANES - 2 * MARGIN * (k % EDGE_PER), 1)
    edge = jnp.where((lane < MARGIN) | (lane >= LANES - MARGIN), edge, 0.0)
    return inner, edge


def joined(center, before, after):
    wide = center.shape[0]
    near = PAD - MARGIN
    overlap = STRIP - near
    return jnp.concatenate(
        [
            before[:near],
            center[:overlap] + before[near:],
            center[overlap : wide - overlap],
            center[wide - overlap :] + after[:overlap],
            after[overlap:],
        ],
        axis=0,
    )


def extended_rows(grid_ref, from_left, from_right, k, items, cells_y):
    before = strip_parts(from_left, k, items)
    after = strip_parts(from_right, k, items)
    inner = joined(grid_ref[k, :, :cells_y], before[0], after[0])
    edge = joined(grid_ref[k, :, cells_y:], before[1], after[1])
    return inner, edge


def pack_kernel(shape, grid_ref, from_left, from_right, up_ref, down_ref):
    cells_x, cells_y, _, _ = shape
    items = grid_ref.shape[0]
    rows = cells_x + 2 * PAD
    lane = lane_index(rows)
    for group in range(0, items, WIDE_PER):
        ups, downs = [], []
        for k in range(group, min(group + WIDE_PER, items)):
            inner, edge = extended_rows(grid_ref, from_left, from_right, k, items, cells_y)
            up = jnp.where(lane >= LANES - REACH, inner, jnp.where(lane < MARGIN, edge, 0.0))
            down = jnp.where(lane < REACH, inner, jnp.where(lane >= LANES - MARGIN, edge, 0.0))
            shift = WIDE_STEP * (k - group)
            ups.append(pltpu.roll(up, shift, 1) if shift else up)
            downs.append(pltpu.roll(down, shift, 1) if shift else down)
        row = group // WIDE_PER * rows
        up_ref[row : row + rows] = functools.reduce(jnp.add, ups).astype(jnp.bfloat16)
        down_ref[row : row + rows] = functools.reduce(jnp.add, downs).astype(jnp.bfloat16)


def shifted(inner, edge, lane):
    below_inner, below_edge = pltpu.roll(inner, 1, 1), pltpu.roll(edge, 1, 1)
    above_inner, above_edge = pltpu.roll(inner, LANES - 1, 1), pltpu.roll(edge, LANES - 1, 1)
    first, last = lane == 0, lane == LANES - 1
    below = (jnp.where(first, below_edge, below_inner), jnp.where(first, below_inner, below_edge))
    above = (jnp.where(last, above_edge, above_inner), jnp.where(last, above_inner, above_edge))
    return below, above


def finish_kernel(
    shape, chunk, fish_ref, cell_ref, frac_ref, grid_ref, left_x, right_x, left_y, right_y,
    next_ref, sampled_ref, moved_ref, carried_ref, sweep_ref, round_ref,
):
    cells_x, cells_y, _, _ = shape
    items = grid_ref.shape[0]
    levels, comps = next_ref.shape[:2]
    slots = cell_ref.shape[3]
    wide_x = cells_x + 2 * MARGIN
    rows = cells_x + 2 * PAD
    lane = lane_index(rows)
    for k in range(items):
        inner, edge = extended_rows(grid_ref, left_x, right_x, k, items, cells_y)
        row = k // WIDE_PER * rows
        before = left_y[row : row + rows].astype(jnp.float32)
        after = right_y[row : row + rows].astype(jnp.float32)
        shift = WIDE_STEP * (k % WIDE_PER)
        if shift:
            before = pltpu.roll(before, LANES - shift, 1)
            after = pltpu.roll(after, LANES - shift, 1)
        inner = inner + jnp.where(lane < MARGIN, before, 0.0)
        inner = inner + jnp.where(lane >= LANES - MARGIN, after, 0.0)
        edge = edge + jnp.where(lane >= LANES - REACH, before, 0.0)
        edge = edge + jnp.where(lane < REACH, after, 0.0)
        moved_ref[0, k, ROWS : ROWS + rows] = inner
        moved_ref[1, k, ROWS : ROWS + rows] = edge

    def around(ref, k, start, size, lane):
        center = tuple(ref[t, k, start : start + size] for t in range(2))
        back = tuple(ref[t, k, start - 1 : start - 1 + size] for t in range(2))
        fore = tuple(ref[t, k, start + 1 : start + 1 + size] for t in range(2))
        below, above = shifted(*center, lane)
        return center, back, fore, below, above

    size = ROWS
    small = lane_index(size)
    for start in range(ROWS, ROWS + rows, size):
        for l in range(levels):
            pieces = [around(moved_ref, l * comps + c, start, size, small) for c in range(comps)]
            for t in range(2):
                speed_x = COURANT * pieces[0][0][t]
                speed_y = COURANT * pieces[1][0][t]
                ahead_x, astern_x = jnp.maximum(speed_x, 0.0), jnp.minimum(speed_x, 0.0)
                ahead_y, astern_y = jnp.maximum(speed_y, 0.0), jnp.minimum(speed_y, 0.0)
                for c in range(comps):
                    center, back, fore, below, above = (part[t] for part in pieces[c])
                    change = ahead_x * (center - back) + astern_x * (fore - center)
                    change = change + ahead_y * (center - below) + astern_y * (above - center)
                    carried_ref[t, l * comps + c, start : start + size] = center - change

    scale = 1.0 / (1.0 + 6.0 * VISCOUS)

    def sweep(ref, start, size, lane):
        results = {}
        centers = {}
        for k in range(items):
            center, back, fore, below, above = around(ref, k, start, size, lane)
            centers[k] = center
            results[k] = [back[t] + fore[t] + below[t] + above[t] for t in range(2)]
        for k in range(items):
            higher = min(k // comps + 1, levels - 1) * comps + k % comps
            lower = max(k // comps - 1, 0) * comps + k % comps
            for t in range(2):
                summed = results[k][t] + centers[higher][t] + centers[lower][t]
                source = carried_ref[t, k, start : start + size]
                results[k][t] = scale * source + (VISCOUS * scale) * summed
        return results

    for start in range(ROWS, ROWS + rows, size):
        results = sweep(carried_ref, start, size, small)
        for k in range(items):
            for t in range(2):
                sweep_ref[t, k, start : start + size] = results[k][t]
    size = 2 * ROWS
    small = lane_index(size)
    near = PAD - MARGIN
    for row in range(0, wide_x, size):
        results = sweep(sweep_ref, ROWS + near + row, size, small)
        for k in range(items):
            place = slice(k * wide_x + row, k * wide_x + row + size)
            for t in range(2):
                lanes = slice(t * cells_y, t * cells_y + LANES)
                round_ref[place, lanes] = results[k][t].astype(jnp.bfloat16)
            if MARGIN <= row < MARGIN + cells_x:
                next_ref[k // comps, k % comps, row - MARGIN : row - MARGIN + size] = results[k][0]

    count = alive_count(fish_ref)
    for first in range(0, slots, chunk):
        lanes = slice(first, first + chunk)
        dense_x, dense_y = marker_weights(cell_ref, frac_ref, lanes, shape)
        alive = alive_lanes(count, first, chunk)
        level = cell_ref[2, 0, :, lanes]
        partial = jnp.dot(round_ref[...], dense_y, preferred_element_type=jnp.float32)
        partial = partial.reshape(levels, comps, wide_x, chunk)
        for c in range(comps):
            picked = partial[levels - 1, c]
            for l in range(levels - 2, -1, -1):
                picked = jnp.where(level == l, partial[l, c], picked)
            sampled = jnp.sum(picked * dense_x, axis=0, keepdims=True)
            sampled_ref[c, 0, :, lanes] = sampled * alive


def whole(count):
    return [pl.BlockSpec(memory_space=pltpu.VMEM)] * count


def exchange(up, down, axis):
    size = lax.axis_size(axis)
    forward = [(i, (i + 1) % size) for i in range(size)]
    backward = [(j, i) for i, j in forward]
    return lax.ppermute(up, axis, forward), lax.ppermute(down, axis, backward)


def body(velocity, marker_cell, marker_frac, marker_force, fish_owner):
    levels, comps, cells_x, cells_y = velocity.shape
    slots = marker_cell.shape[3]
    items = levels * comps
    shape = (cells_x, cells_y, cells_x * lax.axis_size("gx"), cells_y * lax.axis_size("gy"))
    wide_x = cells_x + 2 * MARGIN
    rows = cells_x + 2 * PAD
    chunk = min(512, slots)
    width = cells_y + LANES
    groups = -(-items // EDGE_PER)
    params = pltpu.CompilerParams(vmem_limit_bytes=40 * 1024 * 1024)
    edge_x = jax.ShapeDtypeStruct(((items + groups) * STRIP, LANES), jnp.bfloat16)
    grid, up, down = pl.pallas_call(
        functools.partial(spread_kernel, shape, chunk),
        out_shape=(
            jax.ShapeDtypeStruct((items, wide_x, width), jnp.float32),
            edge_x,
            edge_x,
        ),
        in_specs=whole(5),
        out_specs=tuple(whole(3)),
        scratch_shapes=[
            pltpu.VMEM((items * wide_x, slots), jnp.bfloat16),
            pltpu.VMEM((width, slots), jnp.bfloat16),
        ],
        compiler_params=params,
        name="spread",
    )(fish_owner, velocity, marker_cell, marker_frac, marker_force)
    left_x, right_x = exchange(up, down, "gx")
    edge_y = jax.ShapeDtypeStruct((-(-items // WIDE_PER) * rows, LANES), jnp.bfloat16)
    up, down = pl.pallas_call(
        functools.partial(pack_kernel, shape),
        out_shape=(edge_y, edge_y),
        in_specs=whole(3),
        out_specs=tuple(whole(2)),
        compiler_params=params,
        name="pack",
    )(grid, left_x, right_x)
    left_y, right_y = exchange(up, down, "gy")
    field = pltpu.VMEM((2, items, rows + 2 * ROWS, LANES), jnp.float32)
    return pl.pallas_call(
        functools.partial(finish_kernel, shape, chunk),
        out_shape=(
            jax.ShapeDtypeStruct(velocity.shape, jnp.float32),
            jax.ShapeDtypeStruct((comps, 1, 1, slots), jnp.float32),
        ),
        in_specs=whole(8),
        out_specs=tuple(whole(2)),
        scratch_shapes=[field, field, field, pltpu.VMEM((items * wide_x, width), jnp.bfloat16)],
        compiler_params=params,
        name="finish",
    )(fish_owner, marker_cell, marker_frac, grid, left_x, right_x, left_y, right_y)


def solution(mesh):
    placed = (
        P(None, None, "gx", "gy"),
        P(None, "gx", "gy", None),
        P(None, "gx", "gy", None),
        P(None, "gx", "gy", None),
        P(),
    )
    return jax.shard_map(
        body,
        mesh=mesh,
        in_specs=placed,
        out_specs=(P(None, None, "gx", "gy"), P(None, "gx", "gy", None)),
        check_vma=False,
    )
```

time: 103 us -> 25.5 us (0.25)
  waiting for transfers between devices: 37.2 us -> 7.87 us
  matrix products: 22.2 us -> 0 us
  other arithmetic: 14.2 us -> 0 us
  starting transfers between devices: 20.7 us -> 7.72 us
  Pallas kernels: 0 us -> 5.19 us
  local copies, waits for them, and re-layouts: 6.22 us -> 3.77 us
  loops' own time: 1.27 us -> 0 us
    ppermute x12 -> x4, waiting for transfers between devices: 37.2 us -> 7.87 us  [exchange(): return (lax.ppermute(up, axis, forward), lax.ppermute(down, axis, backward))]
    dot_general x16 -> x0, matrix products: 22.2 us -> none  [the longest x8 11.6 us: sample_block(): lax.dot_general(flat_tile, weight_y, (((1,), (1,)), ((), ())), preferred_...]
    ppermute x12 -> x4, starting transfers between devices: 20.7 us -> 7.72 us  [exchange(): return (lax.ppermute(up, axis, forward), lax.ppermute(down, axis, backward))]
    select_n x16 -> x0, other arithmetic: 5.84 us -> none  [kernel_weight(): jnp.where(jnp.abs(offset) < 2.0, 0.25 * (1.0 + jnp.cos(0.5 * jnp.pi * off...]
    pallas_call x0 -> x3, Pallas kernels: none -> 5.19 us  [the longest x1 3.44 us: body(): pl.pallas_call(functools.partial(finish_kernel, shape, chunk), out_shape=...]
    dot_general x8 -> x0, local copies, waits for them, and re-layouts: 2.11 us -> none  [sample_block(): lax.dot_general(flat_tile, weight_y, (((1,), (1,)), ((), ())), preferred_...]
    convert_element_type x42 -> x0, other arithmetic: 1.82 us -> none  [the longest x1 1.06 us: body(): rounded = smoothed.astype(jnp.bfloat16)]
    unnamed x12, local copies, waits for them, and re-layouts: 2.06 us -> 3.77 us
  transfers between devices with their start and end apart: 12 -> 4, of which waited for: 10 -> 3; matrix products, arithmetic and copies ran while one was open for 0% -> 0% of each run, Pallas kernels for 0% -> 0%
where the time goes in v1:
time: 25.5 us; the launch traced here: 25.2 us
  waiting for transfers between devices  7.87 us (31%)
  starting transfers between devices  7.72 us (30%)
  Pallas kernels  5.19 us (20%)
  local copies, waits for them, and re-layouts  3.77 us (15%)
  between operations  0.65 us (3%)
    ppermute x4, waiting for transfers between devices, exchange(): return (lax.ppermute(up, axis, forward), lax.ppermute(down, axis, backward))  7.87 us
    ppermute x4, starting transfers between devices, exchange(): return (lax.ppermute(up, axis, forward), lax.ppermute(down, axis, backward))  7.72 us
    unnamed x12, local copies, waits for them, and re-layouts  3.77 us
    pallas_call x1, Pallas kernels, body(): pl.pallas_call(functools.partial(finish_kernel, shape, chunk), out_shape=...  3.44 us
    pallas_call x1, Pallas kernels, body(): pl.pallas_call(functools.partial(spread_kernel, shape, chunk), out_shape=...  1.35 us
  transfers between devices with their start and end apart: 4, of which 3 were waited for; matrix products, arithmetic and copies ran while one was open for 0% of the time, Pallas kernels for 0%

profile of v1, /device:TPU:0, one launch (start us, length us, event | category | flops | bytes accessed | tf_op | source)
XLA Modules:
  0.0 25.2 jit_solution(4569386096646223143)
XLA Ops:
  0.6 0.0 copy-start
  0.6 0.9 %copy-done = f32[4,2,64,128]{3,2,1,0:T(8,128)S(1)} copy-done((f32[4,2,64,128]{3,2,1,0:T(8,128)S(1)}, f32[4,2,64,128]{3,2,1,0:T(8,128)}, u32[]{:S(2)}) %copy-start) | copy-done | bytes 262168
  1.6 0.0 copy-start.1
  1.6 0.7 %copy-done.1 = s32[3,1,1,2048]{3,2,1,0:T(1,128)S(1)} copy-done((s32[3,1,1,2048]{3,2,1,0:T(1,128)S(1)}, s32[3,1,1,2048]{3,2,1,0:T(1,128)}, u32[]{:S(2)}) %copy-start.1) | copy-done | bytes 24600
  2.3 0.0 copy-start.2
  2.3 0.7 %copy-done.2 = f32[2,1,1,2048]{3,2,1,0:T(1,128)S(1)} copy-done((f32[2,1,1,2048]{3,2,1,0:T(1,128)S(1)}, f32[2,1,1,2048]{3,2,1,0:T(1,128)}, u32[]{:S(2)}) %copy-start.2) | copy-done | bytes 16408
  3.0 0.0 copy-start.4
  3.0 0.7 %copy-done.4 = f32[2,1,1,2048]{3,2,1,0:T(1,128)S(1)} copy-done((f32[2,1,1,2048]{3,2,1,0:T(1,128)S(1)}, f32[2,1,1,2048]{3,2,1,0:T(1,128)}, u32[]{:S(2)}) %copy-start.4) | copy-done | bytes 16408
  3.8 0.0 copy-start.5
  3.8 0.7 %copy-done.5 = s32[48]{0:T(128)S(1)} copy-done((s32[48]{0:T(128)S(1)}, s32[48]{0:T(128)}, u32[]{:S(2)}) %copy-start.5) | copy-done | bytes 216
  4.4 1.4 %spread.1 = (f32[8,96,256]{2,1,0:T(8,128)S(1)}, bf16[400,128]{1,0:T(8,128)(2,1)S(1)}, bf16[400,128]{1,0:T(8,128)(2,1)S(1)}) custom-call(s32[48]{0:T(128)S(1)} %copy-done.5, f32[4,2,64,128]{3,2,1,0:T(8,128)S(1)} %copy-done, s32[3,1,1,2048]{3,2,1,0:T(1,128)S(1)} %copy-done.1, f32[2,1,1,2048]{3,2,1,0:T(1,128)S(1)} %copy-done.2, f32[2,1,1,2048]{3,2,1,0:T(1,128)S(1)} %copy-done.4), custom_call_target="tpu_custom_call" | custom-call | tf_op jit(solution)/shard_map/spread/pallas_call | solution.py:335
  5.8 0.5 %collective-permute-start = (bf16[400,128]{1,0:T(8,128)(2,1)S(1)}, bf16[400,128]{1,0:T(8,128)(2,1)S(1)}, u32[]{:S(2)}, u32[]{:S(2)}) collective-permute-start(bf16[400,128]{1,0:T(8,128)(2,1)S(1)} %get-tuple-element.8), channel_id=1, source_target_pairs={{0,4},{4,8},{8,12},{12,16},{16,20},{20,24},{24,28},{28,0},{1,5},{5... | collective-permute-start | bytes 307208 | tf_op jit(solution)/shard_map/ppermute | solution.py:320
  6.3 4.1 %collective-permute-start.1 = (bf16[400,128]{1,0:T(8,128)(2,1)S(1)}, bf16[400,128]{1,0:T(8,128)(2,1)S(1)}, u32[]{:S(2)}, u32[]{:S(2)}) collective-permute-start(bf16[400,128]{1,0:T(8,128)(2,1)S(1)} %get-tuple-element.9), channel_id=1, source_target_pairs={{4,0},{8,4},{12,8},{16,12},{20,16},{24,20},{28,24},{0,28},{5,1},{9... | collective-permute-start | bytes 307208 | tf_op jit(solution)/shard_map/ppermute | solution.py:320
  10.4 2.3 %collective-permute-done.from_left.left_x = bf16[400,128]{1,0:T(8,128)(2,1)S(1)} collective-permute-done((bf16[400,128]{1,0:T(8,128)(2,1)S(1)}, bf16[400,128]{1,0:T(8,128)(2,1)S(1)}, u32[]{:S(2)}, u32[]{:S(2)}) %collective-permute-start) | collective-permute-done | bytes 102432 | tf_op jit(solution)/shard_map/ppermute | solution.py:320
  12.7 0.0 collective-permute-done.1.from_right.right_x
  12.7 0.0 copy-start.3
  12.7 0.4 %pack.1 = (bf16[336,128]{1,0:T(8,128)(2,1)S(1)}, bf16[336,128]{1,0:T(8,128)(2,1)S(1)}) custom-call(f32[8,96,256]{2,1,0:T(8,128)S(1)} %get-tuple-element.7.grid_ref, bf16[400,128]{1,0:T(8,128)(2,1)S(1)} %collective-permute-done.from_left.left_x, bf16[400,128]{1,0:T(8,128)(2,1)S(1)} %collective-permute-done.1.from_right.right_x), custom_call_target="tpu_custom_call" | custom-call | tf_op jit(solution)/shard_map/pack/pallas_call | solution.py:353
  13.1 2.1 %collective-permute-start.2 = (bf16[336,128]{1,0:T(8,128)(2,1)S(1)}, bf16[336,128]{1,0:T(8,128)(2,1)S(1)}, u32[]{:S(2)}, u32[]{:S(2)}) collective-permute-start(bf16[336,128]{1,0:T(8,128)(2,1)S(1)} %get-tuple-element.10), channel_id=1, source_target_pairs={{0,1},{1,2},{2,3},{3,0},{4,5},{5,6},{6,7},{7,4},{8,9},{9,10},{10,1... | collective-permute-start | bytes 258056 | tf_op jit(solution)/shard_map/ppermute | solution.py:320
  15.2 1.0 %collective-permute-start.3 = (bf16[336,128]{1,0:T(8,128)(2,1)S(1)}, bf16[336,128]{1,0:T(8,128)(2,1)S(1)}, u32[]{:S(2)}, u32[]{:S(2)}) collective-permute-start(bf16[336,128]{1,0:T(8,128)(2,1)S(1)} %get-tuple-element.11), channel_id=1, source_target_pairs={{1,0},{2,1},{3,2},{0,3},{5,4},{6,5},{7,6},{4,7},{9,8},{10,9},{11,1... | collective-permute-start | bytes 258056 | tf_op jit(solution)/shard_map/ppermute | solution.py:320
  16.2 3.2 %collective-permute-done.2.left_y = bf16[336,128]{1,0:T(8,128)(2,1)S(1)} collective-permute-done((bf16[336,128]{1,0:T(8,128)(2,1)S(1)}, bf16[336,128]{1,0:T(8,128)(2,1)S(1)}, u32[]{:S(2)}, u32[]{:S(2)}) %collective-permute-start.2) | collective-permute-done | bytes 86048 | tf_op jit(solution)/shard_map/ppermute | solution.py:320
  19.4 2.3 %collective-permute-done.3.right_y = bf16[336,128]{1,0:T(8,128)(2,1)S(1)} collective-permute-done((bf16[336,128]{1,0:T(8,128)(2,1)S(1)}, bf16[336,128]{1,0:T(8,128)(2,1)S(1)}, u32[]{:S(2)}, u32[]{:S(2)}) %collective-permute-start.3) | collective-permute-done | bytes 86048 | tf_op jit(solution)/shard_map/ppermute | solution.py:320
  21.8 0.0 copy-done.3
  21.8 3.4 %finish.1 = (f32[4,2,64,128]{3,2,1,0:T(8,128)}, f32[2,1,1,2048]{3,2,1,0:T(1,128)}) custom-call(s32[48]{0:T(128)S(1)} %copy-done.5, s32[3,1,1,2048]{3,2,1,0:T(1,128)S(1)} %copy-done.1, f32[2,1,1,2048]{3,2,1,0:T(1,128)S(1)} %copy-done.3, f32[8,96,256]{2,1,0:T(8,128)S(1)} %get-tuple-element.7.grid_ref, ...), custom_call_target="tpu_custom_call" | custom-call | tf_op jit(solution)/shard_map/finish/pallas_call | solution.py:363
Async XLA Ops:
  0.6 1.0 %copy-start = (f32[4,2,64,128]{3,2,1,0:T(8,128)S(1)}, f32[4,2,64,128]{3,2,1,0:T(8,128)}, u32[]{:S(2)}) copy-start(f32[4,2,64,128]{3,2,1,0:T(8,128)} %velocity_ref.1) | copy-start | bytes 786436
  1.6 0.7 %copy-start.1 = (s32[3,1,1,2048]{3,2,1,0:T(1,128)S(1)}, s32[3,1,1,2048]{3,2,1,0:T(1,128)}, u32[]{:S(2)}) copy-start(s32[3,1,1,2048]{3,2,1,0:T(1,128)} %cell_ref.3) | copy-start | bytes 73732
  2.3 0.7 %copy-start.2 = (f32[2,1,1,2048]{3,2,1,0:T(1,128)S(1)}, f32[2,1,1,2048]{3,2,1,0:T(1,128)}, u32[]{:S(2)}) copy-start(f32[2,1,1,2048]{3,2,1,0:T(1,128)} %frac_ref.3) | copy-start | bytes 49156
  3.0 0.7 %copy-start.4 = (f32[2,1,1,2048]{3,2,1,0:T(1,128)S(1)}, f32[2,1,1,2048]{3,2,1,0:T(1,128)}, u32[]{:S(2)}) copy-start(f32[2,1,1,2048]{3,2,1,0:T(1,128)} %force_ref.1) | copy-start | bytes 49156
  3.8 0.7 %copy-start.5 = (s32[48]{0:T(128)S(1)}, s32[48]{0:T(128)}, u32[]{:S(2)}) copy-start(s32[48]{0:T(128)} %fish_ref.3) | copy-start | bytes 580
  5.8 6.9 %collective-permute-start = (bf16[400,128]{1,0:T(8,128)(2,1)S(1)}, bf16[400,128]{1,0:T(8,128)(2,1)S(1)}, u32[]{:S(2)}, u32[]{:S(2)}) collective-permute-start(bf16[400,128]{1,0:T(8,128)(2,1)S(1)} %get-tuple-element.8), channel_id=1, source_target_pairs={{0,4},{4,8},{8,12},{12,16},{16,20},{20,24},{24,28},{28,0},{1,5},{5... | collective-permute-start | bytes 307208 | tf_op jit(solution)/shard_map/ppermute | solution.py:320
  6.3 6.4 %collective-permute-start.1 = (bf16[400,128]{1,0:T(8,128)(2,1)S(1)}, bf16[400,128]{1,0:T(8,128)(2,1)S(1)}, u32[]{:S(2)}, u32[]{:S(2)}) collective-permute-start(bf16[400,128]{1,0:T(8,128)(2,1)S(1)} %get-tuple-element.9), channel_id=1, source_target_pairs={{4,0},{8,4},{12,8},{16,12},{20,16},{24,20},{28,24},{0,28},{5,1},{9... | collective-permute-start | bytes 307208 | tf_op jit(solution)/shard_map/ppermute | solution.py:320
  12.7 9.1 %copy-start.3 = (f32[2,1,1,2048]{3,2,1,0:T(1,128)S(1)}, f32[2,1,1,2048]{3,2,1,0:T(1,128)}, u32[]{:S(2)}) copy-start(f32[2,1,1,2048]{3,2,1,0:T(1,128)} %frac_ref.3) | copy-start | bytes 49156
  13.1 6.3 %collective-permute-start.2 = (bf16[336,128]{1,0:T(8,128)(2,1)S(1)}, bf16[336,128]{1,0:T(8,128)(2,1)S(1)}, u32[]{:S(2)}, u32[]{:S(2)}) collective-permute-start(bf16[336,128]{1,0:T(8,128)(2,1)S(1)} %get-tuple-element.10), channel_id=1, source_target_pairs={{0,1},{1,2},{2,3},{3,0},{4,5},{5,6},{6,7},{7,4},{8,9},{9,10},{10,1... | collective-permute-start | bytes 258056 | tf_op jit(solution)/shard_map/ppermute | solution.py:320
  15.2 6.6 %collective-permute-start.3 = (bf16[336,128]{1,0:T(8,128)(2,1)S(1)}, bf16[336,128]{1,0:T(8,128)(2,1)S(1)}, u32[]{:S(2)}, u32[]{:S(2)}) collective-permute-start(bf16[336,128]{1,0:T(8,128)(2,1)S(1)} %get-tuple-element.11), channel_id=1, source_target_pairs={{1,0},{2,1},{3,2},{0,3},{5,4},{6,5},{7,6},{4,7},{9,8},{10,9},{11,1... | collective-permute-start | bytes 258056 | tf_op jit(solution)/shard_map/ppermute | solution.py:320

commit v2 on v1

--- a/solution.py
+++ b/solution.py
@@ -19,10 +19,8 @@
 REACH = MARGIN + HALO
 PAD = -(-REACH // ROWS) * ROWS
 STRIP = PAD + MARGIN
-WIDE = REACH + MARGIN
-EDGE_PER = LANES // (2 * MARGIN)
-WIDE_PER = LANES // WIDE
-WIDE_STEP = LANES // WIDE_PER
+SPAN = 2 * MARGIN
+EDGE_PER = LANES // SPAN
 
 
 def half_turn(terms):
@@ -92,24 +90,39 @@
     return jnp.where(slot.astype(jnp.float32) < count, 1.0, 0.0)
 
 
+def is_even(axis):
+    return lax.axis_index(axis) % 2 == 0
+
+
 def spread_kernel(
-    shape, chunk, fish_ref, velocity_ref, cell_ref, frac_ref, force_ref,
-    grid_ref, up_ref, down_ref, left_ref, weight_ref,
+    shape, chunk, fish_hbm, velocity_hbm, cell_hbm, frac_hbm, force_hbm,
+    grid_ref, near_ref, far_ref, dense_x_ref, dense_y_ref, level_ref,
+    left_ref, fish_ref, velocity_ref, cell_ref, frac_ref, force_ref, sems,
 ):
+    pairs = (
+        (cell_hbm, cell_ref), (frac_hbm, frac_ref), (fish_hbm, fish_ref),
+        (force_hbm, force_ref), (velocity_hbm, velocity_ref),
+    )
+    copies = [pltpu.make_async_copy(a, b, sems.at[i]) for i, (a, b) in enumerate(pairs)]
+    for copy in copies:
+        copy.start()
+    for copy in copies[:-1]:
+        copy.wait()
     cells_x, cells_y, _, _ = shape
     levels, comps = velocity_ref.shape[:2]
     slots = cell_ref.shape[3]
-    wide_x = cells_x + 2 * MARGIN
+    wide_x = cells_x + SPAN
     count = alive_count(fish_ref)
+    level_ref[...] = cell_ref[2, 0]
     for first in range(0, slots, chunk):
         lanes = slice(first, first + chunk)
         dense_x, dense_y = marker_weights(cell_ref, frac_ref, lanes, shape)
-        weight_ref[:, lanes] = dense_y
-        alive = alive_lanes(count, first, chunk)
+        dense_x = dense_x * alive_lanes(count, first, chunk)
+        dense_x_ref[:, lanes] = dense_x
+        dense_y_ref[:, lanes] = dense_y
         level = cell_ref[2, 0, :, lanes]
         lefts = [
-            ((force_ref[c, 0, :, lanes] * alive) * dense_x).astype(jnp.bfloat16)
-            for c in range(comps)
+            (force_ref[c, 0, :, lanes] * dense_x).astype(jnp.bfloat16) for c in range(comps)
         ]
         for l in range(levels):
             hot = jnp.broadcast_to(jnp.where(level == l, 1.0, 0.0), (16, chunk))
@@ -119,40 +132,48 @@
                 product = lefts[c].reshape(wide_x // 16, 16, chunk) * hot[None]
                 left_ref[k * wide_x : (k + 1) * wide_x, lanes] = product.reshape(wide_x, chunk)
     total = lax.dot_general(
-        left_ref[...], weight_ref[...], (((1,), (1,)), ((), ())),
+        left_ref[...], dense_y_ref[...], (((1,), (1,)), ((), ())),
         preferred_element_type=jnp.float32,
     )
     items = levels * comps
     grid_ref[...] = total.reshape(items, wide_x, cells_y + LANES)
+    copies[-1].wait()
     for k in range(items):
         grid_ref[k, MARGIN : MARGIN + cells_x, :cells_y] += velocity_ref[k // comps, k % comps]
-    for out_ref, row in ((down_ref, 0), (up_ref, wide_x - STRIP)):
-        parts = [grid_ref[k, row : row + STRIP, :cells_y] for k in range(items)]
+    even = is_even("gx")
+    high = wide_x - STRIP
+    for out_ref, row in ((far_ref, jnp.where(even, 0, high)), (near_ref, jnp.where(even, high, 0))):
+        place = pl.ds(pl.multiple_of(row, ROWS), STRIP)
+        parts = [grid_ref[k, place, :cells_y] for k in range(items)]
         for group in range(0, items, EDGE_PER):
-            edge = None
+            edges = []
             for k in range(group, min(group + EDGE_PER, items)):
-                piece = grid_ref[k, row : row + STRIP, cells_y:]
-                if k > group:
-                    piece = pltpu.roll(piece, 2 * MARGIN * (k - group), 1)
-                    piece = piece + edge
-                edge = piece
-            parts.append(edge)
+                edges.append(rolled(grid_ref[k, place, cells_y:], SPAN * (k - group)))
+            parts.append(functools.reduce(jnp.add, edges))
         out_ref[...] = jnp.concatenate(parts, axis=0).astype(jnp.bfloat16)
+
+
+def rolled(value, shift):
+    shift = shift % LANES
+    return pltpu.roll(value, shift, 1) if shift else value
 
 
 def lane_index(rows):
     return lax.broadcasted_iota(jnp.int32, (rows, LANES), 1)
 
 
-def strip_parts(ref, k, items):
+def strip_parts(near, far, k, items):
     lane = lane_index(STRIP)
-    inner = ref[k * STRIP : (k + 1) * STRIP].astype(jnp.float32)
+    even = is_even("gx")
     row = (items + k // EDGE_PER) * STRIP
-    edge = ref[row : row + STRIP].astype(jnp.float32)
-    if k % EDGE_PER:
-        edge = pltpu.roll(edge, LANES - 2 * MARGIN * (k % EDGE_PER), 1)
-    edge = jnp.where((lane < MARGIN) | (lane >= LANES - MARGIN), edge, 0.0)
-    return inner, edge
+    inners, edges = [], []
+    for ref in (near, far):
+        inners.append(ref[k * STRIP : (k + 1) * STRIP].astype(jnp.float32))
+        edge = rolled(ref[row : row + STRIP].astype(jnp.float32), -SPAN * (k % EDGE_PER))
+        edges.append(jnp.where((lane < MARGIN) | (lane >= LANES - MARGIN), edge, 0.0))
+    before = (jnp.where(even, inners[1], inners[0]), jnp.where(even, edges[1], edges[0]))
+    after = (jnp.where(even, inners[0], inners[1]), jnp.where(even, edges[0], edges[1]))
+    return before, after
 
 
 def joined(center, before, after):
@@ -171,31 +192,62 @@
     )
 
 
-def extended_rows(grid_ref, from_left, from_right, k, items, cells_y):
-    before = strip_parts(from_left, k, items)
-    after = strip_parts(from_right, k, items)
+def extended_rows(grid_ref, near, far, k, items, cells_y):
+    before, after = strip_parts(near, far, k, items)
     inner = joined(grid_ref[k, :, :cells_y], before[0], after[0])
     edge = joined(grid_ref[k, :, cells_y:], before[1], after[1])
     return inner, edge
 
 
-def pack_kernel(shape, grid_ref, from_left, from_right, up_ref, down_ref):
+def folds(rows):
+    return [(row, min(SPAN, rows - row)) for row in range(0, rows, SPAN)]
+
+
+def pack_kernel(shape, grid_ref, near_x, far_x, near_ref, far_ref):
     cells_x, cells_y, _, _ = shape
     items = grid_ref.shape[0]
+    groups = -(-items // EDGE_PER)
     rows = cells_x + 2 * PAD
     lane = lane_index(rows)
-    for group in range(0, items, WIDE_PER):
-        ups, downs = [], []
-        for k in range(group, min(group + WIDE_PER, items)):
-            inner, edge = extended_rows(grid_ref, from_left, from_right, k, items, cells_y)
-            up = jnp.where(lane >= LANES - REACH, inner, jnp.where(lane < MARGIN, edge, 0.0))
-            down = jnp.where(lane < REACH, inner, jnp.where(lane >= LANES - MARGIN, edge, 0.0))
-            shift = WIDE_STEP * (k - group)
-            ups.append(pltpu.roll(up, shift, 1) if shift else up)
-            downs.append(pltpu.roll(down, shift, 1) if shift else down)
-        row = group // WIDE_PER * rows
-        up_ref[row : row + rows] = functools.reduce(jnp.add, ups).astype(jnp.bfloat16)
-        down_ref[row : row + rows] = functools.reduce(jnp.add, downs).astype(jnp.bfloat16)
+    even = is_even("gy")
+    mains = [[[], []] for _ in range(groups)]
+    halos = [[], []]
+    for k in range(items):
+        inner, edge = extended_rows(grid_ref, near_x, far_x, k, items, cells_y)
+        up = jnp.where(lane >= LANES - MARGIN, inner, jnp.where(lane < MARGIN, edge, 0.0))
+        down = jnp.where(lane < MARGIN, inner, jnp.where(lane >= LANES - MARGIN, edge, 0.0))
+        up_halo = (lane >= LANES - REACH) & (lane < LANES - MARGIN)
+        down_halo = (lane >= MARGIN) & (lane < REACH)
+        send = (jnp.where(even, up, down), jnp.where(even, down, up))
+        halo = (
+            rolled(jnp.where(up_halo, inner, 0.0), REACH + HALO * k),
+            rolled(jnp.where(down_halo, inner, 0.0), HALO * k - MARGIN),
+        )
+        halo = (jnp.where(even, halo[0], halo[1]), jnp.where(even, halo[1], halo[0]))
+        for side in range(2):
+            mains[k // EDGE_PER][side].append(rolled(send[side], SPAN * (k % EDGE_PER)))
+            halos[side].append(halo[side])
+    for side, out_ref in enumerate((near_ref, far_ref)):
+        for group in range(groups):
+            total = functools.reduce(jnp.add, mains[group][side])
+            out_ref[group * rows : (group + 1) * rows] = total.astype(jnp.bfloat16)
+        total = functools.reduce(jnp.add, halos[side])
+        folded = rolled(total[:SPAN], 0)
+        for index, (row, size) in enumerate(folds(rows)[1:]):
+            piece = rolled(total[row : row + size], SPAN * (index + 1))
+            if size < SPAN:
+                gap = jnp.zeros((SPAN - size, LANES), jnp.float32)
+                piece = jnp.concatenate([piece, gap], axis=0)
+            folded = folded + piece
+        out_ref[groups * rows : groups * rows + SPAN] = folded.astype(jnp.bfloat16)
+
+
+def unfolded(ref, rows, groups):
+    folded = ref[groups * rows : groups * rows + SPAN].astype(jnp.float32)
+    return jnp.concatenate(
+        [rolled(folded, -SPAN * index)[:size] for index, (_, size) in enumerate(folds(rows))],
+        axis=0,
+    )
 
 
 def shifted(inner, edge, lane):
@@ -208,29 +260,37 @@
 
 
 def finish_kernel(
-    shape, chunk, fish_ref, cell_ref, frac_ref, grid_ref, left_x, right_x, left_y, right_y,
+    shape, chunk, dense_x_ref, dense_y_ref, level_ref, grid_ref, near_x, far_x, near_y, far_y,
     next_ref, sampled_ref, moved_ref, carried_ref, sweep_ref, round_ref,
 ):
     cells_x, cells_y, _, _ = shape
     items = grid_ref.shape[0]
+    groups = -(-items // EDGE_PER)
     levels, comps = next_ref.shape[:2]
-    slots = cell_ref.shape[3]
-    wide_x = cells_x + 2 * MARGIN
+    slots = level_ref.shape[1]
+    wide_x = cells_x + SPAN
     rows = cells_x + 2 * PAD
     lane = lane_index(rows)
+    even = is_even("gy")
+    near_halo, far_halo = unfolded(near_y, rows, groups), unfolded(far_y, rows, groups)
+    before_halo = jnp.where(even, far_halo, near_halo)
+    after_halo = jnp.where(even, near_halo, far_halo)
     for k in range(items):
-        inner, edge = extended_rows(grid_ref, left_x, right_x, k, items, cells_y)
-        row = k // WIDE_PER * rows
-        before = left_y[row : row + rows].astype(jnp.float32)
-        after = right_y[row : row + rows].astype(jnp.float32)
-        shift = WIDE_STEP * (k % WIDE_PER)
-        if shift:
-            before = pltpu.roll(before, LANES - shift, 1)
-            after = pltpu.roll(after, LANES - shift, 1)
+        inner, edge = extended_rows(grid_ref, near_x, far_x, k, items, cells_y)
+        row = k // EDGE_PER * rows
+        near = near_y[row : row + rows].astype(jnp.float32)
+        far = far_y[row : row + rows].astype(jnp.float32)
+        shift = -SPAN * (k % EDGE_PER)
+        before = rolled(jnp.where(even, far, near), shift)
+        after = rolled(jnp.where(even, near, far), shift)
+        low = rolled(before_halo, -REACH - HALO * k)
+        high = rolled(after_halo, MARGIN - HALO * k)
         inner = inner + jnp.where(lane < MARGIN, before, 0.0)
         inner = inner + jnp.where(lane >= LANES - MARGIN, after, 0.0)
-        edge = edge + jnp.where(lane >= LANES - REACH, before, 0.0)
-        edge = edge + jnp.where(lane < REACH, after, 0.0)
+        edge = edge + jnp.where(lane >= LANES - MARGIN, before, 0.0)
+        edge = edge + jnp.where(lane < MARGIN, after, 0.0)
+        edge = jnp.where((lane >= LANES - REACH) & (lane < LANES - MARGIN), low, edge)
+        edge = jnp.where((lane >= MARGIN) & (lane < REACH), high, edge)
         moved_ref[0, k, ROWS : ROWS + rows] = inner
         moved_ref[1, k, ROWS : ROWS + rows] = edge
 
@@ -293,31 +353,33 @@
             if MARGIN <= row < MARGIN + cells_x:
                 next_ref[k // comps, k % comps, row - MARGIN : row - MARGIN + size] = results[k][0]
 
-    count = alive_count(fish_ref)
     for first in range(0, slots, chunk):
         lanes = slice(first, first + chunk)
-        dense_x, dense_y = marker_weights(cell_ref, frac_ref, lanes, shape)
-        alive = alive_lanes(count, first, chunk)
-        level = cell_ref[2, 0, :, lanes]
-        partial = jnp.dot(round_ref[...], dense_y, preferred_element_type=jnp.float32)
+        level = level_ref[:, lanes]
+        partial = jnp.dot(
+            round_ref[...], dense_y_ref[:, lanes], preferred_element_type=jnp.float32
+        )
         partial = partial.reshape(levels, comps, wide_x, chunk)
         for c in range(comps):
             picked = partial[levels - 1, c]
             for l in range(levels - 2, -1, -1):
                 picked = jnp.where(level == l, partial[l, c], picked)
-            sampled = jnp.sum(picked * dense_x, axis=0, keepdims=True)
-            sampled_ref[c, 0, :, lanes] = sampled * alive
+            sampled_ref[c, 0, :, lanes] = jnp.sum(
+                picked * dense_x_ref[:, lanes], axis=0, keepdims=True
+            )
 
 
 def whole(count):
     return [pl.BlockSpec(memory_space=pltpu.VMEM)] * count
 
 
-def exchange(up, down, axis):
+def exchange(near, far, axis):
     size = lax.axis_size(axis)
-    forward = [(i, (i + 1) % size) for i in range(size)]
-    backward = [(j, i) for i, j in forward]
-    return lax.ppermute(up, axis, forward), lax.ppermute(down, axis, backward)
+    if size % 2:
+        raise ValueError("odd axis")
+    near_pairs = [(i, i ^ 1) for i in range(size)]
+    far_pairs = [(i, (i - 1 if i % 2 == 0 else i + 1) % size) for i in range(size)]
+    return lax.ppermute(near, axis, near_pairs), lax.ppermute(far, axis, far_pairs)
 
 
 def body(velocity, marker_cell, marker_frac, marker_force, fish_owner):
@@ -325,40 +387,43 @@
     slots = marker_cell.shape[3]
     items = levels * comps
     shape = (cells_x, cells_y, cells_x * lax.axis_size("gx"), cells_y * lax.axis_size("gy"))
-    wide_x = cells_x + 2 * MARGIN
+    wide_x = cells_x + SPAN
     rows = cells_x + 2 * PAD
     chunk = min(512, slots)
     width = cells_y + LANES
     groups = -(-items // EDGE_PER)
     params = pltpu.CompilerParams(vmem_limit_bytes=40 * 1024 * 1024)
     edge_x = jax.ShapeDtypeStruct(((items + groups) * STRIP, LANES), jnp.bfloat16)
-    grid, up, down = pl.pallas_call(
+    arrays = (fish_owner, velocity, marker_cell, marker_frac, marker_force)
+    grid, near, far, dense_x, dense_y, level = pl.pallas_call(
         functools.partial(spread_kernel, shape, chunk),
         out_shape=(
             jax.ShapeDtypeStruct((items, wide_x, width), jnp.float32),
             edge_x,
             edge_x,
+            jax.ShapeDtypeStruct((wide_x, slots), jnp.float32),
+            jax.ShapeDtypeStruct((width, slots), jnp.bfloat16),
+            jax.ShapeDtypeStruct((1, slots), jnp.int32),
         ),
-        in_specs=whole(5),
-        out_specs=tuple(whole(3)),
-        scratch_shapes=[
-            pltpu.VMEM((items * wide_x, slots), jnp.bfloat16),
-            pltpu.VMEM((width, slots), jnp.bfloat16),
-        ],
+        in_specs=[pl.BlockSpec(memory_space=pltpu.HBM)] * 5,
+        out_specs=tuple(whole(6)),
+        scratch_shapes=[pltpu.VMEM((items * wide_x, slots), jnp.bfloat16)]
+        + [pltpu.VMEM(a.shape, a.dtype) for a in arrays]
+        + [pltpu.SemaphoreType.DMA((5,))],
         compiler_params=params,
         name="spread",
-    )(fish_owner, velocity, marker_cell, marker_frac, marker_force)
-    left_x, right_x = exchange(up, down, "gx")
-    edge_y = jax.ShapeDtypeStruct((-(-items // WIDE_PER) * rows, LANES), jnp.bfloat16)
-    up, down = pl.pallas_call(
+    )(*(pltpu.with_memory_space_constraint(a, pltpu.HBM) for a in arrays))
+    near_x, far_x = exchange(near, far, "gx")
+    edge_y = jax.ShapeDtypeStruct((groups * rows + SPAN, LANES), jnp.bfloat16)
+    near, far = pl.pallas_call(
         functools.partial(pack_kernel, shape),
         out_shape=(edge_y, edge_y),
         in_specs=whole(3),
         out_specs=tuple(whole(2)),
         compiler_params=params,
         name="pack",
-    )(grid, left_x, right_x)
-    left_y, right_y = exchange(up, down, "gy")
+    )(grid, near_x, far_x)
+    near_y, far_y = exchange(near, far, "gy")
     field = pltpu.VMEM((2, items, rows + 2 * ROWS, LANES), jnp.float32)
     return pl.pallas_call(
         functools.partial(finish_kernel, shape, chunk),
@@ -371,7 +436,7 @@
         scratch_shapes=[field, field, field, pltpu.VMEM((items * wide_x, width), jnp.bfloat16)],
         compiler_params=params,
         name="finish",
-    )(fish_owner, marker_cell, marker_frac, grid, left_x, right_x, left_y, right_y)
+    )(dense_x, dense_y, level, grid, near_x, far_x, near_y, far_y)
 
 
 def solution(mesh):

time: 25.5 us -> 21.9 us (0.86)
  local copies, waits for them, and re-layouts: 3.77 us -> 0 us
  waiting for transfers between devices: 7.87 us -> 6.42 us
  Pallas kernels: 5.19 us -> 6.41 us
  starting transfers between devices: 7.72 us -> 8.28 us
    unnamed x12 -> x0, local copies, waits for them, and re-layouts: 3.77 us -> none
    ppermute x4, waiting for transfers between devices: 7.87 us -> 6.42 us  [the longest x2 5.09 us: exchange(): lax.ppermute(far, axis, far_pairs)]
    pallas_call x1, Pallas kernels: 1.35 us -> 2.38 us  [body(): pl.pallas_call(functools.partial(spread_kernel, shape, chunk), out_shape=...]
    ppermute x4, starting transfers between devices: 7.72 us -> 8.28 us  [the longest x2 6.2 us: exchange(): lax.ppermute(far, axis, far_pairs)]
    pallas_call x1, Pallas kernels: 0.4 us -> 0.77 us  [body(): pl.pallas_call(functools.partial(pack_kernel, shape), out_shape=(edge_y,...]
where the time goes in v2:
time: 21.9 us; the launch traced here: 21.8 us
  starting transfers between devices  8.28 us (38%)
  waiting for transfers between devices  6.42 us (29%)
  Pallas kernels  6.41 us (29%)
  between operations  0.65 us (3%)
    ppermute x2, starting transfers between devices, exchange(): lax.ppermute(far, axis, far_pairs)  6.2 us
    ppermute x2, waiting for transfers between devices, exchange(): lax.ppermute(far, axis, far_pairs)  5.09 us
    pallas_call x1, Pallas kernels, body(): pl.pallas_call(functools.partial(finish_kernel, shape, chunk), out_shape=...  3.26 us
    pallas_call x1, Pallas kernels, body(): pl.pallas_call(functools.partial(spread_kernel, shape, chunk), out_shape=...  2.38 us
    ppermute x2, starting transfers between devices, exchange(): lax.ppermute(near, axis, near_pairs)  2.08 us
    ppermute x2, waiting for transfers between devices, exchange(): lax.ppermute(near, axis, near_pairs)  1.33 us
    pallas_call x1, Pallas kernels, body(): pl.pallas_call(functools.partial(pack_kernel, shape), out_shape=(edge_y,...  0.77 us
  transfers between devices with their start and end apart: 4, of which 3 were waited for; matrix products, arithmetic and copies ran while one was open for 0% of the time, Pallas kernels for 0%

profile of v2, /device:TPU:0, one launch (start us, length us, event | category | flops | bytes accessed | tf_op | source)
XLA Modules:
  0.0 21.8 jit_solution(7424058425819417396)
XLA Ops:
  0.6 2.4 %spread.1 = (f32[8,96,256]{2,1,0:T(8,128)S(1)}, bf16[400,128]{1,0:T(8,128)(2,1)S(1)}, bf16[400,128]{1,0:T(8,128)(2,1)S(1)}, f32[96,2048]{1,0:T(8,128)S(1)}, bf16...) custom-call(s32[48]{0:T(128)} %fish_hbm.1, f32[4,2,64,128]{3,2,1,0:T(8,128)} %velocity_hbm.1, ...), custom_call_target="tpu_custom_call" | custom-call | tf_op jit(solution)/shard_map/spread/pallas_call | solution.py:398
  3.0 0.5 %collective-permute-start = (bf16[400,128]{1,0:T(8,128)(2,1)S(1)}, bf16[400,128]{1,0:T(8,128)(2,1)S(1)}, u32[]{:S(2)}, u32[]{:S(2)}) collective-permute-start(bf16[400,128]{1,0:T(8,128)(2,1)S(1)} %get-tuple-element.14), channel_id=1, source_target_pairs={{0,4},{4,0},{8,12},{12,8},{16,20},{20,16},{24,28},{28,24},{1,5},{5... | collective-permute-start | bytes 307208 | tf_op jit(solution)/shard_map/ppermute | solution.py:382
  3.5 4.7 %collective-permute-start.1 = (bf16[400,128]{1,0:T(8,128)(2,1)S(1)}, bf16[400,128]{1,0:T(8,128)(2,1)S(1)}, u32[]{:S(2)}, u32[]{:S(2)}) collective-permute-start(bf16[400,128]{1,0:T(8,128)(2,1)S(1)} %get-tuple-element.15), channel_id=1, source_target_pairs={{0,28},{4,8},{8,4},{12,16},{16,12},{20,24},{24,20},{28,0},{1,29},{... | collective-permute-start | bytes 307208 | tf_op jit(solution)/shard_map/ppermute | solution.py:382
  8.3 0.0 collective-permute-done.near_x
  8.3 2.7 %collective-permute-done.1.far_x = bf16[400,128]{1,0:T(8,128)(2,1)S(1)} collective-permute-done((bf16[400,128]{1,0:T(8,128)(2,1)S(1)}, bf16[400,128]{1,0:T(8,128)(2,1)S(1)}, u32[]{:S(2)}, u32[]{:S(2)}) %collective-permute-start.1) | collective-permute-done | bytes 102432 | tf_op jit(solution)/shard_map/ppermute | solution.py:382
  11.0 0.8 %pack.1 = (bf16[256,128]{1,0:T(8,128)(2,1)S(1)}, bf16[256,128]{1,0:T(8,128)(2,1)S(1)}) custom-call(f32[8,96,256]{2,1,0:T(8,128)S(1)} %get-tuple-element.13.grid_ref, bf16[400,128]{1,0:T(8,128)(2,1)S(1)} %collective-permute-done.near_x, bf16[400,128]{1,0:T(8,128)(2,1)S(1)} %collective-permute-done.1.far_x), custom_call_target="tpu_custom_call" | custom-call | tf_op jit(solution)/shard_map/pack/pallas_call | solution.py:418
  11.8 1.6 %collective-permute-start.2 = (bf16[256,128]{1,0:T(8,128)(2,1)S(1)}, bf16[256,128]{1,0:T(8,128)(2,1)S(1)}, u32[]{:S(2)}, u32[]{:S(2)}) collective-permute-start(bf16[256,128]{1,0:T(8,128)(2,1)S(1)} %get-tuple-element.16), channel_id=1, source_target_pairs={{0,1},{1,0},{2,3},{3,2},{4,5},{5,4},{6,7},{7,6},{8,9},{9,8},{10,11... | collective-permute-start | bytes 196616 | tf_op jit(solution)/shard_map/ppermute | solution.py:382
  13.3 1.5 %collective-permute-start.3 = (bf16[256,128]{1,0:T(8,128)(2,1)S(1)}, bf16[256,128]{1,0:T(8,128)(2,1)S(1)}, u32[]{:S(2)}, u32[]{:S(2)}) collective-permute-start(bf16[256,128]{1,0:T(8,128)(2,1)S(1)} %get-tuple-element.17), channel_id=1, source_target_pairs={{0,3},{1,2},{2,1},{3,0},{4,7},{5,6},{6,5},{7,4},{8,11},{9,10},{10,... | collective-permute-start | bytes 196616 | tf_op jit(solution)/shard_map/ppermute | solution.py:382
  14.8 1.3 %collective-permute-done.2.near_y = bf16[256,128]{1,0:T(8,128)(2,1)S(1)} collective-permute-done((bf16[256,128]{1,0:T(8,128)(2,1)S(1)}, bf16[256,128]{1,0:T(8,128)(2,1)S(1)}, u32[]{:S(2)}, u32[]{:S(2)}) %collective-permute-start.2) | collective-permute-done | bytes 65568 | tf_op jit(solution)/shard_map/ppermute | solution.py:382
  16.1 2.4 %collective-permute-done.3.far_y = bf16[256,128]{1,0:T(8,128)(2,1)S(1)} collective-permute-done((bf16[256,128]{1,0:T(8,128)(2,1)S(1)}, bf16[256,128]{1,0:T(8,128)(2,1)S(1)}, u32[]{:S(2)}, u32[]{:S(2)}) %collective-permute-start.3) | collective-permute-done | bytes 65568 | tf_op jit(solution)/shard_map/ppermute | solution.py:382
  18.5 3.3 %finish.1 = (f32[4,2,64,128]{3,2,1,0:T(8,128)}, f32[2,1,1,2048]{3,2,1,0:T(1,128)}) custom-call(f32[96,2048]{1,0:T(8,128)S(1)} %get-tuple-element.10.dense_x_ref, bf16[256,2048]{1,0:T(8,128)(2,1)S(1)} %get-tuple-element.11.dense_y_ref, s32[1,2048]{1,0:T(1,128)S(1)} %get-tuple-element.12.level_ref, f32[8,96,256]{2,1,0:T(8,128)S(1)} %get-tuple-element.13.grid_ref, ...), custom_call_target="tpu_custom_call" | custom-call | tf_op jit(solution)/shard_map/finish/pallas_call | solution.py:428
Async XLA Ops:
  3.0 5.2 %collective-permute-start = (bf16[400,128]{1,0:T(8,128)(2,1)S(1)}, bf16[400,128]{1,0:T(8,128)(2,1)S(1)}, u32[]{:S(2)}, u32[]{:S(2)}) collective-permute-start(bf16[400,128]{1,0:T(8,128)(2,1)S(1)} %get-tuple-element.14), channel_id=1, source_target_pairs={{0,4},{4,0},{8,12},{12,8},{16,20},{20,16},{24,28},{28,24},{1,5},{5... | collective-permute-start | bytes 307208 | tf_op jit(solution)/shard_map/ppermute | solution.py:382
  3.5 7.4 %collective-permute-start.1 = (bf16[400,128]{1,0:T(8,128)(2,1)S(1)}, bf16[400,128]{1,0:T(8,128)(2,1)S(1)}, u32[]{:S(2)}, u32[]{:S(2)}) collective-permute-start(bf16[400,128]{1,0:T(8,128)(2,1)S(1)} %get-tuple-element.15), channel_id=1, source_target_pairs={{0,28},{4,8},{8,4},{12,16},{16,12},{20,24},{24,20},{28,0},{1,29},{... | collective-permute-start | bytes 307208 | tf_op jit(solution)/shard_map/ppermute | solution.py:382
  11.8 4.4 %collective-permute-start.2 = (bf16[256,128]{1,0:T(8,128)(2,1)S(1)}, bf16[256,128]{1,0:T(8,128)(2,1)S(1)}, u32[]{:S(2)}, u32[]{:S(2)}) collective-permute-start(bf16[256,128]{1,0:T(8,128)(2,1)S(1)} %get-tuple-element.16), channel_id=1, source_target_pairs={{0,1},{1,0},{2,3},{3,2},{4,5},{5,4},{6,7},{7,6},{8,9},{9,8},{10,11... | collective-permute-start | bytes 196616 | tf_op jit(solution)/shard_map/ppermute | solution.py:382
  13.3 5.2 %collective-permute-start.3 = (bf16[256,128]{1,0:T(8,128)(2,1)S(1)}, bf16[256,128]{1,0:T(8,128)(2,1)S(1)}, u32[]{:S(2)}, u32[]{:S(2)}) collective-permute-start(bf16[256,128]{1,0:T(8,128)(2,1)S(1)} %get-tuple-element.17), channel_id=1, source_target_pairs={{0,3},{1,2},{2,1},{3,0},{4,7},{5,6},{6,5},{7,4},{8,11},{9,10},{10,... | collective-permute-start | bytes 196616 | tf_op jit(solution)/shard_map/ppermute | solution.py:382

commit v3 on v2

--- a/solution.py
+++ b/solution.py
@@ -250,21 +250,84 @@
     )
 
 
-def shifted(inner, edge, lane):
-    below_inner, below_edge = pltpu.roll(inner, 1, 1), pltpu.roll(edge, 1, 1)
-    above_inner, above_edge = pltpu.roll(inner, LANES - 1, 1), pltpu.roll(edge, LANES - 1, 1)
-    first, last = lane == 0, lane == LANES - 1
-    below = (jnp.where(first, below_edge, below_inner), jnp.where(first, below_inner, below_edge))
-    above = (jnp.where(last, above_edge, above_inner), jnp.where(last, above_inner, above_edge))
-    return below, above
+def around(ref, k, start, size):
+    center = ref[k, start : start + size]
+    back = ref[k, start - 1 : start - 1 + size]
+    fore = ref[k, start + 1 : start + 1 + size]
+    return center, back, fore, rolled(center, 1), rolled(center, -1)
+
+
+def advect(moved_ref, carried_ref, levels, comps, rows):
+    for start in range(ROWS, ROWS + rows, ROWS):
+        for l in range(levels):
+            pieces = [around(moved_ref, l * comps + c, start, ROWS) for c in range(comps)]
+            speed_x, speed_y = COURANT * pieces[0][0], COURANT * pieces[1][0]
+            ahead_x, astern_x = jnp.maximum(speed_x, 0.0), jnp.minimum(speed_x, 0.0)
+            ahead_y, astern_y = jnp.maximum(speed_y, 0.0), jnp.minimum(speed_y, 0.0)
+            for c in range(comps):
+                center, back, fore, below, above = pieces[c]
+                change = ahead_x * (center - back) + astern_x * (fore - center)
+                change = change + ahead_y * (center - below) + astern_y * (above - center)
+                carried_ref[l * comps + c, start : start + ROWS] = center - change
+
+
+def sweep(ref, carried_ref, levels, comps, start, size):
+    scale = 1.0 / (1.0 + 6.0 * VISCOUS)
+    centers, results = [], []
+    for k in range(levels * comps):
+        center, back, fore, below, above = around(ref, k, start, size)
+        centers.append(center)
+        results.append(back + fore + below + above)
+    for k in range(levels * comps):
+        higher = min(k // comps + 1, levels - 1) * comps + k % comps
+        lower = max(k // comps - 1, 0) * comps + k % comps
+        summed = results[k] + centers[higher] + centers[lower]
+        source = carried_ref[k, start : start + size]
+        results[k] = scale * source + (VISCOUS * scale) * summed
+    return results
+
+
+def first_steps(moved_ref, carried_ref, sweep_ref, levels, comps, rows):
+    advect(moved_ref, carried_ref, levels, comps, rows)
+    for start in range(ROWS, ROWS + rows, ROWS):
+        results = sweep(carried_ref, carried_ref, levels, comps, start, ROWS)
+        for k in range(levels * comps):
+            sweep_ref[k, start : start + ROWS] = results[k]
+
+
+RIM = REACH + HALO
+HALF = LANES // 2
+
+
+def inner_kernel(
+    shape, levels, grid_ref, near_x, far_x, inner_ref, rim_ref, moved_ref, carried_ref, sweep_ref,
+):
+    cells_x, cells_y, _, _ = shape
+    items = grid_ref.shape[0]
+    comps = items // levels
+    wide_x = cells_x + SPAN
+    rows = cells_x + 2 * PAD
+    lane = lane_index(rows)
+    for k in range(items):
+        inner, edge = extended_rows(grid_ref, near_x, far_x, k, items, cells_y)
+        moved_ref[k, ROWS : ROWS + rows] = inner
+        low = jnp.where(lane < RIM, inner, jnp.where(lane >= LANES - MARGIN, edge, 0.0))
+        high = jnp.where(lane >= LANES - RIM, inner, jnp.where(lane < MARGIN, edge, 0.0))
+        rim_ref[k] = low + rolled(high, HALF)
+    first_steps(moved_ref, carried_ref, sweep_ref, levels, comps, rows)
+    for row in range(0, wide_x, ROWS):
+        start = ROWS + PAD - MARGIN + row
+        results = sweep(sweep_ref, carried_ref, levels, comps, start, ROWS)
+        for k in range(items):
+            inner_ref[k, row : row + ROWS] = results[k]
 
 
 def finish_kernel(
-    shape, chunk, dense_x_ref, dense_y_ref, level_ref, grid_ref, near_x, far_x, near_y, far_y,
+    shape, chunk, dense_x_ref, dense_y_ref, level_ref, inner_ref, rim_ref, near_y, far_y,
     next_ref, sampled_ref, moved_ref, carried_ref, sweep_ref, round_ref,
 ):
     cells_x, cells_y, _, _ = shape
-    items = grid_ref.shape[0]
+    items = rim_ref.shape[0]
     groups = -(-items // EDGE_PER)
     levels, comps = next_ref.shape[:2]
     slots = level_ref.shape[1]
@@ -273,85 +336,43 @@
     lane = lane_index(rows)
     even = is_even("gy")
     near_halo, far_halo = unfolded(near_y, rows, groups), unfolded(far_y, rows, groups)
-    before_halo = jnp.where(even, far_halo, near_halo)
-    after_halo = jnp.where(even, near_halo, far_halo)
-    for k in range(items):
-        inner, edge = extended_rows(grid_ref, near_x, far_x, k, items, cells_y)
-        row = k // EDGE_PER * rows
+    before = jnp.where(even, far_halo, near_halo)
+    after = rolled(jnp.where(even, near_halo, far_halo), HALF + MARGIN + REACH)
+    turned = (HALF + MARGIN + REACH) % LANES
+    halo = jnp.where((lane >= turned) & (lane < turned + HALO * items), after, before)
+    for group in range(groups):
+        row = group * rows
         near = near_y[row : row + rows].astype(jnp.float32)
         far = far_y[row : row + rows].astype(jnp.float32)
-        shift = -SPAN * (k % EDGE_PER)
-        before = rolled(jnp.where(even, far, near), shift)
-        after = rolled(jnp.where(even, near, far), shift)
-        low = rolled(before_halo, -REACH - HALO * k)
-        high = rolled(after_halo, MARGIN - HALO * k)
-        inner = inner + jnp.where(lane < MARGIN, before, 0.0)
-        inner = inner + jnp.where(lane >= LANES - MARGIN, after, 0.0)
-        edge = edge + jnp.where(lane >= LANES - MARGIN, before, 0.0)
-        edge = edge + jnp.where(lane < MARGIN, after, 0.0)
-        edge = jnp.where((lane >= LANES - REACH) & (lane < LANES - MARGIN), low, edge)
-        edge = jnp.where((lane >= MARGIN) & (lane < REACH), high, edge)
-        moved_ref[0, k, ROWS : ROWS + rows] = inner
-        moved_ref[1, k, ROWS : ROWS + rows] = edge
-
-    def around(ref, k, start, size, lane):
-        center = tuple(ref[t, k, start : start + size] for t in range(2))
-        back = tuple(ref[t, k, start - 1 : start - 1 + size] for t in range(2))
-        fore = tuple(ref[t, k, start + 1 : start + 1 + size] for t in range(2))
-        below, above = shifted(*center, lane)
-        return center, back, fore, below, above
-
-    size = ROWS
-    small = lane_index(size)
-    for start in range(ROWS, ROWS + rows, size):
-        for l in range(levels):
-            pieces = [around(moved_ref, l * comps + c, start, size, small) for c in range(comps)]
-            for t in range(2):
-                speed_x = COURANT * pieces[0][0][t]
-                speed_y = COURANT * pieces[1][0][t]
-                ahead_x, astern_x = jnp.maximum(speed_x, 0.0), jnp.minimum(speed_x, 0.0)
-                ahead_y, astern_y = jnp.maximum(speed_y, 0.0), jnp.minimum(speed_y, 0.0)
-                for c in range(comps):
-                    center, back, fore, below, above = (part[t] for part in pieces[c])
-                    change = ahead_x * (center - back) + astern_x * (fore - center)
-                    change = change + ahead_y * (center - below) + astern_y * (above - center)
-                    carried_ref[t, l * comps + c, start : start + size] = center - change
-
-    scale = 1.0 / (1.0 + 6.0 * VISCOUS)
-
-    def sweep(ref, start, size, lane):
-        results = {}
-        centers = {}
+        before = jnp.where(even, far, near)
+        after = rolled(jnp.where(even, near, far), HALF)
+        for k in range(group * EDGE_PER, min((group + 1) * EDGE_PER, items)):
+            slot = k % EDGE_PER
+            place = (lane + (LANES + MARGIN - SPAN * slot)) % LANES
+            main = rolled(jnp.where(place < SPAN, before, after), -SPAN * slot)
+            place = (lane + MARGIN) % HALF
+            value = rim_ref[k] + jnp.where(place < SPAN, main, 0.0)
+            outer = rolled(halo, -REACH - HALO * k)
+            low = (lane >= LANES - REACH) & (lane < LANES - MARGIN)
+            high = (lane >= HALF + MARGIN) & (lane < HALF + REACH)
+            moved_ref[k, ROWS : ROWS + rows] = jnp.where(low | high, outer, value)
+
+    first_steps(moved_ref, carried_ref, sweep_ref, levels, comps, rows)
+    size = 2 * ROWS
+    lane = lane_index(size)
+    for row in range(0, wide_x, size):
+        start = ROWS + PAD - MARGIN + row
+        results = sweep(sweep_ref, carried_ref, levels, comps, start, size)
         for k in range(items):
-            center, back, fore, below, above = around(ref, k, start, size, lane)
-            centers[k] = center
-            results[k] = [back[t] + fore[t] + below[t] + above[t] for t in range(2)]
-        for k in range(items):
-            higher = min(k // comps + 1, levels - 1) * comps + k % comps
-            lower = max(k // comps - 1, 0) * comps + k % comps
-            for t in range(2):
-                summed = results[k][t] + centers[higher][t] + centers[lower][t]
-                source = carried_ref[t, k, start : start + size]
-                results[k][t] = scale * source + (VISCOUS * scale) * summed
-        return results
-
-    for start in range(ROWS, ROWS + rows, size):
-        results = sweep(carried_ref, start, size, small)
-        for k in range(items):
-            for t in range(2):
-                sweep_ref[t, k, start : start + size] = results[k][t]
-    size = 2 * ROWS
-    small = lane_index(size)
-    near = PAD - MARGIN
-    for row in range(0, wide_x, size):
-        results = sweep(sweep_ref, ROWS + near + row, size, small)
-        for k in range(items):
+            low, high = results[k], rolled(results[k], HALF)
+            inner = inner_ref[k, row : row + size]
+            inner = jnp.where(lane < REACH, low, jnp.where(lane >= LANES - REACH, high, inner))
+            edge = jnp.where(lane < MARGIN, high, low)
             place = slice(k * wide_x + row, k * wide_x + row + size)
-            for t in range(2):
-                lanes = slice(t * cells_y, t * cells_y + LANES)
-                round_ref[place, lanes] = results[k][t].astype(jnp.bfloat16)
+            round_ref[place, :cells_y] = inner.astype(jnp.bfloat16)
+            round_ref[place, cells_y:] = edge.astype(jnp.bfloat16)
             if MARGIN <= row < MARGIN + cells_x:
-                next_ref[k // comps, k % comps, row - MARGIN : row - MARGIN + size] = results[k][0]
+                next_ref[k // comps, k % comps, row - MARGIN : row - MARGIN + size] = inner
 
     for first in range(0, slots, chunk):
         lanes = slice(first, first + chunk)
@@ -379,7 +400,8 @@
         raise ValueError("odd axis")
     near_pairs = [(i, i ^ 1) for i in range(size)]
     far_pairs = [(i, (i - 1 if i % 2 == 0 else i + 1) % size) for i in range(size)]
-    return lax.ppermute(near, axis, near_pairs), lax.ppermute(far, axis, far_pairs)
+    far = lax.ppermute(far, axis, far_pairs)
+    return lax.ppermute(near, axis, near_pairs), far
 
 
 def body(velocity, marker_cell, marker_frac, marker_force, fish_owner):
@@ -424,19 +446,35 @@
         name="pack",
     )(grid, near_x, far_x)
     near_y, far_y = exchange(near, far, "gy")
-    field = pltpu.VMEM((2, items, rows + 2 * ROWS, LANES), jnp.float32)
+    field = pltpu.VMEM((items, rows + 2 * ROWS, LANES), jnp.float32)
+    inner, rim = pl.pallas_call(
+        functools.partial(inner_kernel, shape, levels),
+        out_shape=(
+            jax.ShapeDtypeStruct((items, wide_x, LANES), jnp.float32),
+            jax.ShapeDtypeStruct((items, rows, LANES), jnp.float32),
+        ),
+        in_specs=whole(3),
+        out_specs=tuple(whole(2)),
+        scratch_shapes=[field, field, field],
+        compiler_params=params,
+        cost_estimate=pl.CostEstimate(
+            flops=40 * items * rows * LANES, bytes_accessed=16 * items * rows * LANES,
+            transcendentals=0,
+        ),
+        name="inner",
+    )(grid, near_x, far_x)
     return pl.pallas_call(
         functools.partial(finish_kernel, shape, chunk),
         out_shape=(
             jax.ShapeDtypeStruct(velocity.shape, jnp.float32),
             jax.ShapeDtypeStruct((comps, 1, 1, slots), jnp.float32),
         ),
-        in_specs=whole(8),
+        in_specs=whole(7),
         out_specs=tuple(whole(2)),
         scratch_shapes=[field, field, field, pltpu.VMEM((items * wide_x, width), jnp.bfloat16)],
         compiler_params=params,
         name="finish",
-    )(dense_x, dense_y, level, grid, near_x, far_x, near_y, far_y)
+    )(dense_x, dense_y, level, inner, rim, near_y, far_y)
 
 
 def solution(mesh):

time: 21.9 us -> 21.4 us (0.977)
  waiting for transfers between devices: 6.42 us -> 5.26 us
  Pallas kernels: 6.41 us -> 7.01 us
    ppermute x4, waiting for transfers between devices: 6.42 us -> 5.26 us  [the longest x2 5.09 us: exchange(): far = lax.ppermute(far, axis, far_pairs)]
    pallas_call x0 -> x1, Pallas kernels: none -> 1.15 us  [body(): pl.pallas_call(functools.partial(inner_kernel, shape, levels), out_shape=...]
    pallas_call x1, Pallas kernels: 3.26 us -> 2.71 us  [body(): pl.pallas_call(functools.partial(finish_kernel, shape, chunk), out_shape=...]
  transfers between devices with their start and end apart: 4 -> 4, of which waited for: 3 -> 3; matrix products, arithmetic and copies ran while one was open for 0% -> 0% of each run, Pallas kernels for 0% -> 5%
where the time goes in v3:
time: 21.4 us; the launch traced here: 21.2 us
  starting transfers between devices  8.28 us (39%)
  Pallas kernels  7.01 us (33%)
  waiting for transfers between devices  5.26 us (25%)
  between operations  0.66 us (3%)
    ppermute x2, starting transfers between devices, exchange(): far = lax.ppermute(far, axis, far_pairs)  6.2 us
    ppermute x2, waiting for transfers between devices, exchange(): far = lax.ppermute(far, axis, far_pairs)  5.09 us
    pallas_call x1, Pallas kernels, body(): pl.pallas_call(functools.partial(finish_kernel, shape, chunk), out_shape=...  2.71 us
    pallas_call x1, Pallas kernels, body(): pl.pallas_call(functools.partial(spread_kernel, shape, chunk), out_shape=...  2.38 us
    ppermute x2, starting transfers between devices, exchange(): return (lax.ppermute(near, axis, near_pairs), far)  2.08 us
    pallas_call x1, Pallas kernels, body(): pl.pallas_call(functools.partial(inner_kernel, shape, levels), out_shape=...  1.15 us
    pallas_call x1, Pallas kernels, body(): pl.pallas_call(functools.partial(pack_kernel, shape), out_shape=(edge_y,...  0.77 us
  transfers between devices with their start and end apart: 4, of which 3 were waited for; matrix products, arithmetic and copies ran while one was open for 0% of the time, Pallas kernels for 5%

profile of v3, /device:TPU:0, one launch (start us, length us, event | category | flops | bytes accessed | tf_op | source)
XLA Modules:
  0.0 21.2 jit_solution(3112907668624235750)
XLA Ops:
  0.6 2.4 %spread.1 = (f32[8,96,256]{2,1,0:T(8,128)S(1)}, bf16[400,128]{1,0:T(8,128)(2,1)S(1)}, bf16[400,128]{1,0:T(8,128)(2,1)S(1)}, f32[96,2048]{1,0:T(8,128)S(1)}, bf16...) custom-call(s32[48]{0:T(128)} %fish_hbm.1, f32[4,2,64,128]{3,2,1,0:T(8,128)} %velocity_hbm.1, ...), custom_call_target="tpu_custom_call" | custom-call | tf_op jit(solution)/shard_map/spread/pallas_call | solution.py:420
  3.0 0.5 %collective-permute-start = (bf16[400,128]{1,0:T(8,128)(2,1)S(1)}, bf16[400,128]{1,0:T(8,128)(2,1)S(1)}, u32[]{:S(2)}, u32[]{:S(2)}) collective-permute-start(bf16[400,128]{1,0:T(8,128)(2,1)S(1)} %get-tuple-element.16), channel_id=1, source_target_pairs={{0,4},{4,0},{8,12},{12,8},{16,20},{20,16},{24,28},{28,24},{1,5},{5... | collective-permute-start | bytes 307208 | tf_op jit(solution)/shard_map/ppermute | solution.py:404
  3.5 4.7 %collective-permute-start.1 = (bf16[400,128]{1,0:T(8,128)(2,1)S(1)}, bf16[400,128]{1,0:T(8,128)(2,1)S(1)}, u32[]{:S(2)}, u32[]{:S(2)}) collective-permute-start(bf16[400,128]{1,0:T(8,128)(2,1)S(1)} %get-tuple-element.17), channel_id=1, source_target_pairs={{0,28},{4,8},{8,4},{12,16},{16,12},{20,24},{24,20},{28,0},{1,29},{... | collective-permute-start | bytes 307208 | tf_op jit(solution)/shard_map/ppermute | solution.py:403
  8.3 0.0 collective-permute-done.near_x
  8.3 2.7 %collective-permute-done.1.far_x = bf16[400,128]{1,0:T(8,128)(2,1)S(1)} collective-permute-done((bf16[400,128]{1,0:T(8,128)(2,1)S(1)}, bf16[400,128]{1,0:T(8,128)(2,1)S(1)}, u32[]{:S(2)}, u32[]{:S(2)}) %collective-permute-start.1) | collective-permute-done | bytes 102432 | tf_op jit(solution)/shard_map/ppermute | solution.py:403
  11.0 0.8 %pack.1 = (bf16[256,128]{1,0:T(8,128)(2,1)S(1)}, bf16[256,128]{1,0:T(8,128)(2,1)S(1)}) custom-call(f32[8,96,256]{2,1,0:T(8,128)S(1)} %get-tuple-element.15.grid_ref, bf16[400,128]{1,0:T(8,128)(2,1)S(1)} %collective-permute-done.near_x, bf16[400,128]{1,0:T(8,128)(2,1)S(1)} %collective-permute-done.1.far_x), custom_call_target="tpu_custom_call" | custom-call | tf_op jit(solution)/shard_map/pack/pallas_call | solution.py:440
  11.8 1.6 %collective-permute-start.2 = (bf16[256,128]{1,0:T(8,128)(2,1)S(1)}, bf16[256,128]{1,0:T(8,128)(2,1)S(1)}, u32[]{:S(2)}, u32[]{:S(2)}) collective-permute-start(bf16[256,128]{1,0:T(8,128)(2,1)S(1)} %get-tuple-element.20), channel_id=1, source_target_pairs={{0,1},{1,0},{2,3},{3,2},{4,5},{5,4},{6,7},{7,6},{8,9},{9,8},{10,11... | collective-permute-start | bytes 196616 | tf_op jit(solution)/shard_map/ppermute | solution.py:404
  13.3 1.5 %collective-permute-start.3 = (bf16[256,128]{1,0:T(8,128)(2,1)S(1)}, bf16[256,128]{1,0:T(8,128)(2,1)S(1)}, u32[]{:S(2)}, u32[]{:S(2)}) collective-permute-start(bf16[256,128]{1,0:T(8,128)(2,1)S(1)} %get-tuple-element.21), channel_id=1, source_target_pairs={{0,3},{1,2},{2,1},{3,0},{4,7},{5,6},{6,5},{7,4},{8,11},{9,10},{10,... | collective-permute-start | bytes 196616 | tf_op jit(solution)/shard_map/ppermute | solution.py:403
  14.8 1.2 %inner.1 = (f32[8,96,128]{2,1,0:T(8,128)S(1)}, f32[8,112,128]{2,1,0:T(8,128)S(1)}) custom-call(f32[8,96,256]{2,1,0:T(8,128)S(1)} %get-tuple-element.15.grid_ref, bf16[400,128]{1,0:T(8,128)(2,1)S(1)} %collective-permute-done.near_x, bf16[400,128]{1,0:T(8,128)(2,1)S(1)} %collective-permute-done.1.far_x), custom_call_target="tpu_custom_call" | custom-call | flops 4587520 | bytes 1835008 | tf_op jit(solution)/shard_map/inner/pallas_call | solution.py:450
  16.0 0.2 collective-permute-done.2.near_y
  16.1 2.4 %collective-permute-done.3.far_y = bf16[256,128]{1,0:T(8,128)(2,1)S(1)} collective-permute-done((bf16[256,128]{1,0:T(8,128)(2,1)S(1)}, bf16[256,128]{1,0:T(8,128)(2,1)S(1)}, u32[]{:S(2)}, u32[]{:S(2)}) %collective-permute-start.3) | collective-permute-done | bytes 65568 | tf_op jit(solution)/shard_map/ppermute | solution.py:403
  18.5 2.7 %finish.1 = (f32[4,2,64,128]{3,2,1,0:T(8,128)}, f32[2,1,1,2048]{3,2,1,0:T(1,128)}) custom-call(f32[96,2048]{1,0:T(8,128)S(1)} %get-tuple-element.12.dense_x_ref, bf16[256,2048]{1,0:T(8,128)(2,1)S(1)} %get-tuple-element.13.dense_y_ref, s32[1,2048]{1,0:T(1,128)S(1)} %get-tuple-element.14.level_ref, f32[8,96,128]{2,1,0:T(8,128)S(1)} %get-tuple-element.18.inner_ref, ...), custom_call_target="tpu_custom_call" | custom-call | tf_op jit(solution)/shard_map/finish/pallas_call | solution.py:466
Async XLA Ops:
  3.0 5.2 %collective-permute-start = (bf16[400,128]{1,0:T(8,128)(2,1)S(1)}, bf16[400,128]{1,0:T(8,128)(2,1)S(1)}, u32[]{:S(2)}, u32[]{:S(2)}) collective-permute-start(bf16[400,128]{1,0:T(8,128)(2,1)S(1)} %get-tuple-element.16), channel_id=1, source_target_pairs={{0,4},{4,0},{8,12},{12,8},{16,20},{20,16},{24,28},{28,24},{1,5},{5... | collective-permute-start | bytes 307208 | tf_op jit(solution)/shard_map/ppermute | solution.py:404
  3.5 7.4 %collective-permute-start.1 = (bf16[400,128]{1,0:T(8,128)(2,1)S(1)}, bf16[400,128]{1,0:T(8,128)(2,1)S(1)}, u32[]{:S(2)}, u32[]{:S(2)}) collective-permute-start(bf16[400,128]{1,0:T(8,128)(2,1)S(1)} %get-tuple-element.17), channel_id=1, source_target_pairs={{0,28},{4,8},{8,4},{12,16},{16,12},{20,24},{24,20},{28,0},{1,29},{... | collective-permute-start | bytes 307208 | tf_op jit(solution)/shard_map/ppermute | solution.py:403
  11.8 4.4 %collective-permute-start.2 = (bf16[256,128]{1,0:T(8,128)(2,1)S(1)}, bf16[256,128]{1,0:T(8,128)(2,1)S(1)}, u32[]{:S(2)}, u32[]{:S(2)}) collective-permute-start(bf16[256,128]{1,0:T(8,128)(2,1)S(1)} %get-tuple-element.20), channel_id=1, source_target_pairs={{0,1},{1,0},{2,3},{3,2},{4,5},{5,4},{6,7},{7,6},{8,9},{9,8},{10,11... | collective-permute-start | bytes 196616 | tf_op jit(solution)/shard_map/ppermute | solution.py:404
  13.3 5.2 %collective-permute-start.3 = (bf16[256,128]{1,0:T(8,128)(2,1)S(1)}, bf16[256,128]{1,0:T(8,128)(2,1)S(1)}, u32[]{:S(2)}, u32[]{:S(2)}) collective-permute-start(bf16[256,128]{1,0:T(8,128)(2,1)S(1)} %get-tuple-element.21), channel_id=1, source_target_pairs={{0,3},{1,2},{2,1},{3,0},{4,7},{5,6},{6,5},{7,4},{8,11},{9,10},{10,... | collective-permute-start | bytes 196616 | tf_op jit(solution)/shard_map/ppermute | solution.py:403

commit v4 on v3

--- a/solution.py
+++ b/solution.py
@@ -96,8 +96,8 @@
 
 def spread_kernel(
     shape, chunk, fish_hbm, velocity_hbm, cell_hbm, frac_hbm, force_hbm,
-    grid_ref, near_ref, far_ref, dense_x_ref, dense_y_ref, level_ref,
-    left_ref, fish_ref, velocity_ref, cell_ref, frac_ref, force_ref, sems,
+    grid_ref, far_ref, near_ref, dense_x_ref, dense_y_ref, level_ref,
+    fish_ref, velocity_ref, cell_ref, frac_ref, force_ref, sems,
 ):
     pairs = (
         (cell_hbm, cell_ref), (frac_hbm, frac_ref), (fish_hbm, fish_ref),
@@ -112,6 +112,7 @@
     levels, comps = velocity_ref.shape[:2]
     slots = cell_ref.shape[3]
     wide_x = cells_x + SPAN
+    items = levels * comps
     count = alive_count(fish_ref)
     level_ref[...] = cell_ref[2, 0]
     for first in range(0, slots, chunk):
@@ -124,19 +125,22 @@
         lefts = [
             (force_ref[c, 0, :, lanes] * dense_x).astype(jnp.bfloat16) for c in range(comps)
         ]
+        pieces = []
         for l in range(levels):
             hot = jnp.broadcast_to(jnp.where(level == l, 1.0, 0.0), (16, chunk))
             hot = hot.astype(jnp.bfloat16)
             for c in range(comps):
-                k = l * comps + c
                 product = lefts[c].reshape(wide_x // 16, 16, chunk) * hot[None]
-                left_ref[k * wide_x : (k + 1) * wide_x, lanes] = product.reshape(wide_x, chunk)
-    total = lax.dot_general(
-        left_ref[...], dense_y_ref[...], (((1,), (1,)), ((), ())),
-        preferred_element_type=jnp.float32,
-    )
-    items = levels * comps
-    grid_ref[...] = total.reshape(items, wide_x, cells_y + LANES)
+                pieces.append(product.reshape(wide_x, chunk))
+        total = lax.dot_general(
+            jnp.concatenate(pieces, axis=0), dense_y, (((1,), (1,)), ((), ())),
+            preferred_element_type=jnp.float32,
+        )
+        total = total.reshape(items, wide_x, cells_y + LANES)
+        if first:
+            grid_ref[...] += total
+        else:
+            grid_ref[...] = total
     copies[-1].wait()
     for k in range(items):
         grid_ref[k, MARGIN : MARGIN + cells_x, :cells_y] += velocity_ref[k // comps, k % comps]
@@ -166,14 +170,22 @@
     lane = lane_index(STRIP)
     even = is_even("gx")
     row = (items + k // EDGE_PER) * STRIP
-    inners, edges = [], []
-    for ref in (near, far):
-        inners.append(ref[k * STRIP : (k + 1) * STRIP].astype(jnp.float32))
-        edge = rolled(ref[row : row + STRIP].astype(jnp.float32), -SPAN * (k % EDGE_PER))
-        edges.append(jnp.where((lane < MARGIN) | (lane >= LANES - MARGIN), edge, 0.0))
-    before = (jnp.where(even, inners[1], inners[0]), jnp.where(even, edges[1], edges[0]))
-    after = (jnp.where(even, inners[0], inners[1]), jnp.where(even, edges[0], edges[1]))
-    return before, after
+    parts = []
+    for first, second in ((far, near), (near, far)):
+        inner = jnp.where(
+            even,
+            first[k * STRIP : (k + 1) * STRIP].astype(jnp.float32),
+            second[k * STRIP : (k + 1) * STRIP].astype(jnp.float32),
+        )
+        edge = jnp.where(
+            even,
+            first[row : row + STRIP].astype(jnp.float32),
+            second[row : row + STRIP].astype(jnp.float32),
+        )
+        edge = rolled(edge, -SPAN * (k % EDGE_PER))
+        edge = jnp.where((lane < MARGIN) | (lane >= LANES - MARGIN), edge, 0.0)
+        parts.append((inner, edge))
+    return parts
 
 
 def joined(center, before, after):
@@ -203,36 +215,36 @@
     return [(row, min(SPAN, rows - row)) for row in range(0, rows, SPAN)]
 
 
-def pack_kernel(shape, grid_ref, near_x, far_x, near_ref, far_ref):
+def pack_kernel(shape, grid_ref, far_x, near_x, far_ref, near_ref):
     cells_x, cells_y, _, _ = shape
     items = grid_ref.shape[0]
     groups = -(-items // EDGE_PER)
     rows = cells_x + 2 * PAD
     lane = lane_index(rows)
     even = is_even("gy")
-    mains = [[[], []] for _ in range(groups)]
-    halos = [[], []]
-    for k in range(items):
-        inner, edge = extended_rows(grid_ref, near_x, far_x, k, items, cells_y)
-        up = jnp.where(lane >= LANES - MARGIN, inner, jnp.where(lane < MARGIN, edge, 0.0))
-        down = jnp.where(lane < MARGIN, inner, jnp.where(lane >= LANES - MARGIN, edge, 0.0))
-        up_halo = (lane >= LANES - REACH) & (lane < LANES - MARGIN)
-        down_halo = (lane >= MARGIN) & (lane < REACH)
-        send = (jnp.where(even, up, down), jnp.where(even, down, up))
-        halo = (
-            rolled(jnp.where(up_halo, inner, 0.0), REACH + HALO * k),
-            rolled(jnp.where(down_halo, inner, 0.0), HALO * k - MARGIN),
-        )
-        halo = (jnp.where(even, halo[0], halo[1]), jnp.where(even, halo[1], halo[0]))
-        for side in range(2):
-            mains[k // EDGE_PER][side].append(rolled(send[side], SPAN * (k % EDGE_PER)))
-            halos[side].append(halo[side])
-    for side, out_ref in enumerate((near_ref, far_ref)):
-        for group in range(groups):
-            total = functools.reduce(jnp.add, mains[group][side])
-            out_ref[group * rows : (group + 1) * rows] = total.astype(jnp.bfloat16)
-        total = functools.reduce(jnp.add, halos[side])
-        folded = rolled(total[:SPAN], 0)
+    up_halo = (lane >= LANES - REACH) & (lane < LANES - MARGIN)
+    down_halo = (lane >= MARGIN) & (lane < REACH)
+    halos = None
+    for group in range(groups):
+        ups, downs = None, None
+        for k in range(group * EDGE_PER, min((group + 1) * EDGE_PER, items)):
+            inner, edge = extended_rows(grid_ref, near_x, far_x, k, items, cells_y)
+            shift = SPAN * (k % EDGE_PER)
+            up = rolled(jnp.where(lane >= LANES - MARGIN, inner, edge), shift)
+            down = rolled(jnp.where(lane < MARGIN, inner, edge), shift)
+            halo = rolled(jnp.where(up_halo | down_halo, inner, 0.0), REACH + HALO * k)
+            ups = up if ups is None else ups + up
+            downs = down if downs is None else downs + down
+            halos = halo if halos is None else halos + halo
+        place = slice(group * rows, (group + 1) * rows)
+        near_ref[place] = jnp.where(even, ups, downs).astype(jnp.bfloat16)
+        far_ref[place] = jnp.where(even, downs, ups).astype(jnp.bfloat16)
+    ups = jnp.where(lane < HALO * items, halos, 0.0)
+    downs = jnp.where(lane < HALO * items, rolled(halos, -MARGIN - REACH), 0.0)
+    for out_ref, total in (
+        (near_ref, jnp.where(even, ups, downs)), (far_ref, jnp.where(even, downs, ups)),
+    ):
+        folded = total[:SPAN]
         for index, (row, size) in enumerate(folds(rows)[1:]):
             piece = rolled(total[row : row + size], SPAN * (index + 1))
             if size < SPAN:
@@ -300,7 +312,7 @@
 
 
 def inner_kernel(
-    shape, levels, grid_ref, near_x, far_x, inner_ref, rim_ref, moved_ref, carried_ref, sweep_ref,
+    shape, levels, grid_ref, far_x, near_x, inner_ref, rim_ref, moved_ref, carried_ref, sweep_ref,
 ):
     cells_x, cells_y, _, _ = shape
     items = grid_ref.shape[0]
@@ -323,7 +335,7 @@
 
 
 def finish_kernel(
-    shape, chunk, dense_x_ref, dense_y_ref, level_ref, inner_ref, rim_ref, near_y, far_y,
+    shape, chunk, dense_x_ref, dense_y_ref, level_ref, inner_ref, rim_ref, far_y, near_y,
     next_ref, sampled_ref, moved_ref, carried_ref, sweep_ref, round_ref,
 ):
     cells_x, cells_y, _, _ = shape
@@ -401,7 +413,7 @@
     near_pairs = [(i, i ^ 1) for i in range(size)]
     far_pairs = [(i, (i - 1 if i % 2 == 0 else i + 1) % size) for i in range(size)]
     far = lax.ppermute(far, axis, far_pairs)
-    return lax.ppermute(near, axis, near_pairs), far
+    return far, lax.ppermute(near, axis, near_pairs)
 
 
 def body(velocity, marker_cell, marker_frac, marker_force, fish_owner):
@@ -417,7 +429,7 @@
     params = pltpu.CompilerParams(vmem_limit_bytes=40 * 1024 * 1024)
     edge_x = jax.ShapeDtypeStruct(((items + groups) * STRIP, LANES), jnp.bfloat16)
     arrays = (fish_owner, velocity, marker_cell, marker_frac, marker_force)
-    grid, near, far, dense_x, dense_y, level = pl.pallas_call(
+    grid, far, near, dense_x, dense_y, level = pl.pallas_call(
         functools.partial(spread_kernel, shape, chunk),
         out_shape=(
             jax.ShapeDtypeStruct((items, wide_x, width), jnp.float32),
@@ -429,23 +441,22 @@
         ),
         in_specs=[pl.BlockSpec(memory_space=pltpu.HBM)] * 5,
         out_specs=tuple(whole(6)),
-        scratch_shapes=[pltpu.VMEM((items * wide_x, slots), jnp.bfloat16)]
-        + [pltpu.VMEM(a.shape, a.dtype) for a in arrays]
+        scratch_shapes=[pltpu.VMEM(a.shape, a.dtype) for a in arrays]
         + [pltpu.SemaphoreType.DMA((5,))],
         compiler_params=params,
         name="spread",
     )(*(pltpu.with_memory_space_constraint(a, pltpu.HBM) for a in arrays))
-    near_x, far_x = exchange(near, far, "gx")
+    far_x, near_x = exchange(near, far, "gx")
     edge_y = jax.ShapeDtypeStruct((groups * rows + SPAN, LANES), jnp.bfloat16)
-    near, far = pl.pallas_call(
+    far, near = pl.pallas_call(
         functools.partial(pack_kernel, shape),
         out_shape=(edge_y, edge_y),
         in_specs=whole(3),
         out_specs=tuple(whole(2)),
         compiler_params=params,
         name="pack",
-    )(grid, near_x, far_x)
-    near_y, far_y = exchange(near, far, "gy")
+    )(grid, far_x, near_x)
+    far_y, near_y = exchange(near, far, "gy")
     field = pltpu.VMEM((items, rows + 2 * ROWS, LANES), jnp.float32)
     inner, rim = pl.pallas_call(
         functools.partial(inner_kernel, shape, levels),
@@ -462,7 +473,7 @@
             transcendentals=0,
         ),
         name="inner",
-    )(grid, near_x, far_x)
+    )(grid, far_x, near_x)
     return pl.pallas_call(
         functools.partial(finish_kernel, shape, chunk),
         out_shape=(
@@ -474,7 +485,7 @@
         scratch_shapes=[field, field, field, pltpu.VMEM((items * wide_x, width), jnp.bfloat16)],
         compiler_params=params,
         name="finish",
-    )(dense_x, dense_y, level, inner, rim, near_y, far_y)
+    )(dense_x, dense_y, level, inner, rim, far_y, near_y)
 
 
 def solution(mesh):

time: 21.4 us -> 21.6 us (level)
  starting transfers between devices: 8.28 us -> 8.66 us
    ppermute x2, starting transfers between devices: 6.2 us -> 8.13 us  [exchange(): far = lax.ppermute(far, axis, far_pairs)]
    ppermute x2, waiting for transfers between devices: 0.17 us -> 2.02 us  [exchange(): return (far, lax.ppermute(near, axis, near_pairs))]
    ppermute x2, waiting for transfers between devices: 5.09 us -> 3.25 us  [exchange(): far = lax.ppermute(far, axis, far_pairs)]
    ppermute x2, starting transfers between devices: 2.08 us -> 0.53 us  [exchange(): return (far, lax.ppermute(near, axis, near_pairs))]
where the time goes in v4:
time: 21.6 us; the launch traced here: 21.5 us
  starting transfers between devices  8.66 us (40%)
  Pallas kernels  6.91 us (32%)
  waiting for transfers between devices  5.27 us (24%)
  between operations  0.65 us (3%)
    ppermute x2, starting transfers between devices, exchange(): far = lax.ppermute(far, axis, far_pairs)  8.13 us
    ppermute x2, waiting for transfers between devices, exchange(): far = lax.ppermute(far, axis, far_pairs)  3.25 us
    pallas_call x1, Pallas kernels, body(): pl.pallas_call(functools.partial(finish_kernel, shape, chunk), out_shape=...  2.71 us
    pallas_call x1, Pallas kernels, body(): pl.pallas_call(functools.partial(spread_kernel, shape, chunk), out_shape=...  2.35 us
    ppermute x2, waiting for transfers between devices, exchange(): return (far, lax.ppermute(near, axis, near_pairs))  2.02 us
    pallas_call x1, Pallas kernels, body(): pl.pallas_call(functools.partial(inner_kernel, shape, levels), out_shape=...  1.08 us
    pallas_call x1, Pallas kernels, body(): pl.pallas_call(functools.partial(pack_kernel, shape), out_shape=(edge_y,...  0.78 us
    ppermute x2, starting transfers between devices, exchange(): return (far, lax.ppermute(near, axis, near_pairs))  0.53 us
  transfers between devices with their start and end apart: 4, of which 3 were waited for; matrix products, arithmetic and copies ran while one was open for 0% of the time, Pallas kernels for 5%

profile of v4, /device:TPU:0, one launch (start us, length us, event | category | flops | bytes accessed | tf_op | source)
XLA Modules:
  0.0 21.5 jit_solution(2868015723715572523)
XLA Ops:
  0.6 2.3 %spread.1 = (f32[8,96,256]{2,1,0:T(8,128)S(1)}, bf16[400,128]{1,0:T(8,128)(2,1)S(1)}, bf16[400,128]{1,0:T(8,128)(2,1)S(1)}, f32[96,2048]{1,0:T(8,128)S(1)}, bf16...) custom-call(s32[48]{0:T(128)} %fish_hbm.1, f32[4,2,64,128]{3,2,1,0:T(8,128)} %velocity_hbm.1, ...), custom_call_target="tpu_custom_call" | custom-call | tf_op jit(solution)/shard_map/spread/pallas_call | solution.py:432
  3.0 4.6 %collective-permute-start = (bf16[400,128]{1,0:T(8,128)(2,1)S(1)}, bf16[400,128]{1,0:T(8,128)(2,1)S(1)}, u32[]{:S(2)}, u32[]{:S(2)}) collective-permute-start(bf16[400,128]{1,0:T(8,128)(2,1)S(1)} %get-tuple-element.16), channel_id=1, source_target_pairs={{0,28},{4,8},{8,4},{12,16},{16,12},{20,24},{24,20},{28,0},{1,29},{... | collective-permute-start | bytes 307208 | tf_op jit(solution)/shard_map/ppermute | solution.py:415
  7.5 0.0 collective-permute-start.1
  7.5 2.6 %collective-permute-done.far_x = bf16[400,128]{1,0:T(8,128)(2,1)S(1)} collective-permute-done((bf16[400,128]{1,0:T(8,128)(2,1)S(1)}, bf16[400,128]{1,0:T(8,128)(2,1)S(1)}, u32[]{:S(2)}, u32[]{:S(2)}) %collective-permute-start) | collective-permute-done | bytes 102432 | tf_op jit(solution)/shard_map/ppermute | solution.py:415
  10.2 0.0 collective-permute-done.1.near_x
  10.2 0.8 %pack.1 = (bf16[256,128]{1,0:T(8,128)(2,1)S(1)}, bf16[256,128]{1,0:T(8,128)(2,1)S(1)}) custom-call(f32[8,96,256]{2,1,0:T(8,128)S(1)} %get-tuple-element.15.grid_ref, bf16[400,128]{1,0:T(8,128)(2,1)S(1)} %collective-permute-done.far_x, bf16[400,128]{1,0:T(8,128)(2,1)S(1)} %collective-permute-done.1.near_x), custom_call_target="tpu_custom_call" | custom-call | tf_op jit(solution)/shard_map/pack/pallas_call | solution.py:451
  10.9 3.6 %collective-permute-start.2 = (bf16[256,128]{1,0:T(8,128)(2,1)S(1)}, bf16[256,128]{1,0:T(8,128)(2,1)S(1)}, u32[]{:S(2)}, u32[]{:S(2)}) collective-permute-start(bf16[256,128]{1,0:T(8,128)(2,1)S(1)} %get-tuple-element.20), channel_id=1, source_target_pairs={{0,3},{1,2},{2,1},{3,0},{4,7},{5,6},{6,5},{7,4},{8,11},{9,10},{10,... | collective-permute-start | bytes 196616 | tf_op jit(solution)/shard_map/ppermute | solution.py:415
  14.5 0.5 %collective-permute-start.3 = (bf16[256,128]{1,0:T(8,128)(2,1)S(1)}, bf16[256,128]{1,0:T(8,128)(2,1)S(1)}, u32[]{:S(2)}, u32[]{:S(2)}) collective-permute-start(bf16[256,128]{1,0:T(8,128)(2,1)S(1)} %get-tuple-element.21), channel_id=1, source_target_pairs={{0,1},{1,0},{2,3},{3,2},{4,5},{5,4},{6,7},{7,6},{8,9},{9,8},{10,11... | collective-permute-start | bytes 196616 | tf_op jit(solution)/shard_map/ppermute | solution.py:416
  15.0 1.1 %inner.1 = (f32[8,96,128]{2,1,0:T(8,128)S(1)}, f32[8,112,128]{2,1,0:T(8,128)S(1)}) custom-call(f32[8,96,256]{2,1,0:T(8,128)S(1)} %get-tuple-element.15.grid_ref, bf16[400,128]{1,0:T(8,128)(2,1)S(1)} %collective-permute-done.far_x, bf16[400,128]{1,0:T(8,128)(2,1)S(1)} %collective-permute-done.1.near_x), custom_call_target="tpu_custom_call" | custom-call | flops 4587520 | bytes 1835008 | tf_op jit(solution)/shard_map/inner/pallas_call | solution.py:461
  16.1 0.6 %collective-permute-done.2.far_y = bf16[256,128]{1,0:T(8,128)(2,1)S(1)} collective-permute-done((bf16[256,128]{1,0:T(8,128)(2,1)S(1)}, bf16[256,128]{1,0:T(8,128)(2,1)S(1)}, u32[]{:S(2)}, u32[]{:S(2)}) %collective-permute-start.2) | collective-permute-done | bytes 65568 | tf_op jit(solution)/shard_map/ppermute | solution.py:415
  16.8 2.0 %collective-permute-done.3.near_y = bf16[256,128]{1,0:T(8,128)(2,1)S(1)} collective-permute-done((bf16[256,128]{1,0:T(8,128)(2,1)S(1)}, bf16[256,128]{1,0:T(8,128)(2,1)S(1)}, u32[]{:S(2)}, u32[]{:S(2)}) %collective-permute-start.3) | collective-permute-done | bytes 65568 | tf_op jit(solution)/shard_map/ppermute | solution.py:416
  18.8 2.7 %finish.1 = (f32[4,2,64,128]{3,2,1,0:T(8,128)}, f32[2,1,1,2048]{3,2,1,0:T(1,128)}) custom-call(f32[96,2048]{1,0:T(8,128)S(1)} %get-tuple-element.12.dense_x_ref, bf16[256,2048]{1,0:T(8,128)(2,1)S(1)} %get-tuple-element.13.dense_y_ref, s32[1,2048]{1,0:T(1,128)S(1)} %get-tuple-element.14.level_ref, f32[8,96,128]{2,1,0:T(8,128)S(1)} %get-tuple-element.18.inner_ref, ...), custom_call_target="tpu_custom_call" | custom-call | tf_op jit(solution)/shard_map/finish/pallas_call | solution.py:477
Async XLA Ops:
  3.0 7.2 %collective-permute-start = (bf16[400,128]{1,0:T(8,128)(2,1)S(1)}, bf16[400,128]{1,0:T(8,128)(2,1)S(1)}, u32[]{:S(2)}, u32[]{:S(2)}) collective-permute-start(bf16[400,128]{1,0:T(8,128)(2,1)S(1)} %get-tuple-element.16), channel_id=1, source_target_pairs={{0,28},{4,8},{8,4},{12,16},{16,12},{20,24},{24,20},{28,0},{1,29},{... | collective-permute-start | bytes 307208 | tf_op jit(solution)/shard_map/ppermute | solution.py:415
  7.5 2.6 %collective-permute-start.1 = (bf16[400,128]{1,0:T(8,128)(2,1)S(1)}, bf16[400,128]{1,0:T(8,128)(2,1)S(1)}, u32[]{:S(2)}, u32[]{:S(2)}) collective-permute-start(bf16[400,128]{1,0:T(8,128)(2,1)S(1)} %get-tuple-element.17), channel_id=1, source_target_pairs={{0,4},{4,0},{8,12},{12,8},{16,20},{20,16},{24,28},{28,24},{1,5},{5... | collective-permute-start | bytes 307208 | tf_op jit(solution)/shard_map/ppermute | solution.py:416
  10.9 5.8 %collective-permute-start.2 = (bf16[256,128]{1,0:T(8,128)(2,1)S(1)}, bf16[256,128]{1,0:T(8,128)(2,1)S(1)}, u32[]{:S(2)}, u32[]{:S(2)}) collective-permute-start(bf16[256,128]{1,0:T(8,128)(2,1)S(1)} %get-tuple-element.20), channel_id=1, source_target_pairs={{0,3},{1,2},{2,1},{3,0},{4,7},{5,6},{6,5},{7,4},{8,11},{9,10},{10,... | collective-permute-start | bytes 196616 | tf_op jit(solution)/shard_map/ppermute | solution.py:415
  14.5 4.3 %collective-permute-start.3 = (bf16[256,128]{1,0:T(8,128)(2,1)S(1)}, bf16[256,128]{1,0:T(8,128)(2,1)S(1)}, u32[]{:S(2)}, u32[]{:S(2)}) collective-permute-start(bf16[256,128]{1,0:T(8,128)(2,1)S(1)} %get-tuple-element.21), channel_id=1, source_target_pairs={{0,1},{1,0},{2,3},{3,2},{4,5},{5,4},{6,7},{7,6},{8,9},{9,8},{10,11... | collective-permute-start | bytes 196616 | tf_op jit(solution)/shard_map/ppermute | solution.py:416

commit v5 on v4

--- a/solution.py
+++ b/solution.py
@@ -54,49 +54,78 @@
     return jnp.where(offset >= extent - MARGIN, offset - extent, offset)
 
 
-def placed_weights(first, rows, offset, weights):
-    width = offset.shape[1]
-    shift = lax.broadcasted_iota(jnp.int32, (rows, width), 0) + first - offset
-    dense = jnp.where(shift == 2, weights[3], 0.0)
-    dense = jnp.where(shift == 1, weights[2], dense)
-    dense = jnp.where(shift == 0, weights[1], dense)
-    return jnp.where(shift == -1, weights[0], dense)
-
-
-def marker_weights(cell_ref, frac_ref, lanes, shape):
-    cells_x, cells_y, extent_x, extent_y = shape
-    low_x = lax.axis_index("gx") * cells_x
-    low_y = lax.axis_index("gy") * cells_y
-    offset_x = local_cell(cell_ref[0, 0, :, lanes], low_x, extent_x)
-    offset_y = local_cell(cell_ref[1, 0, :, lanes], low_y, extent_y)
-    weights_x = four_weights(frac_ref[0, 0, :, lanes])
-    weights_y = four_weights(frac_ref[1, 0, :, lanes])
-    dense_x = placed_weights(-MARGIN, cells_x + 2 * MARGIN, offset_x, weights_x)
-    inner_y = placed_weights(0, cells_y + MARGIN, offset_y, weights_y)
-    outer_y = placed_weights(-MARGIN, MARGIN, offset_y, weights_y)
-    gap = jnp.zeros((LANES - 2 * MARGIN, offset_y.shape[1]), jnp.float32)
-    dense_y = jnp.concatenate([inner_y, gap, outer_y], axis=0).astype(jnp.bfloat16)
-    return dense_x, dense_y
-
-
-def alive_count(fish_ref):
-    me = lax.axis_index("gx") * lax.axis_size("gy") + lax.axis_index("gy")
-    mine = jnp.where(fish_ref[...] == me, 1.0, 0.0)
-    return FISH_MARK * jnp.sum(mine)
-
-
-def alive_lanes(count, first, width):
-    slot = lax.broadcasted_iota(jnp.int32, (1, width), 1) + first
-    return jnp.where(slot.astype(jnp.float32) < count, 1.0, 0.0)
-
-
-def is_even(axis):
-    return lax.axis_index(axis) % 2 == 0
-
-
-def spread_kernel(
+def position():
+    row, col = lax.axis_index("gx"), lax.axis_index("gy")
+    return row, col, row % 2 == 0, col % 2 == 0
+
+
+def tile_weights(offset, weights):
+    shift = lax.broadcasted_iota(jnp.int32, (ROWS, offset.shape[1]), 0) + 1 - offset
+    quarter, phase = shift >> 2, shift & 3
+    value = jnp.where(phase == 3, weights[3], weights[2])
+    value = jnp.where(phase == 1, weights[1], value)
+    return quarter, jnp.where(phase == 0, weights[0], value)
+
+
+def doubled(quarter, value):
+    quarter = jnp.concatenate([quarter, quarter + 2], axis=0).astype(jnp.float32)
+    return quarter.astype(jnp.bfloat16), twice(value)
+
+
+def twice(value):
+    return jnp.concatenate([value, value], axis=0).astype(jnp.bfloat16)
+
+
+def picked_tile(quarter, value, first):
+    zero = jnp.zeros_like(value)
+    return jnp.where(quarter == jnp.array(-first // 4, quarter.dtype), value, zero)
+
+
+def half_spread(quarter_ref, force_ref, dense_y_ref, half_ref, base, lanes):
+    items, rows = half_ref.shape[:2]
+    quarter = quarter_ref[:, lanes] + base
+    quarter = jnp.concatenate([quarter, quarter + 2], axis=0).astype(jnp.float32)
+    quarter = quarter.astype(jnp.bfloat16)
+    left = jnp.concatenate(
+        [
+            picked_tile(quarter, force_ref[k, :, lanes], row)
+            for k in range(items)
+            for row in range(0, rows, 2 * ROWS)
+        ],
+        axis=0,
+    )
+    total = lax.dot_general(
+        left, dense_y_ref[:, lanes], (((1,), (1,)), ((), ())),
+        preferred_element_type=jnp.float32,
+    )
+    total = total.reshape(half_ref.shape)
+    if lanes.start:
+        half_ref[...] += total
+    else:
+        half_ref[...] = total
+
+
+def finish_half(half_ref, velocity_ref, out_ref, low, cells_y):
+    items, rows = half_ref.shape[:2]
+    comps = items // velocity_ref.shape[0]
+    count = rows - MARGIN
+    source = pl.ds(pl.multiple_of(jnp.where(low, 0, count), ROWS), count)
+    target = pl.ds(pl.multiple_of(jnp.where(low, MARGIN, 0), ROWS), count)
+    for k in range(items):
+        half_ref[k, target, :cells_y] += velocity_ref[k // comps, k % comps, source]
+    place = pl.ds(pl.multiple_of(jnp.where(low, 0, rows - STRIP), ROWS), STRIP)
+    parts = [half_ref[k, place, :cells_y] for k in range(items)]
+    for group in range(0, items, EDGE_PER):
+        edges = []
+        for k in range(group, min(group + EDGE_PER, items)):
+            edges.append(rolled(half_ref[k, place, cells_y:], SPAN * (k - group)))
+        parts.append(functools.reduce(jnp.add, edges))
+    out_ref[...] = jnp.concatenate(parts, axis=0).astype(jnp.bfloat16)
+
+
+def far_kernel(
     shape, chunk, fish_hbm, velocity_hbm, cell_hbm, frac_hbm, force_hbm,
-    grid_ref, far_ref, near_ref, dense_x_ref, dense_y_ref, level_ref,
+    half_ref, far_ref, force_out, dense_y_ref, quarter_ref, value_ref, level_ref,
     fish_ref, velocity_ref, cell_ref, frac_ref, force_ref, sems,
 ):
     pairs = (
@@ -106,55 +135,62 @@
     copies = [pltpu.make_async_copy(a, b, sems.at[i]) for i, (a, b) in enumerate(pairs)]
     for copy in copies:
         copy.start()
+    cells_x, cells_y, extent_x, extent_y = shape
+    levels, comps = velocity_ref.shape[:2]
+    slots = cell_ref.shape[3]
+    row, col, even, _ = position()
+    base = jnp.where(even, -MARGIN // 4, cells_x // 8)
     for copy in copies[:-1]:
         copy.wait()
-    cells_x, cells_y, _, _ = shape
-    levels, comps = velocity_ref.shape[:2]
-    slots = cell_ref.shape[3]
-    wide_x = cells_x + SPAN
-    items = levels * comps
-    count = alive_count(fish_ref)
+    mine = jnp.where(fish_ref[...] == row * lax.axis_size("gy") + col, 1.0, 0.0)
+    count = FISH_MARK * jnp.sum(mine)
     level_ref[...] = cell_ref[2, 0]
     for first in range(0, slots, chunk):
         lanes = slice(first, first + chunk)
-        dense_x, dense_y = marker_weights(cell_ref, frac_ref, lanes, shape)
-        dense_x = dense_x * alive_lanes(count, first, chunk)
-        dense_x_ref[:, lanes] = dense_x
-        dense_y_ref[:, lanes] = dense_y
+        offset_x = local_cell(cell_ref[0, 0, :, lanes], row * cells_x, extent_x)
+        offset_y = local_cell(cell_ref[1, 0, :, lanes], col * cells_y, extent_y)
+        slot = lax.broadcasted_iota(jnp.int32, (1, chunk), 1) + first
+        alive = jnp.where(slot.astype(jnp.float32) < count, 1.0, 0.0)
+        quarter, value = tile_weights(offset_x, four_weights(frac_ref[0, 0, :, lanes]))
+        value = value * alive
+        quarter_ref[:, lanes] = quarter
+        value_ref[:, lanes] = value
         level = cell_ref[2, 0, :, lanes]
-        lefts = [
-            (force_ref[c, 0, :, lanes] * dense_x).astype(jnp.bfloat16) for c in range(comps)
-        ]
-        pieces = []
+        pushes = [force_ref[c, 0, :, lanes] * value for c in range(comps)]
         for l in range(levels):
-            hot = jnp.broadcast_to(jnp.where(level == l, 1.0, 0.0), (16, chunk))
-            hot = hot.astype(jnp.bfloat16)
             for c in range(comps):
-                product = lefts[c].reshape(wide_x // 16, 16, chunk) * hot[None]
-                pieces.append(product.reshape(wide_x, chunk))
-        total = lax.dot_general(
-            jnp.concatenate(pieces, axis=0), dense_y, (((1,), (1,)), ((), ())),
-            preferred_element_type=jnp.float32,
+                force_out[l * comps + c, :, lanes] = twice(jnp.where(level == l, pushes[c], 0.0))
+        quarter, value = doubled(
+            *tile_weights(offset_y, four_weights(frac_ref[1, 0, :, lanes]))
         )
-        total = total.reshape(items, wide_x, cells_y + LANES)
-        if first:
-            grid_ref[...] += total
-        else:
-            grid_ref[...] = total
+        dense_y_ref[:, lanes] = jnp.concatenate(
+            [picked_tile(quarter, value, n) for n in range(0, cells_y + MARGIN, 2 * ROWS)]
+            + [jnp.zeros((LANES - SPAN, chunk), jnp.bfloat16)]
+            + [picked_tile(quarter, value, n) for n in range(-MARGIN, 0, 2 * ROWS)],
+            axis=0,
+        )
+        half_spread(quarter_ref, force_out, dense_y_ref, half_ref, base, lanes)
     copies[-1].wait()
-    for k in range(items):
-        grid_ref[k, MARGIN : MARGIN + cells_x, :cells_y] += velocity_ref[k // comps, k % comps]
-    even = is_even("gx")
-    high = wide_x - STRIP
-    for out_ref, row in ((far_ref, jnp.where(even, 0, high)), (near_ref, jnp.where(even, high, 0))):
-        place = pl.ds(pl.multiple_of(row, ROWS), STRIP)
-        parts = [grid_ref[k, place, :cells_y] for k in range(items)]
-        for group in range(0, items, EDGE_PER):
-            edges = []
-            for k in range(group, min(group + EDGE_PER, items)):
-                edges.append(rolled(grid_ref[k, place, cells_y:], SPAN * (k - group)))
-            parts.append(functools.reduce(jnp.add, edges))
-        out_ref[...] = jnp.concatenate(parts, axis=0).astype(jnp.bfloat16)
+    finish_half(half_ref, velocity_ref, far_ref, even, cells_y)
+
+
+def near_kernel(
+    shape, chunk, velocity_ref, far_half_ref, force_ref, dense_y_ref, quarter_ref,
+    grid_ref, near_ref, half_ref,
+):
+    cells_x, cells_y, _, _ = shape
+    slots = quarter_ref.shape[1]
+    rows = half_ref.shape[1]
+    _, _, even, _ = position()
+    base = jnp.where(even, cells_x // 8, -MARGIN // 4)
+    for first in range(0, slots, chunk):
+        lanes = slice(first, first + chunk)
+        half_spread(quarter_ref, force_ref, dense_y_ref, half_ref, base, lanes)
+    finish_half(half_ref, velocity_ref, near_ref, jnp.logical_not(even), cells_y)
+    for ref, row in ((far_half_ref, jnp.where(even, 0, rows)), (half_ref, jnp.where(even, rows, 0))):
+        place = pl.ds(pl.multiple_of(row, ROWS), rows)
+        for k in range(ref.shape[0]):
+            grid_ref[k, place] = ref[k]
 
 
 def rolled(value, shift):
@@ -166,9 +202,8 @@
     return lax.broadcasted_iota(jnp.int32, (rows, LANES), 1)
 
 
-def strip_parts(near, far, k, items):
+def strip_parts(near, far, k, items, even):
     lane = lane_index(STRIP)
-    even = is_even("gx")
     row = (items + k // EDGE_PER) * STRIP
     parts = []
     for first, second in ((far, near), (near, far)):
@@ -204,8 +239,8 @@
     )
 
 
-def extended_rows(grid_ref, near, far, k, items, cells_y):
-    before, after = strip_parts(near, far, k, items)
+def extended_rows(grid_ref, near, far, k, items, cells_y, even):
+    before, after = strip_parts(near, far, k, items, even)
     inner = joined(grid_ref[k, :, :cells_y], before[0], after[0])
     edge = joined(grid_ref[k, :, cells_y:], before[1], after[1])
     return inner, edge
@@ -221,14 +256,14 @@
     groups = -(-items // EDGE_PER)
     rows = cells_x + 2 * PAD
     lane = lane_index(rows)
-    even = is_even("gy")
+    _, _, even_x, even = position()
     up_halo = (lane >= LANES - REACH) & (lane < LANES - MARGIN)
     down_halo = (lane >= MARGIN) & (lane < REACH)
     halos = None
     for group in range(groups):
         ups, downs = None, None
         for k in range(group * EDGE_PER, min((group + 1) * EDGE_PER, items)):
-            inner, edge = extended_rows(grid_ref, near_x, far_x, k, items, cells_y)
+            inner, edge = extended_rows(grid_ref, near_x, far_x, k, items, cells_y, even_x)
             shift = SPAN * (k % EDGE_PER)
             up = rolled(jnp.where(lane >= LANES - MARGIN, inner, edge), shift)
             down = rolled(jnp.where(lane < MARGIN, inner, edge), shift)
@@ -320,8 +355,9 @@
     wide_x = cells_x + SPAN
     rows = cells_x + 2 * PAD
     lane = lane_index(rows)
+    _, _, even_x, _ = position()
     for k in range(items):
-        inner, edge = extended_rows(grid_ref, near_x, far_x, k, items, cells_y)
+        inner, edge = extended_rows(grid_ref, near_x, far_x, k, items, cells_y, even_x)
         moved_ref[k, ROWS : ROWS + rows] = inner
         low = jnp.where(lane < RIM, inner, jnp.where(lane >= LANES - MARGIN, edge, 0.0))
         high = jnp.where(lane >= LANES - RIM, inner, jnp.where(lane < MARGIN, edge, 0.0))
@@ -335,7 +371,7 @@
 
 
 def finish_kernel(
-    shape, chunk, dense_x_ref, dense_y_ref, level_ref, inner_ref, rim_ref, far_y, near_y,
+    shape, chunk, quarter_ref, value_ref, dense_y_ref, level_ref, inner_ref, rim_ref, far_y, near_y,
     next_ref, sampled_ref, moved_ref, carried_ref, sweep_ref, round_ref,
 ):
     cells_x, cells_y, _, _ = shape
@@ -346,7 +382,7 @@
     wide_x = cells_x + SPAN
     rows = cells_x + 2 * PAD
     lane = lane_index(rows)
-    even = is_even("gy")
+    _, _, _, even = position()
     near_halo, far_halo = unfolded(near_y, rows, groups), unfolded(far_y, rows, groups)
     before = jnp.where(even, far_halo, near_halo)
     after = rolled(jnp.where(even, near_halo, far_halo), HALF + MARGIN + REACH)
@@ -393,27 +429,29 @@
             round_ref[...], dense_y_ref[:, lanes], preferred_element_type=jnp.float32
         )
         partial = partial.reshape(levels, comps, wide_x, chunk)
+        quarter, value = quarter_ref[:, lanes], value_ref[:, lanes]
+        heres = [quarter == (MARGIN - row) // 4 for row in range(0, wide_x, ROWS)]
+        aboves = [level == l for l in range(levels - 1)]
         for c in range(comps):
-            picked = partial[levels - 1, c]
-            for l in range(levels - 2, -1, -1):
-                picked = jnp.where(level == l, partial[l, c], picked)
-            sampled_ref[c, 0, :, lanes] = jnp.sum(
-                picked * dense_x_ref[:, lanes], axis=0, keepdims=True
-            )
+            total = jnp.zeros((ROWS, chunk), jnp.float32)
+            for row in range(0, wide_x, ROWS):
+                picked = partial[levels - 1, c, row : row + ROWS]
+                for l in range(levels - 2, -1, -1):
+                    picked = jnp.where(aboves[l], partial[l, c, row : row + ROWS], picked)
+                total = jnp.where(heres[row // ROWS], picked, total)
+            sampled_ref[c, 0, :, lanes] = jnp.sum(total * value, axis=0, keepdims=True)
 
 
 def whole(count):
     return [pl.BlockSpec(memory_space=pltpu.VMEM)] * count
 
 
-def exchange(near, far, axis):
+def swap_pairs(axis):
     size = lax.axis_size(axis)
     if size % 2:
         raise ValueError("odd axis")
-    near_pairs = [(i, i ^ 1) for i in range(size)]
     far_pairs = [(i, (i - 1 if i % 2 == 0 else i + 1) % size) for i in range(size)]
-    far = lax.ppermute(far, axis, far_pairs)
-    return far, lax.ppermute(near, axis, near_pairs)
+    return far_pairs, [(i, i ^ 1) for i in range(size)]
 
 
 def body(velocity, marker_cell, marker_frac, marker_force, fish_owner):
@@ -428,25 +466,42 @@
     groups = -(-items // EDGE_PER)
     params = pltpu.CompilerParams(vmem_limit_bytes=40 * 1024 * 1024)
     edge_x = jax.ShapeDtypeStruct(((items + groups) * STRIP, LANES), jnp.bfloat16)
+    half = (items, wide_x // 2, width)
     arrays = (fish_owner, velocity, marker_cell, marker_frac, marker_force)
-    grid, far, near, dense_x, dense_y, level = pl.pallas_call(
-        functools.partial(spread_kernel, shape, chunk),
+    far_half, far, force, dense_y, quarter, value, level = pl.pallas_call(
+        functools.partial(far_kernel, shape, chunk),
         out_shape=(
-            jax.ShapeDtypeStruct((items, wide_x, width), jnp.float32),
+            jax.ShapeDtypeStruct(half, jnp.float32),
             edge_x,
-            edge_x,
-            jax.ShapeDtypeStruct((wide_x, slots), jnp.float32),
+            jax.ShapeDtypeStruct((items, 2 * ROWS, slots), jnp.bfloat16),
             jax.ShapeDtypeStruct((width, slots), jnp.bfloat16),
+            jax.ShapeDtypeStruct((ROWS, slots), jnp.int32),
+            jax.ShapeDtypeStruct((ROWS, slots), jnp.float32),
             jax.ShapeDtypeStruct((1, slots), jnp.int32),
         ),
         in_specs=[pl.BlockSpec(memory_space=pltpu.HBM)] * 5,
-        out_specs=tuple(whole(6)),
+        out_specs=tuple(whole(7)),
         scratch_shapes=[pltpu.VMEM(a.shape, a.dtype) for a in arrays]
         + [pltpu.SemaphoreType.DMA((5,))],
         compiler_params=params,
-        name="spread",
+        name="spread_far",
     )(*(pltpu.with_memory_space_constraint(a, pltpu.HBM) for a in arrays))
-    far_x, near_x = exchange(near, far, "gx")
+    far_pairs, near_pairs = swap_pairs("gx")
+    far_x = lax.ppermute(far, "gx", far_pairs)
+    grid, near = pl.pallas_call(
+        functools.partial(near_kernel, shape, chunk),
+        out_shape=(jax.ShapeDtypeStruct((items, wide_x, width), jnp.float32), edge_x),
+        in_specs=whole(5),
+        out_specs=tuple(whole(2)),
+        scratch_shapes=[pltpu.VMEM(half, jnp.float32)],
+        compiler_params=params,
+        cost_estimate=pl.CostEstimate(
+            flops=items * wide_x * width * slots, bytes_accessed=4 * items * wide_x * width,
+            transcendentals=0,
+        ),
+        name="spread_near",
+    )(velocity, far_half, force, dense_y, quarter)
+    near_x = lax.ppermute(near, "gx", near_pairs)
     edge_y = jax.ShapeDtypeStruct((groups * rows + SPAN, LANES), jnp.bfloat16)
     far, near = pl.pallas_call(
         functools.partial(pack_kernel, shape),
@@ -456,7 +511,9 @@
         compiler_params=params,
         name="pack",
     )(grid, far_x, near_x)
-    far_y, near_y = exchange(near, far, "gy")
+    far_pairs, near_pairs = swap_pairs("gy")
+    far_y = lax.ppermute(far, "gy", far_pairs)
+    near_y = lax.ppermute(near, "gy", near_pairs)
     field = pltpu.VMEM((items, rows + 2 * ROWS, LANES), jnp.float32)
     inner, rim = pl.pallas_call(
         functools.partial(inner_kernel, shape, levels),
@@ -480,12 +537,12 @@
             jax.ShapeDtypeStruct(velocity.shape, jnp.float32),
             jax.ShapeDtypeStruct((comps, 1, 1, slots), jnp.float32),
         ),
-        in_specs=whole(7),
+        in_specs=whole(8),
         out_specs=tuple(whole(2)),
         scratch_shapes=[field, field, field, pltpu.VMEM((items * wide_x, width), jnp.bfloat16)],
         compiler_params=params,
         name="finish",
-    )(dense_x, dense_y, level, inner, rim, far_y, near_y)
+    )(quarter, value, dense_y, level, inner, rim, far_y, near_y)
 
 
 def solution(mesh):

time: 21.6 us -> 21 us (0.972)
  waiting for transfers between devices: 5.27 us -> 4.4 us
    ppermute x4, waiting for transfers between devices: 5.27 us -> 4.4 us  [the longest x1 1.97 us: body(): near_y = lax.ppermute(near, 'gy', near_pairs)]
    pallas_call x1 -> x2, Pallas kernels: 2.35 us -> 2.46 us  [the longest x1 1.67 us: body(): pl.pallas_call(functools.partial(far_kernel, shape, chunk), out_shape=(ja...]
  transfers between devices with their start and end apart: 4 -> 4, of which waited for: 3 -> 3; matrix products, arithmetic and copies ran while one was open for 0% -> 0% of each run, Pallas kernels for 5% -> 9%
where the time goes in v5:
time: 21 us; the launch traced here: 20.8 us
  starting transfers between devices  8.72 us (42%)
  Pallas kernels  7.05 us (34%)
  waiting for transfers between devices  4.4 us (21%)
  between operations  0.67 us (3%)
    ppermute x1, starting transfers between devices, body(): far_x = lax.ppermute(far, 'gx', far_pairs)  4.55 us
    ppermute x1, starting transfers between devices, body(): far_y = lax.ppermute(far, 'gy', far_pairs)  3.57 us
    pallas_call x1, Pallas kernels, body(): pl.pallas_call(functools.partial(finish_kernel, shape, chunk), out_shape=...  2.73 us
    ppermute x1, waiting for transfers between devices, body(): near_y = lax.ppermute(near, 'gy', near_pairs)  1.97 us
    ppermute x1, waiting for transfers between devices, body(): far_x = lax.ppermute(far, 'gx', far_pairs)  1.75 us
    pallas_call x1, Pallas kernels, body(): pl.pallas_call(functools.partial(far_kernel, shape, chunk), out_shape=(ja...  1.67 us
    pallas_call x1, Pallas kernels, body(): pl.pallas_call(functools.partial(inner_kernel, shape, levels), out_shape=...  1.08 us
    pallas_call x1, Pallas kernels, body(): pl.pallas_call(functools.partial(near_kernel, shape, chunk), out_shape=(j...  0.79 us
  transfers between devices with their start and end apart: 4, of which 3 were waited for; matrix products, arithmetic and copies ran while one was open for 0% of the time, Pallas kernels for 9%

profile of v5, /device:TPU:0, one launch (start us, length us, event | category | flops | bytes accessed | tf_op | source)
XLA Modules:
  0.0 20.8 jit_solution(5454688378048770526)
XLA Ops:
  0.6 0.0 copy-start
  0.6 1.7 %spread_far.1 = (f32[8,48,256]{2,1,0:T(8,128)S(1)}, bf16[400,128]{1,0:T(8,128)(2,1)S(1)}, bf16[8,16,2048]{2,1,0:T(8,128)(2,1)S(1)}, bf16[256,2048]{1,0:T(8,128)(...) custom-call(s32[48]{0:T(128)} %fish_hbm.1, f32[4,2,64,128]{3,2,1,0:T(8,128)} %velocity_ref.1, ...), custom_call_target="tpu_custom_call" | custom-call | tf_op jit(solution)/shard_map/spread_far/pallas_call | solution.py:471
  2.3 4.6 %collective-permute-start = (bf16[400,128]{1,0:T(8,128)(2,1)S(1)}, bf16[400,128]{1,0:T(8,128)(2,1)S(1)}, u32[]{:S(2)}, u32[]{:S(2)}) collective-permute-start(bf16[400,128]{1,0:T(8,128)(2,1)S(1)} %get-tuple-element.22), channel_id=1, source_target_pairs={{0,28},{4,8},{8,4},{12,16},{16,12},{20,24},{24,20},{28,0},{1,29},{... | collective-permute-start | bytes 307208 | tf_op jit(solution)/shard_map/ppermute | solution.py:490
  6.9 0.0 copy-done
  6.9 0.8 %spread_near.1 = (f32[8,96,256]{2,1,0:T(8,128)S(1)}, bf16[400,128]{1,0:T(8,128)(2,1)S(1)}) custom-call(f32[4,2,64,128]{3,2,1,0:T(8,128)S(1)} %copy-done, f32[8,48,256]{2,1,0:T(8,128)S(1)} %get-tuple-element.19.far_half_ref, bf16[8,16,2048]{2,1,0:T(8,128)(2,1)S(1)} %get-tuple-element.20.force_ref, bf16[256,2048]{1,0:T(8,128)(2,1)S(1)} %get-tuple-element.17.dense_y_ref, ...), custom_call_target="tpu_custom_call" | custom-call | flops 402653184 | bytes 786432 | tf_op jit(solution)/shard_map/spread_near/pallas_call | solution.py:491
  7.7 0.1 collective-permute-start.1
  7.7 1.7 %collective-permute-done.far_x = bf16[400,128]{1,0:T(8,128)(2,1)S(1)} collective-permute-done((bf16[400,128]{1,0:T(8,128)(2,1)S(1)}, bf16[400,128]{1,0:T(8,128)(2,1)S(1)}, u32[]{:S(2)}, u32[]{:S(2)}) %collective-permute-start) | collective-permute-done | bytes 102432 | tf_op jit(solution)/shard_map/ppermute | solution.py:490
  9.5 0.0 collective-permute-done.1.near_x
  9.5 0.8 %pack.1 = (bf16[256,128]{1,0:T(8,128)(2,1)S(1)}, bf16[256,128]{1,0:T(8,128)(2,1)S(1)}) custom-call(f32[8,96,256]{2,1,0:T(8,128)S(1)} %get-tuple-element.21.grid_ref, bf16[400,128]{1,0:T(8,128)(2,1)S(1)} %collective-permute-done.far_x, bf16[400,128]{1,0:T(8,128)(2,1)S(1)} %collective-permute-done.1.near_x), custom_call_target="tpu_custom_call" | custom-call | tf_op jit(solution)/shard_map/pack/pallas_call | solution.py:506
  10.3 3.6 %collective-permute-start.2 = (bf16[256,128]{1,0:T(8,128)(2,1)S(1)}, bf16[256,128]{1,0:T(8,128)(2,1)S(1)}, u32[]{:S(2)}, u32[]{:S(2)}) collective-permute-start(bf16[256,128]{1,0:T(8,128)(2,1)S(1)} %get-tuple-element.26), channel_id=1, source_target_pairs={{0,3},{1,2},{2,1},{3,0},{4,7},{5,6},{6,5},{7,4},{8,11},{9,10},{10,... | collective-permute-start | bytes 196616 | tf_op jit(solution)/shard_map/ppermute | solution.py:515
  13.8 0.5 %collective-permute-start.3 = (bf16[256,128]{1,0:T(8,128)(2,1)S(1)}, bf16[256,128]{1,0:T(8,128)(2,1)S(1)}, u32[]{:S(2)}, u32[]{:S(2)}) collective-permute-start(bf16[256,128]{1,0:T(8,128)(2,1)S(1)} %get-tuple-element.27), channel_id=1, source_target_pairs={{0,1},{1,0},{2,3},{3,2},{4,5},{5,4},{6,7},{7,6},{8,9},{9,8},{10,11... | collective-permute-start | bytes 196616 | tf_op jit(solution)/shard_map/ppermute | solution.py:516
  14.4 1.1 %inner.1 = (f32[8,96,128]{2,1,0:T(8,128)S(1)}, f32[8,112,128]{2,1,0:T(8,128)S(1)}) custom-call(f32[8,96,256]{2,1,0:T(8,128)S(1)} %get-tuple-element.21.grid_ref, bf16[400,128]{1,0:T(8,128)(2,1)S(1)} %collective-permute-done.far_x, bf16[400,128]{1,0:T(8,128)(2,1)S(1)} %collective-permute-done.1.near_x), custom_call_target="tpu_custom_call" | custom-call | flops 4587520 | bytes 1835008 | tf_op jit(solution)/shard_map/inner/pallas_call | solution.py:518
  15.5 0.7 %collective-permute-done.2.far_y = bf16[256,128]{1,0:T(8,128)(2,1)S(1)} collective-permute-done((bf16[256,128]{1,0:T(8,128)(2,1)S(1)}, bf16[256,128]{1,0:T(8,128)(2,1)S(1)}, u32[]{:S(2)}, u32[]{:S(2)}) %collective-permute-start.2) | collective-permute-done | bytes 65568 | tf_op jit(solution)/shard_map/ppermute | solution.py:515
  16.1 2.0 %collective-permute-done.3.near_y = bf16[256,128]{1,0:T(8,128)(2,1)S(1)} collective-permute-done((bf16[256,128]{1,0:T(8,128)(2,1)S(1)}, bf16[256,128]{1,0:T(8,128)(2,1)S(1)}, u32[]{:S(2)}, u32[]{:S(2)}) %collective-permute-start.3) | collective-permute-done | bytes 65568 | tf_op jit(solution)/shard_map/ppermute | solution.py:516
  18.1 2.7 %finish.1 = (f32[4,2,64,128]{3,2,1,0:T(8,128)}, f32[2,1,1,2048]{3,2,1,0:T(1,128)}) custom-call(s32[8,2048]{1,0:T(8,128)S(1)} %get-tuple-element.15.quarter_ref, f32[8,2048]{1,0:T(8,128)S(1)} %get-tuple-element.16.value_ref, bf16[256,2048]{1,0:T(8,128)(2,1)S(1)} %get-tuple-element.17.dense_y_ref, s32[1,2048]{1,0:T(1,128)S(1)} %get-tuple-element.18.level_ref, ...), custom_call_target="tpu_custom_call" | custom-call | tf_op jit(solution)/shard_map/finish/pallas_call | solution.py:534
Async XLA Ops:
  0.6 6.2 %copy-start = (f32[4,2,64,128]{3,2,1,0:T(8,128)S(1)}, f32[4,2,64,128]{3,2,1,0:T(8,128)}, u32[]{:S(2)}) copy-start(f32[4,2,64,128]{3,2,1,0:T(8,128)} %velocity_ref.1) | copy-start | bytes 786436
  2.3 7.2 %collective-permute-start = (bf16[400,128]{1,0:T(8,128)(2,1)S(1)}, bf16[400,128]{1,0:T(8,128)(2,1)S(1)}, u32[]{:S(2)}, u32[]{:S(2)}) collective-permute-start(bf16[400,128]{1,0:T(8,128)(2,1)S(1)} %get-tuple-element.22), channel_id=1, source_target_pairs={{0,28},{4,8},{8,4},{12,16},{16,12},{20,24},{24,20},{28,0},{1,29},{... | collective-permute-start | bytes 307208 | tf_op jit(solution)/shard_map/ppermute | solution.py:490
  7.7 1.8 %collective-permute-start.1 = (bf16[400,128]{1,0:T(8,128)(2,1)S(1)}, bf16[400,128]{1,0:T(8,128)(2,1)S(1)}, u32[]{:S(2)}, u32[]{:S(2)}) collective-permute-start(bf16[400,128]{1,0:T(8,128)(2,1)S(1)} %get-tuple-element.23), channel_id=1, source_target_pairs={{0,4},{4,0},{8,12},{12,8},{16,20},{20,16},{24,28},{28,24},{1,5},{5... | collective-permute-start | bytes 307208 | tf_op jit(solution)/shard_map/ppermute | solution.py:504
  10.3 5.9 %collective-permute-start.2 = (bf16[256,128]{1,0:T(8,128)(2,1)S(1)}, bf16[256,128]{1,0:T(8,128)(2,1)S(1)}, u32[]{:S(2)}, u32[]{:S(2)}) collective-permute-start(bf16[256,128]{1,0:T(8,128)(2,1)S(1)} %get-tuple-element.26), channel_id=1, source_target_pairs={{0,3},{1,2},{2,1},{3,0},{4,7},{5,6},{6,5},{7,4},{8,11},{9,10},{10,... | collective-permute-start | bytes 196616 | tf_op jit(solution)/shard_map/ppermute | solution.py:515
  13.8 4.3 %collective-permute-start.3 = (bf16[256,128]{1,0:T(8,128)(2,1)S(1)}, bf16[256,128]{1,0:T(8,128)(2,1)S(1)}, u32[]{:S(2)}, u32[]{:S(2)}) collective-permute-start(bf16[256,128]{1,0:T(8,128)(2,1)S(1)} %get-tuple-element.27), channel_id=1, source_target_pairs={{0,1},{1,0},{2,3},{3,2},{4,5},{5,4},{6,7},{7,6},{8,9},{9,8},{10,11... | collective-permute-start | bytes 196616 | tf_op jit(solution)/shard_map/ppermute | solution.py:516

commit v6 on v5

--- a/solution.py
+++ b/solution.py
@@ -250,7 +250,21 @@
     return [(row, min(SPAN, rows - row)) for row in range(0, rows, SPAN)]
 
 
-def pack_kernel(shape, grid_ref, far_x, near_x, far_ref, near_ref):
+def partners():
+    col, size = lax.axis_index("gy"), lax.axis_size("gy")
+    even = col % 2 == 0
+    return jnp.where(even, (col + size - 1) % size, (col + 1) % size), jnp.where(even, col + 1, col - 1)
+
+
+def by_partner(refs):
+    if len(refs) == 2:
+        return refs
+    count = refs[0].shape[0] // lax.axis_size("gy")
+    return [refs[0].at[pl.ds(pl.multiple_of(p * count, 16), count)] for p in partners()]
+
+
+def pack_kernel(shape, grid_ref, far_x, near_x, *out_refs):
+    far_ref, near_ref = by_partner(out_refs)
     cells_x, cells_y, _, _ = shape
     items = grid_ref.shape[0]
     groups = -(-items // EDGE_PER)
@@ -371,9 +385,10 @@
 
 
 def finish_kernel(
-    shape, chunk, quarter_ref, value_ref, dense_y_ref, level_ref, inner_ref, rim_ref, far_y, near_y,
-    next_ref, sampled_ref, moved_ref, carried_ref, sweep_ref, round_ref,
+    shape, chunk, quarter_ref, value_ref, dense_y_ref, level_ref, inner_ref, rim_ref, *refs,
 ):
+    far_y, near_y = by_partner(refs[:-6])
+    next_ref, sampled_ref, moved_ref, carried_ref, sweep_ref, round_ref = refs[-6:]
     cells_x, cells_y, _, _ = shape
     items = rim_ref.shape[0]
     groups = -(-items // EDGE_PER)
@@ -502,18 +517,25 @@
         name="spread_near",
     )(velocity, far_half, force, dense_y, quarter)
     near_x = lax.ppermute(near, "gx", near_pairs)
-    edge_y = jax.ShapeDtypeStruct((groups * rows + SPAN, LANES), jnp.bfloat16)
-    far, near = pl.pallas_call(
+    size_y = lax.axis_size("gy")
+    together = size_y <= 4
+    edge_rows = groups * rows + SPAN
+    if together:
+        edges_y = (jax.ShapeDtypeStruct((size_y * edge_rows, LANES), jnp.bfloat16),)
+    else:
+        edges_y = (jax.ShapeDtypeStruct((edge_rows, LANES), jnp.bfloat16),) * 2
+    sent = pl.pallas_call(
         functools.partial(pack_kernel, shape),
-        out_shape=(edge_y, edge_y),
+        out_shape=edges_y,
         in_specs=whole(3),
-        out_specs=tuple(whole(2)),
+        out_specs=tuple(whole(len(edges_y))),
         compiler_params=params,
         name="pack",
     )(grid, far_x, near_x)
-    far_pairs, near_pairs = swap_pairs("gy")
-    far_y = lax.ppermute(far, "gy", far_pairs)
-    near_y = lax.ppermute(near, "gy", near_pairs)
+    if together:
+        received = (lax.all_to_all(sent[0], "gy", 0, 0, tiled=True),)
+    else:
+        received = tuple(lax.ppermute(a, "gy", p) for a, p in zip(sent, swap_pairs("gy")))
     field = pltpu.VMEM((items, rows + 2 * ROWS, LANES), jnp.float32)
     inner, rim = pl.pallas_call(
         functools.partial(inner_kernel, shape, levels),
@@ -537,12 +559,12 @@
             jax.ShapeDtypeStruct(velocity.shape, jnp.float32),
             jax.ShapeDtypeStruct((comps, 1, 1, slots), jnp.float32),
         ),
-        in_specs=whole(8),
+        in_specs=whole(6 + len(received)),
         out_specs=tuple(whole(2)),
         scratch_shapes=[field, field, field, pltpu.VMEM((items * wide_x, width), jnp.bfloat16)],
         compiler_params=params,
         name="finish",
-    )(quarter, value, dense_y, level, inner, rim, far_y, near_y)
+    )(quarter, value, dense_y, level, inner, rim, *received)
 
 
 def solution(mesh):

time: 21 us -> 24.1 us (1.15)
  waiting for transfers between devices: 4.4 us -> 6.04 us
  Pallas kernels: 7.05 us -> 7.74 us
  starting transfers between devices: 8.72 us -> 9.39 us
    all_to_all x0 -> x1, starting transfers between devices: none -> 4.78 us  [body(): received = (lax.all_to_all(sent[0], 'gy', 0, 0, tiled=True),)]
    all_to_all x0 -> x1, waiting for transfers between devices: none -> 4.29 us  [body(): received = (lax.all_to_all(sent[0], 'gy', 0, 0, tiled=True),)]
    ppermute x2 -> x0, starting transfers between devices: 4.11 us -> none  [the longest x1 3.57 us: body(): far_y = lax.ppermute(far, 'gy', far_pairs)]
    ppermute x2 -> x0, waiting for transfers between devices: 2.65 us -> none  [the longest x1 1.97 us: body(): near_y = lax.ppermute(near, 'gy', near_pairs)]
    pallas_call x1, Pallas kernels: 0.78 us -> 1.47 us  [body(): pl.pallas_call(functools.partial(pack_kernel, shape), out_shape=edges_y,...]
  transfers between devices with their start and end apart: 4 -> 3, of which waited for: 3 -> 2; matrix products, arithmetic and copies ran while one was open for 0% -> 0% of each run, Pallas kernels for 9% -> 8%
where the time goes in v6:
time: 24.1 us; the launch traced here: 23.8 us
  starting transfers between devices  9.39 us (39%)
  Pallas kernels  7.74 us (32%)
  waiting for transfers between devices  6.04 us (25%)
  between operations  0.66 us (3%)
    all_to_all x1, starting transfers between devices, body(): received = (lax.all_to_all(sent[0], 'gy', 0, 0, tiled=True),)  4.78 us
    ppermute x1, starting transfers between devices, body(): far_x = lax.ppermute(far, 'gx', far_pairs)  4.55 us
    all_to_all x1, waiting for transfers between devices, body(): received = (lax.all_to_all(sent[0], 'gy', 0, 0, tiled=True),)  4.29 us
    pallas_call x1, Pallas kernels, body(): pl.pallas_call(functools.partial(finish_kernel, shape, chunk), out_shape=...  2.73 us
    ppermute x1, waiting for transfers between devices, body(): far_x = lax.ppermute(far, 'gx', far_pairs)  1.75 us
    pallas_call x1, Pallas kernels, body(): pl.pallas_call(functools.partial(far_kernel, shape, chunk), out_shape=(ja...  1.68 us
    pallas_call x1, Pallas kernels, body(): pl.pallas_call(functools.partial(pack_kernel, shape), out_shape=edges_y,...  1.47 us
    pallas_call x1, Pallas kernels, body(): pl.pallas_call(functools.partial(inner_kernel, shape, levels), out_shape=...  1.08 us
  transfers between devices with their start and end apart: 3, of which 2 were waited for; matrix products, arithmetic and copies ran while one was open for 0% of the time, Pallas kernels for 8%

profile of v6, /device:TPU:0, one launch (start us, length us, event | category | flops | bytes accessed | tf_op | source)
XLA Modules:
  0.0 23.8 jit_solution(2451240214622321717)
XLA Ops:
  0.6 0.0 copy-start
  0.6 1.7 %spread_far.1 = (f32[8,48,256]{2,1,0:T(8,128)S(1)}, bf16[400,128]{1,0:T(8,128)(2,1)S(1)}, bf16[8,16,2048]{2,1,0:T(8,128)(2,1)S(1)}, bf16[256,2048]{1,0:T(8,128)(...) custom-call(s32[48]{0:T(128)} %fish_hbm.1, f32[4,2,64,128]{3,2,1,0:T(8,128)} %velocity_ref.1, ...), custom_call_target="tpu_custom_call" | custom-call | tf_op jit(solution)/shard_map/spread_far/pallas_call | solution.py:486
  2.3 4.6 %collective-permute-start = (bf16[400,128]{1,0:T(8,128)(2,1)S(1)}, bf16[400,128]{1,0:T(8,128)(2,1)S(1)}, u32[]{:S(2)}, u32[]{:S(2)}) collective-permute-start(bf16[400,128]{1,0:T(8,128)(2,1)S(1)} %get-tuple-element.20), channel_id=1, source_target_pairs={{0,28},{4,8},{8,4},{12,16},{16,12},{20,24},{24,20},{28,0},{1,29},{... | collective-permute-start | bytes 307208 | tf_op jit(solution)/shard_map/ppermute | solution.py:505
  6.9 0.0 copy-done
  6.9 0.8 %spread_near.1 = (f32[8,96,256]{2,1,0:T(8,128)S(1)}, bf16[400,128]{1,0:T(8,128)(2,1)S(1)}) custom-call(f32[4,2,64,128]{3,2,1,0:T(8,128)S(1)} %copy-done, f32[8,48,256]{2,1,0:T(8,128)S(1)} %get-tuple-element.17.far_half_ref, bf16[8,16,2048]{2,1,0:T(8,128)(2,1)S(1)} %get-tuple-element.18.force_ref, bf16[256,2048]{1,0:T(8,128)(2,1)S(1)} %get-tuple-element.15.dense_y_ref, ...), custom_call_target="tpu_custom_call" | custom-call | flops 402653184 | bytes 786432 | tf_op jit(solution)/shard_map/spread_near/pallas_call | solution.py:506
  7.7 0.1 collective-permute-start.1
  7.7 1.7 %collective-permute-done.far_x = bf16[400,128]{1,0:T(8,128)(2,1)S(1)} collective-permute-done((bf16[400,128]{1,0:T(8,128)(2,1)S(1)}, bf16[400,128]{1,0:T(8,128)(2,1)S(1)}, u32[]{:S(2)}, u32[]{:S(2)}) %collective-permute-start) | collective-permute-done | bytes 102432 | tf_op jit(solution)/shard_map/ppermute | solution.py:505
  9.5 0.0 collective-permute-done.1.near_x
  9.5 1.5 %pack.1 = bf16[1024,128]{1,0:T(8,128)(2,1)} custom-call(f32[8,96,256]{2,1,0:T(8,128)S(1)} %get-tuple-element.19.grid_ref, bf16[400,128]{1,0:T(8,128)(2,1)S(1)} %collective-permute-done.far_x, bf16[400,128]{1,0:T(8,128)(2,1)S(1)} %collective-permute-done.1.near_x), custom_call_target="tpu_custom_call" | custom-call | tf_op jit(solution)/shard_map/pack/pallas_call | solution.py:527
  11.0 4.8 %all-to-all-start = ((bf16[4,256,128]{2,1,0:T(8,128)(2,1)}), bf16[4,256,128]{2,1,0:T(8,128)(2,1)S(1)}, u32[]{:S(2)}, u32[]{:S(2)}) async-start(bf16[4,256,128]{2,1,0:T(8,128)(2,1)} %bitcast), calls=%async_computation | async-start | bytes 524288 | tf_op jit(solution)/shard_map/all_to_all | solution.py:536
  15.7 1.1 %inner.1 = (f32[8,96,128]{2,1,0:T(8,128)S(1)}, f32[8,112,128]{2,1,0:T(8,128)S(1)}) custom-call(f32[8,96,256]{2,1,0:T(8,128)S(1)} %get-tuple-element.19.grid_ref, bf16[400,128]{1,0:T(8,128)(2,1)S(1)} %collective-permute-done.far_x, bf16[400,128]{1,0:T(8,128)(2,1)S(1)} %collective-permute-done.1.near_x), custom_call_target="tpu_custom_call" | custom-call | flops 4587520 | bytes 1835008 | tf_op jit(solution)/shard_map/inner/pallas_call | solution.py:540
  16.8 4.3 %all-to-all-done = bf16[4,256,128]{2,1,0:T(8,128)(2,1)S(1)} async-done(((bf16[4,256,128]{2,1,0:T(8,128)(2,1)}), bf16[4,256,128]{2,1,0:T(8,128)(2,1)S(1)}, u32[]{:S(2)}, u32[]{:S(2)}) %all-to-all-start) | async-done | bytes 262176 | tf_op jit(solution)/shard_map/all_to_all | solution.py:536
  21.1 2.7 %finish.1 = (f32[4,2,64,128]{3,2,1,0:T(8,128)}, f32[2,1,1,2048]{3,2,1,0:T(1,128)}) custom-call(s32[8,2048]{1,0:T(8,128)S(1)} %get-tuple-element.13.quarter_ref, f32[8,2048]{1,0:T(8,128)S(1)} %get-tuple-element.14.value_ref, bf16[256,2048]{1,0:T(8,128)(2,1)S(1)} %get-tuple-element.15.dense_y_ref, s32[1,2048]{1,0:T(1,128)S(1)} %get-tuple-element.16.level_ref, ...), custom_call_target="tpu_custom_call" | custom-call | tf_op jit(solution)/shard_map/finish/pallas_call | solution.py:556
Async XLA Ops:
  0.6 6.2 %copy-start = (f32[4,2,64,128]{3,2,1,0:T(8,128)S(1)}, f32[4,2,64,128]{3,2,1,0:T(8,128)}, u32[]{:S(2)}) copy-start(f32[4,2,64,128]{3,2,1,0:T(8,128)} %velocity_ref.1) | copy-start | bytes 786436
  2.3 7.2 %collective-permute-start = (bf16[400,128]{1,0:T(8,128)(2,1)S(1)}, bf16[400,128]{1,0:T(8,128)(2,1)S(1)}, u32[]{:S(2)}, u32[]{:S(2)}) collective-permute-start(bf16[400,128]{1,0:T(8,128)(2,1)S(1)} %get-tuple-element.20), channel_id=1, source_target_pairs={{0,28},{4,8},{8,4},{12,16},{16,12},{20,24},{24,20},{28,0},{1,29},{... | collective-permute-start | bytes 307208 | tf_op jit(solution)/shard_map/ppermute | solution.py:505
  7.7 1.8 %collective-permute-start.1 = (bf16[400,128]{1,0:T(8,128)(2,1)S(1)}, bf16[400,128]{1,0:T(8,128)(2,1)S(1)}, u32[]{:S(2)}, u32[]{:S(2)}) collective-permute-start(bf16[400,128]{1,0:T(8,128)(2,1)S(1)} %get-tuple-element.21), channel_id=1, source_target_pairs={{0,4},{4,0},{8,12},{12,8},{16,20},{20,16},{24,28},{28,24},{1,5},{5... | collective-permute-start | bytes 307208 | tf_op jit(solution)/shard_map/ppermute | solution.py:519
  11.0 10.2 %all-to-all-start = ((bf16[4,256,128]{2,1,0:T(8,128)(2,1)}), bf16[4,256,128]{2,1,0:T(8,128)(2,1)S(1)}, u32[]{:S(2)}, u32[]{:S(2)}) async-start(bf16[4,256,128]{2,1,0:T(8,128)(2,1)} %bitcast), calls=%async_computation | async-start | bytes 524288 | tf_op jit(solution)/shard_map/all_to_all | solution.py:536

commit v7 on v5

--- a/solution.py
+++ b/solution.py
@@ -125,7 +125,7 @@
 
 def far_kernel(
     shape, chunk, fish_hbm, velocity_hbm, cell_hbm, frac_hbm, force_hbm,
-    half_ref, far_ref, force_out, dense_y_ref, quarter_ref, value_ref, level_ref,
+    half_ref, far_ref, force_out, dense_y_ref, quarter_ref, value_ref, level_ref, parity_ref,
     fish_ref, velocity_ref, cell_ref, frac_ref, force_ref, sems,
 ):
     pairs = (
@@ -138,7 +138,9 @@
     cells_x, cells_y, extent_x, extent_y = shape
     levels, comps = velocity_ref.shape[:2]
     slots = cell_ref.shape[3]
-    row, col, even, _ = position()
+    row, col, even, even_y = position()
+    parity_ref[0:1] = jnp.full((1, LANES), jnp.where(even, 1, 0), jnp.int32)
+    parity_ref[1:2] = jnp.full((1, LANES), jnp.where(even_y, 1, 0), jnp.int32)
     base = jnp.where(even, -MARGIN // 4, cells_x // 8)
     for copy in copies[:-1]:
         copy.wait()
@@ -202,99 +204,93 @@
     return lax.broadcasted_iota(jnp.int32, (rows, LANES), 1)
 
 
-def strip_parts(near, far, k, items, even):
-    lane = lane_index(STRIP)
-    row = (items + k // EDGE_PER) * STRIP
+def ordered(parity, near_ref, far_ref, before_ref, after_ref):
+    rows = near_ref.shape[0]
+    even = jnp.broadcast_to(parity, (2 * ROWS, LANES)) != 0
+    for row in range(0, rows, 2 * ROWS):
+        near = near_ref[row : row + 2 * ROWS].astype(jnp.float32)
+        far = far_ref[row : row + 2 * ROWS].astype(jnp.float32)
+        before_ref[row : row + 2 * ROWS] = jnp.where(even, far, near)
+        after_ref[row : row + 2 * ROWS] = jnp.where(even, near, far)
+
+
+def strip_tile(ref, k, items, row):
+    lane = lane_index(ROWS)
+    inner = ref[k * STRIP + row : k * STRIP + row + ROWS]
+    start = (items + k // EDGE_PER) * STRIP + row
+    edge = rolled(ref[start : start + ROWS], -SPAN * (k % EDGE_PER))
+    return inner, jnp.where((lane < MARGIN) | (lane >= LANES - MARGIN), edge, 0.0)
+
+
+def extended_tile(grid_ref, before_ref, after_ref, k, row, cells_y):
+    items, wide = grid_ref.shape[:2]
+    near = PAD - MARGIN
     parts = []
-    for first, second in ((far, near), (near, far)):
-        inner = jnp.where(
-            even,
-            first[k * STRIP : (k + 1) * STRIP].astype(jnp.float32),
-            second[k * STRIP : (k + 1) * STRIP].astype(jnp.float32),
-        )
-        edge = jnp.where(
-            even,
-            first[row : row + STRIP].astype(jnp.float32),
-            second[row : row + STRIP].astype(jnp.float32),
-        )
-        edge = rolled(edge, -SPAN * (k % EDGE_PER))
-        edge = jnp.where((lane < MARGIN) | (lane >= LANES - MARGIN), edge, 0.0)
-        parts.append((inner, edge))
-    return parts
-
-
-def joined(center, before, after):
-    wide = center.shape[0]
-    near = PAD - MARGIN
-    overlap = STRIP - near
-    return jnp.concatenate(
-        [
-            before[:near],
-            center[:overlap] + before[near:],
-            center[overlap : wide - overlap],
-            center[wide - overlap :] + after[:overlap],
-            after[overlap:],
-        ],
-        axis=0,
-    )
-
-
-def extended_rows(grid_ref, near, far, k, items, cells_y, even):
-    before, after = strip_parts(near, far, k, items, even)
-    inner = joined(grid_ref[k, :, :cells_y], before[0], after[0])
-    edge = joined(grid_ref[k, :, cells_y:], before[1], after[1])
-    return inner, edge
-
-
-def folds(rows):
-    return [(row, min(SPAN, rows - row)) for row in range(0, rows, SPAN)]
-
-
-def pack_kernel(shape, grid_ref, far_x, near_x, far_ref, near_ref):
+    if near <= row < near + wide:
+        place = slice(row - near, row - near + ROWS)
+        parts.append((grid_ref[k, place, :cells_y], grid_ref[k, place, cells_y:]))
+    if row < STRIP:
+        parts.append(strip_tile(before_ref, k, items, row))
+    if row >= wide + 2 * near - STRIP:
+        parts.append(strip_tile(after_ref, k, items, row - (wide + 2 * near - STRIP)))
+    return tuple(functools.reduce(jnp.add, part) for part in zip(*parts))
+
+
+def pack_kernel(
+    shape, parity_ref, grid_ref, far_x, near_x, far_ref, near_ref, before_ref, after_ref,
+):
     cells_x, cells_y, _, _ = shape
     items = grid_ref.shape[0]
     groups = -(-items // EDGE_PER)
     rows = cells_x + 2 * PAD
-    lane = lane_index(rows)
-    _, _, even_x, even = position()
+    lane = lane_index(ROWS)
+    ordered(parity_ref[0:1], near_x, far_x, before_ref, after_ref)
+    even = jnp.broadcast_to(parity_ref[1:2], (2 * ROWS, LANES)) != 0
     up_halo = (lane >= LANES - REACH) & (lane < LANES - MARGIN)
     down_halo = (lane >= MARGIN) & (lane < REACH)
-    halos = None
-    for group in range(groups):
-        ups, downs = None, None
-        for k in range(group * EDGE_PER, min((group + 1) * EDGE_PER, items)):
-            inner, edge = extended_rows(grid_ref, near_x, far_x, k, items, cells_y, even_x)
-            shift = SPAN * (k % EDGE_PER)
-            up = rolled(jnp.where(lane >= LANES - MARGIN, inner, edge), shift)
-            down = rolled(jnp.where(lane < MARGIN, inner, edge), shift)
-            halo = rolled(jnp.where(up_halo | down_halo, inner, 0.0), REACH + HALO * k)
-            ups = up if ups is None else ups + up
-            downs = down if downs is None else downs + down
-            halos = halo if halos is None else halos + halo
-        place = slice(group * rows, (group + 1) * rows)
-        near_ref[place] = jnp.where(even, ups, downs).astype(jnp.bfloat16)
-        far_ref[place] = jnp.where(even, downs, ups).astype(jnp.bfloat16)
-    ups = jnp.where(lane < HALO * items, halos, 0.0)
-    downs = jnp.where(lane < HALO * items, rolled(halos, -MARGIN - REACH), 0.0)
-    for out_ref, total in (
-        (near_ref, jnp.where(even, ups, downs)), (far_ref, jnp.where(even, downs, ups)),
-    ):
-        folded = total[:SPAN]
-        for index, (row, size) in enumerate(folds(rows)[1:]):
-            piece = rolled(total[row : row + size], SPAN * (index + 1))
-            if size < SPAN:
-                gap = jnp.zeros((SPAN - size, LANES), jnp.float32)
-                piece = jnp.concatenate([piece, gap], axis=0)
-            folded = folded + piece
-        out_ref[groups * rows : groups * rows + SPAN] = folded.astype(jnp.bfloat16)
-
-
-def unfolded(ref, rows, groups):
-    folded = ref[groups * rows : groups * rows + SPAN].astype(jnp.float32)
-    return jnp.concatenate(
-        [rolled(folded, -SPAN * index)[:size] for index, (_, size) in enumerate(folds(rows))],
-        axis=0,
-    )
+
+    def store(row, up, down):
+        near_ref[row : row + 2 * ROWS] = jnp.where(even, up, down).astype(jnp.bfloat16)
+        far_ref[row : row + 2 * ROWS] = jnp.where(even, down, up).astype(jnp.bfloat16)
+
+    folded = {}
+    for pair in range(0, rows, 2 * ROWS):
+        packed = [[], []]
+        for row in (pair, pair + ROWS):
+            sums = [[None] * groups, [None] * groups]
+            halo = None
+            for k in range(items):
+                inner, edge = extended_tile(grid_ref, before_ref, after_ref, k, row, cells_y)
+                shift = SPAN * (k % EDGE_PER)
+                sides = (
+                    rolled(jnp.where(lane >= LANES - MARGIN, inner, edge), shift),
+                    rolled(jnp.where(lane < MARGIN, inner, edge), shift),
+                )
+                for side, group in ((0, k // EDGE_PER), (1, k // EDGE_PER)):
+                    old = sums[side][group]
+                    sums[side][group] = sides[side] if old is None else old + sides[side]
+                extra = rolled(jnp.where(up_halo | down_halo, inner, 0.0), REACH + HALO * k)
+                halo = extra if halo is None else halo + extra
+            fold, place = row // SPAN, row % SPAN
+            used = lane < HALO * items
+            turned = rolled(halo, -MARGIN - REACH)
+            for side, value in enumerate((halo, turned)):
+                value = rolled(jnp.where(used, value, 0.0), SPAN * fold)
+                key = (side, place)
+                folded[key] = folded[key] + value if key in folded else value
+                packed[side].append(sums[side])
+        for group in range(groups):
+            up, down = (
+                jnp.concatenate([part[group] for part in packed[side]], axis=0)
+                for side in range(2)
+            )
+            store(group * rows + pair, up, down)
+    for place in range(0, SPAN, 2 * ROWS):
+        up, down = (
+            jnp.concatenate([folded[side, place], folded[side, place + ROWS]], axis=0)
+            for side in range(2)
+        )
+        store(groups * rows + place, up, down)
 
 
 def around(ref, k, start, size):
@@ -347,21 +343,23 @@
 
 
 def inner_kernel(
-    shape, levels, grid_ref, far_x, near_x, inner_ref, rim_ref, moved_ref, carried_ref, sweep_ref,
+    shape, levels, parity_ref, grid_ref, far_x, near_x, inner_ref, rim_ref,
+    moved_ref, carried_ref, sweep_ref, before_ref, after_ref,
 ):
     cells_x, cells_y, _, _ = shape
     items = grid_ref.shape[0]
     comps = items // levels
     wide_x = cells_x + SPAN
     rows = cells_x + 2 * PAD
-    lane = lane_index(rows)
-    _, _, even_x, _ = position()
-    for k in range(items):
-        inner, edge = extended_rows(grid_ref, near_x, far_x, k, items, cells_y, even_x)
-        moved_ref[k, ROWS : ROWS + rows] = inner
-        low = jnp.where(lane < RIM, inner, jnp.where(lane >= LANES - MARGIN, edge, 0.0))
-        high = jnp.where(lane >= LANES - RIM, inner, jnp.where(lane < MARGIN, edge, 0.0))
-        rim_ref[k] = low + rolled(high, HALF)
+    lane = lane_index(ROWS)
+    ordered(parity_ref[0:1], near_x, far_x, before_ref, after_ref)
+    for row in range(0, rows, ROWS):
+        for k in range(items):
+            inner, edge = extended_tile(grid_ref, before_ref, after_ref, k, row, cells_y)
+            moved_ref[k, ROWS + row : 2 * ROWS + row] = inner
+            low = jnp.where(lane < RIM, inner, jnp.where(lane >= LANES - MARGIN, edge, 0.0))
+            high = jnp.where(lane >= LANES - RIM, inner, jnp.where(lane < MARGIN, edge, 0.0))
+            rim_ref[k, row : row + ROWS] = low + rolled(high, HALF)
     first_steps(moved_ref, carried_ref, sweep_ref, levels, comps, rows)
     for row in range(0, wide_x, ROWS):
         start = ROWS + PAD - MARGIN + row
@@ -371,8 +369,9 @@
 
 
 def finish_kernel(
-    shape, chunk, quarter_ref, value_ref, dense_y_ref, level_ref, inner_ref, rim_ref, far_y, near_y,
-    next_ref, sampled_ref, moved_ref, carried_ref, sweep_ref, round_ref,
+    shape, chunk, parity_ref, quarter_ref, value_ref, dense_y_ref, level_ref, inner_ref, rim_ref,
+    far_y, near_y, next_ref, sampled_ref,
+    moved_ref, carried_ref, sweep_ref, before_ref, after_ref, round_ref,
 ):
     cells_x, cells_y, _, _ = shape
     items = rim_ref.shape[0]
@@ -381,29 +380,31 @@
     slots = level_ref.shape[1]
     wide_x = cells_x + SPAN
     rows = cells_x + 2 * PAD
-    lane = lane_index(rows)
-    _, _, _, even = position()
-    near_halo, far_halo = unfolded(near_y, rows, groups), unfolded(far_y, rows, groups)
-    before = jnp.where(even, far_halo, near_halo)
-    after = rolled(jnp.where(even, near_halo, far_halo), HALF + MARGIN + REACH)
-    turned = (HALF + MARGIN + REACH) % LANES
-    halo = jnp.where((lane >= turned) & (lane < turned + HALO * items), after, before)
-    for group in range(groups):
-        row = group * rows
-        near = near_y[row : row + rows].astype(jnp.float32)
-        far = far_y[row : row + rows].astype(jnp.float32)
-        before = jnp.where(even, far, near)
-        after = rolled(jnp.where(even, near, far), HALF)
-        for k in range(group * EDGE_PER, min((group + 1) * EDGE_PER, items)):
-            slot = k % EDGE_PER
-            place = (lane + (LANES + MARGIN - SPAN * slot)) % LANES
-            main = rolled(jnp.where(place < SPAN, before, after), -SPAN * slot)
-            place = (lane + MARGIN) % HALF
-            value = rim_ref[k] + jnp.where(place < SPAN, main, 0.0)
-            outer = rolled(halo, -REACH - HALO * k)
-            low = (lane >= LANES - REACH) & (lane < LANES - MARGIN)
-            high = (lane >= HALF + MARGIN) & (lane < HALF + REACH)
-            moved_ref[k, ROWS : ROWS + rows] = jnp.where(low | high, outer, value)
+    lane = lane_index(ROWS)
+    ordered(parity_ref[1:2], near_y, far_y, before_ref, after_ref)
+    turned = HALF + MARGIN + REACH
+    high_halo = (lane >= turned) & (lane < turned + HALO * items)
+    both = (lane + MARGIN) % HALF < SPAN
+    outer = ((lane >= LANES - REACH) & (lane < LANES - MARGIN)) | (
+        (lane >= HALF + MARGIN) & (lane < HALF + REACH)
+    )
+    windows = [(lane + (LANES + MARGIN - SPAN * slot)) % LANES < SPAN for slot in range(EDGE_PER)]
+    for row in range(0, rows, ROWS):
+        start = groups * rows + row % SPAN
+        fold = SPAN * (row // SPAN)
+        low = rolled(before_ref[start : start + ROWS], -fold)
+        high = rolled(after_ref[start : start + ROWS], turned - fold)
+        halo = jnp.where(high_halo, high, low)
+        for group in range(groups):
+            start = group * rows + row
+            before = before_ref[start : start + ROWS]
+            after = rolled(after_ref[start : start + ROWS], HALF)
+            for k in range(group * EDGE_PER, min((group + 1) * EDGE_PER, items)):
+                slot = k % EDGE_PER
+                main = rolled(jnp.where(windows[slot], before, after), -SPAN * slot)
+                value = rim_ref[k, row : row + ROWS] + jnp.where(both, main, 0.0)
+                value = jnp.where(outer, rolled(halo, -REACH - HALO * k), value)
+                moved_ref[k, ROWS + row : 2 * ROWS + row] = value
 
     first_steps(moved_ref, carried_ref, sweep_ref, levels, comps, rows)
     size = 2 * ROWS
@@ -468,7 +469,7 @@
     edge_x = jax.ShapeDtypeStruct(((items + groups) * STRIP, LANES), jnp.bfloat16)
     half = (items, wide_x // 2, width)
     arrays = (fish_owner, velocity, marker_cell, marker_frac, marker_force)
-    far_half, far, force, dense_y, quarter, value, level = pl.pallas_call(
+    far_half, far, force, dense_y, quarter, value, level, parity = pl.pallas_call(
         functools.partial(far_kernel, shape, chunk),
         out_shape=(
             jax.ShapeDtypeStruct(half, jnp.float32),
@@ -478,9 +479,10 @@
             jax.ShapeDtypeStruct((ROWS, slots), jnp.int32),
             jax.ShapeDtypeStruct((ROWS, slots), jnp.float32),
             jax.ShapeDtypeStruct((1, slots), jnp.int32),
+            jax.ShapeDtypeStruct((2, LANES), jnp.int32),
         ),
         in_specs=[pl.BlockSpec(memory_space=pltpu.HBM)] * 5,
-        out_specs=tuple(whole(7)),
+        out_specs=tuple(whole(8)),
         scratch_shapes=[pltpu.VMEM(a.shape, a.dtype) for a in arrays]
         + [pltpu.SemaphoreType.DMA((5,))],
         compiler_params=params,
@@ -506,11 +508,12 @@
     far, near = pl.pallas_call(
         functools.partial(pack_kernel, shape),
         out_shape=(edge_y, edge_y),
-        in_specs=whole(3),
+        in_specs=whole(4),
         out_specs=tuple(whole(2)),
+        scratch_shapes=[pltpu.VMEM(edge_x.shape, jnp.float32)] * 2,
         compiler_params=params,
         name="pack",
-    )(grid, far_x, near_x)
+    )(parity, grid, far_x, near_x)
     far_pairs, near_pairs = swap_pairs("gy")
     far_y = lax.ppermute(far, "gy", far_pairs)
     near_y = lax.ppermute(near, "gy", near_pairs)
@@ -521,28 +524,30 @@
             jax.ShapeDtypeStruct((items, wide_x, LANES), jnp.float32),
             jax.ShapeDtypeStruct((items, rows, LANES), jnp.float32),
         ),
-        in_specs=whole(3),
+        in_specs=whole(4),
         out_specs=tuple(whole(2)),
-        scratch_shapes=[field, field, field],
+        scratch_shapes=[field, field, field] + [pltpu.VMEM(edge_x.shape, jnp.float32)] * 2,
         compiler_params=params,
         cost_estimate=pl.CostEstimate(
             flops=40 * items * rows * LANES, bytes_accessed=16 * items * rows * LANES,
             transcendentals=0,
         ),
         name="inner",
-    )(grid, far_x, near_x)
+    )(parity, grid, far_x, near_x)
     return pl.pallas_call(
         functools.partial(finish_kernel, shape, chunk),
         out_shape=(
             jax.ShapeDtypeStruct(velocity.shape, jnp.float32),
             jax.ShapeDtypeStruct((comps, 1, 1, slots), jnp.float32),
         ),
-        in_specs=whole(8),
+        in_specs=whole(9),
         out_specs=tuple(whole(2)),
-        scratch_shapes=[field, field, field, pltpu.VMEM((items * wide_x, width), jnp.bfloat16)],
+        scratch_shapes=[field, field, field]
+        + [pltpu.VMEM(edge_y.shape, jnp.float32)] * 2
+        + [pltpu.VMEM((items * wide_x, width), jnp.bfloat16)],
         compiler_params=params,
         name="finish",
-    )(quarter, value, dense_y, level, inner, rim, far_y, near_y)
+    )(parity, quarter, value, dense_y, level, inner, rim, far_y, near_y)
 
 
 def solution(mesh):

time: 21 us -> 22.2 us (1.057)
  Pallas kernels: 7.05 us -> 8.61 us
  waiting for transfers between devices: 4.4 us -> 4.02 us
    pallas_call x1, Pallas kernels: 0.78 us -> 2.04 us  [body(): pl.pallas_call(functools.partial(pack_kernel, shape), out_shape=(edge_y,...]
    pallas_call x1, Pallas kernels: 1.08 us -> 1.46 us  [body(): pl.pallas_call(functools.partial(inner_kernel, shape, levels), out_shape=...]
    ppermute x1, waiting for transfers between devices: 0.67 us -> 0.3 us  [body(): far_y = lax.ppermute(far, 'gy', far_pairs)]
  transfers between devices with their start and end apart: 4 -> 4, of which waited for: 3 -> 3; matrix products, arithmetic and copies ran while one was open for 0% -> 0% of each run, Pallas kernels for 9% -> 10%
where the time goes in v7:
time: 22.2 us; the launch traced here: 22 us
  starting transfers between devices  8.72 us (39%)
  Pallas kernels  8.61 us (39%)
  waiting for transfers between devices  4.02 us (18%)
  between operations  0.67 us (3%)
    ppermute x1, starting transfers between devices, body(): far_x = lax.ppermute(far, 'gx', far_pairs)  4.55 us
    ppermute x1, starting transfers between devices, body(): far_y = lax.ppermute(far, 'gy', far_pairs)  3.57 us
    pallas_call x1, Pallas kernels, body(): pl.pallas_call(functools.partial(finish_kernel, shape, chunk), out_shape=...  2.64 us
    pallas_call x1, Pallas kernels, body(): pl.pallas_call(functools.partial(pack_kernel, shape), out_shape=(edge_y,...  2.04 us
    ppermute x1, waiting for transfers between devices, body(): near_y = lax.ppermute(near, 'gy', near_pairs)  1.97 us
    ppermute x1, waiting for transfers between devices, body(): far_x = lax.ppermute(far, 'gx', far_pairs)  1.75 us
    pallas_call x1, Pallas kernels, body(): pl.pallas_call(functools.partial(far_kernel, shape, chunk), out_shape=(ja...  1.67 us
    pallas_call x1, Pallas kernels, body(): pl.pallas_call(functools.partial(inner_kernel, shape, levels), out_shape=...  1.46 us
  transfers between devices with their start and end apart: 4, of which 3 were waited for; matrix products, arithmetic and copies ran while one was open for 0% of the time, Pallas kernels for 10%

profile of v7, /device:TPU:0, one launch (start us, length us, event | category | flops | bytes accessed | tf_op | source)
XLA Modules:
  0.0 22.0 jit_solution(7685575425808871704)
XLA Ops:
  0.6 0.0 copy-start
  0.6 1.7 %spread_far.1 = (f32[8,48,256]{2,1,0:T(8,128)S(1)}, bf16[400,128]{1,0:T(8,128)(2,1)S(1)}, bf16[8,16,2048]{2,1,0:T(8,128)(2,1)S(1)}, bf16[256,2048]{1,0:T(8,128)(...) custom-call(s32[48]{0:T(128)} %fish_hbm.1, ...), custom_call_target="tpu_custom_call" | custom-call | tf_op jit(solution)/shard_map/spread_far/pallas_call | solution.py:472
  2.3 4.6 %collective-permute-start = (bf16[400,128]{1,0:T(8,128)(2,1)S(1)}, bf16[400,128]{1,0:T(8,128)(2,1)S(1)}, u32[]{:S(2)}, u32[]{:S(2)}) collective-permute-start(bf16[400,128]{1,0:T(8,128)(2,1)S(1)} %get-tuple-element.24), channel_id=1, source_target_pairs={{0,28},{4,8},{8,4},{12,16},{16,12},{20,24},{24,20},{28,0},{1,29},{... | collective-permute-start | bytes 307208 | tf_op jit(solution)/shard_map/ppermute | solution.py:492
  6.9 0.0 copy-done
  6.9 0.8 %spread_near.1 = (f32[8,96,256]{2,1,0:T(8,128)S(1)}, bf16[400,128]{1,0:T(8,128)(2,1)S(1)}) custom-call(f32[4,2,64,128]{3,2,1,0:T(8,128)S(1)} %copy-done, f32[8,48,256]{2,1,0:T(8,128)S(1)} %get-tuple-element.21.far_half_ref, bf16[8,16,2048]{2,1,0:T(8,128)(2,1)S(1)} %get-tuple-element.22.force_ref, bf16[256,2048]{1,0:T(8,128)(2,1)S(1)} %get-tuple-element.19.dense_y_ref, ...), custom_call_target="tpu_custom_call" | custom-call | flops 402653184 | bytes 786432 | tf_op jit(solution)/shard_map/spread_near/pallas_call | solution.py:493
  7.7 0.1 collective-permute-start.1
  7.7 1.7 %collective-permute-done.far_x = bf16[400,128]{1,0:T(8,128)(2,1)S(1)} collective-permute-done((bf16[400,128]{1,0:T(8,128)(2,1)S(1)}, bf16[400,128]{1,0:T(8,128)(2,1)S(1)}, u32[]{:S(2)}, u32[]{:S(2)}) %collective-permute-start) | collective-permute-done | bytes 102432 | tf_op jit(solution)/shard_map/ppermute | solution.py:492
  9.5 0.0 collective-permute-done.1.near_x
  9.5 2.0 %pack.1 = (bf16[256,128]{1,0:T(8,128)(2,1)S(1)}, bf16[256,128]{1,0:T(8,128)(2,1)S(1)}) custom-call(s32[2,128]{1,0:T(2,128)S(1)} %get-tuple-element.16.parity_ref, f32[8,96,256]{2,1,0:T(8,128)S(1)} %get-tuple-element.23.grid_ref, bf16[400,128]{1,0:T(8,128)(2,1)S(1)} %collective-permute-done.far_x, bf16[400,128]{1,0:T(8,128)(2,1)S(1)} %collective-permute-done.1.near_x), custom_call_target="tpu_custom_call" | custom-call | tf_op jit(solution)/shard_map/pack/pallas_call | solution.py:508
  11.5 3.6 %collective-permute-start.2 = (bf16[256,128]{1,0:T(8,128)(2,1)S(1)}, bf16[256,128]{1,0:T(8,128)(2,1)S(1)}, u32[]{:S(2)}, u32[]{:S(2)}) collective-permute-start(bf16[256,128]{1,0:T(8,128)(2,1)S(1)} %get-tuple-element.28), channel_id=1, source_target_pairs={{0,3},{1,2},{2,1},{3,0},{4,7},{5,6},{6,5},{7,4},{8,11},{9,10},{10,... | collective-permute-start | bytes 196616 | tf_op jit(solution)/shard_map/ppermute | solution.py:518
  15.1 0.5 %collective-permute-start.3 = (bf16[256,128]{1,0:T(8,128)(2,1)S(1)}, bf16[256,128]{1,0:T(8,128)(2,1)S(1)}, u32[]{:S(2)}, u32[]{:S(2)}) collective-permute-start(bf16[256,128]{1,0:T(8,128)(2,1)S(1)} %get-tuple-element.29), channel_id=1, source_target_pairs={{0,1},{1,0},{2,3},{3,2},{4,5},{5,4},{6,7},{7,6},{8,9},{9,8},{10,11... | collective-permute-start | bytes 196616 | tf_op jit(solution)/shard_map/ppermute | solution.py:519
  15.6 1.5 %inner.1 = (f32[8,96,128]{2,1,0:T(8,128)S(1)}, f32[8,112,128]{2,1,0:T(8,128)S(1)}) custom-call(s32[2,128]{1,0:T(2,128)S(1)} %get-tuple-element.16.parity_ref, f32[8,96,256]{2,1,0:T(8,128)S(1)} %get-tuple-element.23.grid_ref, bf16[400,128]{1,0:T(8,128)(2,1)S(1)} %collective-permute-done.far_x, bf16[400,128]{1,0:T(8,128)(2,1)S(1)} %collective-permute-done.1.near_x), custom_call_target="tpu_custom_call" | custom-call | flops 4587520 | bytes 1835008 | tf_op jit(solution)/shard_map/inner/pallas_call | solution.py:521
  17.1 0.3 %collective-permute-done.2.far_y = bf16[256,128]{1,0:T(8,128)(2,1)S(1)} collective-permute-done((bf16[256,128]{1,0:T(8,128)(2,1)S(1)}, bf16[256,128]{1,0:T(8,128)(2,1)S(1)}, u32[]{:S(2)}, u32[]{:S(2)}) %collective-permute-start.2) | collective-permute-done | bytes 65568 | tf_op jit(solution)/shard_map/ppermute | solution.py:518
  17.4 2.0 %collective-permute-done.3.near_y = bf16[256,128]{1,0:T(8,128)(2,1)S(1)} collective-permute-done((bf16[256,128]{1,0:T(8,128)(2,1)S(1)}, bf16[256,128]{1,0:T(8,128)(2,1)S(1)}, u32[]{:S(2)}, u32[]{:S(2)}) %collective-permute-start.3) | collective-permute-done | bytes 65568 | tf_op jit(solution)/shard_map/ppermute | solution.py:519
  19.4 2.6 %finish.1 = (f32[4,2,64,128]{3,2,1,0:T(8,128)}, f32[2,1,1,2048]{3,2,1,0:T(1,128)}) custom-call(s32[2,128]{1,0:T(2,128)S(1)} %get-tuple-element.16.parity_ref, s32[8,2048]{1,0:T(8,128)S(1)} %get-tuple-element.17.quarter_ref, f32[8,2048]{1,0:T(8,128)S(1)} %get-tuple-element.18.value_ref, bf16[256,2048]{1,0:T(8,128)(2,1)S(1)} %get-tuple-element.19.dense_y_ref, ...), custom_call_target="tpu_custom_call" | custom-call | tf_op jit(solution)/shard_map/finish/pallas_call | solution.py:537
Async XLA Ops:
  0.6 6.2 %copy-start = (f32[4,2,64,128]{3,2,1,0:T(8,128)S(1)}, f32[4,2,64,128]{3,2,1,0:T(8,128)}, u32[]{:S(2)}) copy-start(f32[4,2,64,128]{3,2,1,0:T(8,128)} %velocity_ref.1) | copy-start | bytes 786436
  2.3 7.2 %collective-permute-start = (bf16[400,128]{1,0:T(8,128)(2,1)S(1)}, bf16[400,128]{1,0:T(8,128)(2,1)S(1)}, u32[]{:S(2)}, u32[]{:S(2)}) collective-permute-start(bf16[400,128]{1,0:T(8,128)(2,1)S(1)} %get-tuple-element.24), channel_id=1, source_target_pairs={{0,28},{4,8},{8,4},{12,16},{16,12},{20,24},{24,20},{28,0},{1,29},{... | collective-permute-start | bytes 307208 | tf_op jit(solution)/shard_map/ppermute | solution.py:492
  7.7 1.8 %collective-permute-start.1 = (bf16[400,128]{1,0:T(8,128)(2,1)S(1)}, bf16[400,128]{1,0:T(8,128)(2,1)S(1)}, u32[]{:S(2)}, u32[]{:S(2)}) collective-permute-start(bf16[400,128]{1,0:T(8,128)(2,1)S(1)} %get-tuple-element.25), channel_id=1, source_target_pairs={{0,4},{4,0},{8,12},{12,8},{16,20},{20,16},{24,28},{28,24},{1,5},{5... | collective-permute-start | bytes 307208 | tf_op jit(solution)/shard_map/ppermute | solution.py:506
  11.5 5.9 %collective-permute-start.2 = (bf16[256,128]{1,0:T(8,128)(2,1)S(1)}, bf16[256,128]{1,0:T(8,128)(2,1)S(1)}, u32[]{:S(2)}, u32[]{:S(2)}) collective-permute-start(bf16[256,128]{1,0:T(8,128)(2,1)S(1)} %get-tuple-element.28), channel_id=1, source_target_pairs={{0,3},{1,2},{2,1},{3,0},{4,7},{5,6},{6,5},{7,4},{8,11},{9,10},{10,... | collective-permute-start | bytes 196616 | tf_op jit(solution)/shard_map/ppermute | solution.py:518
  15.1 4.3 %collective-permute-start.3 = (bf16[256,128]{1,0:T(8,128)(2,1)S(1)}, bf16[256,128]{1,0:T(8,128)(2,1)S(1)}, u32[]{:S(2)}, u32[]{:S(2)}) collective-permute-start(bf16[256,128]{1,0:T(8,128)(2,1)S(1)} %get-tuple-element.29), channel_id=1, source_target_pairs={{0,1},{1,0},{2,3},{3,2},{4,5},{5,4},{6,7},{7,6},{8,9},{9,8},{10,11... | collective-permute-start | bytes 196616 | tf_op jit(solution)/shard_map/ppermute | solution.py:519

commit v8 on v7

--- a/solution.py
+++ b/solution.py
@@ -125,8 +125,9 @@
 
 def far_kernel(
     shape, chunk, fish_hbm, velocity_hbm, cell_hbm, frac_hbm, force_hbm,
-    half_ref, far_ref, force_out, dense_y_ref, quarter_ref, value_ref, level_ref, parity_ref,
-    fish_ref, velocity_ref, cell_ref, frac_ref, force_ref, sems,
+    half_ref, far_ref, force_out, dense_y_ref, quarter_ref, value_ref,
+    quarter_y_ref, value_y_ref, level_ref, parity_ref, velocity_ref,
+    fish_ref, cell_ref, frac_ref, force_ref, sems,
 ):
     pairs = (
         (cell_hbm, cell_ref), (frac_hbm, frac_ref), (fish_hbm, fish_ref),
@@ -162,9 +163,10 @@
         for l in range(levels):
             for c in range(comps):
                 force_out[l * comps + c, :, lanes] = twice(jnp.where(level == l, pushes[c], 0.0))
-        quarter, value = doubled(
-            *tile_weights(offset_y, four_weights(frac_ref[1, 0, :, lanes]))
-        )
+        quarter, value = tile_weights(offset_y, four_weights(frac_ref[1, 0, :, lanes]))
+        quarter_y_ref[:, lanes] = quarter
+        value_y_ref[:, lanes] = value
+        quarter, value = doubled(quarter, value)
         dense_y_ref[:, lanes] = jnp.concatenate(
             [picked_tile(quarter, value, n) for n in range(0, cells_y + MARGIN, 2 * ROWS)]
             + [jnp.zeros((LANES - SPAN, chunk), jnp.bfloat16)]
@@ -204,93 +206,86 @@
     return lax.broadcasted_iota(jnp.int32, (rows, LANES), 1)
 
 
-def ordered(parity, near_ref, far_ref, before_ref, after_ref):
-    rows = near_ref.shape[0]
-    even = jnp.broadcast_to(parity, (2 * ROWS, LANES)) != 0
-    for row in range(0, rows, 2 * ROWS):
-        near = near_ref[row : row + 2 * ROWS].astype(jnp.float32)
-        far = far_ref[row : row + 2 * ROWS].astype(jnp.float32)
-        before_ref[row : row + 2 * ROWS] = jnp.where(even, far, near)
-        after_ref[row : row + 2 * ROWS] = jnp.where(even, near, far)
-
-
-def strip_tile(ref, k, items, row):
-    lane = lane_index(ROWS)
-    inner = ref[k * STRIP + row : k * STRIP + row + ROWS]
-    start = (items + k // EDGE_PER) * STRIP + row
-    edge = rolled(ref[start : start + ROWS], -SPAN * (k % EDGE_PER))
-    return inner, jnp.where((lane < MARGIN) | (lane >= LANES - MARGIN), edge, 0.0)
-
-
-def extended_tile(grid_ref, before_ref, after_ref, k, row, cells_y):
-    items, wide = grid_ref.shape[:2]
+def ordered(parity, near_ref, far_ref):
+    even = jnp.broadcast_to(parity, near_ref.shape) != 0
+    near, far = near_ref[...].astype(jnp.float32), far_ref[...].astype(jnp.float32)
+    return jnp.where(even, far, near), jnp.where(even, near, far)
+
+
+def joined(center, before, after):
+    wide = center.shape[0]
     near = PAD - MARGIN
-    parts = []
-    if near <= row < near + wide:
-        place = slice(row - near, row - near + ROWS)
-        parts.append((grid_ref[k, place, :cells_y], grid_ref[k, place, cells_y:]))
-    if row < STRIP:
-        parts.append(strip_tile(before_ref, k, items, row))
-    if row >= wide + 2 * near - STRIP:
-        parts.append(strip_tile(after_ref, k, items, row - (wide + 2 * near - STRIP)))
-    return tuple(functools.reduce(jnp.add, part) for part in zip(*parts))
-
-
-def pack_kernel(
-    shape, parity_ref, grid_ref, far_x, near_x, far_ref, near_ref, before_ref, after_ref,
-):
+    overlap = STRIP - near
+    return jnp.concatenate(
+        [
+            before[:near],
+            center[:overlap] + before[near:],
+            center[overlap : wide - overlap],
+            center[wide - overlap :] + after[:overlap],
+            after[overlap:],
+        ],
+        axis=0,
+    )
+
+
+def extended_rows(parity, grid_ref, near_ref, far_ref, cells_y):
+    items = grid_ref.shape[0]
+    groups = -(-items // EDGE_PER)
+    size = groups * STRIP
+    before, after = ordered(parity, near_ref, far_ref)
+    packed = jnp.concatenate([before[items * STRIP :], after[items * STRIP :]], axis=0)
+    lane = lane_index(2 * size)
+    kept = (lane < MARGIN) | (lane >= LANES - MARGIN)
+    edges = [jnp.where(kept, rolled(packed, -SPAN * slot), 0.0) for slot in range(EDGE_PER)]
+    for k in range(items):
+        place = slice(k * STRIP, (k + 1) * STRIP)
+        inner = joined(grid_ref[k, :, :cells_y], before[place], after[place])
+        start = k // EDGE_PER * STRIP
+        edge = edges[k % EDGE_PER]
+        edge = joined(
+            grid_ref[k, :, cells_y:],
+            edge[start : start + STRIP],
+            edge[size + start : size + start + STRIP],
+        )
+        yield k, inner, edge
+
+
+def pack_kernel(shape, parity_ref, grid_ref, far_x, near_x, far_ref, near_ref):
     cells_x, cells_y, _, _ = shape
     items = grid_ref.shape[0]
     groups = -(-items // EDGE_PER)
     rows = cells_x + 2 * PAD
-    lane = lane_index(ROWS)
-    ordered(parity_ref[0:1], near_x, far_x, before_ref, after_ref)
-    even = jnp.broadcast_to(parity_ref[1:2], (2 * ROWS, LANES)) != 0
+    lane = lane_index(rows)
+    even = jnp.broadcast_to(parity_ref[1:2], (rows, LANES)) != 0
     up_halo = (lane >= LANES - REACH) & (lane < LANES - MARGIN)
     down_halo = (lane >= MARGIN) & (lane < REACH)
-
-    def store(row, up, down):
-        near_ref[row : row + 2 * ROWS] = jnp.where(even, up, down).astype(jnp.bfloat16)
-        far_ref[row : row + 2 * ROWS] = jnp.where(even, down, up).astype(jnp.bfloat16)
-
-    folded = {}
-    for pair in range(0, rows, 2 * ROWS):
-        packed = [[], []]
-        for row in (pair, pair + ROWS):
-            sums = [[None] * groups, [None] * groups]
-            halo = None
-            for k in range(items):
-                inner, edge = extended_tile(grid_ref, before_ref, after_ref, k, row, cells_y)
-                shift = SPAN * (k % EDGE_PER)
-                sides = (
-                    rolled(jnp.where(lane >= LANES - MARGIN, inner, edge), shift),
-                    rolled(jnp.where(lane < MARGIN, inner, edge), shift),
-                )
-                for side, group in ((0, k // EDGE_PER), (1, k // EDGE_PER)):
-                    old = sums[side][group]
-                    sums[side][group] = sides[side] if old is None else old + sides[side]
-                extra = rolled(jnp.where(up_halo | down_halo, inner, 0.0), REACH + HALO * k)
-                halo = extra if halo is None else halo + extra
-            fold, place = row // SPAN, row % SPAN
-            used = lane < HALO * items
-            turned = rolled(halo, -MARGIN - REACH)
-            for side, value in enumerate((halo, turned)):
-                value = rolled(jnp.where(used, value, 0.0), SPAN * fold)
-                key = (side, place)
-                folded[key] = folded[key] + value if key in folded else value
-                packed[side].append(sums[side])
-        for group in range(groups):
-            up, down = (
-                jnp.concatenate([part[group] for part in packed[side]], axis=0)
-                for side in range(2)
-            )
-            store(group * rows + pair, up, down)
-    for place in range(0, SPAN, 2 * ROWS):
-        up, down = (
-            jnp.concatenate([folded[side, place], folded[side, place + ROWS]], axis=0)
-            for side in range(2)
-        )
-        store(groups * rows + place, up, down)
+    halos, ups, downs = None, None, None
+    for k, inner, edge in extended_rows(parity_ref[0:1], grid_ref, near_x, far_x, cells_y):
+        slot = k % EDGE_PER
+        up = rolled(jnp.where(lane >= LANES - MARGIN, inner, edge), SPAN * slot)
+        down = rolled(jnp.where(lane < MARGIN, inner, edge), SPAN * slot)
+        halo = rolled(jnp.where(up_halo | down_halo, inner, 0.0), REACH + HALO * k)
+        ups = ups + up if slot else up
+        downs = downs + down if slot else down
+        halos = halos + halo if k else halo
+        if slot == EDGE_PER - 1 or k == items - 1:
+            place = slice(k // EDGE_PER * rows, (k // EDGE_PER + 1) * rows)
+            near_ref[place] = jnp.where(even, ups, downs).astype(jnp.bfloat16)
+            far_ref[place] = jnp.where(even, downs, ups).astype(jnp.bfloat16)
+    used = lane < HALO * items
+    ups = jnp.where(used, halos, 0.0)
+    downs = jnp.where(used, rolled(halos, -MARGIN - REACH), 0.0)
+    folded = None
+    for row in range(0, rows, SPAN):
+        size = min(SPAN, rows - row)
+        parts = [value[row : row + size] for value in (ups, downs)]
+        if size < SPAN:
+            parts = [jnp.concatenate([p, jnp.zeros((SPAN - size, LANES), p.dtype)], 0) for p in parts]
+        part = rolled(jnp.concatenate(parts, axis=0), row)
+        folded = folded + part if row else part
+    up, down, even = folded[:SPAN], folded[SPAN:], even[:SPAN]
+    near_ref[groups * rows :] = jnp.where(even, up, down).astype(jnp.bfloat16)
+    far_ref[groups * rows :] = jnp.where(even, down, up).astype(jnp.bfloat16)
 
 
 def around(ref, k, start, size):
@@ -342,34 +337,95 @@
 HALF = LANES // 2
 
 
+def weight_kernel(
+    shape, chunk, parity_ref, quarter_ref, value_ref, level_ref, inner_ref, rim_ref, parity_out
+):
+    parity_out[...] = parity_ref[...]
+    _, cells_y, _, _ = shape
+    slots = quarter_ref.shape[1]
+    size = 2 * ROWS
+    levels = inner_ref.shape[0] // LANES
+    row = lax.broadcasted_iota(jnp.int32, (size, chunk), 0)
+
+    def cut(tile, keep):
+        return jnp.where(keep, tile.astype(jnp.float32), 0.0).astype(jnp.bfloat16)
+
+    for first in range(0, slots, chunk):
+        lanes = slice(first, first + chunk)
+        level = level_ref[:, lanes]
+        for l in range(levels):
+            value = jnp.where(level == l, value_ref[:, lanes], 0.0)
+            quarter, value = doubled(quarter_ref[:, lanes], value)
+            for start in range(0, LANES, size):
+                inner = picked_tile(quarter, value, start)
+                if start < REACH:
+                    inner = cut(inner, row + start >= REACH)
+                if start + size > cells_y - REACH:
+                    inner = cut(inner, row + start < cells_y - REACH)
+                if start >= LANES - MARGIN:
+                    rim = picked_tile(quarter, value, start - LANES)
+                elif start + size > HALF - REACH and start < HALF + MARGIN:
+                    rim = picked_tile(quarter, value, start + cells_y - HALF)
+                    rim = cut(rim, row + start >= HALF - REACH) if start < HALF - REACH else rim
+                elif start < REACH:
+                    rim = picked_tile(quarter, value, start)
+                    rim = cut(rim, row + start < REACH) if start + size > REACH else rim
+                else:
+                    rim = jnp.zeros_like(value)
+                place = slice(l * LANES + start, l * LANES + start + size)
+                inner_ref[place, lanes] = inner
+                rim_ref[place, lanes] = rim
+
+
+def sampled_part(round_ref, weight_ref, quarter_ref, value_ref, lanes, comps):
+    wide_x = round_ref.shape[0] // comps
+    partial = jnp.dot(round_ref[...], weight_ref[:, lanes], preferred_element_type=jnp.float32)
+    quarter, value = quarter_ref[:, lanes], value_ref[:, lanes]
+    totals = [jnp.zeros_like(value)] * comps
+    for row in range(0, wide_x, ROWS):
+        here = quarter == (MARGIN - row) // 4
+        for c in range(comps):
+            start = c * wide_x + row
+            totals[c] = jnp.where(here, partial[start : start + ROWS], totals[c])
+    return [jnp.sum(total * value, axis=0, keepdims=True) for total in totals]
+
+
 def inner_kernel(
-    shape, levels, parity_ref, grid_ref, far_x, near_x, inner_ref, rim_ref,
-    moved_ref, carried_ref, sweep_ref, before_ref, after_ref,
+    shape, chunk, levels, parity_ref, quarter_ref, value_ref, weight_ref, grid_ref, far_x, near_x,
+    inner_ref, rim_ref, sampled_ref, moved_ref, carried_ref, sweep_ref, round_ref,
 ):
     cells_x, cells_y, _, _ = shape
     items = grid_ref.shape[0]
     comps = items // levels
+    slots = quarter_ref.shape[1]
     wide_x = cells_x + SPAN
     rows = cells_x + 2 * PAD
-    lane = lane_index(ROWS)
-    ordered(parity_ref[0:1], near_x, far_x, before_ref, after_ref)
-    for row in range(0, rows, ROWS):
+    lane = lane_index(rows)
+    for k, inner, edge in extended_rows(parity_ref[0:1], grid_ref, near_x, far_x, cells_y):
+        moved_ref[k, ROWS : ROWS + rows] = inner
+        low = jnp.where(lane < RIM, inner, jnp.where(lane >= LANES - MARGIN, edge, 0.0))
+        high = jnp.where(lane >= LANES - RIM, inner, jnp.where(lane < MARGIN, edge, 0.0))
+        rim_ref[k] = low + rolled(high, HALF)
+    first_steps(moved_ref, carried_ref, sweep_ref, levels, comps, rows)
+    size = 2 * ROWS
+    for row in range(0, wide_x, size):
+        start = ROWS + PAD - MARGIN + row
+        results = sweep(sweep_ref, carried_ref, levels, comps, start, size)
         for k in range(items):
-            inner, edge = extended_tile(grid_ref, before_ref, after_ref, k, row, cells_y)
-            moved_ref[k, ROWS + row : 2 * ROWS + row] = inner
-            low = jnp.where(lane < RIM, inner, jnp.where(lane >= LANES - MARGIN, edge, 0.0))
-            high = jnp.where(lane >= LANES - RIM, inner, jnp.where(lane < MARGIN, edge, 0.0))
-            rim_ref[k, row : row + ROWS] = low + rolled(high, HALF)
-    first_steps(moved_ref, carried_ref, sweep_ref, levels, comps, rows)
-    for row in range(0, wide_x, ROWS):
-        start = ROWS + PAD - MARGIN + row
-        results = sweep(sweep_ref, carried_ref, levels, comps, start, ROWS)
-        for k in range(items):
-            inner_ref[k, row : row + ROWS] = results[k]
+            level, c = k // comps, k % comps
+            place = slice(c * wide_x + row, c * wide_x + row + size)
+            round_ref[place, level * LANES : (level + 1) * LANES] = results[k].astype(jnp.bfloat16)
+            if MARGIN <= row < MARGIN + cells_x:
+                inner_ref[k, row - MARGIN : row - MARGIN + size] = results[k]
+    for first in range(0, slots, chunk):
+        lanes = slice(first, first + chunk)
+        parts = sampled_part(round_ref, weight_ref, quarter_ref, value_ref, lanes, comps)
+        for c in range(comps):
+            sampled_ref[c : c + 1, lanes] = parts[c]
 
 
 def finish_kernel(
-    shape, chunk, parity_ref, quarter_ref, value_ref, dense_y_ref, level_ref, inner_ref, rim_ref,
+    shape, chunk, parity_ref, quarter_ref, value_ref, weight_ref, inner_ref, rim_ref, part_ref,
     far_y, near_y, next_ref, sampled_ref,
     moved_ref, carried_ref, sweep_ref, before_ref, after_ref, round_ref,
 ):
@@ -377,11 +433,11 @@
     items = rim_ref.shape[0]
     groups = -(-items // EDGE_PER)
     levels, comps = next_ref.shape[:2]
-    slots = level_ref.shape[1]
+    slots = quarter_ref.shape[1]
     wide_x = cells_x + SPAN
     rows = cells_x + 2 * PAD
     lane = lane_index(ROWS)
-    ordered(parity_ref[1:2], near_y, far_y, before_ref, after_ref)
+    before_ref[...], after_ref[...] = ordered(parity_ref[1:2], near_y, far_y)
     turned = HALF + MARGIN + REACH
     high_halo = (lane >= turned) & (lane < turned + HALO * items)
     both = (lane + MARGIN) % HALF < SPAN
@@ -413,34 +469,23 @@
         start = ROWS + PAD - MARGIN + row
         results = sweep(sweep_ref, carried_ref, levels, comps, start, size)
         for k in range(items):
+            level, c = k // comps, k % comps
+            place = slice(c * wide_x + row, c * wide_x + row + size)
+            round_ref[place, level * LANES : (level + 1) * LANES] = results[k].astype(jnp.bfloat16)
+        if not MARGIN <= row < MARGIN + cells_x:
+            continue
+        place = slice(row - MARGIN, row - MARGIN + size)
+        for k in range(items):
             low, high = results[k], rolled(results[k], HALF)
-            inner = inner_ref[k, row : row + size]
+            inner = inner_ref[k, place]
             inner = jnp.where(lane < REACH, low, jnp.where(lane >= LANES - REACH, high, inner))
-            edge = jnp.where(lane < MARGIN, high, low)
-            place = slice(k * wide_x + row, k * wide_x + row + size)
-            round_ref[place, :cells_y] = inner.astype(jnp.bfloat16)
-            round_ref[place, cells_y:] = edge.astype(jnp.bfloat16)
-            if MARGIN <= row < MARGIN + cells_x:
-                next_ref[k // comps, k % comps, row - MARGIN : row - MARGIN + size] = inner
+            next_ref[k // comps, k % comps, place] = inner
 
     for first in range(0, slots, chunk):
         lanes = slice(first, first + chunk)
-        level = level_ref[:, lanes]
-        partial = jnp.dot(
-            round_ref[...], dense_y_ref[:, lanes], preferred_element_type=jnp.float32
-        )
-        partial = partial.reshape(levels, comps, wide_x, chunk)
-        quarter, value = quarter_ref[:, lanes], value_ref[:, lanes]
-        heres = [quarter == (MARGIN - row) // 4 for row in range(0, wide_x, ROWS)]
-        aboves = [level == l for l in range(levels - 1)]
+        parts = sampled_part(round_ref, weight_ref, quarter_ref, value_ref, lanes, comps)
         for c in range(comps):
-            total = jnp.zeros((ROWS, chunk), jnp.float32)
-            for row in range(0, wide_x, ROWS):
-                picked = partial[levels - 1, c, row : row + ROWS]
-                for l in range(levels - 2, -1, -1):
-                    picked = jnp.where(aboves[l], partial[l, c, row : row + ROWS], picked)
-                total = jnp.where(heres[row // ROWS], picked, total)
-            sampled_ref[c, 0, :, lanes] = jnp.sum(total * value, axis=0, keepdims=True)
+            sampled_ref[c, 0, :, lanes] = part_ref[c : c + 1, lanes] + parts[c]
 
 
 def whole(count):
@@ -465,11 +510,12 @@
     chunk = min(512, slots)
     width = cells_y + LANES
     groups = -(-items // EDGE_PER)
-    params = pltpu.CompilerParams(vmem_limit_bytes=40 * 1024 * 1024)
+    params = pltpu.CompilerParams(vmem_limit_bytes=32 * 1024 * 1024)
     edge_x = jax.ShapeDtypeStruct(((items + groups) * STRIP, LANES), jnp.bfloat16)
     half = (items, wide_x // 2, width)
     arrays = (fish_owner, velocity, marker_cell, marker_frac, marker_force)
-    far_half, far, force, dense_y, quarter, value, level, parity = pl.pallas_call(
+    far_half, far, force, dense_y, quarter, value, quarter_y, value_y, level, parity, near_velocity = (
+        pl.pallas_call(
         functools.partial(far_kernel, shape, chunk),
         out_shape=(
             jax.ShapeDtypeStruct(half, jnp.float32),
@@ -478,16 +524,20 @@
             jax.ShapeDtypeStruct((width, slots), jnp.bfloat16),
             jax.ShapeDtypeStruct((ROWS, slots), jnp.int32),
             jax.ShapeDtypeStruct((ROWS, slots), jnp.float32),
+            jax.ShapeDtypeStruct((ROWS, slots), jnp.int32),
+            jax.ShapeDtypeStruct((ROWS, slots), jnp.float32),
             jax.ShapeDtypeStruct((1, slots), jnp.int32),
             jax.ShapeDtypeStruct((2, LANES), jnp.int32),
+            jax.ShapeDtypeStruct(velocity.shape, velocity.dtype),
         ),
         in_specs=[pl.BlockSpec(memory_space=pltpu.HBM)] * 5,
-        out_specs=tuple(whole(8)),
-        scratch_shapes=[pltpu.VMEM(a.shape, a.dtype) for a in arrays]
+        out_specs=tuple(whole(11)),
+        scratch_shapes=[pltpu.VMEM(a.shape, a.dtype) for a in arrays if a is not velocity]
         + [pltpu.SemaphoreType.DMA((5,))],
         compiler_params=params,
         name="spread_far",
     )(*(pltpu.with_memory_space_constraint(a, pltpu.HBM) for a in arrays))
+    )
     far_pairs, near_pairs = swap_pairs("gx")
     far_x = lax.ppermute(far, "gx", far_pairs)
     grid, near = pl.pallas_call(
@@ -502,15 +552,27 @@
             transcendentals=0,
         ),
         name="spread_near",
-    )(velocity, far_half, force, dense_y, quarter)
+    )(near_velocity, far_half, force, dense_y, quarter)
     near_x = lax.ppermute(near, "gx", near_pairs)
+    weights = jax.ShapeDtypeStruct((levels * LANES, slots), jnp.bfloat16)
+    inner_weight, rim_weight, parity = pl.pallas_call(
+        functools.partial(weight_kernel, shape, chunk),
+        out_shape=(weights, weights, jax.ShapeDtypeStruct(parity.shape, parity.dtype)),
+        in_specs=whole(4),
+        out_specs=tuple(whole(3)),
+        compiler_params=params,
+        cost_estimate=pl.CostEstimate(
+            flops=2 * levels * LANES * slots, bytes_accessed=4 * levels * LANES * slots,
+            transcendentals=0,
+        ),
+        name="weights",
+    )(parity, quarter_y, value_y, level)
     edge_y = jax.ShapeDtypeStruct((groups * rows + SPAN, LANES), jnp.bfloat16)
     far, near = pl.pallas_call(
         functools.partial(pack_kernel, shape),
         out_shape=(edge_y, edge_y),
         in_specs=whole(4),
         out_specs=tuple(whole(2)),
-        scratch_shapes=[pltpu.VMEM(edge_x.shape, jnp.float32)] * 2,
         compiler_params=params,
         name="pack",
     )(parity, grid, far_x, near_x)
@@ -518,22 +580,25 @@
     far_y = lax.ppermute(far, "gy", far_pairs)
     near_y = lax.ppermute(near, "gy", near_pairs)
     field = pltpu.VMEM((items, rows + 2 * ROWS, LANES), jnp.float32)
-    inner, rim = pl.pallas_call(
-        functools.partial(inner_kernel, shape, levels),
+    rounded = pltpu.VMEM((comps * wide_x, levels * LANES), jnp.bfloat16)
+    inner, rim, part = pl.pallas_call(
+        functools.partial(inner_kernel, shape, chunk, levels),
         out_shape=(
-            jax.ShapeDtypeStruct((items, wide_x, LANES), jnp.float32),
+            jax.ShapeDtypeStruct((items, cells_x, LANES), jnp.float32),
             jax.ShapeDtypeStruct((items, rows, LANES), jnp.float32),
+            jax.ShapeDtypeStruct((comps, slots), jnp.float32),
         ),
-        in_specs=whole(4),
-        out_specs=tuple(whole(2)),
-        scratch_shapes=[field, field, field] + [pltpu.VMEM(edge_x.shape, jnp.float32)] * 2,
+        in_specs=whole(7),
+        out_specs=tuple(whole(3)),
+        scratch_shapes=[field, field, field, rounded],
         compiler_params=params,
         cost_estimate=pl.CostEstimate(
-            flops=40 * items * rows * LANES, bytes_accessed=16 * items * rows * LANES,
+            flops=2 * items * wide_x * LANES * slots, bytes_accessed=16 * items * rows * LANES,
             transcendentals=0,
         ),
         name="inner",
-    )(parity, grid, far_x, near_x)
+    )(parity, quarter, value, inner_weight, grid, far_x, near_x)
+    strip_y = pltpu.VMEM(edge_y.shape, jnp.float32)
     return pl.pallas_call(
         functools.partial(finish_kernel, shape, chunk),
         out_shape=(
@@ -542,12 +607,10 @@
         ),
         in_specs=whole(9),
         out_specs=tuple(whole(2)),
-        scratch_shapes=[field, field, field]
-        + [pltpu.VMEM(edge_y.shape, jnp.float32)] * 2
-        + [pltpu.VMEM((items * wide_x, width), jnp.bfloat16)],
+        scratch_shapes=[field, field, field, strip_y, strip_y, rounded],
         compiler_params=params,
         name="finish",
-    )(parity, quarter, value, dense_y, level, inner, rim, far_y, near_y)
+    )(parity, quarter, value, rim_weight, inner, rim, part, far_y, near_y)
 
 
 def solution(mesh):

time: 22.2 us -> 22 us (level)
  waiting for transfers between devices: 4.02 us -> 3.61 us
  Pallas kernels: 8.61 us -> 8.84 us
    pallas_call x1, Pallas kernels: 2.04 us -> 0.52 us  [body(): pl.pallas_call(functools.partial(pack_kernel, shape), out_shape=(edge_y,...]
    pallas_call x1, Pallas kernels: 2.64 us -> 4.04 us  [body(): pl.pallas_call(functools.partial(finish_kernel, shape, chunk), out_shape=...]
    ppermute x1, waiting for transfers between devices: 1.75 us -> 1.3 us  [body(): far_x = lax.ppermute(far, 'gx', far_pairs)]
    pallas_call x1 -> x2, Pallas kernels: 1.46 us -> 1.86 us  [the longest x1 1.41 us: body(): pl.pallas_call(functools.partial(inner_kernel, shape, chunk, levels), out...]
  transfers between devices with their start and end apart: 4 -> 4, of which waited for: 3 -> 3; matrix products, arithmetic and copies ran while one was open for 0% -> 0% of each run, Pallas kernels for 10% -> 12%
where the time goes in v8:
time: 22 us; the launch traced here: 21.8 us
  Pallas kernels  8.84 us (40%)
  starting transfers between devices  8.72 us (40%)
  waiting for transfers between devices  3.61 us (16%)
  between operations  0.67 us (3%)
    ppermute x1, starting transfers between devices, body(): far_x = lax.ppermute(far, 'gx', far_pairs)  4.55 us
    pallas_call x1, Pallas kernels, body(): pl.pallas_call(functools.partial(finish_kernel, shape, chunk), out_shape=...  4.04 us
    ppermute x1, starting transfers between devices, body(): far_y = lax.ppermute(far, 'gy', far_pairs)  3.57 us
    ppermute x1, waiting for transfers between devices, body(): near_y = lax.ppermute(near, 'gy', near_pairs)  1.98 us
    pallas_call x1, Pallas kernels, body(): pl.pallas_call(functools.partial(far_kernel, shape, chunk), out_shape=(ja...  1.63 us
    pallas_call x1, Pallas kernels, body(): pl.pallas_call(functools.partial(inner_kernel, shape, chunk, levels), out...  1.41 us
    ppermute x1, waiting for transfers between devices, body(): far_x = lax.ppermute(far, 'gx', far_pairs)  1.3 us
    pallas_call x1, Pallas kernels, body(): pl.pallas_call(functools.partial(near_kernel, shape, chunk), out_shape=(j...  0.79 us
  transfers between devices with their start and end apart: 4, of which 3 were waited for; matrix products, arithmetic and copies ran while one was open for 0% of the time, Pallas kernels for 12%

profile of v8, /device:TPU:0, one launch (start us, length us, event | category | flops | bytes accessed | tf_op | source)
XLA Modules:
  0.0 21.8 jit_solution(11907033787291515138)
XLA Ops:
  0.6 1.6 %spread_far.1 = (f32[8,48,256]{2,1,0:T(8,128)S(1)}, bf16[400,128]{1,0:T(8,128)(2,1)S(1)}, bf16[8,16,2048]{2,1,0:T(8,128)(2,1)S(1)}, bf16[256,2048]{1,0:T(8,128)(...) custom-call(s32[48]{0:T(128)} %fish_hbm.1, ...), custom_call_target="tpu_custom_call" | custom-call | tf_op jit(solution)/shard_map/spread_far/pallas_call | solution.py:518
  2.3 4.6 %collective-permute-start = (bf16[400,128]{1,0:T(8,128)(2,1)S(1)}, bf16[400,128]{1,0:T(8,128)(2,1)S(1)}, u32[]{:S(2)}, u32[]{:S(2)}) collective-permute-start(bf16[400,128]{1,0:T(8,128)(2,1)S(1)} %get-tuple-element.37), channel_id=1, source_target_pairs={{0,28},{4,8},{8,4},{12,16},{16,12},{20,24},{24,20},{28,0},{1,29},{... | collective-permute-start | bytes 307208 | tf_op jit(solution)/shard_map/ppermute | solution.py:542
  6.8 0.8 %spread_near.1 = (f32[8,96,256]{2,1,0:T(8,128)S(1)}, bf16[400,128]{1,0:T(8,128)(2,1)S(1)}) custom-call(f32[4,2,64,128]{3,2,1,0:T(8,128)S(1)} %get-tuple-element.32.velocity_ref, f32[8,48,256]{2,1,0:T(8,128)S(1)} %get-tuple-element.33.far_half_ref, bf16[8,16,2048]{2,1,0:T(8,128)(2,1)S(1)} %get-tuple-element.34.force_ref, ...), custom_call_target="tpu_custom_call" | custom-call | flops 402653184 | bytes 786432 | tf_op jit(solution)/shard_map/spread_near/pallas_call | solution.py:543
  7.6 0.1 collective-permute-start.1
  7.7 0.4 %weights.1 = (bf16[512,2048]{1,0:T(8,128)(2,1)S(1)}, bf16[512,2048]{1,0:T(8,128)(2,1)S(1)}, s32[2,128]{1,0:T(2,128)S(1)}) custom-call(s32[2,128]{1,0:T(2,128)S(1)} %get-tuple-element.23.parity_ref, s32[8,2048]{1,0:T(8,128)S(1)} %get-tuple-element.24.quarter_ref, f32[8,2048]{1,0:T(8,128)S(1)} %get-tuple-element.25.value_ref, ...), custom_call_target="tpu_custom_call" | custom-call | flops 2097152 | bytes 4194304 | tf_op jit(solution)/shard_map/weights/pallas_call | solution.py:558
  8.1 1.3 %collective-permute-done.far_x = bf16[400,128]{1,0:T(8,128)(2,1)S(1)} collective-permute-done((bf16[400,128]{1,0:T(8,128)(2,1)S(1)}, bf16[400,128]{1,0:T(8,128)(2,1)S(1)}, u32[]{:S(2)}, u32[]{:S(2)}) %collective-permute-start) | collective-permute-done | bytes 102432 | tf_op jit(solution)/shard_map/ppermute | solution.py:542
  9.4 0.0 collective-permute-done.1.near_x
  9.4 0.5 %pack.1 = (bf16[256,128]{1,0:T(8,128)(2,1)S(1)}, bf16[256,128]{1,0:T(8,128)(2,1)S(1)}) custom-call(s32[2,128]{1,0:T(2,128)S(1)} %get-tuple-element.27.parity_ref, f32[8,96,256]{2,1,0:T(8,128)S(1)} %get-tuple-element.36.grid_ref, bf16[400,128]{1,0:T(8,128)(2,1)S(1)} %collective-permute-done.far_x, bf16[400,128]{1,0:T(8,128)(2,1)S(1)} %collective-permute-done.1.near_x), custom_call_target="tpu_custom_call" | custom-call | tf_op jit(solution)/shard_map/pack/pallas_call | solution.py:571
  10.0 3.6 %collective-permute-start.2 = (bf16[256,128]{1,0:T(8,128)(2,1)S(1)}, bf16[256,128]{1,0:T(8,128)(2,1)S(1)}, u32[]{:S(2)}, u32[]{:S(2)}) collective-permute-start(bf16[256,128]{1,0:T(8,128)(2,1)S(1)} %get-tuple-element.42), channel_id=1, source_target_pairs={{0,3},{1,2},{2,1},{3,0},{4,7},{5,6},{6,5},{7,4},{8,11},{9,10},{10,... | collective-permute-start | bytes 196616 | tf_op jit(solution)/shard_map/ppermute | solution.py:580
  13.5 0.5 %collective-permute-start.3 = (bf16[256,128]{1,0:T(8,128)(2,1)S(1)}, bf16[256,128]{1,0:T(8,128)(2,1)S(1)}, u32[]{:S(2)}, u32[]{:S(2)}) collective-permute-start(bf16[256,128]{1,0:T(8,128)(2,1)S(1)} %get-tuple-element.43), channel_id=1, source_target_pairs={{0,1},{1,0},{2,3},{3,2},{4,5},{5,4},{6,7},{7,6},{8,9},{9,8},{10,11... | collective-permute-start | bytes 196616 | tf_op jit(solution)/shard_map/ppermute | solution.py:581
  14.1 1.4 %inner.1 = (f32[8,64,128]{2,1,0:T(8,128)S(1)}, f32[8,112,128]{2,1,0:T(8,128)S(1)}, f32[2,2048]{1,0:T(2,128)S(1)}) custom-call(s32[2,128]{1,0:T(2,128)S(1)} %get-tuple-element.27.parity_ref, s32[8,2048]{1,0:T(8,128)S(1)} %get-tuple-element.28.quarter_ref, f32[8,2048]{1,0:T(8,128)S(1)} %get-tuple-element.29.value_ref, ...), custom_call_target="tpu_custom_call" | custom-call | flops 402653184 | bytes 1835008 | tf_op jit(solution)/shard_map/inner/pallas_call | solution.py:584
  15.5 0.3 %collective-permute-done.2.far_y = bf16[256,128]{1,0:T(8,128)(2,1)S(1)} collective-permute-done((bf16[256,128]{1,0:T(8,128)(2,1)S(1)}, bf16[256,128]{1,0:T(8,128)(2,1)S(1)}, u32[]{:S(2)}, u32[]{:S(2)}) %collective-permute-start.2) | collective-permute-done | bytes 65568 | tf_op jit(solution)/shard_map/ppermute | solution.py:580
  15.8 2.0 %collective-permute-done.3.near_y = bf16[256,128]{1,0:T(8,128)(2,1)S(1)} collective-permute-done((bf16[256,128]{1,0:T(8,128)(2,1)S(1)}, bf16[256,128]{1,0:T(8,128)(2,1)S(1)}, u32[]{:S(2)}, u32[]{:S(2)}) %collective-permute-start.3) | collective-permute-done | bytes 65568 | tf_op jit(solution)/shard_map/ppermute | solution.py:581
  17.8 4.0 %finish.1 = (f32[4,2,64,128]{3,2,1,0:T(8,128)}, f32[2,1,1,2048]{3,2,1,0:T(1,128)}) custom-call(s32[2,128]{1,0:T(2,128)S(1)} %get-tuple-element.27.parity_ref, s32[8,2048]{1,0:T(8,128)S(1)} %get-tuple-element.28.quarter_ref, f32[8,2048]{1,0:T(8,128)S(1)} %get-tuple-element.29.value_ref, bf16[512,2048]{1,0:T(8,128)(2,1)S(1)} %get-tuple-element.30.weight_ref, ...), custom_call_target="tpu_custom_call" | custom-call | tf_op jit(solution)/shard_map/finish/pallas_call | solution.py:602
Async XLA Ops:
  2.3 7.2 %collective-permute-start = (bf16[400,128]{1,0:T(8,128)(2,1)S(1)}, bf16[400,128]{1,0:T(8,128)(2,1)S(1)}, u32[]{:S(2)}, u32[]{:S(2)}) collective-permute-start(bf16[400,128]{1,0:T(8,128)(2,1)S(1)} %get-tuple-element.37), channel_id=1, source_target_pairs={{0,28},{4,8},{8,4},{12,16},{16,12},{20,24},{24,20},{28,0},{1,29},{... | collective-permute-start | bytes 307208 | tf_op jit(solution)/shard_map/ppermute | solution.py:542
  7.6 1.8 %collective-permute-start.1 = (bf16[400,128]{1,0:T(8,128)(2,1)S(1)}, bf16[400,128]{1,0:T(8,128)(2,1)S(1)}, u32[]{:S(2)}, u32[]{:S(2)}) collective-permute-start(bf16[400,128]{1,0:T(8,128)(2,1)S(1)} %get-tuple-element.38), channel_id=1, source_target_pairs={{0,4},{4,0},{8,12},{12,8},{16,20},{20,16},{24,28},{28,24},{1,5},{5... | collective-permute-start | bytes 307208 | tf_op jit(solution)/shard_map/ppermute | solution.py:556
  10.0 5.9 %collective-permute-start.2 = (bf16[256,128]{1,0:T(8,128)(2,1)S(1)}, bf16[256,128]{1,0:T(8,128)(2,1)S(1)}, u32[]{:S(2)}, u32[]{:S(2)}) collective-permute-start(bf16[256,128]{1,0:T(8,128)(2,1)S(1)} %get-tuple-element.42), channel_id=1, source_target_pairs={{0,3},{1,2},{2,1},{3,0},{4,7},{5,6},{6,5},{7,4},{8,11},{9,10},{10,... | collective-permute-start | bytes 196616 | tf_op jit(solution)/shard_map/ppermute | solution.py:580
  13.5 4.3 %collective-permute-start.3 = (bf16[256,128]{1,0:T(8,128)(2,1)S(1)}, bf16[256,128]{1,0:T(8,128)(2,1)S(1)}, u32[]{:S(2)}, u32[]{:S(2)}) collective-permute-start(bf16[256,128]{1,0:T(8,128)(2,1)S(1)} %get-tuple-element.43), channel_id=1, source_target_pairs={{0,1},{1,0},{2,3},{3,2},{4,5},{5,4},{6,7},{7,6},{8,9},{9,8},{10,11... | collective-permute-start | bytes 196616 | tf_op jit(solution)/shard_map/ppermute | solution.py:581

commit v9 on v8

--- a/solution.py
+++ b/solution.py
@@ -424,10 +424,16 @@
             sampled_ref[c : c + 1, lanes] = parts[c]
 
 
+def unfolded(value, rows, groups):
+    folded = value[groups * rows :]
+    return jnp.concatenate(
+        [rolled(folded, -row)[: min(SPAN, rows - row)] for row in range(0, rows, SPAN)], axis=0
+    )
+
+
 def finish_kernel(
     shape, chunk, parity_ref, quarter_ref, value_ref, weight_ref, inner_ref, rim_ref, part_ref,
-    far_y, near_y, next_ref, sampled_ref,
-    moved_ref, carried_ref, sweep_ref, before_ref, after_ref, round_ref,
+    far_y, near_y, next_ref, sampled_ref, moved_ref, carried_ref, sweep_ref, round_ref,
 ):
     cells_x, cells_y, _, _ = shape
     items = rim_ref.shape[0]
@@ -436,31 +442,27 @@
     slots = quarter_ref.shape[1]
     wide_x = cells_x + SPAN
     rows = cells_x + 2 * PAD
-    lane = lane_index(ROWS)
-    before_ref[...], after_ref[...] = ordered(parity_ref[1:2], near_y, far_y)
+    lane = lane_index(rows)
+    befores, afters = ordered(parity_ref[1:2], near_y, far_y)
     turned = HALF + MARGIN + REACH
     high_halo = (lane >= turned) & (lane < turned + HALO * items)
     both = (lane + MARGIN) % HALF < SPAN
     outer = ((lane >= LANES - REACH) & (lane < LANES - MARGIN)) | (
         (lane >= HALF + MARGIN) & (lane < HALF + REACH)
     )
-    windows = [(lane + (LANES + MARGIN - SPAN * slot)) % LANES < SPAN for slot in range(EDGE_PER)]
-    for row in range(0, rows, ROWS):
-        start = groups * rows + row % SPAN
-        fold = SPAN * (row // SPAN)
-        low = rolled(before_ref[start : start + ROWS], -fold)
-        high = rolled(after_ref[start : start + ROWS], turned - fold)
-        halo = jnp.where(high_halo, high, low)
-        for group in range(groups):
-            start = group * rows + row
-            before = before_ref[start : start + ROWS]
-            after = rolled(after_ref[start : start + ROWS], HALF)
-            for k in range(group * EDGE_PER, min((group + 1) * EDGE_PER, items)):
-                slot = k % EDGE_PER
-                main = rolled(jnp.where(windows[slot], before, after), -SPAN * slot)
-                value = rim_ref[k, row : row + ROWS] + jnp.where(both, main, 0.0)
-                value = jnp.where(outer, rolled(halo, -REACH - HALO * k), value)
-                moved_ref[k, ROWS + row : 2 * ROWS + row] = value
+    halo = jnp.where(
+        high_halo, rolled(unfolded(afters, rows, groups), turned), unfolded(befores, rows, groups)
+    )
+    for group in range(groups):
+        before = befores[group * rows : (group + 1) * rows]
+        after = rolled(afters[group * rows : (group + 1) * rows], HALF)
+        for k in range(group * EDGE_PER, min((group + 1) * EDGE_PER, items)):
+            slot = k % EDGE_PER
+            window = (lane + (LANES + MARGIN - SPAN * slot)) % LANES < SPAN
+            main = rolled(jnp.where(window, before, after), -SPAN * slot)
+            value = rim_ref[k] + jnp.where(both, main, 0.0)
+            value = jnp.where(outer, rolled(halo, -REACH - HALO * k), value)
+            moved_ref[k, ROWS : ROWS + rows] = value
 
     first_steps(moved_ref, carried_ref, sweep_ref, levels, comps, rows)
     size = 2 * ROWS
@@ -598,7 +600,6 @@
         ),
         name="inner",
     )(parity, quarter, value, inner_weight, grid, far_x, near_x)
-    strip_y = pltpu.VMEM(edge_y.shape, jnp.float32)
     return pl.pallas_call(
         functools.partial(finish_kernel, shape, chunk),
         out_shape=(
@@ -607,7 +608,7 @@
         ),
         in_specs=whole(9),
         out_specs=tuple(whole(2)),
-        scratch_shapes=[field, field, field, strip_y, strip_y, rounded],
+        scratch_shapes=[field, field, field, rounded],
         compiler_params=params,
         name="finish",
     )(parity, quarter, value, rim_weight, inner, rim, part, far_y, near_y)

time: 22 us -> 20 us (0.909)
  Pallas kernels: 8.84 us -> 6.87 us
    pallas_call x1, Pallas kernels: 4.04 us -> 2.07 us  [body(): pl.pallas_call(functools.partial(finish_kernel, shape, chunk), out_shape=...]
  transfers between devices with their start and end apart: 4 -> 4, of which waited for: 3 -> 3; matrix products, arithmetic and copies ran while one was open for 0% -> 0% of each run, Pallas kernels for 12% -> 13%
where the time goes in v9:
time: 20 us; the launch traced here: 19.9 us
  starting transfers between devices  8.72 us (44%)
  Pallas kernels  6.87 us (34%)
  waiting for transfers between devices  3.61 us (18%)
  between operations  0.67 us (3%)
    ppermute x1, starting transfers between devices, body(): far_x = lax.ppermute(far, 'gx', far_pairs)  4.55 us
    ppermute x1, starting transfers between devices, body(): far_y = lax.ppermute(far, 'gy', far_pairs)  3.57 us
    pallas_call x1, Pallas kernels, body(): pl.pallas_call(functools.partial(finish_kernel, shape, chunk), out_shape=...  2.07 us
    ppermute x1, waiting for transfers between devices, body(): near_y = lax.ppermute(near, 'gy', near_pairs)  1.98 us
    pallas_call x1, Pallas kernels, body(): pl.pallas_call(functools.partial(far_kernel, shape, chunk), out_shape=(ja...  1.63 us
    pallas_call x1, Pallas kernels, body(): pl.pallas_call(functools.partial(inner_kernel, shape, chunk, levels), out...  1.41 us
    ppermute x1, waiting for transfers between devices, body(): far_x = lax.ppermute(far, 'gx', far_pairs)  1.3 us
    pallas_call x1, Pallas kernels, body(): pl.pallas_call(functools.partial(near_kernel, shape, chunk), out_shape=(j...  0.79 us
  transfers between devices with their start and end apart: 4, of which 3 were waited for; matrix products, arithmetic and copies ran while one was open for 0% of the time, Pallas kernels for 13%

profile of v9, /device:TPU:0, one launch (start us, length us, event | category | flops | bytes accessed | tf_op | source)
XLA Modules:
  0.0 19.9 jit_solution(17630041638767863569)
XLA Ops:
  0.6 1.6 %spread_far.1 = (f32[8,48,256]{2,1,0:T(8,128)S(1)}, bf16[400,128]{1,0:T(8,128)(2,1)S(1)}, bf16[8,16,2048]{2,1,0:T(8,128)(2,1)S(1)}, bf16[256,2048]{1,0:T(8,128)(...) custom-call(s32[48]{0:T(128)} %fish_hbm.1, ...), custom_call_target="tpu_custom_call" | custom-call | tf_op jit(solution)/shard_map/spread_far/pallas_call | solution.py:520
  2.3 4.6 %collective-permute-start = (bf16[400,128]{1,0:T(8,128)(2,1)S(1)}, bf16[400,128]{1,0:T(8,128)(2,1)S(1)}, u32[]{:S(2)}, u32[]{:S(2)}) collective-permute-start(bf16[400,128]{1,0:T(8,128)(2,1)S(1)} %get-tuple-element.37), channel_id=1, source_target_pairs={{0,28},{4,8},{8,4},{12,16},{16,12},{20,24},{24,20},{28,0},{1,29},{... | collective-permute-start | bytes 307208 | tf_op jit(solution)/shard_map/ppermute | solution.py:544
  6.8 0.8 %spread_near.1 = (f32[8,96,256]{2,1,0:T(8,128)S(1)}, bf16[400,128]{1,0:T(8,128)(2,1)S(1)}) custom-call(f32[4,2,64,128]{3,2,1,0:T(8,128)S(1)} %get-tuple-element.32.velocity_ref, f32[8,48,256]{2,1,0:T(8,128)S(1)} %get-tuple-element.33.far_half_ref, bf16[8,16,2048]{2,1,0:T(8,128)(2,1)S(1)} %get-tuple-element.34.force_ref, ...), custom_call_target="tpu_custom_call" | custom-call | flops 402653184 | bytes 786432 | tf_op jit(solution)/shard_map/spread_near/pallas_call | solution.py:545
  7.6 0.1 collective-permute-start.1
  7.7 0.4 %weights.1 = (bf16[512,2048]{1,0:T(8,128)(2,1)S(1)}, bf16[512,2048]{1,0:T(8,128)(2,1)S(1)}, s32[2,128]{1,0:T(2,128)S(1)}) custom-call(s32[2,128]{1,0:T(2,128)S(1)} %get-tuple-element.23.parity_ref, s32[8,2048]{1,0:T(8,128)S(1)} %get-tuple-element.24.quarter_ref, f32[8,2048]{1,0:T(8,128)S(1)} %get-tuple-element.25.value_ref, ...), custom_call_target="tpu_custom_call" | custom-call | flops 2097152 | bytes 4194304 | tf_op jit(solution)/shard_map/weights/pallas_call | solution.py:560
  8.1 1.3 %collective-permute-done.far_x = bf16[400,128]{1,0:T(8,128)(2,1)S(1)} collective-permute-done((bf16[400,128]{1,0:T(8,128)(2,1)S(1)}, bf16[400,128]{1,0:T(8,128)(2,1)S(1)}, u32[]{:S(2)}, u32[]{:S(2)}) %collective-permute-start) | collective-permute-done | bytes 102432 | tf_op jit(solution)/shard_map/ppermute | solution.py:544
  9.4 0.0 collective-permute-done.1.near_x
  9.4 0.5 %pack.1 = (bf16[256,128]{1,0:T(8,128)(2,1)S(1)}, bf16[256,128]{1,0:T(8,128)(2,1)S(1)}) custom-call(s32[2,128]{1,0:T(2,128)S(1)} %get-tuple-element.27.parity_ref, f32[8,96,256]{2,1,0:T(8,128)S(1)} %get-tuple-element.36.grid_ref, bf16[400,128]{1,0:T(8,128)(2,1)S(1)} %collective-permute-done.far_x, bf16[400,128]{1,0:T(8,128)(2,1)S(1)} %collective-permute-done.1.near_x), custom_call_target="tpu_custom_call" | custom-call | tf_op jit(solution)/shard_map/pack/pallas_call | solution.py:573
  10.0 3.6 %collective-permute-start.2 = (bf16[256,128]{1,0:T(8,128)(2,1)S(1)}, bf16[256,128]{1,0:T(8,128)(2,1)S(1)}, u32[]{:S(2)}, u32[]{:S(2)}) collective-permute-start(bf16[256,128]{1,0:T(8,128)(2,1)S(1)} %get-tuple-element.42), channel_id=1, source_target_pairs={{0,3},{1,2},{2,1},{3,0},{4,7},{5,6},{6,5},{7,4},{8,11},{9,10},{10,... | collective-permute-start | bytes 196616 | tf_op jit(solution)/shard_map/ppermute | solution.py:582
  13.5 0.5 %collective-permute-start.3 = (bf16[256,128]{1,0:T(8,128)(2,1)S(1)}, bf16[256,128]{1,0:T(8,128)(2,1)S(1)}, u32[]{:S(2)}, u32[]{:S(2)}) collective-permute-start(bf16[256,128]{1,0:T(8,128)(2,1)S(1)} %get-tuple-element.43), channel_id=1, source_target_pairs={{0,1},{1,0},{2,3},{3,2},{4,5},{5,4},{6,7},{7,6},{8,9},{9,8},{10,11... | collective-permute-start | bytes 196616 | tf_op jit(solution)/shard_map/ppermute | solution.py:583
  14.1 1.4 %inner.1 = (f32[8,64,128]{2,1,0:T(8,128)S(1)}, f32[8,112,128]{2,1,0:T(8,128)S(1)}, f32[2,2048]{1,0:T(2,128)S(1)}) custom-call(s32[2,128]{1,0:T(2,128)S(1)} %get-tuple-element.27.parity_ref, s32[8,2048]{1,0:T(8,128)S(1)} %get-tuple-element.28.quarter_ref, f32[8,2048]{1,0:T(8,128)S(1)} %get-tuple-element.29.value_ref, ...), custom_call_target="tpu_custom_call" | custom-call | flops 402653184 | bytes 1835008 | tf_op jit(solution)/shard_map/inner/pallas_call | solution.py:586
  15.5 0.3 %collective-permute-done.2.far_y = bf16[256,128]{1,0:T(8,128)(2,1)S(1)} collective-permute-done((bf16[256,128]{1,0:T(8,128)(2,1)S(1)}, bf16[256,128]{1,0:T(8,128)(2,1)S(1)}, u32[]{:S(2)}, u32[]{:S(2)}) %collective-permute-start.2) | collective-permute-done | bytes 65568 | tf_op jit(solution)/shard_map/ppermute | solution.py:582
  15.8 2.0 %collective-permute-done.3.near_y = bf16[256,128]{1,0:T(8,128)(2,1)S(1)} collective-permute-done((bf16[256,128]{1,0:T(8,128)(2,1)S(1)}, bf16[256,128]{1,0:T(8,128)(2,1)S(1)}, u32[]{:S(2)}, u32[]{:S(2)}) %collective-permute-start.3) | collective-permute-done | bytes 65568 | tf_op jit(solution)/shard_map/ppermute | solution.py:583
  17.8 2.1 %finish.1 = (f32[4,2,64,128]{3,2,1,0:T(8,128)}, f32[2,1,1,2048]{3,2,1,0:T(1,128)}) custom-call(s32[2,128]{1,0:T(2,128)S(1)} %get-tuple-element.27.parity_ref, s32[8,2048]{1,0:T(8,128)S(1)} %get-tuple-element.28.quarter_ref, f32[8,2048]{1,0:T(8,128)S(1)} %get-tuple-element.29.value_ref, bf16[512,2048]{1,0:T(8,128)(2,1)S(1)} %get-tuple-element.30.weight_ref, ...), custom_call_target="tpu_custom_call" | custom-call | tf_op jit(solution)/shard_map/finish/pallas_call | solution.py:603
Async XLA Ops:
  2.3 7.2 %collective-permute-start = (bf16[400,128]{1,0:T(8,128)(2,1)S(1)}, bf16[400,128]{1,0:T(8,128)(2,1)S(1)}, u32[]{:S(2)}, u32[]{:S(2)}) collective-permute-start(bf16[400,128]{1,0:T(8,128)(2,1)S(1)} %get-tuple-element.37), channel_id=1, source_target_pairs={{0,28},{4,8},{8,4},{12,16},{16,12},{20,24},{24,20},{28,0},{1,29},{... | collective-permute-start | bytes 307208 | tf_op jit(solution)/shard_map/ppermute | solution.py:544
  7.6 1.8 %collective-permute-start.1 = (bf16[400,128]{1,0:T(8,128)(2,1)S(1)}, bf16[400,128]{1,0:T(8,128)(2,1)S(1)}, u32[]{:S(2)}, u32[]{:S(2)}) collective-permute-start(bf16[400,128]{1,0:T(8,128)(2,1)S(1)} %get-tuple-element.38), channel_id=1, source_target_pairs={{0,4},{4,0},{8,12},{12,8},{16,20},{20,16},{24,28},{28,24},{1,5},{5... | collective-permute-start | bytes 307208 | tf_op jit(solution)/shard_map/ppermute | solution.py:558
  10.0 5.9 %collective-permute-start.2 = (bf16[256,128]{1,0:T(8,128)(2,1)S(1)}, bf16[256,128]{1,0:T(8,128)(2,1)S(1)}, u32[]{:S(2)}, u32[]{:S(2)}) collective-permute-start(bf16[256,128]{1,0:T(8,128)(2,1)S(1)} %get-tuple-element.42), channel_id=1, source_target_pairs={{0,3},{1,2},{2,1},{3,0},{4,7},{5,6},{6,5},{7,4},{8,11},{9,10},{10,... | collective-permute-start | bytes 196616 | tf_op jit(solution)/shard_map/ppermute | solution.py:582
  13.5 4.3 %collective-permute-start.3 = (bf16[256,128]{1,0:T(8,128)(2,1)S(1)}, bf16[256,128]{1,0:T(8,128)(2,1)S(1)}, u32[]{:S(2)}, u32[]{:S(2)}) collective-permute-start(bf16[256,128]{1,0:T(8,128)(2,1)S(1)} %get-tuple-element.43), channel_id=1, source_target_pairs={{0,1},{1,0},{2,3},{3,2},{4,5},{5,4},{6,7},{7,6},{8,9},{9,8},{10,11... | collective-permute-start | bytes 196616 | tf_op jit(solution)/shard_map/ppermute | solution.py:583

commit v10 on v9

--- a/solution.py
+++ b/solution.py
@@ -56,7 +56,7 @@
 
 def position():
     row, col = lax.axis_index("gx"), lax.axis_index("gy")
-    return row, col, row % 2 == 0, col % 2 == 0
+    return row, col, (row & 1) == 0, (col & 1) == 0
 
 
 def tile_weights(offset, weights):
@@ -446,7 +446,7 @@
     befores, afters = ordered(parity_ref[1:2], near_y, far_y)
     turned = HALF + MARGIN + REACH
     high_halo = (lane >= turned) & (lane < turned + HALO * items)
-    both = (lane + MARGIN) % HALF < SPAN
+    both = ((lane + MARGIN) & (HALF - 1)) < SPAN
     outer = ((lane >= LANES - REACH) & (lane < LANES - MARGIN)) | (
         (lane >= HALF + MARGIN) & (lane < HALF + REACH)
     )
@@ -458,7 +458,7 @@
         after = rolled(afters[group * rows : (group + 1) * rows], HALF)
         for k in range(group * EDGE_PER, min((group + 1) * EDGE_PER, items)):
             slot = k % EDGE_PER
-            window = (lane + (LANES + MARGIN - SPAN * slot)) % LANES < SPAN
+            window = ((lane + (LANES + MARGIN - SPAN * slot)) & (LANES - 1)) < SPAN
             main = rolled(jnp.where(window, before, after), -SPAN * slot)
             value = rim_ref[k] + jnp.where(both, main, 0.0)
             value = jnp.where(outer, rolled(halo, -REACH - HALO * k), value)
@@ -518,7 +518,7 @@
     arrays = (fish_owner, velocity, marker_cell, marker_frac, marker_force)
     far_half, far, force, dense_y, quarter, value, quarter_y, value_y, level, parity, near_velocity = (
         pl.pallas_call(
-        functools.partial(far_kernel, shape, chunk),
+        functools.partial(far_kernel, shape, slots),
         out_shape=(
             jax.ShapeDtypeStruct(half, jnp.float32),
             edge_x,
@@ -543,7 +543,7 @@
     far_pairs, near_pairs = swap_pairs("gx")
     far_x = lax.ppermute(far, "gx", far_pairs)
     grid, near = pl.pallas_call(
-        functools.partial(near_kernel, shape, chunk),
+        functools.partial(near_kernel, shape, slots),
         out_shape=(jax.ShapeDtypeStruct((items, wide_x, width), jnp.float32), edge_x),
         in_specs=whole(5),
         out_specs=tuple(whole(2)),

time: 20 us -> 20 us (level)
  no operation moved by 1% of the time
where the time goes in v10:
time: 20 us; the launch traced here: 19.9 us
  starting transfers between devices  8.72 us (44%)
  Pallas kernels  6.87 us (34%)
  waiting for transfers between devices  3.61 us (18%)
  between operations  0.67 us (3%)
    ppermute x1, starting transfers between devices, body(): far_x = lax.ppermute(far, 'gx', far_pairs)  4.55 us
    ppermute x1, starting transfers between devices, body(): far_y = lax.ppermute(far, 'gy', far_pairs)  3.57 us
    pallas_call x1, Pallas kernels, body(): pl.pallas_call(functools.partial(finish_kernel, shape, chunk), out_shape=...  2.07 us
    ppermute x1, waiting for transfers between devices, body(): near_y = lax.ppermute(near, 'gy', near_pairs)  1.98 us
    pallas_call x1, Pallas kernels, body(): pl.pallas_call(functools.partial(far_kernel, shape, slots), out_shape=(ja...  1.65 us
    pallas_call x1, Pallas kernels, body(): pl.pallas_call(functools.partial(inner_kernel, shape, chunk, levels), out...  1.41 us
    ppermute x1, waiting for transfers between devices, body(): far_x = lax.ppermute(far, 'gx', far_pairs)  1.3 us
    pallas_call x1, Pallas kernels, body(): pl.pallas_call(functools.partial(near_kernel, shape, slots), out_shape=(j...  0.79 us
  transfers between devices with their start and end apart: 4, of which 3 were waited for; matrix products, arithmetic and copies ran while one was open for 0% of the time, Pallas kernels for 13%

profile of v10, /device:TPU:0, one launch (start us, length us, event | category | flops | bytes accessed | tf_op | source)
XLA Modules:
  0.0 19.9 jit_solution(15803438517846749698)
XLA Ops:
  0.6 1.6 %spread_far.1 = (f32[8,48,256]{2,1,0:T(8,128)S(1)}, bf16[400,128]{1,0:T(8,128)(2,1)S(1)}, bf16[8,16,2048]{2,1,0:T(8,128)(2,1)S(1)}, bf16[256,2048]{1,0:T(8,128)(...) custom-call(s32[48]{0:T(128)} %fish_hbm.1, ...), custom_call_target="tpu_custom_call" | custom-call | tf_op jit(solution)/shard_map/spread_far/pallas_call | solution.py:520
  2.3 4.6 %collective-permute-start = (bf16[400,128]{1,0:T(8,128)(2,1)S(1)}, bf16[400,128]{1,0:T(8,128)(2,1)S(1)}, u32[]{:S(2)}, u32[]{:S(2)}) collective-permute-start(bf16[400,128]{1,0:T(8,128)(2,1)S(1)} %get-tuple-element.37), channel_id=1, source_target_pairs={{0,28},{4,8},{8,4},{12,16},{16,12},{20,24},{24,20},{28,0},{1,29},{... | collective-permute-start | bytes 307208 | tf_op jit(solution)/shard_map/ppermute | solution.py:544
  6.8 0.8 %spread_near.1 = (f32[8,96,256]{2,1,0:T(8,128)S(1)}, bf16[400,128]{1,0:T(8,128)(2,1)S(1)}) custom-call(f32[4,2,64,128]{3,2,1,0:T(8,128)S(1)} %get-tuple-element.32.velocity_ref, f32[8,48,256]{2,1,0:T(8,128)S(1)} %get-tuple-element.33.far_half_ref, bf16[8,16,2048]{2,1,0:T(8,128)(2,1)S(1)} %get-tuple-element.34.force_ref, ...), custom_call_target="tpu_custom_call" | custom-call | flops 402653184 | bytes 786432 | tf_op jit(solution)/shard_map/spread_near/pallas_call | solution.py:545
  7.6 0.1 collective-permute-start.1
  7.7 0.4 %weights.1 = (bf16[512,2048]{1,0:T(8,128)(2,1)S(1)}, bf16[512,2048]{1,0:T(8,128)(2,1)S(1)}, s32[2,128]{1,0:T(2,128)S(1)}) custom-call(s32[2,128]{1,0:T(2,128)S(1)} %get-tuple-element.23.parity_ref, s32[8,2048]{1,0:T(8,128)S(1)} %get-tuple-element.24.quarter_ref, f32[8,2048]{1,0:T(8,128)S(1)} %get-tuple-element.25.value_ref, ...), custom_call_target="tpu_custom_call" | custom-call | flops 2097152 | bytes 4194304 | tf_op jit(solution)/shard_map/weights/pallas_call | solution.py:560
  8.1 1.3 %collective-permute-done.far_x = bf16[400,128]{1,0:T(8,128)(2,1)S(1)} collective-permute-done((bf16[400,128]{1,0:T(8,128)(2,1)S(1)}, bf16[400,128]{1,0:T(8,128)(2,1)S(1)}, u32[]{:S(2)}, u32[]{:S(2)}) %collective-permute-start) | collective-permute-done | bytes 102432 | tf_op jit(solution)/shard_map/ppermute | solution.py:544
  9.4 0.0 collective-permute-done.1.near_x
  9.5 0.5 %pack.1 = (bf16[256,128]{1,0:T(8,128)(2,1)S(1)}, bf16[256,128]{1,0:T(8,128)(2,1)S(1)}) custom-call(s32[2,128]{1,0:T(2,128)S(1)} %get-tuple-element.27.parity_ref, f32[8,96,256]{2,1,0:T(8,128)S(1)} %get-tuple-element.36.grid_ref, bf16[400,128]{1,0:T(8,128)(2,1)S(1)} %collective-permute-done.far_x, bf16[400,128]{1,0:T(8,128)(2,1)S(1)} %collective-permute-done.1.near_x), custom_call_target="tpu_custom_call" | custom-call | tf_op jit(solution)/shard_map/pack/pallas_call | solution.py:573
  10.0 3.6 %collective-permute-start.2 = (bf16[256,128]{1,0:T(8,128)(2,1)S(1)}, bf16[256,128]{1,0:T(8,128)(2,1)S(1)}, u32[]{:S(2)}, u32[]{:S(2)}) collective-permute-start(bf16[256,128]{1,0:T(8,128)(2,1)S(1)} %get-tuple-element.42), channel_id=1, source_target_pairs={{0,3},{1,2},{2,1},{3,0},{4,7},{5,6},{6,5},{7,4},{8,11},{9,10},{10,... | collective-permute-start | bytes 196616 | tf_op jit(solution)/shard_map/ppermute | solution.py:582
  13.5 0.5 %collective-permute-start.3 = (bf16[256,128]{1,0:T(8,128)(2,1)S(1)}, bf16[256,128]{1,0:T(8,128)(2,1)S(1)}, u32[]{:S(2)}, u32[]{:S(2)}) collective-permute-start(bf16[256,128]{1,0:T(8,128)(2,1)S(1)} %get-tuple-element.43), channel_id=1, source_target_pairs={{0,1},{1,0},{2,3},{3,2},{4,5},{5,4},{6,7},{7,6},{8,9},{9,8},{10,11... | collective-permute-start | bytes 196616 | tf_op jit(solution)/shard_map/ppermute | solution.py:583
  14.1 1.4 %inner.1 = (f32[8,64,128]{2,1,0:T(8,128)S(1)}, f32[8,112,128]{2,1,0:T(8,128)S(1)}, f32[2,2048]{1,0:T(2,128)S(1)}) custom-call(s32[2,128]{1,0:T(2,128)S(1)} %get-tuple-element.27.parity_ref, s32[8,2048]{1,0:T(8,128)S(1)} %get-tuple-element.28.quarter_ref, f32[8,2048]{1,0:T(8,128)S(1)} %get-tuple-element.29.value_ref, ...), custom_call_target="tpu_custom_call" | custom-call | flops 402653184 | bytes 1835008 | tf_op jit(solution)/shard_map/inner/pallas_call | solution.py:586
  15.5 0.3 %collective-permute-done.2.far_y = bf16[256,128]{1,0:T(8,128)(2,1)S(1)} collective-permute-done((bf16[256,128]{1,0:T(8,128)(2,1)S(1)}, bf16[256,128]{1,0:T(8,128)(2,1)S(1)}, u32[]{:S(2)}, u32[]{:S(2)}) %collective-permute-start.2) | collective-permute-done | bytes 65568 | tf_op jit(solution)/shard_map/ppermute | solution.py:582
  15.8 2.0 %collective-permute-done.3.near_y = bf16[256,128]{1,0:T(8,128)(2,1)S(1)} collective-permute-done((bf16[256,128]{1,0:T(8,128)(2,1)S(1)}, bf16[256,128]{1,0:T(8,128)(2,1)S(1)}, u32[]{:S(2)}, u32[]{:S(2)}) %collective-permute-start.3) | collective-permute-done | bytes 65568 | tf_op jit(solution)/shard_map/ppermute | solution.py:583
  17.8 2.1 %finish.1 = (f32[4,2,64,128]{3,2,1,0:T(8,128)}, f32[2,1,1,2048]{3,2,1,0:T(1,128)}) custom-call(s32[2,128]{1,0:T(2,128)S(1)} %get-tuple-element.27.parity_ref, s32[8,2048]{1,0:T(8,128)S(1)} %get-tuple-element.28.quarter_ref, f32[8,2048]{1,0:T(8,128)S(1)} %get-tuple-element.29.value_ref, bf16[512,2048]{1,0:T(8,128)(2,1)S(1)} %get-tuple-element.30.weight_ref, ...), custom_call_target="tpu_custom_call" | custom-call | tf_op jit(solution)/shard_map/finish/pallas_call | solution.py:603
Async XLA Ops:
  2.3 7.2 %collective-permute-start = (bf16[400,128]{1,0:T(8,128)(2,1)S(1)}, bf16[400,128]{1,0:T(8,128)(2,1)S(1)}, u32[]{:S(2)}, u32[]{:S(2)}) collective-permute-start(bf16[400,128]{1,0:T(8,128)(2,1)S(1)} %get-tuple-element.37), channel_id=1, source_target_pairs={{0,28},{4,8},{8,4},{12,16},{16,12},{20,24},{24,20},{28,0},{1,29},{... | collective-permute-start | bytes 307208 | tf_op jit(solution)/shard_map/ppermute | solution.py:544
  7.6 1.8 %collective-permute-start.1 = (bf16[400,128]{1,0:T(8,128)(2,1)S(1)}, bf16[400,128]{1,0:T(8,128)(2,1)S(1)}, u32[]{:S(2)}, u32[]{:S(2)}) collective-permute-start(bf16[400,128]{1,0:T(8,128)(2,1)S(1)} %get-tuple-element.38), channel_id=1, source_target_pairs={{0,4},{4,0},{8,12},{12,8},{16,20},{20,16},{24,28},{28,24},{1,5},{5... | collective-permute-start | bytes 307208 | tf_op jit(solution)/shard_map/ppermute | solution.py:558
  10.0 5.9 %collective-permute-start.2 = (bf16[256,128]{1,0:T(8,128)(2,1)S(1)}, bf16[256,128]{1,0:T(8,128)(2,1)S(1)}, u32[]{:S(2)}, u32[]{:S(2)}) collective-permute-start(bf16[256,128]{1,0:T(8,128)(2,1)S(1)} %get-tuple-element.42), channel_id=1, source_target_pairs={{0,3},{1,2},{2,1},{3,0},{4,7},{5,6},{6,5},{7,4},{8,11},{9,10},{10,... | collective-permute-start | bytes 196616 | tf_op jit(solution)/shard_map/ppermute | solution.py:582
  13.5 4.3 %collective-permute-start.3 = (bf16[256,128]{1,0:T(8,128)(2,1)S(1)}, bf16[256,128]{1,0:T(8,128)(2,1)S(1)}, u32[]{:S(2)}, u32[]{:S(2)}) collective-permute-start(bf16[256,128]{1,0:T(8,128)(2,1)S(1)} %get-tuple-element.43), channel_id=1, source_target_pairs={{0,1},{1,0},{2,3},{3,2},{4,5},{5,4},{6,7},{7,6},{8,9},{9,8},{10,11... | collective-permute-start | bytes 196616 | tf_op jit(solution)/shard_map/ppermute | solution.py:583

commit v11 on v10

--- a/solution.py
+++ b/solution.py
@@ -256,10 +256,10 @@
     groups = -(-items // EDGE_PER)
     rows = cells_x + 2 * PAD
     lane = lane_index(rows)
-    even = jnp.broadcast_to(parity_ref[1:2], (rows, LANES)) != 0
     up_halo = (lane >= LANES - REACH) & (lane < LANES - MARGIN)
     down_halo = (lane >= MARGIN) & (lane < REACH)
     halos, ups, downs = None, None, None
+    packed = [[], []]
     for k, inner, edge in extended_rows(parity_ref[0:1], grid_ref, near_x, far_x, cells_y):
         slot = k % EDGE_PER
         up = rolled(jnp.where(lane >= LANES - MARGIN, inner, edge), SPAN * slot)
@@ -269,10 +269,11 @@
         downs = downs + down if slot else down
         halos = halos + halo if k else halo
         if slot == EDGE_PER - 1 or k == items - 1:
-            place = slice(k // EDGE_PER * rows, (k // EDGE_PER + 1) * rows)
-            near_ref[place] = jnp.where(even, ups, downs).astype(jnp.bfloat16)
-            far_ref[place] = jnp.where(even, downs, ups).astype(jnp.bfloat16)
-    used = lane < HALO * items
+            packed[0].append(squeezed(ups))
+            packed[1].append(squeezed(downs))
+    halos = squeezed(halos)
+    rows = halos.shape[0]
+    used = lane_index(rows) < HALO * items
     ups = jnp.where(used, halos, 0.0)
     downs = jnp.where(used, rolled(halos, -MARGIN - REACH), 0.0)
     folded = None
@@ -283,9 +284,21 @@
             parts = [jnp.concatenate([p, jnp.zeros((SPAN - size, LANES), p.dtype)], 0) for p in parts]
         part = rolled(jnp.concatenate(parts, axis=0), row)
         folded = folded + part if row else part
-    up, down, even = folded[:SPAN], folded[SPAN:], even[:SPAN]
-    near_ref[groups * rows :] = jnp.where(even, up, down).astype(jnp.bfloat16)
-    far_ref[groups * rows :] = jnp.where(even, down, up).astype(jnp.bfloat16)
+    up = jnp.concatenate(packed[0] + [folded[:SPAN]], axis=0)
+    down = jnp.concatenate(packed[1] + [folded[SPAN:]], axis=0)
+    even = jnp.broadcast_to(parity_ref[1:2], up.shape) != 0
+    near_ref[...] = jnp.where(even, up, down).astype(jnp.bfloat16)
+    far_ref[...] = jnp.where(even, down, up).astype(jnp.bfloat16)
+
+
+def squeezed(value):
+    row = lax.broadcasted_iota(jnp.int32, (ROWS, LANES), 0)
+    shared = jnp.where(row >= PAD - REACH, value[:ROWS], value[-ROWS:])
+    return jnp.concatenate([shared, value[ROWS:-ROWS]], axis=0)
+
+
+def expanded(value):
+    return jnp.concatenate([value, value[:ROWS]], axis=0)
 
 
 def around(ref, k, start, size):
@@ -424,16 +437,18 @@
             sampled_ref[c : c + 1, lanes] = parts[c]
 
 
-def unfolded(value, rows, groups):
-    folded = value[groups * rows :]
-    return jnp.concatenate(
-        [rolled(folded, -row)[: min(SPAN, rows - row)] for row in range(0, rows, SPAN)], axis=0
+def unfolded(folded, rows):
+    return expanded(
+        jnp.concatenate(
+            [rolled(folded, -row)[: min(SPAN, rows - row)] for row in range(0, rows, SPAN)], axis=0
+        )
     )
 
 
 def finish_kernel(
     shape, chunk, parity_ref, quarter_ref, value_ref, weight_ref, inner_ref, rim_ref, part_ref,
-    far_y, near_y, next_ref, sampled_ref, moved_ref, carried_ref, sweep_ref, round_ref,
+    far_y, near_y, next_hbm, sampled_ref,
+    moved_ref, carried_ref, sweep_ref, round_ref, next_ref, sem,
 ):
     cells_x, cells_y, _, _ = shape
     items = rim_ref.shape[0]
@@ -450,12 +465,15 @@
     outer = ((lane >= LANES - REACH) & (lane < LANES - MARGIN)) | (
         (lane >= HALF + MARGIN) & (lane < HALF + REACH)
     )
+    size = rows - ROWS
     halo = jnp.where(
-        high_halo, rolled(unfolded(afters, rows, groups), turned), unfolded(befores, rows, groups)
+        high_halo,
+        rolled(unfolded(afters[groups * size :], size), turned),
+        unfolded(befores[groups * size :], size),
     )
     for group in range(groups):
-        before = befores[group * rows : (group + 1) * rows]
-        after = rolled(afters[group * rows : (group + 1) * rows], HALF)
+        before = expanded(befores[group * size : (group + 1) * size])
+        after = expanded(rolled(afters[group * size : (group + 1) * size], HALF))
         for k in range(group * EDGE_PER, min((group + 1) * EDGE_PER, items)):
             slot = k % EDGE_PER
             window = ((lane + (LANES + MARGIN - SPAN * slot)) & (LANES - 1)) < SPAN
@@ -482,12 +500,15 @@
             inner = inner_ref[k, place]
             inner = jnp.where(lane < REACH, low, jnp.where(lane >= LANES - REACH, high, inner))
             next_ref[k // comps, k % comps, place] = inner
+    copy = pltpu.make_async_copy(next_ref, next_hbm, sem)
+    copy.start()
 
     for first in range(0, slots, chunk):
         lanes = slice(first, first + chunk)
         parts = sampled_part(round_ref, weight_ref, quarter_ref, value_ref, lanes, comps)
         for c in range(comps):
             sampled_ref[c, 0, :, lanes] = part_ref[c : c + 1, lanes] + parts[c]
+    copy.wait()
 
 
 def whole(count):
@@ -569,7 +590,7 @@
         ),
         name="weights",
     )(parity, quarter_y, value_y, level)
-    edge_y = jax.ShapeDtypeStruct((groups * rows + SPAN, LANES), jnp.bfloat16)
+    edge_y = jax.ShapeDtypeStruct((groups * (rows - ROWS) + SPAN, LANES), jnp.bfloat16)
     far, near = pl.pallas_call(
         functools.partial(pack_kernel, shape),
         out_shape=(edge_y, edge_y),
@@ -607,8 +628,9 @@
             jax.ShapeDtypeStruct((comps, 1, 1, slots), jnp.float32),
         ),
         in_specs=whole(9),
-        out_specs=tuple(whole(2)),
-        scratch_shapes=[field, field, field, rounded],
+        out_specs=(pl.BlockSpec(memory_space=pltpu.HBM), whole(1)[0]),
+        scratch_shapes=[field, field, field, rounded, pltpu.VMEM(velocity.shape, velocity.dtype)]
+        + [pltpu.SemaphoreType.DMA],
         compiler_params=params,
         name="finish",
     )(parity, quarter, value, rim_weight, inner, rim, part, far_y, near_y)

time: 20 us -> 20.5 us (1.025)
  Pallas kernels: 6.87 us -> 7.34 us
    pallas_call x1, Pallas kernels: 2.07 us -> 2.54 us  [body(): pl.pallas_call(functools.partial(finish_kernel, shape, chunk), out_shape=...]
where the time goes in v11:
time: 20.5 us; the launch traced here: 20.3 us
  starting transfers between devices  8.72 us (43%)
  Pallas kernels  7.34 us (36%)
  waiting for transfers between devices  3.57 us (17%)
  between operations  0.67 us (3%)
    ppermute x1, starting transfers between devices, body(): far_x = lax.ppermute(far, 'gx', far_pairs)  4.55 us
    ppermute x1, starting transfers between devices, body(): far_y = lax.ppermute(far, 'gy', far_pairs)  3.57 us
    pallas_call x1, Pallas kernels, body(): pl.pallas_call(functools.partial(finish_kernel, shape, chunk), out_shape=...  2.54 us
    ppermute x1, waiting for transfers between devices, body(): near_y = lax.ppermute(near, 'gy', near_pairs)  2.02 us
    pallas_call x1, Pallas kernels, body(): pl.pallas_call(functools.partial(far_kernel, shape, slots), out_shape=(ja...  1.65 us
    pallas_call x1, Pallas kernels, body(): pl.pallas_call(functools.partial(inner_kernel, shape, chunk, levels), out...  1.41 us
    ppermute x1, waiting for transfers between devices, body(): far_x = lax.ppermute(far, 'gx', far_pairs)  1.3 us
    pallas_call x1, Pallas kernels, body(): pl.pallas_call(functools.partial(near_kernel, shape, slots), out_shape=(j...  0.79 us
  transfers between devices with their start and end apart: 4, of which 3 were waited for; matrix products, arithmetic and copies ran while one was open for 0% of the time, Pallas kernels for 13%

profile of v11, /device:TPU:0, one launch (start us, length us, event | category | flops | bytes accessed | tf_op | source)
XLA Modules:
  0.0 20.3 jit_solution(13568876794078607965)
XLA Ops:
  0.6 1.6 %spread_far.1 = (f32[8,48,256]{2,1,0:T(8,128)S(1)}, bf16[400,128]{1,0:T(8,128)(2,1)S(1)}, bf16[8,16,2048]{2,1,0:T(8,128)(2,1)S(1)}, bf16[256,2048]{1,0:T(8,128)(...) custom-call(s32[48]{0:T(128)} %fish_hbm.1, ...), custom_call_target="tpu_custom_call" | custom-call | tf_op jit(solution)/shard_map/spread_far/pallas_call | solution.py:541
  2.3 4.6 %collective-permute-start = (bf16[400,128]{1,0:T(8,128)(2,1)S(1)}, bf16[400,128]{1,0:T(8,128)(2,1)S(1)}, u32[]{:S(2)}, u32[]{:S(2)}) collective-permute-start(bf16[400,128]{1,0:T(8,128)(2,1)S(1)} %get-tuple-element.37), channel_id=1, source_target_pairs={{0,28},{4,8},{8,4},{12,16},{16,12},{20,24},{24,20},{28,0},{1,29},{... | collective-permute-start | bytes 307208 | tf_op jit(solution)/shard_map/ppermute | solution.py:565
  6.8 0.8 %spread_near.1 = (f32[8,96,256]{2,1,0:T(8,128)S(1)}, bf16[400,128]{1,0:T(8,128)(2,1)S(1)}) custom-call(f32[4,2,64,128]{3,2,1,0:T(8,128)S(1)} %get-tuple-element.32.velocity_ref, f32[8,48,256]{2,1,0:T(8,128)S(1)} %get-tuple-element.33.far_half_ref, bf16[8,16,2048]{2,1,0:T(8,128)(2,1)S(1)} %get-tuple-element.34.force_ref, ...), custom_call_target="tpu_custom_call" | custom-call | flops 402653184 | bytes 786432 | tf_op jit(solution)/shard_map/spread_near/pallas_call | solution.py:566
  7.6 0.1 collective-permute-start.1
  7.7 0.4 %weights.1 = (bf16[512,2048]{1,0:T(8,128)(2,1)S(1)}, bf16[512,2048]{1,0:T(8,128)(2,1)S(1)}, s32[2,128]{1,0:T(2,128)S(1)}) custom-call(s32[2,128]{1,0:T(2,128)S(1)} %get-tuple-element.23.parity_ref, s32[8,2048]{1,0:T(8,128)S(1)} %get-tuple-element.24.quarter_ref, f32[8,2048]{1,0:T(8,128)S(1)} %get-tuple-element.25.value_ref, ...), custom_call_target="tpu_custom_call" | custom-call | flops 2097152 | bytes 4194304 | tf_op jit(solution)/shard_map/weights/pallas_call | solution.py:581
  8.1 1.3 %collective-permute-done.far_x = bf16[400,128]{1,0:T(8,128)(2,1)S(1)} collective-permute-done((bf16[400,128]{1,0:T(8,128)(2,1)S(1)}, bf16[400,128]{1,0:T(8,128)(2,1)S(1)}, u32[]{:S(2)}, u32[]{:S(2)}) %collective-permute-start) | collective-permute-done | bytes 102432 | tf_op jit(solution)/shard_map/ppermute | solution.py:565
  9.4 0.0 collective-permute-done.1.near_x
  9.5 0.5 %pack.1 = (bf16[240,128]{1,0:T(8,128)(2,1)S(1)}, bf16[240,128]{1,0:T(8,128)(2,1)S(1)}) custom-call(s32[2,128]{1,0:T(2,128)S(1)} %get-tuple-element.27.parity_ref, f32[8,96,256]{2,1,0:T(8,128)S(1)} %get-tuple-element.36.grid_ref, bf16[400,128]{1,0:T(8,128)(2,1)S(1)} %collective-permute-done.far_x, bf16[400,128]{1,0:T(8,128)(2,1)S(1)} %collective-permute-done.1.near_x), custom_call_target="tpu_custom_call" | custom-call | tf_op jit(solution)/shard_map/pack/pallas_call | solution.py:594
  10.0 3.6 %collective-permute-start.2 = (bf16[240,128]{1,0:T(8,128)(2,1)S(1)}, bf16[240,128]{1,0:T(8,128)(2,1)S(1)}, u32[]{:S(2)}, u32[]{:S(2)}) collective-permute-start(bf16[240,128]{1,0:T(8,128)(2,1)S(1)} %get-tuple-element.42), channel_id=1, source_target_pairs={{0,3},{1,2},{2,1},{3,0},{4,7},{5,6},{6,5},{7,4},{8,11},{9,10},{10,... | collective-permute-start | bytes 184328 | tf_op jit(solution)/shard_map/ppermute | solution.py:603
  13.5 0.5 %collective-permute-start.3 = (bf16[240,128]{1,0:T(8,128)(2,1)S(1)}, bf16[240,128]{1,0:T(8,128)(2,1)S(1)}, u32[]{:S(2)}, u32[]{:S(2)}) collective-permute-start(bf16[240,128]{1,0:T(8,128)(2,1)S(1)} %get-tuple-element.43), channel_id=1, source_target_pairs={{0,1},{1,0},{2,3},{3,2},{4,5},{5,4},{6,7},{7,6},{8,9},{9,8},{10,11... | collective-permute-start | bytes 184328 | tf_op jit(solution)/shard_map/ppermute | solution.py:604
  14.1 1.4 %inner.1 = (f32[8,64,128]{2,1,0:T(8,128)S(1)}, f32[8,112,128]{2,1,0:T(8,128)S(1)}, f32[2,2048]{1,0:T(2,128)S(1)}) custom-call(s32[2,128]{1,0:T(2,128)S(1)} %get-tuple-element.27.parity_ref, s32[8,2048]{1,0:T(8,128)S(1)} %get-tuple-element.28.quarter_ref, f32[8,2048]{1,0:T(8,128)S(1)} %get-tuple-element.29.value_ref, ...), custom_call_target="tpu_custom_call" | custom-call | flops 402653184 | bytes 1835008 | tf_op jit(solution)/shard_map/inner/pallas_call | solution.py:607
  15.5 0.2 %collective-permute-done.2.far_y = bf16[240,128]{1,0:T(8,128)(2,1)S(1)} collective-permute-done((bf16[240,128]{1,0:T(8,128)(2,1)S(1)}, bf16[240,128]{1,0:T(8,128)(2,1)S(1)}, u32[]{:S(2)}, u32[]{:S(2)}) %collective-permute-start.2) | collective-permute-done | bytes 61472 | tf_op jit(solution)/shard_map/ppermute | solution.py:603
  15.7 2.0 %collective-permute-done.3.near_y = bf16[240,128]{1,0:T(8,128)(2,1)S(1)} collective-permute-done((bf16[240,128]{1,0:T(8,128)(2,1)S(1)}, bf16[240,128]{1,0:T(8,128)(2,1)S(1)}, u32[]{:S(2)}, u32[]{:S(2)}) %collective-permute-start.3) | collective-permute-done | bytes 61472 | tf_op jit(solution)/shard_map/ppermute | solution.py:604
  17.8 2.5 %finish.1 = (f32[4,2,64,128]{3,2,1,0:T(8,128)}, f32[2,1,1,2048]{3,2,1,0:T(1,128)}) custom-call(s32[2,128]{1,0:T(2,128)S(1)} %get-tuple-element.27.parity_ref, s32[8,2048]{1,0:T(8,128)S(1)} %get-tuple-element.28.quarter_ref, f32[8,2048]{1,0:T(8,128)S(1)} %get-tuple-element.29.value_ref, bf16[512,2048]{1,0:T(8,128)(2,1)S(1)} %get-tuple-element.30.weight_ref, ...), custom_call_target="tpu_custom_call" | custom-call | tf_op jit(solution)/shard_map/finish/pallas_call | solution.py:624
Async XLA Ops:
  2.3 7.2 %collective-permute-start = (bf16[400,128]{1,0:T(8,128)(2,1)S(1)}, bf16[400,128]{1,0:T(8,128)(2,1)S(1)}, u32[]{:S(2)}, u32[]{:S(2)}) collective-permute-start(bf16[400,128]{1,0:T(8,128)(2,1)S(1)} %get-tuple-element.37), channel_id=1, source_target_pairs={{0,28},{4,8},{8,4},{12,16},{16,12},{20,24},{24,20},{28,0},{1,29},{... | collective-permute-start | bytes 307208 | tf_op jit(solution)/shard_map/ppermute | solution.py:565
  7.6 1.8 %collective-permute-start.1 = (bf16[400,128]{1,0:T(8,128)(2,1)S(1)}, bf16[400,128]{1,0:T(8,128)(2,1)S(1)}, u32[]{:S(2)}, u32[]{:S(2)}) collective-permute-start(bf16[400,128]{1,0:T(8,128)(2,1)S(1)} %get-tuple-element.38), channel_id=1, source_target_pairs={{0,4},{4,0},{8,12},{12,8},{16,20},{20,16},{24,28},{28,24},{1,5},{5... | collective-permute-start | bytes 307208 | tf_op jit(solution)/shard_map/ppermute | solution.py:579
  10.0 5.8 %collective-permute-start.2 = (bf16[240,128]{1,0:T(8,128)(2,1)S(1)}, bf16[240,128]{1,0:T(8,128)(2,1)S(1)}, u32[]{:S(2)}, u32[]{:S(2)}) collective-permute-start(bf16[240,128]{1,0:T(8,128)(2,1)S(1)} %get-tuple-element.42), channel_id=1, source_target_pairs={{0,3},{1,2},{2,1},{3,0},{4,7},{5,6},{6,5},{7,4},{8,11},{9,10},{10,... | collective-permute-start | bytes 184328 | tf_op jit(solution)/shard_map/ppermute | solution.py:603
  13.5 4.2 %collective-permute-start.3 = (bf16[240,128]{1,0:T(8,128)(2,1)S(1)}, bf16[240,128]{1,0:T(8,128)(2,1)S(1)}, u32[]{:S(2)}, u32[]{:S(2)}) collective-permute-start(bf16[240,128]{1,0:T(8,128)(2,1)S(1)} %get-tuple-element.43), channel_id=1, source_target_pairs={{0,1},{1,0},{2,3},{3,2},{4,5},{5,4},{6,7},{7,6},{8,9},{9,8},{10,11... | collective-permute-start | bytes 184328 | tf_op jit(solution)/shard_map/ppermute | solution.py:604

commit v12 on v11

--- a/solution.py
+++ b/solution.py
@@ -302,24 +302,22 @@
 
 
 def around(ref, k, start, size):
-    center = ref[k, start : start + size]
-    back = ref[k, start - 1 : start - 1 + size]
-    fore = ref[k, start + 1 : start + 1 + size]
+    center = ref[k, pl.ds(start, size)]
+    back = ref[k, pl.ds(start - 1, size)]
+    fore = ref[k, pl.ds(start + 1, size)]
     return center, back, fore, rolled(center, 1), rolled(center, -1)
 
 
-def advect(moved_ref, carried_ref, levels, comps, rows):
-    for start in range(ROWS, ROWS + rows, ROWS):
-        for l in range(levels):
-            pieces = [around(moved_ref, l * comps + c, start, ROWS) for c in range(comps)]
-            speed_x, speed_y = COURANT * pieces[0][0], COURANT * pieces[1][0]
-            ahead_x, astern_x = jnp.maximum(speed_x, 0.0), jnp.minimum(speed_x, 0.0)
-            ahead_y, astern_y = jnp.maximum(speed_y, 0.0), jnp.minimum(speed_y, 0.0)
-            for c in range(comps):
-                center, back, fore, below, above = pieces[c]
-                change = ahead_x * (center - back) + astern_x * (fore - center)
-                change = change + ahead_y * (center - below) + astern_y * (above - center)
-                carried_ref[l * comps + c, start : start + ROWS] = center - change
+def tiles(count, body):
+    def step(index, carry):
+        body(index)
+        return carry
+
+    lax.fori_loop(0, count, step, 0)
+
+
+def tile_start(index, size=ROWS):
+    return pl.multiple_of(index * size, size)
 
 
 def sweep(ref, carried_ref, levels, comps, start, size):
@@ -333,17 +331,33 @@
         higher = min(k // comps + 1, levels - 1) * comps + k % comps
         lower = max(k // comps - 1, 0) * comps + k % comps
         summed = results[k] + centers[higher] + centers[lower]
-        source = carried_ref[k, start : start + size]
+        source = carried_ref[k, pl.ds(start, size)]
         results[k] = scale * source + (VISCOUS * scale) * summed
     return results
 
 
 def first_steps(moved_ref, carried_ref, sweep_ref, levels, comps, rows):
-    advect(moved_ref, carried_ref, levels, comps, rows)
-    for start in range(ROWS, ROWS + rows, ROWS):
+    def advect(index):
+        start = ROWS + tile_start(index)
+        for l in range(levels):
+            pieces = [around(moved_ref, l * comps + c, start, ROWS) for c in range(comps)]
+            speed_x, speed_y = COURANT * pieces[0][0], COURANT * pieces[1][0]
+            ahead_x, astern_x = jnp.maximum(speed_x, 0.0), jnp.minimum(speed_x, 0.0)
+            ahead_y, astern_y = jnp.maximum(speed_y, 0.0), jnp.minimum(speed_y, 0.0)
+            for c in range(comps):
+                center, back, fore, below, above = pieces[c]
+                change = ahead_x * (center - back) + astern_x * (fore - center)
+                change = change + ahead_y * (center - below) + astern_y * (above - center)
+                carried_ref[l * comps + c, pl.ds(start, ROWS)] = center - change
+
+    def first_sweep(index):
+        start = ROWS + tile_start(index)
         results = sweep(carried_ref, carried_ref, levels, comps, start, ROWS)
         for k in range(levels * comps):
-            sweep_ref[k, start : start + ROWS] = results[k]
+            sweep_ref[k, pl.ds(start, ROWS)] = results[k]
+
+    tiles(rows // ROWS, advect)
+    tiles(rows // ROWS, first_sweep)
 
 
 RIM = REACH + HALO
@@ -447,8 +461,7 @@
 
 def finish_kernel(
     shape, chunk, parity_ref, quarter_ref, value_ref, weight_ref, inner_ref, rim_ref, part_ref,
-    far_y, near_y, next_hbm, sampled_ref,
-    moved_ref, carried_ref, sweep_ref, round_ref, next_ref, sem,
+    far_y, near_y, next_ref, sampled_ref, moved_ref, carried_ref, sweep_ref, round_ref,
 ):
     cells_x, cells_y, _, _ = shape
     items = rim_ref.shape[0]
@@ -500,15 +513,12 @@
             inner = inner_ref[k, place]
             inner = jnp.where(lane < REACH, low, jnp.where(lane >= LANES - REACH, high, inner))
             next_ref[k // comps, k % comps, place] = inner
-    copy = pltpu.make_async_copy(next_ref, next_hbm, sem)
-    copy.start()
 
     for first in range(0, slots, chunk):
         lanes = slice(first, first + chunk)
         parts = sampled_part(round_ref, weight_ref, quarter_ref, value_ref, lanes, comps)
         for c in range(comps):
             sampled_ref[c, 0, :, lanes] = part_ref[c : c + 1, lanes] + parts[c]
-    copy.wait()
 
 
 def whole(count):
@@ -628,9 +638,8 @@
             jax.ShapeDtypeStruct((comps, 1, 1, slots), jnp.float32),
         ),
         in_specs=whole(9),
-        out_specs=(pl.BlockSpec(memory_space=pltpu.HBM), whole(1)[0]),
-        scratch_shapes=[field, field, field, rounded, pltpu.VMEM(velocity.shape, velocity.dtype)]
-        + [pltpu.SemaphoreType.DMA],
+        out_specs=tuple(whole(2)),
+        scratch_shapes=[field, field, field, rounded],
         compiler_params=params,
         name="finish",
     )(parity, quarter, value, rim_weight, inner, rim, part, far_y, near_y)

time: 20.5 us -> 22.2 us (1.083)
  Pallas kernels: 7.34 us -> 11.1 us
  waiting for transfers between devices: 3.57 us -> 1.47 us
    pallas_call x1, Pallas kernels: 1.41 us -> 3.51 us  [body(): pl.pallas_call(functools.partial(inner_kernel, shape, chunk, levels), out...]
    ppermute x1, waiting for transfers between devices: 2.02 us -> 0.16 us  [body(): near_y = lax.ppermute(near, 'gy', near_pairs)]
    pallas_call x1, Pallas kernels: 2.54 us -> 4.24 us  [body(): pl.pallas_call(functools.partial(finish_kernel, shape, chunk), out_shape=...]
    ppermute x1, waiting for transfers between devices: 0.25 us -> 0.01 us  [body(): far_y = lax.ppermute(far, 'gy', far_pairs)]
  transfers between devices with their start and end apart: 4 -> 4, of which waited for: 3 -> 2; matrix products, arithmetic and copies ran while one was open for 0% -> 0% of each run, Pallas kernels for 13% -> 22%
where the time goes in v12:
time: 22.2 us; the launch traced here: 22 us
  Pallas kernels  11.1 us (50%)
  starting transfers between devices  8.72 us (39%)
  waiting for transfers between devices  1.47 us (7%)
  between operations  0.68 us (3%)
    ppermute x1, starting transfers between devices, body(): far_x = lax.ppermute(far, 'gx', far_pairs)  4.55 us
    pallas_call x1, Pallas kernels, body(): pl.pallas_call(functools.partial(finish_kernel, shape, chunk), out_shape=...  4.24 us
    ppermute x1, starting transfers between devices, body(): far_y = lax.ppermute(far, 'gy', far_pairs)  3.57 us
    pallas_call x1, Pallas kernels, body(): pl.pallas_call(functools.partial(inner_kernel, shape, chunk, levels), out...  3.51 us
    pallas_call x1, Pallas kernels, body(): pl.pallas_call(functools.partial(far_kernel, shape, slots), out_shape=(ja...  1.65 us
    ppermute x1, waiting for transfers between devices, body(): far_x = lax.ppermute(far, 'gx', far_pairs)  1.3 us
    pallas_call x1, Pallas kernels, body(): pl.pallas_call(functools.partial(near_kernel, shape, slots), out_shape=(j...  0.79 us
    ppermute x1, starting transfers between devices, body(): near_y = lax.ppermute(near, 'gy', near_pairs)  0.54 us
  transfers between devices with their start and end apart: 4, of which 2 were waited for; matrix products, arithmetic and copies ran while one was open for 0% of the time, Pallas kernels for 22%

profile of v12, /device:TPU:0, one launch (start us, length us, event | category | flops | bytes accessed | tf_op | source)
XLA Modules:
  0.0 22.0 jit_solution(6178373462445420157)
XLA Ops:
  0.6 1.6 %spread_far.1 = (f32[8,48,256]{2,1,0:T(8,128)S(1)}, bf16[400,128]{1,0:T(8,128)(2,1)S(1)}, bf16[8,16,2048]{2,1,0:T(8,128)(2,1)S(1)}, bf16[256,2048]{1,0:T(8,128)(...) custom-call(s32[48]{0:T(128)} %fish_hbm.1, ...), custom_call_target="tpu_custom_call" | custom-call | tf_op jit(solution)/shard_map/spread_far/pallas_call | solution.py:551
  2.3 4.6 %collective-permute-start = (bf16[400,128]{1,0:T(8,128)(2,1)S(1)}, bf16[400,128]{1,0:T(8,128)(2,1)S(1)}, u32[]{:S(2)}, u32[]{:S(2)}) collective-permute-start(bf16[400,128]{1,0:T(8,128)(2,1)S(1)} %get-tuple-element.37), channel_id=1, source_target_pairs={{0,28},{4,8},{8,4},{12,16},{16,12},{20,24},{24,20},{28,0},{1,29},{... | collective-permute-start | bytes 307208 | tf_op jit(solution)/shard_map/ppermute | solution.py:575
  6.8 0.8 %spread_near.1 = (f32[8,96,256]{2,1,0:T(8,128)S(1)}, bf16[400,128]{1,0:T(8,128)(2,1)S(1)}) custom-call(f32[4,2,64,128]{3,2,1,0:T(8,128)S(1)} %get-tuple-element.32.velocity_ref, f32[8,48,256]{2,1,0:T(8,128)S(1)} %get-tuple-element.33.far_half_ref, bf16[8,16,2048]{2,1,0:T(8,128)(2,1)S(1)} %get-tuple-element.34.force_ref, ...), custom_call_target="tpu_custom_call" | custom-call | flops 402653184 | bytes 786432 | tf_op jit(solution)/shard_map/spread_near/pallas_call | solution.py:576
  7.6 0.1 collective-permute-start.1
  7.7 0.4 %weights.1 = (bf16[512,2048]{1,0:T(8,128)(2,1)S(1)}, bf16[512,2048]{1,0:T(8,128)(2,1)S(1)}, s32[2,128]{1,0:T(2,128)S(1)}) custom-call(s32[2,128]{1,0:T(2,128)S(1)} %get-tuple-element.23.parity_ref, s32[8,2048]{1,0:T(8,128)S(1)} %get-tuple-element.24.quarter_ref, f32[8,2048]{1,0:T(8,128)S(1)} %get-tuple-element.25.value_ref, ...), custom_call_target="tpu_custom_call" | custom-call | flops 2097152 | bytes 4194304 | tf_op jit(solution)/shard_map/weights/pallas_call | solution.py:591
  8.1 1.3 %collective-permute-done.far_x = bf16[400,128]{1,0:T(8,128)(2,1)S(1)} collective-permute-done((bf16[400,128]{1,0:T(8,128)(2,1)S(1)}, bf16[400,128]{1,0:T(8,128)(2,1)S(1)}, u32[]{:S(2)}, u32[]{:S(2)}) %collective-permute-start) | collective-permute-done | bytes 102432 | tf_op jit(solution)/shard_map/ppermute | solution.py:575
  9.4 0.0 collective-permute-done.1.near_x
  9.5 0.5 %pack.1 = (bf16[240,128]{1,0:T(8,128)(2,1)S(1)}, bf16[240,128]{1,0:T(8,128)(2,1)S(1)}) custom-call(s32[2,128]{1,0:T(2,128)S(1)} %get-tuple-element.27.parity_ref, f32[8,96,256]{2,1,0:T(8,128)S(1)} %get-tuple-element.36.grid_ref, bf16[400,128]{1,0:T(8,128)(2,1)S(1)} %collective-permute-done.far_x, bf16[400,128]{1,0:T(8,128)(2,1)S(1)} %collective-permute-done.1.near_x), custom_call_target="tpu_custom_call" | custom-call | tf_op jit(solution)/shard_map/pack/pallas_call | solution.py:604
  10.0 3.6 %collective-permute-start.2 = (bf16[240,128]{1,0:T(8,128)(2,1)S(1)}, bf16[240,128]{1,0:T(8,128)(2,1)S(1)}, u32[]{:S(2)}, u32[]{:S(2)}) collective-permute-start(bf16[240,128]{1,0:T(8,128)(2,1)S(1)} %get-tuple-element.42), channel_id=1, source_target_pairs={{0,3},{1,2},{2,1},{3,0},{4,7},{5,6},{6,5},{7,4},{8,11},{9,10},{10,... | collective-permute-start | bytes 184328 | tf_op jit(solution)/shard_map/ppermute | solution.py:613
  13.5 0.5 %collective-permute-start.3 = (bf16[240,128]{1,0:T(8,128)(2,1)S(1)}, bf16[240,128]{1,0:T(8,128)(2,1)S(1)}, u32[]{:S(2)}, u32[]{:S(2)}) collective-permute-start(bf16[240,128]{1,0:T(8,128)(2,1)S(1)} %get-tuple-element.43), channel_id=1, source_target_pairs={{0,1},{1,0},{2,3},{3,2},{4,5},{5,4},{6,7},{7,6},{8,9},{9,8},{10,11... | collective-permute-start | bytes 184328 | tf_op jit(solution)/shard_map/ppermute | solution.py:614
  14.1 3.5 %inner.1 = (f32[8,64,128]{2,1,0:T(8,128)S(1)}, f32[8,112,128]{2,1,0:T(8,128)S(1)}, f32[2,2048]{1,0:T(2,128)S(1)}) custom-call(s32[2,128]{1,0:T(2,128)S(1)} %get-tuple-element.27.parity_ref, s32[8,2048]{1,0:T(8,128)S(1)} %get-tuple-element.28.quarter_ref, f32[8,2048]{1,0:T(8,128)S(1)} %get-tuple-element.29.value_ref, ...), custom_call_target="tpu_custom_call" | custom-call | flops 402653184 | bytes 1835008 | tf_op jit(solution)/shard_map/inner/pallas_call | solution.py:617
  17.6 0.0 collective-permute-done.2.far_y
  17.6 0.2 collective-permute-done.3.near_y
  17.8 4.2 %finish.1 = (f32[4,2,64,128]{3,2,1,0:T(8,128)}, f32[2,1,1,2048]{3,2,1,0:T(1,128)}) custom-call(s32[2,128]{1,0:T(2,128)S(1)} %get-tuple-element.27.parity_ref, s32[8,2048]{1,0:T(8,128)S(1)} %get-tuple-element.28.quarter_ref, f32[8,2048]{1,0:T(8,128)S(1)} %get-tuple-element.29.value_ref, bf16[512,2048]{1,0:T(8,128)(2,1)S(1)} %get-tuple-element.30.weight_ref, ...), custom_call_target="tpu_custom_call" | custom-call | tf_op jit(solution)/shard_map/finish/pallas_call | solution.py:634
Async XLA Ops:
  2.3 7.2 %collective-permute-start = (bf16[400,128]{1,0:T(8,128)(2,1)S(1)}, bf16[400,128]{1,0:T(8,128)(2,1)S(1)}, u32[]{:S(2)}, u32[]{:S(2)}) collective-permute-start(bf16[400,128]{1,0:T(8,128)(2,1)S(1)} %get-tuple-element.37), channel_id=1, source_target_pairs={{0,28},{4,8},{8,4},{12,16},{16,12},{20,24},{24,20},{28,0},{1,29},{... | collective-permute-start | bytes 307208 | tf_op jit(solution)/shard_map/ppermute | solution.py:575
  7.6 1.8 %collective-permute-start.1 = (bf16[400,128]{1,0:T(8,128)(2,1)S(1)}, bf16[400,128]{1,0:T(8,128)(2,1)S(1)}, u32[]{:S(2)}, u32[]{:S(2)}) collective-permute-start(bf16[400,128]{1,0:T(8,128)(2,1)S(1)} %get-tuple-element.38), channel_id=1, source_target_pairs={{0,4},{4,0},{8,12},{12,8},{16,20},{20,16},{24,28},{28,24},{1,5},{5... | collective-permute-start | bytes 307208 | tf_op jit(solution)/shard_map/ppermute | solution.py:589
  10.0 7.6 %collective-permute-start.2 = (bf16[240,128]{1,0:T(8,128)(2,1)S(1)}, bf16[240,128]{1,0:T(8,128)(2,1)S(1)}, u32[]{:S(2)}, u32[]{:S(2)}) collective-permute-start(bf16[240,128]{1,0:T(8,128)(2,1)S(1)} %get-tuple-element.42), channel_id=1, source_target_pairs={{0,3},{1,2},{2,1},{3,0},{4,7},{5,6},{6,5},{7,4},{8,11},{9,10},{10,... | collective-permute-start | bytes 184328 | tf_op jit(solution)/shard_map/ppermute | solution.py:613
  13.5 4.2 %collective-permute-start.3 = (bf16[240,128]{1,0:T(8,128)(2,1)S(1)}, bf16[240,128]{1,0:T(8,128)(2,1)S(1)}, u32[]{:S(2)}, u32[]{:S(2)}) collective-permute-start(bf16[240,128]{1,0:T(8,128)(2,1)S(1)} %get-tuple-element.43), channel_id=1, source_target_pairs={{0,1},{1,0},{2,3},{3,2},{4,5},{5,4},{6,7},{7,6},{8,9},{9,8},{10,11... | collective-permute-start | bytes 184328 | tf_op jit(solution)/shard_map/ppermute | solution.py:614

commit v13 on v11

--- a/solution.py
+++ b/solution.py
@@ -15,6 +15,7 @@
 COURANT = 0.25
 VISCOUS = 1.5
 ROWS = 8
+STEP = 2 * ROWS
 
 REACH = MARGIN + HALO
 PAD = -(-REACH // ROWS) * ROWS
@@ -309,9 +310,9 @@
 
 
 def advect(moved_ref, carried_ref, levels, comps, rows):
-    for start in range(ROWS, ROWS + rows, ROWS):
+    for start in range(ROWS, ROWS + rows, STEP):
         for l in range(levels):
-            pieces = [around(moved_ref, l * comps + c, start, ROWS) for c in range(comps)]
+            pieces = [around(moved_ref, l * comps + c, start, STEP) for c in range(comps)]
             speed_x, speed_y = COURANT * pieces[0][0], COURANT * pieces[1][0]
             ahead_x, astern_x = jnp.maximum(speed_x, 0.0), jnp.minimum(speed_x, 0.0)
             ahead_y, astern_y = jnp.maximum(speed_y, 0.0), jnp.minimum(speed_y, 0.0)
@@ -319,7 +320,7 @@
                 center, back, fore, below, above = pieces[c]
                 change = ahead_x * (center - back) + astern_x * (fore - center)
                 change = change + ahead_y * (center - below) + astern_y * (above - center)
-                carried_ref[l * comps + c, start : start + ROWS] = center - change
+                carried_ref[l * comps + c, start : start + STEP] = center - change
 
 
 def sweep(ref, carried_ref, levels, comps, start, size):
@@ -340,10 +341,10 @@
 
 def first_steps(moved_ref, carried_ref, sweep_ref, levels, comps, rows):
     advect(moved_ref, carried_ref, levels, comps, rows)
-    for start in range(ROWS, ROWS + rows, ROWS):
-        results = sweep(carried_ref, carried_ref, levels, comps, start, ROWS)
+    for start in range(ROWS, ROWS + rows, STEP):
+        results = sweep(carried_ref, carried_ref, levels, comps, start, STEP)
         for k in range(levels * comps):
-            sweep_ref[k, start : start + ROWS] = results[k]
+            sweep_ref[k, start : start + STEP] = results[k]
 
 
 RIM = REACH + HALO
@@ -447,8 +448,7 @@
 
 def finish_kernel(
     shape, chunk, parity_ref, quarter_ref, value_ref, weight_ref, inner_ref, rim_ref, part_ref,
-    far_y, near_y, next_hbm, sampled_ref,
-    moved_ref, carried_ref, sweep_ref, round_ref, next_ref, sem,
+    far_y, near_y, next_ref, sampled_ref, moved_ref, carried_ref, sweep_ref, round_ref,
 ):
     cells_x, cells_y, _, _ = shape
     items = rim_ref.shape[0]
@@ -500,15 +500,12 @@
             inner = inner_ref[k, place]
             inner = jnp.where(lane < REACH, low, jnp.where(lane >= LANES - REACH, high, inner))
             next_ref[k // comps, k % comps, place] = inner
-    copy = pltpu.make_async_copy(next_ref, next_hbm, sem)
-    copy.start()
 
     for first in range(0, slots, chunk):
         lanes = slice(first, first + chunk)
         parts = sampled_part(round_ref, weight_ref, quarter_ref, value_ref, lanes, comps)
         for c in range(comps):
             sampled_ref[c, 0, :, lanes] = part_ref[c : c + 1, lanes] + parts[c]
-    copy.wait()
 
 
 def whole(count):
@@ -628,9 +625,8 @@
             jax.ShapeDtypeStruct((comps, 1, 1, slots), jnp.float32),
         ),
         in_specs=whole(9),
-        out_specs=(pl.BlockSpec(memory_space=pltpu.HBM), whole(1)[0]),
-        scratch_shapes=[field, field, field, rounded, pltpu.VMEM(velocity.shape, velocity.dtype)]
-        + [pltpu.SemaphoreType.DMA],
+        out_specs=tuple(whole(2)),
+        scratch_shapes=[field, field, field, rounded],
         compiler_params=params,
         name="finish",
     )(parity, quarter, value, rim_weight, inner, rim, part, far_y, near_y)

time: 20.5 us -> 20.1 us (0.980)
  Pallas kernels: 7.34 us -> 6.99 us
    pallas_call x1, Pallas kernels: 2.54 us -> 2.18 us  [body(): pl.pallas_call(functools.partial(finish_kernel, shape, chunk), out_shape=...]
where the time goes in v13:
time: 20.1 us; the launch traced here: 19.9 us
  starting transfers between devices  8.72 us (43%)
  Pallas kernels  6.99 us (35%)
  waiting for transfers between devices  3.56 us (18%)
  between operations  0.67 us (3%)
    ppermute x1, starting transfers between devices, body(): far_x = lax.ppermute(far, 'gx', far_pairs)  4.55 us
    ppermute x1, starting transfers between devices, body(): far_y = lax.ppermute(far, 'gy', far_pairs)  3.57 us
    pallas_call x1, Pallas kernels, body(): pl.pallas_call(functools.partial(finish_kernel, shape, chunk), out_shape=...  2.18 us
    ppermute x1, waiting for transfers between devices, body(): near_y = lax.ppermute(near, 'gy', near_pairs)  2.02 us
    pallas_call x1, Pallas kernels, body(): pl.pallas_call(functools.partial(far_kernel, shape, slots), out_shape=(ja...  1.65 us
    pallas_call x1, Pallas kernels, body(): pl.pallas_call(functools.partial(inner_kernel, shape, chunk, levels), out...  1.42 us
    ppermute x1, waiting for transfers between devices, body(): far_x = lax.ppermute(far, 'gx', far_pairs)  1.3 us
    pallas_call x1, Pallas kernels, body(): pl.pallas_call(functools.partial(near_kernel, shape, slots), out_shape=(j...  0.79 us
  transfers between devices with their start and end apart: 4, of which 3 were waited for; matrix products, arithmetic and copies ran while one was open for 0% of the time, Pallas kernels for 13%

profile of v13, /device:TPU:0, one launch (start us, length us, event | category | flops | bytes accessed | tf_op | source)
XLA Modules:
  0.0 19.9 jit_solution(6966264454701019360)
XLA Ops:
  0.6 1.6 %spread_far.1 = (f32[8,48,256]{2,1,0:T(8,128)S(1)}, bf16[400,128]{1,0:T(8,128)(2,1)S(1)}, bf16[8,16,2048]{2,1,0:T(8,128)(2,1)S(1)}, bf16[256,2048]{1,0:T(8,128)(...) custom-call(s32[48]{0:T(128)} %fish_hbm.1, ...), custom_call_target="tpu_custom_call" | custom-call | tf_op jit(solution)/shard_map/spread_far/pallas_call | solution.py:538
  2.3 4.6 %collective-permute-start = (bf16[400,128]{1,0:T(8,128)(2,1)S(1)}, bf16[400,128]{1,0:T(8,128)(2,1)S(1)}, u32[]{:S(2)}, u32[]{:S(2)}) collective-permute-start(bf16[400,128]{1,0:T(8,128)(2,1)S(1)} %get-tuple-element.37), channel_id=1, source_target_pairs={{0,28},{4,8},{8,4},{12,16},{16,12},{20,24},{24,20},{28,0},{1,29},{... | collective-permute-start | bytes 307208 | tf_op jit(solution)/shard_map/ppermute | solution.py:562
  6.8 0.8 %spread_near.1 = (f32[8,96,256]{2,1,0:T(8,128)S(1)}, bf16[400,128]{1,0:T(8,128)(2,1)S(1)}) custom-call(f32[4,2,64,128]{3,2,1,0:T(8,128)S(1)} %get-tuple-element.32.velocity_ref, f32[8,48,256]{2,1,0:T(8,128)S(1)} %get-tuple-element.33.far_half_ref, bf16[8,16,2048]{2,1,0:T(8,128)(2,1)S(1)} %get-tuple-element.34.force_ref, ...), custom_call_target="tpu_custom_call" | custom-call | flops 402653184 | bytes 786432 | tf_op jit(solution)/shard_map/spread_near/pallas_call | solution.py:563
  7.6 0.1 collective-permute-start.1
  7.7 0.4 %weights.1 = (bf16[512,2048]{1,0:T(8,128)(2,1)S(1)}, bf16[512,2048]{1,0:T(8,128)(2,1)S(1)}, s32[2,128]{1,0:T(2,128)S(1)}) custom-call(s32[2,128]{1,0:T(2,128)S(1)} %get-tuple-element.23.parity_ref, s32[8,2048]{1,0:T(8,128)S(1)} %get-tuple-element.24.quarter_ref, f32[8,2048]{1,0:T(8,128)S(1)} %get-tuple-element.25.value_ref, ...), custom_call_target="tpu_custom_call" | custom-call | flops 2097152 | bytes 4194304 | tf_op jit(solution)/shard_map/weights/pallas_call | solution.py:578
  8.1 1.3 %collective-permute-done.far_x = bf16[400,128]{1,0:T(8,128)(2,1)S(1)} collective-permute-done((bf16[400,128]{1,0:T(8,128)(2,1)S(1)}, bf16[400,128]{1,0:T(8,128)(2,1)S(1)}, u32[]{:S(2)}, u32[]{:S(2)}) %collective-permute-start) | collective-permute-done | bytes 102432 | tf_op jit(solution)/shard_map/ppermute | solution.py:562
  9.4 0.0 collective-permute-done.1.near_x
  9.5 0.5 %pack.1 = (bf16[240,128]{1,0:T(8,128)(2,1)S(1)}, bf16[240,128]{1,0:T(8,128)(2,1)S(1)}) custom-call(s32[2,128]{1,0:T(2,128)S(1)} %get-tuple-element.27.parity_ref, f32[8,96,256]{2,1,0:T(8,128)S(1)} %get-tuple-element.36.grid_ref, bf16[400,128]{1,0:T(8,128)(2,1)S(1)} %collective-permute-done.far_x, bf16[400,128]{1,0:T(8,128)(2,1)S(1)} %collective-permute-done.1.near_x), custom_call_target="tpu_custom_call" | custom-call | tf_op jit(solution)/shard_map/pack/pallas_call | solution.py:591
  10.0 3.6 %collective-permute-start.2 = (bf16[240,128]{1,0:T(8,128)(2,1)S(1)}, bf16[240,128]{1,0:T(8,128)(2,1)S(1)}, u32[]{:S(2)}, u32[]{:S(2)}) collective-permute-start(bf16[240,128]{1,0:T(8,128)(2,1)S(1)} %get-tuple-element.42), channel_id=1, source_target_pairs={{0,3},{1,2},{2,1},{3,0},{4,7},{5,6},{6,5},{7,4},{8,11},{9,10},{10,... | collective-permute-start | bytes 184328 | tf_op jit(solution)/shard_map/ppermute | solution.py:600
  13.5 0.5 %collective-permute-start.3 = (bf16[240,128]{1,0:T(8,128)(2,1)S(1)}, bf16[240,128]{1,0:T(8,128)(2,1)S(1)}, u32[]{:S(2)}, u32[]{:S(2)}) collective-permute-start(bf16[240,128]{1,0:T(8,128)(2,1)S(1)} %get-tuple-element.43), channel_id=1, source_target_pairs={{0,1},{1,0},{2,3},{3,2},{4,5},{5,4},{6,7},{7,6},{8,9},{9,8},{10,11... | collective-permute-start | bytes 184328 | tf_op jit(solution)/shard_map/ppermute | solution.py:601
  14.1 1.4 %inner.1 = (f32[8,64,128]{2,1,0:T(8,128)S(1)}, f32[8,112,128]{2,1,0:T(8,128)S(1)}, f32[2,2048]{1,0:T(2,128)S(1)}) custom-call(s32[2,128]{1,0:T(2,128)S(1)} %get-tuple-element.27.parity_ref, s32[8,2048]{1,0:T(8,128)S(1)} %get-tuple-element.28.quarter_ref, f32[8,2048]{1,0:T(8,128)S(1)} %get-tuple-element.29.value_ref, ...), custom_call_target="tpu_custom_call" | custom-call | flops 402653184 | bytes 1835008 | tf_op jit(solution)/shard_map/inner/pallas_call | solution.py:604
  15.5 0.2 %collective-permute-done.2.far_y = bf16[240,128]{1,0:T(8,128)(2,1)S(1)} collective-permute-done((bf16[240,128]{1,0:T(8,128)(2,1)S(1)}, bf16[240,128]{1,0:T(8,128)(2,1)S(1)}, u32[]{:S(2)}, u32[]{:S(2)}) %collective-permute-start.2) | collective-permute-done | bytes 61472 | tf_op jit(solution)/shard_map/ppermute | solution.py:600
  15.7 2.0 %collective-permute-done.3.near_y = bf16[240,128]{1,0:T(8,128)(2,1)S(1)} collective-permute-done((bf16[240,128]{1,0:T(8,128)(2,1)S(1)}, bf16[240,128]{1,0:T(8,128)(2,1)S(1)}, u32[]{:S(2)}, u32[]{:S(2)}) %collective-permute-start.3) | collective-permute-done | bytes 61472 | tf_op jit(solution)/shard_map/ppermute | solution.py:601
  17.8 2.2 %finish.1 = (f32[4,2,64,128]{3,2,1,0:T(8,128)}, f32[2,1,1,2048]{3,2,1,0:T(1,128)}) custom-call(s32[2,128]{1,0:T(2,128)S(1)} %get-tuple-element.27.parity_ref, s32[8,2048]{1,0:T(8,128)S(1)} %get-tuple-element.28.quarter_ref, f32[8,2048]{1,0:T(8,128)S(1)} %get-tuple-element.29.value_ref, bf16[512,2048]{1,0:T(8,128)(2,1)S(1)} %get-tuple-element.30.weight_ref, ...), custom_call_target="tpu_custom_call" | custom-call | tf_op jit(solution)/shard_map/finish/pallas_call | solution.py:621
Async XLA Ops:
  2.3 7.2 %collective-permute-start = (bf16[400,128]{1,0:T(8,128)(2,1)S(1)}, bf16[400,128]{1,0:T(8,128)(2,1)S(1)}, u32[]{:S(2)}, u32[]{:S(2)}) collective-permute-start(bf16[400,128]{1,0:T(8,128)(2,1)S(1)} %get-tuple-element.37), channel_id=1, source_target_pairs={{0,28},{4,8},{8,4},{12,16},{16,12},{20,24},{24,20},{28,0},{1,29},{... | collective-permute-start | bytes 307208 | tf_op jit(solution)/shard_map/ppermute | solution.py:562
  7.6 1.8 %collective-permute-start.1 = (bf16[400,128]{1,0:T(8,128)(2,1)S(1)}, bf16[400,128]{1,0:T(8,128)(2,1)S(1)}, u32[]{:S(2)}, u32[]{:S(2)}) collective-permute-start(bf16[400,128]{1,0:T(8,128)(2,1)S(1)} %get-tuple-element.38), channel_id=1, source_target_pairs={{0,4},{4,0},{8,12},{12,8},{16,20},{20,16},{24,28},{28,24},{1,5},{5... | collective-permute-start | bytes 307208 | tf_op jit(solution)/shard_map/ppermute | solution.py:576
  10.0 5.8 %collective-permute-start.2 = (bf16[240,128]{1,0:T(8,128)(2,1)S(1)}, bf16[240,128]{1,0:T(8,128)(2,1)S(1)}, u32[]{:S(2)}, u32[]{:S(2)}) collective-permute-start(bf16[240,128]{1,0:T(8,128)(2,1)S(1)} %get-tuple-element.42), channel_id=1, source_target_pairs={{0,3},{1,2},{2,1},{3,0},{4,7},{5,6},{6,5},{7,4},{8,11},{9,10},{10,... | collective-permute-start | bytes 184328 | tf_op jit(solution)/shard_map/ppermute | solution.py:600
  13.5 4.2 %collective-permute-start.3 = (bf16[240,128]{1,0:T(8,128)(2,1)S(1)}, bf16[240,128]{1,0:T(8,128)(2,1)S(1)}, u32[]{:S(2)}, u32[]{:S(2)}) collective-permute-start(bf16[240,128]{1,0:T(8,128)(2,1)S(1)} %get-tuple-element.43), channel_id=1, source_target_pairs={{0,1},{1,0},{2,3},{3,2},{4,5},{5,4},{6,7},{7,6},{8,9},{9,8},{10,11... | collective-permute-start | bytes 184328 | tf_op jit(solution)/shard_map/ppermute | solution.py:601

commit v14 on v13

--- a/solution.py
+++ b/solution.py
@@ -251,7 +251,7 @@
         yield k, inner, edge
 
 
-def pack_kernel(shape, parity_ref, grid_ref, far_x, near_x, far_ref, near_ref):
+def pack_kernel(shape, parity_ref, grid_ref, far_x, near_x, near_ref, far_ref):
     cells_x, cells_y, _, _ = shape
     items = grid_ref.shape[0]
     groups = -(-items // EDGE_PER)
@@ -448,7 +448,7 @@
 
 def finish_kernel(
     shape, chunk, parity_ref, quarter_ref, value_ref, weight_ref, inner_ref, rim_ref, part_ref,
-    far_y, near_y, next_ref, sampled_ref, moved_ref, carried_ref, sweep_ref, round_ref,
+    near_y, far_y, next_ref, sampled_ref, moved_ref, carried_ref, sweep_ref, round_ref,
 ):
     cells_x, cells_y, _, _ = shape
     items = rim_ref.shape[0]
@@ -588,7 +588,7 @@
         name="weights",
     )(parity, quarter_y, value_y, level)
     edge_y = jax.ShapeDtypeStruct((groups * (rows - ROWS) + SPAN, LANES), jnp.bfloat16)
-    far, near = pl.pallas_call(
+    near, far = pl.pallas_call(
         functools.partial(pack_kernel, shape),
         out_shape=(edge_y, edge_y),
         in_specs=whole(4),
@@ -597,8 +597,8 @@
         name="pack",
     )(parity, grid, far_x, near_x)
     far_pairs, near_pairs = swap_pairs("gy")
+    near_y = lax.ppermute(near, "gy", near_pairs)
     far_y = lax.ppermute(far, "gy", far_pairs)
-    near_y = lax.ppermute(near, "gy", near_pairs)
     field = pltpu.VMEM((items, rows + 2 * ROWS, LANES), jnp.float32)
     rounded = pltpu.VMEM((comps * wide_x, levels * LANES), jnp.bfloat16)
     inner, rim, part = pl.pallas_call(
@@ -629,7 +629,7 @@
         scratch_shapes=[field, field, field, rounded],
         compiler_params=params,
         name="finish",
-    )(parity, quarter, value, rim_weight, inner, rim, part, far_y, near_y)
+    )(parity, quarter, value, rim_weight, inner, rim, part, near_y, far_y)
 
 
 def solution(mesh):

time: 20.1 us -> 20 us (level)
    ppermute x1, starting transfers between devices: 3.57 us -> 1.49 us  [body(): far_y = lax.ppermute(far, 'gy', far_pairs)]
    ppermute x1, starting transfers between devices: 0.54 us -> 2.62 us  [body(): near_y = lax.ppermute(near, 'gy', near_pairs)]
    ppermute x1, waiting for transfers between devices: 2.02 us -> 0.01 us  [body(): near_y = lax.ppermute(near, 'gy', near_pairs)]
    ppermute x1, waiting for transfers between devices: 0.24 us -> 2.2 us  [body(): far_y = lax.ppermute(far, 'gy', far_pairs)]
  transfers between devices with their start and end apart: 4 -> 4, of which waited for: 3 -> 2; matrix products, arithmetic and copies ran while one was open for 0% -> 0% of each run, Pallas kernels for 13% -> 13%
where the time goes in v14:
time: 20 us; the launch traced here: 19.9 us
  starting transfers between devices  8.72 us (44%)
  Pallas kernels  6.99 us (35%)
  waiting for transfers between devices  3.5 us (18%)
  between operations  0.68 us (3%)
    ppermute x1, starting transfers between devices, body(): far_x = lax.ppermute(far, 'gx', far_pairs)  4.55 us
    ppermute x1, starting transfers between devices, body(): near_y = lax.ppermute(near, 'gy', near_pairs)  2.62 us
    ppermute x1, waiting for transfers between devices, body(): far_y = lax.ppermute(far, 'gy', far_pairs)  2.2 us
    pallas_call x1, Pallas kernels, body(): pl.pallas_call(functools.partial(finish_kernel, shape, chunk), out_shape=...  2.19 us
    pallas_call x1, Pallas kernels, body(): pl.pallas_call(functools.partial(far_kernel, shape, slots), out_shape=(ja...  1.65 us
    ppermute x1, starting transfers between devices, body(): far_y = lax.ppermute(far, 'gy', far_pairs)  1.49 us
    pallas_call x1, Pallas kernels, body(): pl.pallas_call(functools.partial(inner_kernel, shape, chunk, levels), out...  1.42 us
    ppermute x1, waiting for transfers between devices, body(): far_x = lax.ppermute(far, 'gx', far_pairs)  1.3 us
  transfers between devices with their start and end apart: 4, of which 2 were waited for; matrix products, arithmetic and copies ran while one was open for 0% of the time, Pallas kernels for 13%

profile of v14, /device:TPU:0, one launch (start us, length us, event | category | flops | bytes accessed | tf_op | source)
XLA Modules:
  0.0 19.9 jit_solution(5295783586485799198)
XLA Ops:
  0.6 1.6 %spread_far.1 = (f32[8,48,256]{2,1,0:T(8,128)S(1)}, bf16[400,128]{1,0:T(8,128)(2,1)S(1)}, bf16[8,16,2048]{2,1,0:T(8,128)(2,1)S(1)}, bf16[256,2048]{1,0:T(8,128)(...) custom-call(s32[48]{0:T(128)} %fish_hbm.1, ...), custom_call_target="tpu_custom_call" | custom-call | tf_op jit(solution)/shard_map/spread_far/pallas_call | solution.py:538
  2.3 4.6 %collective-permute-start = (bf16[400,128]{1,0:T(8,128)(2,1)S(1)}, bf16[400,128]{1,0:T(8,128)(2,1)S(1)}, u32[]{:S(2)}, u32[]{:S(2)}) collective-permute-start(bf16[400,128]{1,0:T(8,128)(2,1)S(1)} %get-tuple-element.37), channel_id=1, source_target_pairs={{0,28},{4,8},{8,4},{12,16},{16,12},{20,24},{24,20},{28,0},{1,29},{... | collective-permute-start | bytes 307208 | tf_op jit(solution)/shard_map/ppermute | solution.py:562
  6.8 0.8 %spread_near.1 = (f32[8,96,256]{2,1,0:T(8,128)S(1)}, bf16[400,128]{1,0:T(8,128)(2,1)S(1)}) custom-call(f32[4,2,64,128]{3,2,1,0:T(8,128)S(1)} %get-tuple-element.32.velocity_ref, f32[8,48,256]{2,1,0:T(8,128)S(1)} %get-tuple-element.33.far_half_ref, bf16[8,16,2048]{2,1,0:T(8,128)(2,1)S(1)} %get-tuple-element.34.force_ref, ...), custom_call_target="tpu_custom_call" | custom-call | flops 402653184 | bytes 786432 | tf_op jit(solution)/shard_map/spread_near/pallas_call | solution.py:563
  7.6 0.1 collective-permute-start.1
  7.7 0.4 %weights.1 = (bf16[512,2048]{1,0:T(8,128)(2,1)S(1)}, bf16[512,2048]{1,0:T(8,128)(2,1)S(1)}, s32[2,128]{1,0:T(2,128)S(1)}) custom-call(s32[2,128]{1,0:T(2,128)S(1)} %get-tuple-element.23.parity_ref, s32[8,2048]{1,0:T(8,128)S(1)} %get-tuple-element.24.quarter_ref, f32[8,2048]{1,0:T(8,128)S(1)} %get-tuple-element.25.value_ref, ...), custom_call_target="tpu_custom_call" | custom-call | flops 2097152 | bytes 4194304 | tf_op jit(solution)/shard_map/weights/pallas_call | solution.py:578
  8.1 1.3 %collective-permute-done.far_x = bf16[400,128]{1,0:T(8,128)(2,1)S(1)} collective-permute-done((bf16[400,128]{1,0:T(8,128)(2,1)S(1)}, bf16[400,128]{1,0:T(8,128)(2,1)S(1)}, u32[]{:S(2)}, u32[]{:S(2)}) %collective-permute-start) | collective-permute-done | bytes 102432 | tf_op jit(solution)/shard_map/ppermute | solution.py:562
  9.4 0.0 collective-permute-done.1.near_x
  9.5 0.5 %pack.1 = (bf16[240,128]{1,0:T(8,128)(2,1)S(1)}, bf16[240,128]{1,0:T(8,128)(2,1)S(1)}) custom-call(s32[2,128]{1,0:T(2,128)S(1)} %get-tuple-element.27.parity_ref, f32[8,96,256]{2,1,0:T(8,128)S(1)} %get-tuple-element.36.grid_ref, bf16[400,128]{1,0:T(8,128)(2,1)S(1)} %collective-permute-done.far_x, bf16[400,128]{1,0:T(8,128)(2,1)S(1)} %collective-permute-done.1.near_x), custom_call_target="tpu_custom_call" | custom-call | tf_op jit(solution)/shard_map/pack/pallas_call | solution.py:591
  10.0 2.6 %collective-permute-start.2 = (bf16[240,128]{1,0:T(8,128)(2,1)S(1)}, bf16[240,128]{1,0:T(8,128)(2,1)S(1)}, u32[]{:S(2)}, u32[]{:S(2)}) collective-permute-start(bf16[240,128]{1,0:T(8,128)(2,1)S(1)} %get-tuple-element.42), channel_id=1, source_target_pairs={{0,1},{1,0},{2,3},{3,2},{4,5},{5,4},{6,7},{7,6},{8,9},{9,8},{10,11... | collective-permute-start | bytes 184328 | tf_op jit(solution)/shard_map/ppermute | solution.py:600
  12.6 1.5 %collective-permute-start.3 = (bf16[240,128]{1,0:T(8,128)(2,1)S(1)}, bf16[240,128]{1,0:T(8,128)(2,1)S(1)}, u32[]{:S(2)}, u32[]{:S(2)}) collective-permute-start(bf16[240,128]{1,0:T(8,128)(2,1)S(1)} %get-tuple-element.43), channel_id=1, source_target_pairs={{0,3},{1,2},{2,1},{3,0},{4,7},{5,6},{6,5},{7,4},{8,11},{9,10},{10,... | collective-permute-start | bytes 184328 | tf_op jit(solution)/shard_map/ppermute | solution.py:601
  14.1 1.4 %inner.1 = (f32[8,64,128]{2,1,0:T(8,128)S(1)}, f32[8,112,128]{2,1,0:T(8,128)S(1)}, f32[2,2048]{1,0:T(2,128)S(1)}) custom-call(s32[2,128]{1,0:T(2,128)S(1)} %get-tuple-element.27.parity_ref, s32[8,2048]{1,0:T(8,128)S(1)} %get-tuple-element.28.quarter_ref, f32[8,2048]{1,0:T(8,128)S(1)} %get-tuple-element.29.value_ref, ...), custom_call_target="tpu_custom_call" | custom-call | flops 402653184 | bytes 1835008 | tf_op jit(solution)/shard_map/inner/pallas_call | solution.py:604
  15.5 0.0 collective-permute-done.2.near_y
  15.5 2.2 %collective-permute-done.3.far_y = bf16[240,128]{1,0:T(8,128)(2,1)S(1)} collective-permute-done((bf16[240,128]{1,0:T(8,128)(2,1)S(1)}, bf16[240,128]{1,0:T(8,128)(2,1)S(1)}, u32[]{:S(2)}, u32[]{:S(2)}) %collective-permute-start.3) | collective-permute-done | bytes 61472 | tf_op jit(solution)/shard_map/ppermute | solution.py:601
  17.7 2.2 %finish.1 = (f32[4,2,64,128]{3,2,1,0:T(8,128)}, f32[2,1,1,2048]{3,2,1,0:T(1,128)}) custom-call(s32[2,128]{1,0:T(2,128)S(1)} %get-tuple-element.27.parity_ref, s32[8,2048]{1,0:T(8,128)S(1)} %get-tuple-element.28.quarter_ref, f32[8,2048]{1,0:T(8,128)S(1)} %get-tuple-element.29.value_ref, bf16[512,2048]{1,0:T(8,128)(2,1)S(1)} %get-tuple-element.30.weight_ref, ...), custom_call_target="tpu_custom_call" | custom-call | tf_op jit(solution)/shard_map/finish/pallas_call | solution.py:621
Async XLA Ops:
  2.3 7.2 %collective-permute-start = (bf16[400,128]{1,0:T(8,128)(2,1)S(1)}, bf16[400,128]{1,0:T(8,128)(2,1)S(1)}, u32[]{:S(2)}, u32[]{:S(2)}) collective-permute-start(bf16[400,128]{1,0:T(8,128)(2,1)S(1)} %get-tuple-element.37), channel_id=1, source_target_pairs={{0,28},{4,8},{8,4},{12,16},{16,12},{20,24},{24,20},{28,0},{1,29},{... | collective-permute-start | bytes 307208 | tf_op jit(solution)/shard_map/ppermute | solution.py:562
  7.6 1.8 %collective-permute-start.1 = (bf16[400,128]{1,0:T(8,128)(2,1)S(1)}, bf16[400,128]{1,0:T(8,128)(2,1)S(1)}, u32[]{:S(2)}, u32[]{:S(2)}) collective-permute-start(bf16[400,128]{1,0:T(8,128)(2,1)S(1)} %get-tuple-element.38), channel_id=1, source_target_pairs={{0,4},{4,0},{8,12},{12,8},{16,20},{20,16},{24,28},{28,24},{1,5},{5... | collective-permute-start | bytes 307208 | tf_op jit(solution)/shard_map/ppermute | solution.py:576
  10.0 5.5 %collective-permute-start.2 = (bf16[240,128]{1,0:T(8,128)(2,1)S(1)}, bf16[240,128]{1,0:T(8,128)(2,1)S(1)}, u32[]{:S(2)}, u32[]{:S(2)}) collective-permute-start(bf16[240,128]{1,0:T(8,128)(2,1)S(1)} %get-tuple-element.42), channel_id=1, source_target_pairs={{0,1},{1,0},{2,3},{3,2},{4,5},{5,4},{6,7},{7,6},{8,9},{9,8},{10,11... | collective-permute-start | bytes 184328 | tf_op jit(solution)/shard_map/ppermute | solution.py:600
  12.6 5.1 %collective-permute-start.3 = (bf16[240,128]{1,0:T(8,128)(2,1)S(1)}, bf16[240,128]{1,0:T(8,128)(2,1)S(1)}, u32[]{:S(2)}, u32[]{:S(2)}) collective-permute-start(bf16[240,128]{1,0:T(8,128)(2,1)S(1)} %get-tuple-element.43), channel_id=1, source_target_pairs={{0,3},{1,2},{2,1},{3,0},{4,7},{5,6},{6,5},{7,4},{8,11},{9,10},{10,... | collective-permute-start | bytes 184328 | tf_op jit(solution)/shard_map/ppermute | solution.py:601

commit v15 on v14

--- a/solution.py
+++ b/solution.py
@@ -208,9 +208,11 @@
 
 
 def ordered(parity, near_ref, far_ref):
-    even = jnp.broadcast_to(parity, near_ref.shape) != 0
-    near, far = near_ref[...].astype(jnp.float32), far_ref[...].astype(jnp.float32)
-    return jnp.where(even, far, near), jnp.where(even, near, far)
+    even = jnp.broadcast_to(parity.astype(jnp.float32), (2 * ROWS, LANES)).astype(jnp.bfloat16)
+    even = jnp.concatenate([even] * (near_ref.shape[0] // (2 * ROWS)), axis=0) != 0
+    near, far = near_ref[...], far_ref[...]
+    before, after = jnp.where(even, far, near), jnp.where(even, near, far)
+    return before.astype(jnp.float32), after.astype(jnp.float32)
 
 
 def joined(center, before, after):
@@ -602,7 +604,7 @@
     field = pltpu.VMEM((items, rows + 2 * ROWS, LANES), jnp.float32)
     rounded = pltpu.VMEM((comps * wide_x, levels * LANES), jnp.bfloat16)
     inner, rim, part = pl.pallas_call(
-        functools.partial(inner_kernel, shape, chunk, levels),
+        functools.partial(inner_kernel, shape, slots, levels),
         out_shape=(
             jax.ShapeDtypeStruct((items, cells_x, LANES), jnp.float32),
             jax.ShapeDtypeStruct((items, rows, LANES), jnp.float32),
@@ -619,7 +621,7 @@
         name="inner",
     )(parity, quarter, value, inner_weight, grid, far_x, near_x)
     return pl.pallas_call(
-        functools.partial(finish_kernel, shape, chunk),
+        functools.partial(finish_kernel, shape, slots),
         out_shape=(
             jax.ShapeDtypeStruct(velocity.shape, jnp.float32),
             jax.ShapeDtypeStruct((comps, 1, 1, slots), jnp.float32),

time: 20 us -> 20 us (level)
  no operation moved by 1% of the time
where the time goes in v15:
time: 20 us; the launch traced here: 19.9 us
  starting transfers between devices  8.72 us (44%)
  Pallas kernels  6.99 us (35%)
  waiting for transfers between devices  3.5 us (18%)
  between operations  0.68 us (3%)
    ppermute x1, starting transfers between devices, body(): far_x = lax.ppermute(far, 'gx', far_pairs)  4.55 us
    ppermute x1, starting transfers between devices, body(): near_y = lax.ppermute(near, 'gy', near_pairs)  2.62 us
    ppermute x1, waiting for transfers between devices, body(): far_y = lax.ppermute(far, 'gy', far_pairs)  2.2 us
    pallas_call x1, Pallas kernels, body(): pl.pallas_call(functools.partial(finish_kernel, shape, slots), out_shape=...  2.19 us
    pallas_call x1, Pallas kernels, body(): pl.pallas_call(functools.partial(far_kernel, shape, slots), out_shape=(ja...  1.65 us
    ppermute x1, starting transfers between devices, body(): far_y = lax.ppermute(far, 'gy', far_pairs)  1.49 us
    pallas_call x1, Pallas kernels, body(): pl.pallas_call(functools.partial(inner_kernel, shape, slots, levels), out...  1.42 us
    ppermute x1, waiting for transfers between devices, body(): far_x = lax.ppermute(far, 'gx', far_pairs)  1.3 us
  transfers between devices with their start and end apart: 4, of which 2 were waited for; matrix products, arithmetic and copies ran while one was open for 0% of the time, Pallas kernels for 13%

profile of v15, /device:TPU:0, one launch (start us, length us, event | category | flops | bytes accessed | tf_op | source)
XLA Modules:
  0.0 19.9 jit_solution(7016784527274747850)
XLA Ops:
  0.6 1.6 %spread_far.1 = (f32[8,48,256]{2,1,0:T(8,128)S(1)}, bf16[400,128]{1,0:T(8,128)(2,1)S(1)}, bf16[8,16,2048]{2,1,0:T(8,128)(2,1)S(1)}, bf16[256,2048]{1,0:T(8,128)(...) custom-call(s32[48]{0:T(128)} %fish_hbm.1, ...), custom_call_target="tpu_custom_call" | custom-call | tf_op jit(solution)/shard_map/spread_far/pallas_call | solution.py:540
  2.3 4.6 %collective-permute-start = (bf16[400,128]{1,0:T(8,128)(2,1)S(1)}, bf16[400,128]{1,0:T(8,128)(2,1)S(1)}, u32[]{:S(2)}, u32[]{:S(2)}) collective-permute-start(bf16[400,128]{1,0:T(8,128)(2,1)S(1)} %get-tuple-element.37), channel_id=1, source_target_pairs={{0,28},{4,8},{8,4},{12,16},{16,12},{20,24},{24,20},{28,0},{1,29},{... | collective-permute-start | bytes 307208 | tf_op jit(solution)/shard_map/ppermute | solution.py:564
  6.8 0.8 %spread_near.1 = (f32[8,96,256]{2,1,0:T(8,128)S(1)}, bf16[400,128]{1,0:T(8,128)(2,1)S(1)}) custom-call(f32[4,2,64,128]{3,2,1,0:T(8,128)S(1)} %get-tuple-element.32.velocity_ref, f32[8,48,256]{2,1,0:T(8,128)S(1)} %get-tuple-element.33.far_half_ref, bf16[8,16,2048]{2,1,0:T(8,128)(2,1)S(1)} %get-tuple-element.34.force_ref, ...), custom_call_target="tpu_custom_call" | custom-call | flops 402653184 | bytes 786432 | tf_op jit(solution)/shard_map/spread_near/pallas_call | solution.py:565
  7.6 0.1 collective-permute-start.1
  7.7 0.4 %weights.1 = (bf16[512,2048]{1,0:T(8,128)(2,1)S(1)}, bf16[512,2048]{1,0:T(8,128)(2,1)S(1)}, s32[2,128]{1,0:T(2,128)S(1)}) custom-call(s32[2,128]{1,0:T(2,128)S(1)} %get-tuple-element.23.parity_ref, s32[8,2048]{1,0:T(8,128)S(1)} %get-tuple-element.24.quarter_ref, f32[8,2048]{1,0:T(8,128)S(1)} %get-tuple-element.25.value_ref, ...), custom_call_target="tpu_custom_call" | custom-call | flops 2097152 | bytes 4194304 | tf_op jit(solution)/shard_map/weights/pallas_call | solution.py:580
  8.1 1.3 %collective-permute-done.far_x = bf16[400,128]{1,0:T(8,128)(2,1)S(1)} collective-permute-done((bf16[400,128]{1,0:T(8,128)(2,1)S(1)}, bf16[400,128]{1,0:T(8,128)(2,1)S(1)}, u32[]{:S(2)}, u32[]{:S(2)}) %collective-permute-start) | collective-permute-done | bytes 102432 | tf_op jit(solution)/shard_map/ppermute | solution.py:564
  9.4 0.0 collective-permute-done.1.near_x
  9.5 0.5 %pack.1 = (bf16[240,128]{1,0:T(8,128)(2,1)S(1)}, bf16[240,128]{1,0:T(8,128)(2,1)S(1)}) custom-call(s32[2,128]{1,0:T(2,128)S(1)} %get-tuple-element.27.parity_ref, f32[8,96,256]{2,1,0:T(8,128)S(1)} %get-tuple-element.36.grid_ref, bf16[400,128]{1,0:T(8,128)(2,1)S(1)} %collective-permute-done.far_x, bf16[400,128]{1,0:T(8,128)(2,1)S(1)} %collective-permute-done.1.near_x), custom_call_target="tpu_custom_call" | custom-call | tf_op jit(solution)/shard_map/pack/pallas_call | solution.py:593
  10.0 2.6 %collective-permute-start.2 = (bf16[240,128]{1,0:T(8,128)(2,1)S(1)}, bf16[240,128]{1,0:T(8,128)(2,1)S(1)}, u32[]{:S(2)}, u32[]{:S(2)}) collective-permute-start(bf16[240,128]{1,0:T(8,128)(2,1)S(1)} %get-tuple-element.42), channel_id=1, source_target_pairs={{0,1},{1,0},{2,3},{3,2},{4,5},{5,4},{6,7},{7,6},{8,9},{9,8},{10,11... | collective-permute-start | bytes 184328 | tf_op jit(solution)/shard_map/ppermute | solution.py:602
  12.6 1.5 %collective-permute-start.3 = (bf16[240,128]{1,0:T(8,128)(2,1)S(1)}, bf16[240,128]{1,0:T(8,128)(2,1)S(1)}, u32[]{:S(2)}, u32[]{:S(2)}) collective-permute-start(bf16[240,128]{1,0:T(8,128)(2,1)S(1)} %get-tuple-element.43), channel_id=1, source_target_pairs={{0,3},{1,2},{2,1},{3,0},{4,7},{5,6},{6,5},{7,4},{8,11},{9,10},{10,... | collective-permute-start | bytes 184328 | tf_op jit(solution)/shard_map/ppermute | solution.py:603
  14.1 1.4 %inner.1 = (f32[8,64,128]{2,1,0:T(8,128)S(1)}, f32[8,112,128]{2,1,0:T(8,128)S(1)}, f32[2,2048]{1,0:T(2,128)S(1)}) custom-call(s32[2,128]{1,0:T(2,128)S(1)} %get-tuple-element.27.parity_ref, s32[8,2048]{1,0:T(8,128)S(1)} %get-tuple-element.28.quarter_ref, f32[8,2048]{1,0:T(8,128)S(1)} %get-tuple-element.29.value_ref, ...), custom_call_target="tpu_custom_call" | custom-call | flops 402653184 | bytes 1835008 | tf_op jit(solution)/shard_map/inner/pallas_call | solution.py:606
  15.5 0.0 collective-permute-done.2.near_y
  15.5 2.2 %collective-permute-done.3.far_y = bf16[240,128]{1,0:T(8,128)(2,1)S(1)} collective-permute-done((bf16[240,128]{1,0:T(8,128)(2,1)S(1)}, bf16[240,128]{1,0:T(8,128)(2,1)S(1)}, u32[]{:S(2)}, u32[]{:S(2)}) %collective-permute-start.3) | collective-permute-done | bytes 61472 | tf_op jit(solution)/shard_map/ppermute | solution.py:603
  17.7 2.2 %finish.1 = (f32[4,2,64,128]{3,2,1,0:T(8,128)}, f32[2,1,1,2048]{3,2,1,0:T(1,128)}) custom-call(s32[2,128]{1,0:T(2,128)S(1)} %get-tuple-element.27.parity_ref, s32[8,2048]{1,0:T(8,128)S(1)} %get-tuple-element.28.quarter_ref, f32[8,2048]{1,0:T(8,128)S(1)} %get-tuple-element.29.value_ref, bf16[512,2048]{1,0:T(8,128)(2,1)S(1)} %get-tuple-element.30.weight_ref, ...), custom_call_target="tpu_custom_call" | custom-call | tf_op jit(solution)/shard_map/finish/pallas_call | solution.py:623
Async XLA Ops:
  2.3 7.2 %collective-permute-start = (bf16[400,128]{1,0:T(8,128)(2,1)S(1)}, bf16[400,128]{1,0:T(8,128)(2,1)S(1)}, u32[]{:S(2)}, u32[]{:S(2)}) collective-permute-start(bf16[400,128]{1,0:T(8,128)(2,1)S(1)} %get-tuple-element.37), channel_id=1, source_target_pairs={{0,28},{4,8},{8,4},{12,16},{16,12},{20,24},{24,20},{28,0},{1,29},{... | collective-permute-start | bytes 307208 | tf_op jit(solution)/shard_map/ppermute | solution.py:564
  7.6 1.8 %collective-permute-start.1 = (bf16[400,128]{1,0:T(8,128)(2,1)S(1)}, bf16[400,128]{1,0:T(8,128)(2,1)S(1)}, u32[]{:S(2)}, u32[]{:S(2)}) collective-permute-start(bf16[400,128]{1,0:T(8,128)(2,1)S(1)} %get-tuple-element.38), channel_id=1, source_target_pairs={{0,4},{4,0},{8,12},{12,8},{16,20},{20,16},{24,28},{28,24},{1,5},{5... | collective-permute-start | bytes 307208 | tf_op jit(solution)/shard_map/ppermute | solution.py:578
  10.0 5.5 %collective-permute-start.2 = (bf16[240,128]{1,0:T(8,128)(2,1)S(1)}, bf16[240,128]{1,0:T(8,128)(2,1)S(1)}, u32[]{:S(2)}, u32[]{:S(2)}) collective-permute-start(bf16[240,128]{1,0:T(8,128)(2,1)S(1)} %get-tuple-element.42), channel_id=1, source_target_pairs={{0,1},{1,0},{2,3},{3,2},{4,5},{5,4},{6,7},{7,6},{8,9},{9,8},{10,11... | collective-permute-start | bytes 184328 | tf_op jit(solution)/shard_map/ppermute | solution.py:602
  12.6 5.1 %collective-permute-start.3 = (bf16[240,128]{1,0:T(8,128)(2,1)S(1)}, bf16[240,128]{1,0:T(8,128)(2,1)S(1)}, u32[]{:S(2)}, u32[]{:S(2)}) collective-permute-start(bf16[240,128]{1,0:T(8,128)(2,1)S(1)} %get-tuple-element.43), channel_id=1, source_target_pairs={{0,3},{1,2},{2,1},{3,0},{4,7},{5,6},{6,5},{7,4},{8,11},{9,10},{10,... | collective-permute-start | bytes 184328 | tf_op jit(solution)/shard_map/ppermute | solution.py:603

commit v16 on v14

--- a/solution.py
+++ b/solution.py
@@ -448,7 +448,8 @@
 
 def finish_kernel(
     shape, chunk, parity_ref, quarter_ref, value_ref, weight_ref, inner_ref, rim_ref, part_ref,
-    near_y, far_y, next_ref, sampled_ref, moved_ref, carried_ref, sweep_ref, round_ref,
+    near_y, far_y, next_hbm, sampled_hbm,
+    moved_ref, carried_ref, sweep_ref, round_ref, next_ref, sampled_ref, sems,
 ):
     cells_x, cells_y, _, _ = shape
     items = rim_ref.shape[0]
@@ -506,6 +507,13 @@
         parts = sampled_part(round_ref, weight_ref, quarter_ref, value_ref, lanes, comps)
         for c in range(comps):
             sampled_ref[c, 0, :, lanes] = part_ref[c : c + 1, lanes] + parts[c]
+    pieces = [(next_ref.at[k // comps, k % comps], next_hbm.at[k // comps, k % comps]) for k in range(items)]
+    pieces.append((sampled_ref, sampled_hbm))
+    copies = [pltpu.make_async_copy(a, b, sems.at[i]) for i, (a, b) in enumerate(pieces)]
+    for copy in copies:
+        copy.start()
+    for copy in copies:
+        copy.wait()
 
 
 def whole(count):
@@ -625,8 +633,9 @@
             jax.ShapeDtypeStruct((comps, 1, 1, slots), jnp.float32),
         ),
         in_specs=whole(9),
-        out_specs=tuple(whole(2)),
-        scratch_shapes=[field, field, field, rounded],
+        out_specs=(pl.BlockSpec(memory_space=pltpu.HBM),) * 2,
+        scratch_shapes=[field, field, field, rounded, pltpu.VMEM(velocity.shape, velocity.dtype)]
+        + [pltpu.VMEM((comps, 1, 1, slots), jnp.float32), pltpu.SemaphoreType.DMA((items + 1,))],
         compiler_params=params,
         name="finish",
     )(parity, quarter, value, rim_weight, inner, rim, part, near_y, far_y)

time: 20 us -> 20.1 us (level)
  no operation moved by 1% of the time
where the time goes in v16:
time: 20.1 us; the launch traced here: 20 us
  starting transfers between devices  8.72 us (43%)
  Pallas kernels  7.06 us (35%)
  waiting for transfers between devices  3.5 us (17%)
  between operations  0.68 us (3%)
    ppermute x1, starting transfers between devices, body(): far_x = lax.ppermute(far, 'gx', far_pairs)  4.55 us
    ppermute x1, starting transfers between devices, body(): near_y = lax.ppermute(near, 'gy', near_pairs)  2.62 us
    pallas_call x1, Pallas kernels, body(): pl.pallas_call(functools.partial(finish_kernel, shape, chunk), out_shape=...  2.26 us
    ppermute x1, waiting for transfers between devices, body(): far_y = lax.ppermute(far, 'gy', far_pairs)  2.2 us
    pallas_call x1, Pallas kernels, body(): pl.pallas_call(functools.partial(far_kernel, shape, slots), out_shape=(ja...  1.65 us
    ppermute x1, starting transfers between devices, body(): far_y = lax.ppermute(far, 'gy', far_pairs)  1.49 us
    pallas_call x1, Pallas kernels, body(): pl.pallas_call(functools.partial(inner_kernel, shape, chunk, levels), out...  1.42 us
    ppermute x1, waiting for transfers between devices, body(): far_x = lax.ppermute(far, 'gx', far_pairs)  1.3 us
  transfers between devices with their start and end apart: 4, of which 2 were waited for; matrix products, arithmetic and copies ran while one was open for 0% of the time, Pallas kernels for 13%

profile of v16, /device:TPU:0, one launch (start us, length us, event | category | flops | bytes accessed | tf_op | source)
XLA Modules:
  0.0 20.0 jit_solution(16213666607597127773)
XLA Ops:
  0.6 1.6 %spread_far.1 = (f32[8,48,256]{2,1,0:T(8,128)S(1)}, bf16[400,128]{1,0:T(8,128)(2,1)S(1)}, bf16[8,16,2048]{2,1,0:T(8,128)(2,1)S(1)}, bf16[256,2048]{1,0:T(8,128)(...) custom-call(s32[48]{0:T(128)} %fish_hbm.1, ...), custom_call_target="tpu_custom_call" | custom-call | tf_op jit(solution)/shard_map/spread_far/pallas_call | solution.py:546
  2.3 4.6 %collective-permute-start = (bf16[400,128]{1,0:T(8,128)(2,1)S(1)}, bf16[400,128]{1,0:T(8,128)(2,1)S(1)}, u32[]{:S(2)}, u32[]{:S(2)}) collective-permute-start(bf16[400,128]{1,0:T(8,128)(2,1)S(1)} %get-tuple-element.37), channel_id=1, source_target_pairs={{0,28},{4,8},{8,4},{12,16},{16,12},{20,24},{24,20},{28,0},{1,29},{... | collective-permute-start | bytes 307208 | tf_op jit(solution)/shard_map/ppermute | solution.py:570
  6.8 0.8 %spread_near.1 = (f32[8,96,256]{2,1,0:T(8,128)S(1)}, bf16[400,128]{1,0:T(8,128)(2,1)S(1)}) custom-call(f32[4,2,64,128]{3,2,1,0:T(8,128)S(1)} %get-tuple-element.32.velocity_ref, f32[8,48,256]{2,1,0:T(8,128)S(1)} %get-tuple-element.33.far_half_ref, bf16[8,16,2048]{2,1,0:T(8,128)(2,1)S(1)} %get-tuple-element.34.force_ref, ...), custom_call_target="tpu_custom_call" | custom-call | flops 402653184 | bytes 786432 | tf_op jit(solution)/shard_map/spread_near/pallas_call | solution.py:571
  7.6 0.1 collective-permute-start.1
  7.7 0.4 %weights.1 = (bf16[512,2048]{1,0:T(8,128)(2,1)S(1)}, bf16[512,2048]{1,0:T(8,128)(2,1)S(1)}, s32[2,128]{1,0:T(2,128)S(1)}) custom-call(s32[2,128]{1,0:T(2,128)S(1)} %get-tuple-element.23.parity_ref, s32[8,2048]{1,0:T(8,128)S(1)} %get-tuple-element.24.quarter_ref, f32[8,2048]{1,0:T(8,128)S(1)} %get-tuple-element.25.value_ref, ...), custom_call_target="tpu_custom_call" | custom-call | flops 2097152 | bytes 4194304 | tf_op jit(solution)/shard_map/weights/pallas_call | solution.py:586
  8.1 1.3 %collective-permute-done.far_x = bf16[400,128]{1,0:T(8,128)(2,1)S(1)} collective-permute-done((bf16[400,128]{1,0:T(8,128)(2,1)S(1)}, bf16[400,128]{1,0:T(8,128)(2,1)S(1)}, u32[]{:S(2)}, u32[]{:S(2)}) %collective-permute-start) | collective-permute-done | bytes 102432 | tf_op jit(solution)/shard_map/ppermute | solution.py:570
  9.4 0.0 collective-permute-done.1.near_x
  9.5 0.5 %pack.1 = (bf16[240,128]{1,0:T(8,128)(2,1)S(1)}, bf16[240,128]{1,0:T(8,128)(2,1)S(1)}) custom-call(s32[2,128]{1,0:T(2,128)S(1)} %get-tuple-element.27.parity_ref, f32[8,96,256]{2,1,0:T(8,128)S(1)} %get-tuple-element.36.grid_ref, bf16[400,128]{1,0:T(8,128)(2,1)S(1)} %collective-permute-done.far_x, bf16[400,128]{1,0:T(8,128)(2,1)S(1)} %collective-permute-done.1.near_x), custom_call_target="tpu_custom_call" | custom-call | tf_op jit(solution)/shard_map/pack/pallas_call | solution.py:599
  10.0 2.6 %collective-permute-start.2 = (bf16[240,128]{1,0:T(8,128)(2,1)S(1)}, bf16[240,128]{1,0:T(8,128)(2,1)S(1)}, u32[]{:S(2)}, u32[]{:S(2)}) collective-permute-start(bf16[240,128]{1,0:T(8,128)(2,1)S(1)} %get-tuple-element.42), channel_id=1, source_target_pairs={{0,1},{1,0},{2,3},{3,2},{4,5},{5,4},{6,7},{7,6},{8,9},{9,8},{10,11... | collective-permute-start | bytes 184328 | tf_op jit(solution)/shard_map/ppermute | solution.py:608
  12.6 1.5 %collective-permute-start.3 = (bf16[240,128]{1,0:T(8,128)(2,1)S(1)}, bf16[240,128]{1,0:T(8,128)(2,1)S(1)}, u32[]{:S(2)}, u32[]{:S(2)}) collective-permute-start(bf16[240,128]{1,0:T(8,128)(2,1)S(1)} %get-tuple-element.43), channel_id=1, source_target_pairs={{0,3},{1,2},{2,1},{3,0},{4,7},{5,6},{6,5},{7,4},{8,11},{9,10},{10,... | collective-permute-start | bytes 184328 | tf_op jit(solution)/shard_map/ppermute | solution.py:609
  14.1 1.4 %inner.1 = (f32[8,64,128]{2,1,0:T(8,128)S(1)}, f32[8,112,128]{2,1,0:T(8,128)S(1)}, f32[2,2048]{1,0:T(2,128)S(1)}) custom-call(s32[2,128]{1,0:T(2,128)S(1)} %get-tuple-element.27.parity_ref, s32[8,2048]{1,0:T(8,128)S(1)} %get-tuple-element.28.quarter_ref, f32[8,2048]{1,0:T(8,128)S(1)} %get-tuple-element.29.value_ref, ...), custom_call_target="tpu_custom_call" | custom-call | flops 402653184 | bytes 1835008 | tf_op jit(solution)/shard_map/inner/pallas_call | solution.py:612
  15.5 0.0 collective-permute-done.2.near_y
  15.5 2.2 %collective-permute-done.3.far_y = bf16[240,128]{1,0:T(8,128)(2,1)S(1)} collective-permute-done((bf16[240,128]{1,0:T(8,128)(2,1)S(1)}, bf16[240,128]{1,0:T(8,128)(2,1)S(1)}, u32[]{:S(2)}, u32[]{:S(2)}) %collective-permute-start.3) | collective-permute-done | bytes 61472 | tf_op jit(solution)/shard_map/ppermute | solution.py:609
  17.7 2.3 %finish.1 = (f32[4,2,64,128]{3,2,1,0:T(8,128)}, f32[2,1,1,2048]{3,2,1,0:T(1,128)}) custom-call(s32[2,128]{1,0:T(2,128)S(1)} %get-tuple-element.27.parity_ref, s32[8,2048]{1,0:T(8,128)S(1)} %get-tuple-element.28.quarter_ref, f32[8,2048]{1,0:T(8,128)S(1)} %get-tuple-element.29.value_ref, bf16[512,2048]{1,0:T(8,128)(2,1)S(1)} %get-tuple-element.30.weight_ref, ...), custom_call_target="tpu_custom_call" | custom-call | tf_op jit(solution)/shard_map/finish/pallas_call | solution.py:629
Async XLA Ops:
  2.3 7.2 %collective-permute-start = (bf16[400,128]{1,0:T(8,128)(2,1)S(1)}, bf16[400,128]{1,0:T(8,128)(2,1)S(1)}, u32[]{:S(2)}, u32[]{:S(2)}) collective-permute-start(bf16[400,128]{1,0:T(8,128)(2,1)S(1)} %get-tuple-element.37), channel_id=1, source_target_pairs={{0,28},{4,8},{8,4},{12,16},{16,12},{20,24},{24,20},{28,0},{1,29},{... | collective-permute-start | bytes 307208 | tf_op jit(solution)/shard_map/ppermute | solution.py:570
  7.6 1.8 %collective-permute-start.1 = (bf16[400,128]{1,0:T(8,128)(2,1)S(1)}, bf16[400,128]{1,0:T(8,128)(2,1)S(1)}, u32[]{:S(2)}, u32[]{:S(2)}) collective-permute-start(bf16[400,128]{1,0:T(8,128)(2,1)S(1)} %get-tuple-element.38), channel_id=1, source_target_pairs={{0,4},{4,0},{8,12},{12,8},{16,20},{20,16},{24,28},{28,24},{1,5},{5... | collective-permute-start | bytes 307208 | tf_op jit(solution)/shard_map/ppermute | solution.py:584
  10.0 5.5 %collective-permute-start.2 = (bf16[240,128]{1,0:T(8,128)(2,1)S(1)}, bf16[240,128]{1,0:T(8,128)(2,1)S(1)}, u32[]{:S(2)}, u32[]{:S(2)}) collective-permute-start(bf16[240,128]{1,0:T(8,128)(2,1)S(1)} %get-tuple-element.42), channel_id=1, source_target_pairs={{0,1},{1,0},{2,3},{3,2},{4,5},{5,4},{6,7},{7,6},{8,9},{9,8},{10,11... | collective-permute-start | bytes 184328 | tf_op jit(solution)/shard_map/ppermute | solution.py:608
  12.6 5.1 %collective-permute-start.3 = (bf16[240,128]{1,0:T(8,128)(2,1)S(1)}, bf16[240,128]{1,0:T(8,128)(2,1)S(1)}, u32[]{:S(2)}, u32[]{:S(2)}) collective-permute-start(bf16[240,128]{1,0:T(8,128)(2,1)S(1)} %get-tuple-element.43), channel_id=1, source_target_pairs={{0,3},{1,2},{2,1},{3,0},{4,7},{5,6},{6,5},{7,4},{8,11},{9,10},{10,... | collective-permute-start | bytes 184328 | tf_op jit(solution)/shard_map/ppermute | solution.py:609

commit v17 on v14

--- a/solution.py
+++ b/solution.py
@@ -125,7 +125,7 @@
 
 
 def far_kernel(
-    shape, chunk, fish_hbm, velocity_hbm, cell_hbm, frac_hbm, force_hbm,
+    shape, fish_hbm, velocity_hbm, cell_hbm, frac_hbm, force_hbm,
     half_ref, far_ref, force_out, dense_y_ref, quarter_ref, value_ref,
     quarter_y_ref, value_y_ref, level_ref, parity_ref, velocity_ref,
     fish_ref, cell_ref, frac_ref, force_ref, sems,
@@ -144,37 +144,36 @@
     parity_ref[0:1] = jnp.full((1, LANES), jnp.where(even, 1, 0), jnp.int32)
     parity_ref[1:2] = jnp.full((1, LANES), jnp.where(even_y, 1, 0), jnp.int32)
     base = jnp.where(even, -MARGIN // 4, cells_x // 8)
-    for copy in copies[:-1]:
+    for copy in copies[:2]:
+        copy.wait()
+    level_ref[...] = cell_ref[2, 0]
+    offset_x = local_cell(cell_ref[0, 0], row * cells_x, extent_x)
+    offset_y = local_cell(cell_ref[1, 0], col * cells_y, extent_y)
+    quarter_x, value_x = tile_weights(offset_x, four_weights(frac_ref[0, 0]))
+    quarter_ref[...] = quarter_x
+    quarter, value = tile_weights(offset_y, four_weights(frac_ref[1, 0]))
+    quarter_y_ref[...] = quarter
+    value_y_ref[...] = value
+    quarter, value = doubled(quarter, value)
+    dense_y_ref[...] = jnp.concatenate(
+        [picked_tile(quarter, value, n) for n in range(0, cells_y + MARGIN, 2 * ROWS)]
+        + [jnp.zeros((LANES - SPAN, slots), jnp.bfloat16)]
+        + [picked_tile(quarter, value, n) for n in range(-MARGIN, 0, 2 * ROWS)],
+        axis=0,
+    )
+    for copy in copies[2:-1]:
         copy.wait()
     mine = jnp.where(fish_ref[...] == row * lax.axis_size("gy") + col, 1.0, 0.0)
     count = FISH_MARK * jnp.sum(mine)
-    level_ref[...] = cell_ref[2, 0]
-    for first in range(0, slots, chunk):
-        lanes = slice(first, first + chunk)
-        offset_x = local_cell(cell_ref[0, 0, :, lanes], row * cells_x, extent_x)
-        offset_y = local_cell(cell_ref[1, 0, :, lanes], col * cells_y, extent_y)
-        slot = lax.broadcasted_iota(jnp.int32, (1, chunk), 1) + first
-        alive = jnp.where(slot.astype(jnp.float32) < count, 1.0, 0.0)
-        quarter, value = tile_weights(offset_x, four_weights(frac_ref[0, 0, :, lanes]))
-        value = value * alive
-        quarter_ref[:, lanes] = quarter
-        value_ref[:, lanes] = value
-        level = cell_ref[2, 0, :, lanes]
-        pushes = [force_ref[c, 0, :, lanes] * value for c in range(comps)]
-        for l in range(levels):
-            for c in range(comps):
-                force_out[l * comps + c, :, lanes] = twice(jnp.where(level == l, pushes[c], 0.0))
-        quarter, value = tile_weights(offset_y, four_weights(frac_ref[1, 0, :, lanes]))
-        quarter_y_ref[:, lanes] = quarter
-        value_y_ref[:, lanes] = value
-        quarter, value = doubled(quarter, value)
-        dense_y_ref[:, lanes] = jnp.concatenate(
-            [picked_tile(quarter, value, n) for n in range(0, cells_y + MARGIN, 2 * ROWS)]
-            + [jnp.zeros((LANES - SPAN, chunk), jnp.bfloat16)]
-            + [picked_tile(quarter, value, n) for n in range(-MARGIN, 0, 2 * ROWS)],
-            axis=0,
-        )
-        half_spread(quarter_ref, force_out, dense_y_ref, half_ref, base, lanes)
+    slot = lax.broadcasted_iota(jnp.int32, (1, slots), 1)
+    value = value_x * jnp.where(slot.astype(jnp.float32) < count, 1.0, 0.0)
+    value_ref[...] = value
+    level = cell_ref[2, 0]
+    pushes = [force_ref[c, 0] * value for c in range(comps)]
+    for l in range(levels):
+        for c in range(comps):
+            force_out[l * comps + c] = twice(jnp.where(level == l, pushes[c], 0.0))
+    half_spread(quarter_ref, force_out, dense_y_ref, half_ref, base, slice(0, slots))
     copies[-1].wait()
     finish_half(half_ref, velocity_ref, far_ref, even, cells_y)
 
@@ -536,7 +535,7 @@
     arrays = (fish_owner, velocity, marker_cell, marker_frac, marker_force)
     far_half, far, force, dense_y, quarter, value, quarter_y, value_y, level, parity, near_velocity = (
         pl.pallas_call(
-        functools.partial(far_kernel, shape, slots),
+        functools.partial(far_kernel, shape),
         out_shape=(
             jax.ShapeDtypeStruct(half, jnp.float32),
             edge_x,

time: 20 us -> 20.2 us (1.010)
  no operation moved by 1% of the time
where the time goes in v17:
time: 20.2 us; the launch traced here: 20 us
  starting transfers between devices  8.73 us (43%)
  Pallas kernels  7.14 us (35%)
  waiting for transfers between devices  3.5 us (17%)
  between operations  0.68 us (3%)
    ppermute x1, starting transfers between devices, body(): far_x = lax.ppermute(far, 'gx', far_pairs)  4.55 us
    ppermute x1, starting transfers between devices, body(): near_y = lax.ppermute(near, 'gy', near_pairs)  2.62 us
    ppermute x1, waiting for transfers between devices, body(): far_y = lax.ppermute(far, 'gy', far_pairs)  2.19 us
    pallas_call x1, Pallas kernels, body(): pl.pallas_call(functools.partial(finish_kernel, shape, chunk), out_shape=...  2.19 us
    pallas_call x1, Pallas kernels, body(): pl.pallas_call(functools.partial(far_kernel, shape), out_shape=(jax.Shape...  1.8 us
    ppermute x1, starting transfers between devices, body(): far_y = lax.ppermute(far, 'gy', far_pairs)  1.49 us
    pallas_call x1, Pallas kernels, body(): pl.pallas_call(functools.partial(inner_kernel, shape, chunk, levels), out...  1.42 us
    ppermute x1, waiting for transfers between devices, body(): far_x = lax.ppermute(far, 'gx', far_pairs)  1.3 us
  transfers between devices with their start and end apart: 4, of which 2 were waited for; matrix products, arithmetic and copies ran while one was open for 0% of the time, Pallas kernels for 13%

profile of v17, /device:TPU:0, one launch (start us, length us, event | category | flops | bytes accessed | tf_op | source)
XLA Modules:
  0.0 20.0 jit_solution(16724787025559227197)
XLA Ops:
  0.6 1.8 %spread_far.1 = (f32[8,48,256]{2,1,0:T(8,128)S(1)}, bf16[400,128]{1,0:T(8,128)(2,1)S(1)}, bf16[8,16,2048]{2,1,0:T(8,128)(2,1)S(1)}, bf16[256,2048]{1,0:T(8,128)(...) custom-call(s32[48]{0:T(128)} %fish_hbm.1, ...), custom_call_target="tpu_custom_call" | custom-call | tf_op jit(solution)/shard_map/spread_far/pallas_call | solution.py:537
  2.4 4.6 %collective-permute-start = (bf16[400,128]{1,0:T(8,128)(2,1)S(1)}, bf16[400,128]{1,0:T(8,128)(2,1)S(1)}, u32[]{:S(2)}, u32[]{:S(2)}) collective-permute-start(bf16[400,128]{1,0:T(8,128)(2,1)S(1)} %get-tuple-element.37), channel_id=1, source_target_pairs={{0,28},{4,8},{8,4},{12,16},{16,12},{20,24},{24,20},{28,0},{1,29},{... | collective-permute-start | bytes 307208 | tf_op jit(solution)/shard_map/ppermute | solution.py:561
  7.0 0.8 %spread_near.1 = (f32[8,96,256]{2,1,0:T(8,128)S(1)}, bf16[400,128]{1,0:T(8,128)(2,1)S(1)}) custom-call(f32[4,2,64,128]{3,2,1,0:T(8,128)S(1)} %get-tuple-element.32.velocity_ref, f32[8,48,256]{2,1,0:T(8,128)S(1)} %get-tuple-element.33.far_half_ref, bf16[8,16,2048]{2,1,0:T(8,128)(2,1)S(1)} %get-tuple-element.34.force_ref, ...), custom_call_target="tpu_custom_call" | custom-call | flops 402653184 | bytes 786432 | tf_op jit(solution)/shard_map/spread_near/pallas_call | solution.py:562
  7.8 0.1 collective-permute-start.1
  7.8 0.4 %weights.1 = (bf16[512,2048]{1,0:T(8,128)(2,1)S(1)}, bf16[512,2048]{1,0:T(8,128)(2,1)S(1)}, s32[2,128]{1,0:T(2,128)S(1)}) custom-call(s32[2,128]{1,0:T(2,128)S(1)} %get-tuple-element.23.parity_ref, s32[8,2048]{1,0:T(8,128)S(1)} %get-tuple-element.24.quarter_ref, f32[8,2048]{1,0:T(8,128)S(1)} %get-tuple-element.25.value_ref, ...), custom_call_target="tpu_custom_call" | custom-call | flops 2097152 | bytes 4194304 | tf_op jit(solution)/shard_map/weights/pallas_call | solution.py:577
  8.3 1.3 %collective-permute-done.far_x = bf16[400,128]{1,0:T(8,128)(2,1)S(1)} collective-permute-done((bf16[400,128]{1,0:T(8,128)(2,1)S(1)}, bf16[400,128]{1,0:T(8,128)(2,1)S(1)}, u32[]{:S(2)}, u32[]{:S(2)}) %collective-permute-start) | collective-permute-done | bytes 102432 | tf_op jit(solution)/shard_map/ppermute | solution.py:561
  9.6 0.0 collective-permute-done.1.near_x
  9.6 0.5 %pack.1 = (bf16[240,128]{1,0:T(8,128)(2,1)S(1)}, bf16[240,128]{1,0:T(8,128)(2,1)S(1)}) custom-call(s32[2,128]{1,0:T(2,128)S(1)} %get-tuple-element.27.parity_ref, f32[8,96,256]{2,1,0:T(8,128)S(1)} %get-tuple-element.36.grid_ref, bf16[400,128]{1,0:T(8,128)(2,1)S(1)} %collective-permute-done.far_x, bf16[400,128]{1,0:T(8,128)(2,1)S(1)} %collective-permute-done.1.near_x), custom_call_target="tpu_custom_call" | custom-call | tf_op jit(solution)/shard_map/pack/pallas_call | solution.py:590
  10.1 2.6 %collective-permute-start.2 = (bf16[240,128]{1,0:T(8,128)(2,1)S(1)}, bf16[240,128]{1,0:T(8,128)(2,1)S(1)}, u32[]{:S(2)}, u32[]{:S(2)}) collective-permute-start(bf16[240,128]{1,0:T(8,128)(2,1)S(1)} %get-tuple-element.42), channel_id=1, source_target_pairs={{0,1},{1,0},{2,3},{3,2},{4,5},{5,4},{6,7},{7,6},{8,9},{9,8},{10,11... | collective-permute-start | bytes 184328 | tf_op jit(solution)/shard_map/ppermute | solution.py:599
  12.7 1.5 %collective-permute-start.3 = (bf16[240,128]{1,0:T(8,128)(2,1)S(1)}, bf16[240,128]{1,0:T(8,128)(2,1)S(1)}, u32[]{:S(2)}, u32[]{:S(2)}) collective-permute-start(bf16[240,128]{1,0:T(8,128)(2,1)S(1)} %get-tuple-element.43), channel_id=1, source_target_pairs={{0,3},{1,2},{2,1},{3,0},{4,7},{5,6},{6,5},{7,4},{8,11},{9,10},{10,... | collective-permute-start | bytes 184328 | tf_op jit(solution)/shard_map/ppermute | solution.py:600
  14.2 1.4 %inner.1 = (f32[8,64,128]{2,1,0:T(8,128)S(1)}, f32[8,112,128]{2,1,0:T(8,128)S(1)}, f32[2,2048]{1,0:T(2,128)S(1)}) custom-call(s32[2,128]{1,0:T(2,128)S(1)} %get-tuple-element.27.parity_ref, s32[8,2048]{1,0:T(8,128)S(1)} %get-tuple-element.28.quarter_ref, f32[8,2048]{1,0:T(8,128)S(1)} %get-tuple-element.29.value_ref, ...), custom_call_target="tpu_custom_call" | custom-call | flops 402653184 | bytes 1835008 | tf_op jit(solution)/shard_map/inner/pallas_call | solution.py:603
  15.7 0.0 collective-permute-done.2.near_y
  15.7 2.2 %collective-permute-done.3.far_y = bf16[240,128]{1,0:T(8,128)(2,1)S(1)} collective-permute-done((bf16[240,128]{1,0:T(8,128)(2,1)S(1)}, bf16[240,128]{1,0:T(8,128)(2,1)S(1)}, u32[]{:S(2)}, u32[]{:S(2)}) %collective-permute-start.3) | collective-permute-done | bytes 61472 | tf_op jit(solution)/shard_map/ppermute | solution.py:600
  17.9 2.2 %finish.1 = (f32[4,2,64,128]{3,2,1,0:T(8,128)}, f32[2,1,1,2048]{3,2,1,0:T(1,128)}) custom-call(s32[2,128]{1,0:T(2,128)S(1)} %get-tuple-element.27.parity_ref, s32[8,2048]{1,0:T(8,128)S(1)} %get-tuple-element.28.quarter_ref, f32[8,2048]{1,0:T(8,128)S(1)} %get-tuple-element.29.value_ref, bf16[512,2048]{1,0:T(8,128)(2,1)S(1)} %get-tuple-element.30.weight_ref, ...), custom_call_target="tpu_custom_call" | custom-call | tf_op jit(solution)/shard_map/finish/pallas_call | solution.py:620
Async XLA Ops:
  2.4 7.2 %collective-permute-start = (bf16[400,128]{1,0:T(8,128)(2,1)S(1)}, bf16[400,128]{1,0:T(8,128)(2,1)S(1)}, u32[]{:S(2)}, u32[]{:S(2)}) collective-permute-start(bf16[400,128]{1,0:T(8,128)(2,1)S(1)} %get-tuple-element.37), channel_id=1, source_target_pairs={{0,28},{4,8},{8,4},{12,16},{16,12},{20,24},{24,20},{28,0},{1,29},{... | collective-permute-start | bytes 307208 | tf_op jit(solution)/shard_map/ppermute | solution.py:561
  7.8 1.8 %collective-permute-start.1 = (bf16[400,128]{1,0:T(8,128)(2,1)S(1)}, bf16[400,128]{1,0:T(8,128)(2,1)S(1)}, u32[]{:S(2)}, u32[]{:S(2)}) collective-permute-start(bf16[400,128]{1,0:T(8,128)(2,1)S(1)} %get-tuple-element.38), channel_id=1, source_target_pairs={{0,4},{4,0},{8,12},{12,8},{16,20},{20,16},{24,28},{28,24},{1,5},{5... | collective-permute-start | bytes 307208 | tf_op jit(solution)/shard_map/ppermute | solution.py:575
  10.1 5.5 %collective-permute-start.2 = (bf16[240,128]{1,0:T(8,128)(2,1)S(1)}, bf16[240,128]{1,0:T(8,128)(2,1)S(1)}, u32[]{:S(2)}, u32[]{:S(2)}) collective-permute-start(bf16[240,128]{1,0:T(8,128)(2,1)S(1)} %get-tuple-element.42), channel_id=1, source_target_pairs={{0,1},{1,0},{2,3},{3,2},{4,5},{5,4},{6,7},{7,6},{8,9},{9,8},{10,11... | collective-permute-start | bytes 184328 | tf_op jit(solution)/shard_map/ppermute | solution.py:599
  12.7 5.1 %collective-permute-start.3 = (bf16[240,128]{1,0:T(8,128)(2,1)S(1)}, bf16[240,128]{1,0:T(8,128)(2,1)S(1)}, u32[]{:S(2)}, u32[]{:S(2)}) collective-permute-start(bf16[240,128]{1,0:T(8,128)(2,1)S(1)} %get-tuple-element.43), channel_id=1, source_target_pairs={{0,3},{1,2},{2,1},{3,0},{4,7},{5,6},{6,5},{7,4},{8,11},{9,10},{10,... | collective-permute-start | bytes 184328 | tf_op jit(solution)/shard_map/ppermute | solution.py:600

commit v18 on v14

--- a/solution.py
+++ b/solution.py
@@ -160,10 +160,13 @@
         quarter_ref[:, lanes] = quarter
         value_ref[:, lanes] = value
         level = cell_ref[2, 0, :, lanes]
-        pushes = [force_ref[c, 0, :, lanes] * value for c in range(comps)]
+        pushes = [twice(force_ref[c, 0, :, lanes] * value) for c in range(comps)]
+        level = jnp.broadcast_to(level.astype(jnp.float32), pushes[0].shape).astype(jnp.bfloat16)
         for l in range(levels):
+            here = level == jnp.array(l, jnp.bfloat16)
             for c in range(comps):
-                force_out[l * comps + c, :, lanes] = twice(jnp.where(level == l, pushes[c], 0.0))
+                push = jnp.where(here, pushes[c], jnp.zeros_like(pushes[c]))
+                force_out[l * comps + c, :, lanes] = push
         quarter, value = tile_weights(offset_y, four_weights(frac_ref[1, 0, :, lanes]))
         quarter_y_ref[:, lanes] = quarter
         value_y_ref[:, lanes] = value
@@ -536,7 +539,7 @@
     arrays = (fish_owner, velocity, marker_cell, marker_frac, marker_force)
     far_half, far, force, dense_y, quarter, value, quarter_y, value_y, level, parity, near_velocity = (
         pl.pallas_call(
-        functools.partial(far_kernel, shape, slots),
+        functools.partial(far_kernel, shape, min(1024, slots)),
         out_shape=(
             jax.ShapeDtypeStruct(half, jnp.float32),
             edge_x,

time: 20 us -> 20 us (level)
  no operation moved by 1% of the time
where the time goes in v18:
time: 20 us; the launch traced here: 19.9 us
  starting transfers between devices  8.72 us (44%)
  Pallas kernels  7 us (35%)
  waiting for transfers between devices  3.49 us (17%)
  between operations  0.68 us (3%)
    ppermute x1, starting transfers between devices, body(): far_x = lax.ppermute(far, 'gx', far_pairs)  4.56 us
    ppermute x1, starting transfers between devices, body(): near_y = lax.ppermute(near, 'gy', near_pairs)  2.6 us
    pallas_call x1, Pallas kernels, body(): pl.pallas_call(functools.partial(finish_kernel, shape, chunk), out_shape=...  2.19 us
    ppermute x1, waiting for transfers between devices, body(): far_y = lax.ppermute(far, 'gy', far_pairs)  2.18 us
    pallas_call x1, Pallas kernels, body(): pl.pallas_call(functools.partial(far_kernel, shape, min(1024, slots)), ou...  1.65 us
    ppermute x1, starting transfers between devices, body(): far_y = lax.ppermute(far, 'gy', far_pairs)  1.5 us
    pallas_call x1, Pallas kernels, body(): pl.pallas_call(functools.partial(inner_kernel, shape, chunk, levels), out...  1.42 us
    ppermute x1, waiting for transfers between devices, body(): far_x = lax.ppermute(far, 'gx', far_pairs)  1.3 us
  transfers between devices with their start and end apart: 4, of which 2 were waited for; matrix products, arithmetic and copies ran while one was open for 0% of the time, Pallas kernels for 13%

profile of v18, /device:TPU:0, one launch (start us, length us, event | category | flops | bytes accessed | tf_op | source)
XLA Modules:
  0.0 19.9 jit_solution(17144286729576979355)
XLA Ops:
  0.6 1.7 %spread_far.1 = (f32[8,48,256]{2,1,0:T(8,128)S(1)}, bf16[400,128]{1,0:T(8,128)(2,1)S(1)}, bf16[8,16,2048]{2,1,0:T(8,128)(2,1)S(1)}, bf16[256,2048]{1,0:T(8,128)(...) custom-call(s32[48]{0:T(128)} %fish_hbm.1, ...), custom_call_target="tpu_custom_call" | custom-call | tf_op jit(solution)/shard_map/spread_far/pallas_call | solution.py:541
  2.3 4.6 %collective-permute-start = (bf16[400,128]{1,0:T(8,128)(2,1)S(1)}, bf16[400,128]{1,0:T(8,128)(2,1)S(1)}, u32[]{:S(2)}, u32[]{:S(2)}) collective-permute-start(bf16[400,128]{1,0:T(8,128)(2,1)S(1)} %get-tuple-element.37), channel_id=1, source_target_pairs={{0,28},{4,8},{8,4},{12,16},{16,12},{20,24},{24,20},{28,0},{1,29},{... | collective-permute-start | bytes 307208 | tf_op jit(solution)/shard_map/ppermute | solution.py:565
  6.8 0.8 %spread_near.1 = (f32[8,96,256]{2,1,0:T(8,128)S(1)}, bf16[400,128]{1,0:T(8,128)(2,1)S(1)}) custom-call(f32[4,2,64,128]{3,2,1,0:T(8,128)S(1)} %get-tuple-element.32.velocity_ref, f32[8,48,256]{2,1,0:T(8,128)S(1)} %get-tuple-element.33.far_half_ref, bf16[8,16,2048]{2,1,0:T(8,128)(2,1)S(1)} %get-tuple-element.34.force_ref, ...), custom_call_target="tpu_custom_call" | custom-call | flops 402653184 | bytes 786432 | tf_op jit(solution)/shard_map/spread_near/pallas_call | solution.py:566
  7.6 0.1 collective-permute-start.1
  7.7 0.4 %weights.1 = (bf16[512,2048]{1,0:T(8,128)(2,1)S(1)}, bf16[512,2048]{1,0:T(8,128)(2,1)S(1)}, s32[2,128]{1,0:T(2,128)S(1)}) custom-call(s32[2,128]{1,0:T(2,128)S(1)} %get-tuple-element.23.parity_ref, s32[8,2048]{1,0:T(8,128)S(1)} %get-tuple-element.24.quarter_ref, f32[8,2048]{1,0:T(8,128)S(1)} %get-tuple-element.25.value_ref, ...), custom_call_target="tpu_custom_call" | custom-call | flops 2097152 | bytes 4194304 | tf_op jit(solution)/shard_map/weights/pallas_call | solution.py:581
  8.2 1.3 %collective-permute-done.far_x = bf16[400,128]{1,0:T(8,128)(2,1)S(1)} collective-permute-done((bf16[400,128]{1,0:T(8,128)(2,1)S(1)}, bf16[400,128]{1,0:T(8,128)(2,1)S(1)}, u32[]{:S(2)}, u32[]{:S(2)}) %collective-permute-start) | collective-permute-done | bytes 102432 | tf_op jit(solution)/shard_map/ppermute | solution.py:565
  9.5 0.0 collective-permute-done.1.near_x
  9.5 0.5 %pack.1 = (bf16[240,128]{1,0:T(8,128)(2,1)S(1)}, bf16[240,128]{1,0:T(8,128)(2,1)S(1)}) custom-call(s32[2,128]{1,0:T(2,128)S(1)} %get-tuple-element.27.parity_ref, f32[8,96,256]{2,1,0:T(8,128)S(1)} %get-tuple-element.36.grid_ref, bf16[400,128]{1,0:T(8,128)(2,1)S(1)} %collective-permute-done.far_x, bf16[400,128]{1,0:T(8,128)(2,1)S(1)} %collective-permute-done.1.near_x), custom_call_target="tpu_custom_call" | custom-call | tf_op jit(solution)/shard_map/pack/pallas_call | solution.py:594
  10.0 2.6 %collective-permute-start.2 = (bf16[240,128]{1,0:T(8,128)(2,1)S(1)}, bf16[240,128]{1,0:T(8,128)(2,1)S(1)}, u32[]{:S(2)}, u32[]{:S(2)}) collective-permute-start(bf16[240,128]{1,0:T(8,128)(2,1)S(1)} %get-tuple-element.42), channel_id=1, source_target_pairs={{0,1},{1,0},{2,3},{3,2},{4,5},{5,4},{6,7},{7,6},{8,9},{9,8},{10,11... | collective-permute-start | bytes 184328 | tf_op jit(solution)/shard_map/ppermute | solution.py:603
  12.6 1.5 %collective-permute-start.3 = (bf16[240,128]{1,0:T(8,128)(2,1)S(1)}, bf16[240,128]{1,0:T(8,128)(2,1)S(1)}, u32[]{:S(2)}, u32[]{:S(2)}) collective-permute-start(bf16[240,128]{1,0:T(8,128)(2,1)S(1)} %get-tuple-element.43), channel_id=1, source_target_pairs={{0,3},{1,2},{2,1},{3,0},{4,7},{5,6},{6,5},{7,4},{8,11},{9,10},{10,... | collective-permute-start | bytes 184328 | tf_op jit(solution)/shard_map/ppermute | solution.py:604
  14.1 1.4 %inner.1 = (f32[8,64,128]{2,1,0:T(8,128)S(1)}, f32[8,112,128]{2,1,0:T(8,128)S(1)}, f32[2,2048]{1,0:T(2,128)S(1)}) custom-call(s32[2,128]{1,0:T(2,128)S(1)} %get-tuple-element.27.parity_ref, s32[8,2048]{1,0:T(8,128)S(1)} %get-tuple-element.28.quarter_ref, f32[8,2048]{1,0:T(8,128)S(1)} %get-tuple-element.29.value_ref, ...), custom_call_target="tpu_custom_call" | custom-call | flops 402653184 | bytes 1835008 | tf_op jit(solution)/shard_map/inner/pallas_call | solution.py:607
  15.5 0.0 collective-permute-done.2.near_y
  15.5 2.2 %collective-permute-done.3.far_y = bf16[240,128]{1,0:T(8,128)(2,1)S(1)} collective-permute-done((bf16[240,128]{1,0:T(8,128)(2,1)S(1)}, bf16[240,128]{1,0:T(8,128)(2,1)S(1)}, u32[]{:S(2)}, u32[]{:S(2)}) %collective-permute-start.3) | collective-permute-done | bytes 61472 | tf_op jit(solution)/shard_map/ppermute | solution.py:604
  17.7 2.2 %finish.1 = (f32[4,2,64,128]{3,2,1,0:T(8,128)}, f32[2,1,1,2048]{3,2,1,0:T(1,128)}) custom-call(s32[2,128]{1,0:T(2,128)S(1)} %get-tuple-element.27.parity_ref, s32[8,2048]{1,0:T(8,128)S(1)} %get-tuple-element.28.quarter_ref, f32[8,2048]{1,0:T(8,128)S(1)} %get-tuple-element.29.value_ref, bf16[512,2048]{1,0:T(8,128)(2,1)S(1)} %get-tuple-element.30.weight_ref, ...), custom_call_target="tpu_custom_call" | custom-call | tf_op jit(solution)/shard_map/finish/pallas_call | solution.py:624
Async XLA Ops:
  2.3 7.2 %collective-permute-start = (bf16[400,128]{1,0:T(8,128)(2,1)S(1)}, bf16[400,128]{1,0:T(8,128)(2,1)S(1)}, u32[]{:S(2)}, u32[]{:S(2)}) collective-permute-start(bf16[400,128]{1,0:T(8,128)(2,1)S(1)} %get-tuple-element.37), channel_id=1, source_target_pairs={{0,28},{4,8},{8,4},{12,16},{16,12},{20,24},{24,20},{28,0},{1,29},{... | collective-permute-start | bytes 307208 | tf_op jit(solution)/shard_map/ppermute | solution.py:565
  7.6 1.8 %collective-permute-start.1 = (bf16[400,128]{1,0:T(8,128)(2,1)S(1)}, bf16[400,128]{1,0:T(8,128)(2,1)S(1)}, u32[]{:S(2)}, u32[]{:S(2)}) collective-permute-start(bf16[400,128]{1,0:T(8,128)(2,1)S(1)} %get-tuple-element.38), channel_id=1, source_target_pairs={{0,4},{4,0},{8,12},{12,8},{16,20},{20,16},{24,28},{28,24},{1,5},{5... | collective-permute-start | bytes 307208 | tf_op jit(solution)/shard_map/ppermute | solution.py:579
  10.0 5.5 %collective-permute-start.2 = (bf16[240,128]{1,0:T(8,128)(2,1)S(1)}, bf16[240,128]{1,0:T(8,128)(2,1)S(1)}, u32[]{:S(2)}, u32[]{:S(2)}) collective-permute-start(bf16[240,128]{1,0:T(8,128)(2,1)S(1)} %get-tuple-element.42), channel_id=1, source_target_pairs={{0,1},{1,0},{2,3},{3,2},{4,5},{5,4},{6,7},{7,6},{8,9},{9,8},{10,11... | collective-permute-start | bytes 184328 | tf_op jit(solution)/shard_map/ppermute | solution.py:603
  12.6 5.1 %collective-permute-start.3 = (bf16[240,128]{1,0:T(8,128)(2,1)S(1)}, bf16[240,128]{1,0:T(8,128)(2,1)S(1)}, u32[]{:S(2)}, u32[]{:S(2)}) collective-permute-start(bf16[240,128]{1,0:T(8,128)(2,1)S(1)} %get-tuple-element.43), channel_id=1, source_target_pairs={{0,3},{1,2},{2,1},{3,0},{4,7},{5,6},{6,5},{7,4},{8,11},{9,10},{10,... | collective-permute-start | bytes 184328 | tf_op jit(solution)/shard_map/ppermute | solution.py:604
